TPU v7x, 32 devices: a whole 2x2x4 slice. The times are simulated.
32 devices in a mesh: grp: 2 (over y), slab: 16 (over z, x, core).
Axes of the slice: x: 2, y: 2, z: 4, core: 2. Of those that a mesh axis runs over, the one named last changes fastest.
Arguments:
- orbital_alpha: bfloat16 [2, 1536, 2560], P('grp', 'slab'), may hold values from -0.75 to 0.75
- orbital_beta: bfloat16 [2, 1536, 2560], P('grp', 'slab'), may hold values from -0.75 to 0.75
- occ_alpha: float32 [2], replicated, may hold values from -2 to -0.3
- occ_beta: float32 [2], replicated, may hold values from -2 to -0.3
- virt_alpha: float32 [1536], replicated, may hold values from 0.1 to 3
- virt_beta: float32 [1536], replicated, may hold values from 0.1 to 3
Outputs:
- grad_alpha: float32 [2, 1536, 2560], P('grp', 'slab')
- grad_beta: float32 [2, 1536, 2560], P('grp', 'slab')
All inputs are finite; a program needn't handle non-finite values.
Results may differ from a plain program's by a relative error of at most 0.0013.
Values may be sent and summed in bfloat16 or wider, within the bound.
No kernel may reach another device: no remote copies, remote signals or barrier semaphores. Data moves between devices by JAX's collectives and lax.ppermute only.
A program may use at most 128 MiB of HBM per device.

v0:
```python
import jax
import jax.numpy as jnp
from jax import lax
from jax.sharding import PartitionSpec as P


def passed_along(value, axis, by):
    length = lax.axis_size(axis)
    return lax.ppermute(value, axis, [(i, (i + by) % length) for i in range(length)])


def body(orbital_alpha, orbital_beta, occ_alpha, occ_beta, virt_alpha, virt_beta):
    groups = lax.axis_size("grp")
    grp_index = lax.axis_index("grp")
    slab_index = lax.axis_index("slab")
    occ_count, virt_width, aux_width = orbital_alpha.shape
    beta_count = orbital_beta.shape[0]
    virt_total = virt_width * lax.axis_size("slab")
    own_virt = lax.dynamic_slice_in_dim(virt_beta, slab_index * virt_width, virt_width, 0)
    own_occ = lax.dynamic_slice_in_dim(occ_alpha, grp_index * occ_count, occ_count, 0)
    piece = lax.all_gather(orbital_alpha, "slab", axis=1, tiled=True)
    block_rows = jnp.einsum(
        "iaq,jbq->aijb", piece, orbital_beta, preferred_element_type=jnp.float32
    )
    panel_beta = orbital_beta
    amps_list = []
    panel_list = []
    beta_accum = jnp.zeros((beta_count, virt_width, aux_width), jnp.float32)
    for section_index in range(groups):
        source = (grp_index - section_index) % groups
        if section_index == 0:
            integrals = block_rows
        else:
            integrals = jnp.einsum(
                "iaq,jbq->aijb", piece, panel_beta, preferred_element_type=jnp.float32
            )
        occ_source = lax.dynamic_slice_in_dim(occ_beta, source * beta_count, beta_count, 0)
        denominator = (
            virt_alpha[:, None, None, None]
            + own_virt[None, None, None, :]
            - own_occ[None, :, None, None]
            - occ_source[None, None, :, None]
        )
        amplitudes = (-integrals / denominator).astype(jnp.bfloat16)
        beta_term = jnp.einsum(
            "aijb,iaq->jbq", amplitudes, piece, preferred_element_type=jnp.float32
        )
        amps_list.append(amplitudes.reshape(virt_total * occ_count, beta_count * virt_width))
        panel_list.append(panel_beta.reshape(beta_count * virt_width, aux_width))
        beta_accum = passed_along(beta_accum + beta_term, "grp", 1)
        if section_index + 1 < groups:
            panel_beta = passed_along(panel_beta, "grp", 1)
    amps_joined = jnp.concatenate(amps_list, axis=1)
    panels_joined = jnp.concatenate(panel_list, axis=0)
    partial_value = jnp.dot(amps_joined, panels_joined, preferred_element_type=jnp.float32)
    summed = lax.psum_scatter(partial_value, "slab", scatter_dimension=0, tiled=True)
    grad_alpha = jnp.transpose(summed.reshape(virt_width, occ_count, aux_width), (1, 0, 2))
    return (grad_alpha, beta_accum)


def solution(mesh):
    in_specs = (P("grp", "slab", None), P("grp", "slab", None), P(), P(), P(), P())
    out_specs = (P("grp", "slab", None), P("grp", "slab", None))
    return jax.shard_map(body, mesh=mesh, in_specs=in_specs, out_specs=out_specs, check_vma=False)
```

profile of v0, /device:TPU:0, one launch (start us, length us, event | category | flops | bytes accessed | tf_op | source)
XLA Modules:
  0.0 267.5 jit_solution(10380967631541708868)
XLA Ops:
  7.2 0.0 copy-start.2
  7.2 0.0 all-gather.2.cloned.1.call-start
  7.2 0.7 all-gather.2.cloned.1.call-update
  7.9 0.0 reduce-scatter.2.cloned.1.call-start
  8.0 3.0 %collective-permute-start = (bf16[1,96,2560]{2,1,0:T(8,128)(2,1)}, bf16[1,96,2560]{2,1,0:T(8,128)(2,1)S(1)}, u32[]{:S(2)}, u32[]{:S(2)}) collective-permute-start(bf16[1,96,2560]{2,1,0:T(8,128)(2,1)} %param.7), channel_id=1, source_target_pairs={{0,16},{16,0},{1,17},{17,1},{2,18},{18,2},{3,19},{19,3},{4,20},{20... | collective-permute-start | bytes 1474568 | tf_op jit(solution)/shard_map/ppermute | solution.py:9
  11.0 0.8 dynamic_slice.12
  11.8 1.3 dynamic_slice.13
  13.0 1.3 fusion.57
  14.3 70.3 %all-gather.2.cloned.1.call-done = bf16[1,1536,2560]{2,1,0:T(8,128)(2,1)} async-done(((bf16[1,96,2560]{2,1,0:T(8,128)(2,1)}), bf16[1,1536,2560]{2,1,0:T(8,128)(2,1)}) %all-gather.2.cloned.1.call-update) | async-done | bytes 7864336 | tf_op jit(solution)/shard_map/all_gather | solution.py:21
  84.6 0.0 copy-start
  84.6 0.0 copy-start.1
  84.6 8.2 %fusion.44 = bf16[1536,96]{0,1:T(8,128)(2,1)S(1)} fusion(bf16[1,1536,2560]{2,1,0:T(8,128)(2,1)} %all-gather.2.cloned.1.call-done, f32[]{:T(128)} %bitcast.5, f32[]{:T(128)} %bitcast.4, f32[96]{0:T(128)S(1)} %dynamic_slice.12, f32[1536]{0:T(1024)} %param.10, bf16[1,96,2560]{2,1,0:T(8,128)(2,1)} %param.7), kind=kOutput, calls=%fused_computation.20 | convolution fusion | flops 755859456 | bytes 8657288 | tf_op jit(solution)/shard_map/iaq,jbq->aijb/dot_general | solution.py:22
  92.8 0.0 collective-permute-done
  92.8 0.0 copy-done.2
  92.8 0.0 copy-done
  92.8 3.8 %fusion.35 = bf16[1536,96]{0,1:T(8,128)(2,1)S(1)} fusion(bf16[1,1536,2560]{2,1,0:T(8,128)(2,1)S(1)} %copy-done, f32[]{:T(128)} %bitcast.11, f32[]{:T(128)} %bitcast.4, f32[96]{0:T(128)S(1)} %dynamic_slice.12, f32[1536]{0:T(1024)S(1)} %copy-done.2, bf16[1,96,2560]{2,1,0:T(8,128)(2,1)S(1)} %collective-permute-done), kind=kOutput, calls=%fused_computation.17 | convolution fusion | flops 755859456 | bytes 8657288 | tf_op jit(solution)/shard_map/iaq,jbq->aijb/dot_general | solution.py:34
  96.6 0.0 copy-done.1
  96.6 7.8 %fusion.47 = f32[1536,2560]{1,0:T(8,128)} fusion(bf16[96,2560]{1,0:T(8,128)(2,1)S(1)} %bitcast.80, bf16[96,2560]{1,0:T(8,128)(2,1)S(1)} %bitcast.79, bf16[1536,96]{0,1:T(8,128)(2,1)S(1)} %fusion.35, bf16[1536,96]{0,1:T(8,128)(2,1)S(1)} %fusion.44), kind=kOutput, calls=%fused_computation.21 | convolution fusion | flops 1513095168 | bytes 17301504 | tf_op jit(solution)/shard_map/dot_general | solution.py:55
  104.4 0.0 reduce-scatter.2.cloned.1.call-update
  104.4 4.6 %fusion.8 = f32[1,96,2560]{2,1,0:T(8,128)S(1)} fusion(bf16[1536,96]{0,1:T(8,128)(2,1)S(1)} %fusion.44, bf16[1,1536,2560]{2,1,0:T(8,128)(2,1)} %all-gather.2.cloned.1.call-done), kind=kOutput, calls=%fused_computation.8 | convolution fusion | flops 754974720 | bytes 9142272 | tf_op jit(solution)/shard_map/aijb,iaq->jbq/dot_general | solution.py:45
  109.0 1.5 collective-permute-start.1
  110.5 22.4 %collective-permute-done.1 = f32[1,96,2560]{2,1,0:T(8,128)S(1)} collective-permute-done((f32[1,96,2560]{2,1,0:T(8,128)S(1)}, f32[1,96,2560]{2,1,0:T(8,128)S(1)}, u32[]{:S(2)}, u32[]{:S(2)}) %collective-permute-start.1) | collective-permute-done | bytes 983072 | tf_op jit(solution)/shard_map/ppermute | solution.py:9
  133.0 4.6 %fusion.14 = f32[1,96,2560]{2,1,0:T(8,128)S(1)} fusion(f32[1,96,2560]{2,1,0:T(8,128)S(1)} %collective-permute-done.1, bf16[1536,96]{0,1:T(8,128)(2,1)S(1)} %fusion.35, bf16[1,1536,2560]{2,1,0:T(8,128)(2,1)} %all-gather.2.cloned.1.call-done), kind=kOutput, calls=%fused_computation.10 | convolution fusion | flops 755220480 | bytes 10125312 | tf_op jit(solution)/shard_map/aijb,iaq->jbq/dot_general | solution.py:45
  137.6 1.5 collective-permute-start.2
  139.1 21.6 %collective-permute-done.2 = f32[1,96,2560]{2,1,0:T(8,128)S(1)} collective-permute-done((f32[1,96,2560]{2,1,0:T(8,128)S(1)}, f32[1,96,2560]{2,1,0:T(8,128)S(1)}, u32[]{:S(2)}, u32[]{:S(2)}) %collective-permute-start.2) | collective-permute-done | bytes 983072 | tf_op jit(solution)/shard_map/ppermute | solution.py:9
  160.7 99.0 %reduce-scatter.2.cloned.1.call-done = f32[96,2560]{1,0:T(8,128)} async-done(((f32[1536,2560]{1,0:T(8,128)}), f32[96,2560]{1,0:T(8,128)}) %reduce-scatter.2.cloned.1.call-update) | async-done | bytes 983056 | tf_op jit(solution)/shard_map/reduce_scatter | solution.py:56
  259.7 0.9 copy.10
Async XLA Ops:
  7.2 85.6 %copy-start.2 = (f32[1536]{0:T(1024)S(1)}, f32[1536]{0:T(1024)}, u32[]{:S(2)}) copy-start(f32[1536]{0:T(1024)} %param.10) | copy-start | bytes 18436
  7.2 77.4 %all-gather.2.cloned.1.call-start = ((), (), s32[]{:S(2)}) async-start(), calls=%async_computation.1 | async-start | bytes 8355840 | tf_op jit(solution)/shard_map/all_gather | solution.py:21
  7.9 251.8 %reduce-scatter.2.cloned.1.call-start = ((), (), s32[]{:S(2)}) async-start(), calls=%async_computation.2 | async-start | bytes 16711680 | tf_op jit(solution)/shard_map/reduce_scatter | solution.py:56
  8.0 84.8 %collective-permute-start = (bf16[1,96,2560]{2,1,0:T(8,128)(2,1)}, bf16[1,96,2560]{2,1,0:T(8,128)(2,1)S(1)}, u32[]{:S(2)}, u32[]{:S(2)}) collective-permute-start(bf16[1,96,2560]{2,1,0:T(8,128)(2,1)} %param.7), channel_id=1, source_target_pairs={{0,16},{16,0},{1,17},{17,1},{2,18},{18,2},{3,19},{19,3},{4,20},{20... | collective-permute-start | bytes 1474568 | tf_op jit(solution)/shard_map/ppermute | solution.py:9
  84.6 8.2 %copy-start = (bf16[1,1536,2560]{2,1,0:T(8,128)(2,1)S(1)}, bf16[1,1536,2560]{2,1,0:T(8,128)(2,1)}, u32[]{:S(2)}) copy-start(bf16[1,1536,2560]{2,1,0:T(8,128)(2,1)} %all-gather.2.cloned.1.call-done) | copy-start | bytes 23592964
  84.6 12.0 %copy-start.1 = (bf16[1,96,2560]{2,1,0:T(8,128)(2,1)S(1)}, bf16[1,96,2560]{2,1,0:T(8,128)(2,1)}, u32[]{:S(2)}) copy-start(bf16[1,96,2560]{2,1,0:T(8,128)(2,1)} %param.7) | copy-start | bytes 1474564
  109.0 24.0 %collective-permute-start.1 = (f32[1,96,2560]{2,1,0:T(8,128)S(1)}, f32[1,96,2560]{2,1,0:T(8,128)S(1)}, u32[]{:S(2)}, u32[]{:S(2)}) collective-permute-start(f32[1,96,2560]{2,1,0:T(8,128)S(1)} %fusion.8), channel_id=1, source_target_pairs={{0,16},{16,0},{1,17},{17,1},{2,18},{18,2},{3,19},{19,3},{4,20},{20... | collective-permute-start | bytes 2949128 | tf_op jit(solution)/shard_map/ppermute | solution.py:9
  137.6 23.2 %collective-permute-start.2 = (f32[1,96,2560]{2,1,0:T(8,128)S(1)}, f32[1,96,2560]{2,1,0:T(8,128)S(1)}, u32[]{:S(2)}, u32[]{:S(2)}) collective-permute-start(f32[1,96,2560]{2,1,0:T(8,128)S(1)} %fusion.14), channel_id=1, source_target_pairs={{0,16},{16,0},{1,17},{17,1},{2,18},{18,2},{3,19},{19,3},{4,20},{20... | collective-permute-start | bytes 2949128 | tf_op jit(solution)/shard_map/ppermute | solution.py:9
Sparse Core Ops, SparseCore 0:
  10.3 74.2 all-gather.1
  104.5 155.1 reduce-scatter.1
where the time goes:
time: 268 us
  waiting for transfers between devices  214 us (80%)
  matrix products  28.9 us (11%)
  between operations  14.1 us (5%)
  starting transfers between devices  6.19 us (2%)
  local copies, waits for them, and re-layouts  4.31 us (2%)
    reduce_scatter x1, waiting for transfers between devices, body(): lax.psum_scatter(partial_value, 'slab', scatter_dimension=0, tiled=True)  99 us
    all_gather x1, waiting for transfers between devices, body(): piece = lax.all_gather(orbital_alpha, 'slab', axis=1, tiled=True)  70.3 us
    ppermute x3, waiting for transfers between devices, passed_along(): lax.ppermute(value, axis, [(i, (i + by) % length) for i in range(length)])  44.1 us
    dot_general x2, matrix products, body(): jnp.einsum('aijb,iaq->jbq', amplitudes, piece, preferred_element_type=jnp...  9.22 us
    dot_general x1, matrix products, body(): jnp.einsum('iaq,jbq->aijb', piece, orbital_beta, preferred_element_type=j...  8.15 us
    dot_general x1, matrix products, body(): jnp.dot(amps_joined, panels_joined, preferred_element_type=jnp.float32)  7.76 us
    ppermute x3, starting transfers between devices, passed_along(): lax.ppermute(value, axis, [(i, (i + by) % length) for i in range(length)])  6.11 us
  transfers between devices with their start and end apart: 5, of which 4 were waited for; matrix products, arithmetic and copies ran while one was open for 8% of the time, Pallas kernels for 0%

commit v1 on v0

v1 whole, which is shorter than its diff:
```python
import functools

import jax
import jax.numpy as jnp
from jax import lax
from jax.experimental import pallas as pl
from jax.experimental.pallas import tpu as pltpu
from jax.sharding import PartitionSpec as P

VMEM_BYTES = 44 * 1024 * 1024


def bits_of(groups, slabs):
    slab_bits = slabs.bit_length() - 1
    total = (groups * slabs).bit_length() - 1
    shared = min(slab_bits - 1, total // 2)
    alpha = list(range(shared, 0, -1))
    beta = list(range(total - 1, slab_bits - 1, -1))
    beta = list(range(slab_bits - 1, shared, -1)) + beta + [0]
    return alpha, beta


def exchange(value, bit, devices):
    return lax.ppermute(value, ("grp", "slab"), [(d, d ^ (1 << bit)) for d in range(devices)])


def gathered(own, bits, devices):
    pieces = {0: own}
    for bit in bits:
        pieces.update({m | (1 << bit): exchange(v, bit, devices) for m, v in list(pieces.items())})
    return pieces


def contract_first(n_a, n_b, width, *refs):
    a_refs, b_refs = refs[:n_a], refs[n_a:n_a + n_b]
    va, oa, vb, ob = refs[n_a + n_b:n_a + n_b + 4]
    outs = refs[n_a + n_b + 4:]
    t_ref, bcat, gb = outs[0], outs[1], outs[2:2 + n_b]
    acat, tt = outs[2 + n_b:]
    aux = acat.shape[1]
    for p in range(n_a):
        acat[p * width:(p + 1) * width, :] = a_refs[p][...]
    for p in range(n_b):
        bcat[p * width:(p + 1) * width, :] = b_refs[p][...]
    cols = n_b * width
    step = 256 if cols % 256 == 0 else width
    for c in range(0, cols, step):
        integrals = lax.dot_general(
            acat[...], bcat[c:c + step, :], (((1,), (1,)), ((), ())), preferred_element_type=jnp.float32
        )
        den = ((va[...] + vb[:, c:c + step]) - oa[...]) - ob[:, c:c + step]
        amps = (-integrals / den).astype(jnp.bfloat16)
        t_ref[:, c:c + step] = amps
        tt[c:c + step, :] = amps.T
    tile = 512 if aux % 512 == 0 else 128

    def one(k, _):
        at = pl.ds(pl.multiple_of(k * tile, tile), tile)
        acc = jnp.dot(tt[...], acat[:, at], preferred_element_type=jnp.float32)
        for p in range(n_b):
            gb[p][:, at] = acc[p * width:(p + 1) * width, :]
        return 0

    lax.fori_loop(0, aux // tile, one, 0)


def contract_second(n_a, width, t_ref, bcat, *ga):
    aux = bcat.shape[1]
    tile = 512 if aux % 512 == 0 else 128

    def one(k, _):
        at = pl.ds(pl.multiple_of(k * tile, tile), tile)
        acc = jnp.dot(t_ref[...], bcat[:, at], preferred_element_type=jnp.float32)
        for p in range(n_a):
            ga[p][:, at] = acc[p * width:(p + 1) * width, :]
        return 0

    lax.fori_loop(0, aux // tile, one, 0)


def body(orbital_alpha, orbital_beta, occ_alpha, occ_beta, virt_alpha, virt_beta):
    groups, slabs = lax.axis_size("grp"), lax.axis_size("slab")
    devices = groups * slabs
    me = lax.axis_index("grp") * slabs + lax.axis_index("slab")
    own_occ, width, aux = orbital_alpha.shape
    own_a = orbital_alpha.reshape(own_occ * width, aux)
    own_b = orbital_beta.reshape(own_occ * width, aux)
    width = own_occ * width
    alpha_bits, beta_bits = bits_of(groups, slabs)

    def energies(masks, virt, occ):
        v_parts, o_parts = [], []
        for m in masks:
            other = jnp.bitwise_xor(me, m)
            slab, grp = other % slabs, other // slabs
            v = lax.dynamic_slice_in_dim(virt, slab * (width // own_occ), width // own_occ, 0)
            o = lax.dynamic_slice_in_dim(occ, grp * own_occ, own_occ, 0)
            v_parts.append(jnp.tile(v, own_occ))
            o_parts.append(jnp.repeat(o, width // own_occ))
        return jnp.concatenate(v_parts), jnp.concatenate(o_parts)

    wide_a, wide_b = own_a.astype(jnp.float32), own_b.astype(jnp.float32)
    stats = jnp.stack([
        jnp.max(jnp.sum(wide_a * wide_a, axis=1)),
        jnp.max(jnp.sum(wide_b * wide_b, axis=1)),
        jnp.maximum(jnp.max(jnp.abs(wide_a)), jnp.max(jnp.abs(wide_b))),
    ])
    stats = jnp.broadcast_to(stats[:, None], (3, 128))
    for bit in sorted(alpha_bits + beta_bits):
        stats = jnp.maximum(stats, exchange(stats, bit, devices))
    smallest = jnp.min(virt_alpha) + jnp.min(virt_beta) - jnp.max(occ_alpha) - jnp.max(occ_beta)
    summed = slabs * groups * width
    bound = jnp.sqrt(stats[0, 0]) * jnp.sqrt(stats[1, 0]) / smallest * stats[2, 0] * summed
    scale = 32768.0 / jnp.maximum(bound, 2e-34)
    unscale = jnp.maximum(bound, 2e-34) / 32768.0

    pieces_a = gathered(own_a, alpha_bits, devices)
    pieces_b = gathered(own_b, beta_bits, devices)
    masks_a, masks_b = sorted(pieces_a), sorted(pieces_b)
    n_a, n_b = len(masks_a), len(masks_b)
    va, oa = energies(masks_a, virt_alpha, occ_alpha)
    vb, ob = energies(masks_b, virt_beta, occ_beta)
    rows, cols = n_a * width, n_b * width
    piece = jax.ShapeDtypeStruct((width, aux), jnp.float32)
    first = pl.pallas_call(
        functools.partial(contract_first, n_a, n_b, width),
        out_shape=[jax.ShapeDtypeStruct((rows, cols), jnp.bfloat16), jax.ShapeDtypeStruct((cols, aux), jnp.bfloat16)]
        + [piece] * n_b,
        scratch_shapes=[pltpu.VMEM((rows, aux), jnp.bfloat16), pltpu.VMEM((cols, rows), jnp.bfloat16)],
        compiler_params=pltpu.CompilerParams(vmem_limit_bytes=VMEM_BYTES),
        cost_estimate=pl.CostEstimate(
            flops=4 * rows * cols * aux, bytes_accessed=(rows + 2 * cols) * aux * 2 + cols * aux * 4, transcendentals=0
        ),
        name="amplitudes_and_beta",
    )(*[pieces_a[m] for m in masks_a], *[pieces_b[m] for m in masks_b], va[:, None], oa[:, None], vb[None, :], ob[None, :])
    amps, bcat = first[0], first[1]
    gb = dict(zip(masks_b, first[2:]))
    ga = dict(zip(masks_a, pl.pallas_call(
        functools.partial(contract_second, n_a, width),
        out_shape=[piece] * n_a,
        compiler_params=pltpu.CompilerParams(vmem_limit_bytes=VMEM_BYTES),
        cost_estimate=pl.CostEstimate(
            flops=2 * rows * cols * aux, bytes_accessed=cols * aux * 2 + rows * aux * 4, transcendentals=0
        ),
        name="alpha",
    )(amps, bcat)))

    def narrow(value):
        return (value * scale).astype(jnp.float16)

    def wide(value):
        return value.astype(jnp.float32) * unscale

    def scattered(parts, bits):
        for bit in bits:
            flag = 1 << bit
            kept = {}
            for m in sorted((m for m in parts if m & flag), reverse=True):
                if bit == 0:
                    arrived = exchange(parts[m], bit, devices)
                else:
                    arrived = wide(exchange(narrow(parts[m]), bit, devices))
                kept[m ^ flag] = parts[m ^ flag] + arrived
            parts = kept
        return parts[0]

    grad_beta = scattered(gb, beta_bits[::-1])
    grad_alpha = scattered(ga, alpha_bits[::-1])
    return (grad_alpha.reshape(orbital_alpha.shape), grad_beta.reshape(orbital_beta.shape))


def solution(mesh):
    in_specs = (P("grp", "slab", None), P("grp", "slab", None), P(), P(), P(), P())
    out_specs = (P("grp", "slab", None), P("grp", "slab", None))
    return jax.shard_map(body, mesh=mesh, in_specs=in_specs, out_specs=out_specs, check_vma=False)
```

time: 268 us -> 142 us (0.53)
  waiting for transfers between devices: 214 us -> 65.6 us
  matrix products: 28.9 us -> 0 us
  starting transfers between devices: 6.19 us -> 26.4 us
  other arithmetic: 0 us -> 14.9 us
  Pallas kernels: 0 us -> 11.9 us
  local copies, waits for them, and re-layouts: 4.31 us -> 15.4 us
  between operations: 14.1 us -> 6.77 us
    reduce_scatter x1 -> x0, waiting for transfers between devices: 99 us -> none  [body(): lax.psum_scatter(partial_value, 'slab', scatter_dimension=0, tiled=True)]
    all_gather x1 -> x0, waiting for transfers between devices: 70.3 us -> none  [body(): piece = lax.all_gather(orbital_alpha, 'slab', axis=1, tiled=True)]
    dot_general x5 -> x0, matrix products: 28.9 us -> none  [the longest x2 9.22 us: body(): jnp.einsum('aijb,iaq->jbq', amplitudes, piece, preferred_element_type=jnp...]
    ppermute x3 -> x25, waiting for transfers between devices: 44.1 us -> 65.6 us  [exchange(): lax.ppermute(value, ('grp', 'slab'), [(d, d ^ 1 << bit) for d in range(de...]
    ppermute x3 -> x25, starting transfers between devices: 6.11 us -> 26.4 us  [exchange(): lax.ppermute(value, ('grp', 'slab'), [(d, d ^ 1 << bit) for d in range(de...]
    pallas_call x0 -> x2, Pallas kernels: none -> 11.9 us  [the longest x1 9.52 us: body(): pl.pallas_call(functools.partial(contract_first, n_a, n_b, width), out_sh...]
    reshape x0 -> x12, local copies, waits for them, and re-layouts: none -> 7.5 us  [energies(): o_parts.append(jnp.repeat(o, width // own_occ))]
    reduce_max x0 -> x4, other arithmetic: none -> 3.84 us  [the longest x1 1.33 us: body(): jnp.max(occ_beta)]
  transfers between devices with their start and end apart: 5 -> 25, of which waited for: 4 -> 10; matrix products, arithmetic and copies ran while one was open for 8% -> 18% of each run, Pallas kernels for 0% -> 2%
where the time goes in v1:
time: 142 us; the launch traced here: 141 us
  waiting for transfers between devices  65.6 us (46%)
  starting transfers between devices  26.4 us (19%)
  local copies, waits for them, and re-layouts  15.4 us (11%)
  other arithmetic  14.9 us (10%)
  Pallas kernels  11.9 us (8%)
  between operations  6.77 us (5%)
    ppermute x25, waiting for transfers between devices, exchange(): lax.ppermute(value, ('grp', 'slab'), [(d, d ^ 1 << bit) for d in range(de...  65.6 us
    ppermute x25, starting transfers between devices, exchange(): lax.ppermute(value, ('grp', 'slab'), [(d, d ^ 1 << bit) for d in range(de...  26.4 us
    pallas_call x1, Pallas kernels, body(): pl.pallas_call(functools.partial(contract_first, n_a, n_b, width), out_sh...  9.52 us
    reshape x12, local copies, waits for them, and re-layouts, energies(): o_parts.append(jnp.repeat(o, width // own_occ))  7.5 us
    unnamed x10, local copies, waits for them, and re-layouts  4.18 us
  transfers between devices with their start and end apart: 25, of which 10 were waited for; matrix products, arithmetic and copies ran while one was open for 18% of the time, Pallas kernels for 2%

profile of v1, /device:TPU:0, one launch (start us, length us, event | category | flops | bytes accessed | tf_op | source)
XLA Modules:
  0.0 141.0 jit_solution(16050901411686055750)
XLA Ops:
  0.6 4.1 %collective-permute-start.4 = (bf16[96,2560]{1,0:T(8,128)(2,1)}, bf16[96,2560]{1,0:T(8,128)(2,1)S(1)}, u32[]{:S(2)}, u32[]{:S(2)}) collective-permute-start(bf16[96,2560]{1,0:T(8,128)(2,1)} %bitcast.30), channel_id=1, source_target_pairs={{0,8},{1,9},{2,10},{3,11},{4,12},{5,13},{6,14},{7,15},{8,0},{9,1},... | collective-permute-start | bytes 1474568 | tf_op jit(solution)/shard_map/ppermute | solution.py:24
  4.7 1.5 %collective-permute-start.6 = (bf16[96,2560]{1,0:T(8,128)(2,1)}, bf16[96,2560]{1,0:T(8,128)(2,1)S(1)}, u32[]{:S(2)}, u32[]{:S(2)}) collective-permute-start(bf16[96,2560]{1,0:T(8,128)(2,1)} %bitcast.31), channel_id=1, source_target_pairs={{0,16},{1,17},{2,18},{3,19},{4,20},{5,21},{6,22},{7,23},{8,24},{9,... | collective-permute-start | bytes 1474568 | tf_op jit(solution)/shard_map/ppermute | solution.py:24
  6.3 1.6 %collective-permute-start.1 = (bf16[96,2560]{1,0:T(8,128)(2,1)}, bf16[96,2560]{1,0:T(8,128)(2,1)S(1)}, u32[]{:S(2)}, u32[]{:S(2)}) collective-permute-start(bf16[96,2560]{1,0:T(8,128)(2,1)} %bitcast.27), channel_id=1, source_target_pairs={{0,4},{1,5},{2,6},{3,7},{4,0},{5,1},{6,2},{7,3},{8,12},{9,13},{10,... | collective-permute-start | bytes 1474568 | tf_op jit(solution)/shard_map/ppermute | solution.py:24
  7.8 1.8 %fusion = (f32[96]{0:T(128)S(1)}, f32[]{:T(128)}) fusion(bf16[1,96,2560]{2,1,0:T(8,128)(2,1)} %param.6), kind=kLoop, calls=%fused_computation.4 | loop fusion | flops 1228703 | bytes 491908 | tf_op jit(solution)/shard_map/reduce_sum | solution.py:104
  10.3 1.7 %fusion.2 = (f32[96]{0:T(128)S(1)}, f32[]{:T(128)}) fusion(bf16[1,96,2560]{2,1,0:T(8,128)(2,1)} %param.7), kind=kLoop, calls=%fused_computation.6 | loop fusion | flops 1228703 | bytes 491908 | tf_op jit(solution)/shard_map/reduce_sum | solution.py:105
  13.9 12.9 %collective-permute-done.4.refs_6_ = bf16[96,2560]{1,0:T(8,128)(2,1)S(1)} collective-permute-done((bf16[96,2560]{1,0:T(8,128)(2,1)}, bf16[96,2560]{1,0:T(8,128)(2,1)S(1)}, u32[]{:S(2)}, u32[]{:S(2)}) %collective-permute-start.4) | collective-permute-done | bytes 491552 | tf_op jit(solution)/shard_map/ppermute | solution.py:24
  26.8 1.6 %collective-permute-start.8 = (bf16[96,2560]{1,0:T(8,128)(2,1)S(1)}, bf16[96,2560]{1,0:T(8,128)(2,1)S(1)}, u32[]{:S(2)}, u32[]{:S(2)}) collective-permute-start(bf16[96,2560]{1,0:T(8,128)(2,1)S(1)} %collective-permute-done.4.refs_6_), channel_id=1, source_target_pairs={{0,16},{1,17},{2,18},{3,19},{4,20},{5,21},{6,22},{7,23},{8,24},{9,... | collective-permute-start | bytes 1474568 | tf_op jit(solution)/shard_map/ppermute | solution.py:24
  28.4 1.3 pad_maximum_fusion.2
  31.0 1.5 %collective-permute-start.11 = (f32[3,128]{1,0:T(4,128)S(1)}, f32[3,128]{1,0:T(4,128)S(1)}, u32[]{:S(2)}, u32[]{:S(2)}) collective-permute-start(f32[3,128]{1,0:T(4,128)S(1)} %broadcast_maximum_fusion), channel_id=1, source_target_pairs={{0,2},{1,3},{2,0},{3,1},{4,6},{5,7},{6,4},{7,5},{8,10},{9,11},{10,... | collective-permute-start | bytes 4616 | tf_op jit(solution)/shard_map/ppermute | solution.py:24
  32.5 2.1 %collective-permute-done.11 = f32[3,128]{1,0:T(4,128)S(1)} collective-permute-done((f32[3,128]{1,0:T(4,128)S(1)}, f32[3,128]{1,0:T(4,128)S(1)}, u32[]{:S(2)}, u32[]{:S(2)}) %collective-permute-start.11) | collective-permute-done | bytes 1568 | tf_op jit(solution)/shard_map/ppermute | solution.py:24
  35.4 2.9 %collective-permute-done.12 = f32[3,128]{1,0:T(4,128)S(1)} collective-permute-done((f32[3,128]{1,0:T(4,128)S(1)}, f32[3,128]{1,0:T(4,128)S(1)}, u32[]{:S(2)}, u32[]{:S(2)}) %collective-permute-start.12) | collective-permute-done | bytes 1568 | tf_op jit(solution)/shard_map/ppermute | solution.py:24
  38.2 2.0 %collective-permute-start.13 = (f32[3,128]{1,0:T(4,128)S(1)}, f32[3,128]{1,0:T(4,128)S(1)}, u32[]{:S(2)}, u32[]{:S(2)}) collective-permute-start(f32[3,128]{1,0:T(4,128)S(1)} %max.25), channel_id=1, source_target_pairs={{0,8},{1,9},{2,10},{3,11},{4,12},{5,13},{6,14},{7,15},{8,0},{9,1},... | collective-permute-start | bytes 4616 | tf_op jit(solution)/shard_map/ppermute | solution.py:24
  40.3 2.5 %collective-permute-done.13 = f32[3,128]{1,0:T(4,128)S(1)} collective-permute-done((f32[3,128]{1,0:T(4,128)S(1)}, f32[3,128]{1,0:T(4,128)S(1)}, u32[]{:S(2)}, u32[]{:S(2)}) %collective-permute-start.13) | collective-permute-done | bytes 1568 | tf_op jit(solution)/shard_map/ppermute | solution.py:24
  43.2 3.1 %collective-permute-done.14 = f32[3,128]{1,0:T(4,128)S(1)} collective-permute-done((f32[3,128]{1,0:T(4,128)S(1)}, f32[3,128]{1,0:T(4,128)S(1)}, u32[]{:S(2)}, u32[]{:S(2)}) %collective-permute-start.14) | collective-permute-done | bytes 1568 | tf_op jit(solution)/shard_map/ppermute | solution.py:24
  46.3 1.5 %collective-permute-start = (bf16[96,2560]{1,0:T(8,128)(2,1)}, bf16[96,2560]{1,0:T(8,128)(2,1)S(1)}, u32[]{:S(2)}, u32[]{:S(2)}) collective-permute-start(bf16[96,2560]{1,0:T(8,128)(2,1)} %bitcast.28), channel_id=1, source_target_pairs={{0,2},{1,3},{2,0},{3,1},{4,6},{5,7},{6,4},{7,5},{8,10},{9,11},{10,... | collective-permute-start | bytes 1474568 | tf_op jit(solution)/shard_map/ppermute | solution.py:24
  48.9 1.3 reduce_max.58
  50.1 1.3 reduce_max.59
  51.4 1.7 %fusion.7 = (f32[1]{0:T(128)}, f32[1]{0:T(128)}, f32[1]{0:T(128)}, f32[1]{0:T(128)}, f32[1]{0:T(128)}, /*index=5*/f32[1]{0:T(128)}, f32[1]{0:T(128)}, f32[1]{0:T...) fusion(f32[2]{0:T(128)} %param.9, s32[]{:T(128)S(6)} %select_n.195, s32[]{:T(128)S(6)} %select_n.193, ...), kind=kLoop, calls=%fused_computation.23 | loop fusion | bytes 140 | tf_op jit(solution)/shard_map/dynamic_slice | solution.py:97
  58.3 1.3 reduce_min.18
  59.6 1.3 reduce_min.19
  72.2 9.5 %amplitudes_and_beta.1 = (bf16[384,768]{1,0:T(8,128)(2,1)S(1)}, bf16[768,2560]{1,0:T(8,128)(2,1)}, f32[96,2560]{1,0:T(8,128)S(1)}, f32[96,2560]{1,0:T(8,128)S(1)...) custom-call(bf16[96,2560]{1,0:T(8,128)(2,1)S(1)} %bitcast.29, ...), custom_call_target="tpu_custom_call" | custom-call | flops 3019898880 | bytes 17694720 | tf_op jit(solution)/shard_map/amplitudes_and_beta/pallas_call | solution.py:125
  82.7 2.1 %copy-done.2 = bf16[768,2560]{1,0:T(8,128)(2,1)S(1)} copy-done((bf16[768,2560]{1,0:T(8,128)(2,1)S(1)}, bf16[768,2560]{1,0:T(8,128)(2,1)}, u32[]{:S(2)}) %copy-start.2) | copy-done | bytes 3932184
  84.9 2.3 %alpha.1 = (f32[96,2560]{1,0:T(8,128)S(1)}, f32[96,2560]{1,0:T(8,128)S(1)}, f32[96,2560]{1,0:T(8,128)S(1)}, f32[96,2560]{1,0:T(8,128)S(1)}) custom-call(bf16[384,768]{1,0:T(8,128)(2,1)S(1)} %get-tuple-element.16.t_ref, bf16[768,2560]{1,0:T(8,128)(2,1)S(1)} %copy-done.2), custom_call_target="tpu_custom_call" | custom-call | flops 1509949440 | bytes 7864320 | tf_op jit(solution)/shard_map/alpha/pallas_call | solution.py:138
  87.3 1.6 %collective-permute-start.16 = (f16[96,2560]{1,0:T(8,128)(2,1)S(1)}, f16[96,2560]{1,0:T(8,128)(2,1)S(1)}, u32[]{:S(2)}, u32[]{:S(2)}) collective-permute-start(f16[96,2560]{1,0:T(8,128)(2,1)S(1)} %multiply_convert_fusion.4), channel_id=1, source_target_pairs={{0,2},{1,3},{2,0},{3,1},{4,6},{5,7},{6,4},{7,5},{8,10},{9,11},{10,... | collective-permute-start | bytes 1474568 | tf_op jit(solution)/shard_map/ppermute | solution.py:24
  89.0 12.0 %collective-permute-done.16 = f16[96,2560]{1,0:T(8,128)(2,1)S(1)} collective-permute-done((f16[96,2560]{1,0:T(8,128)(2,1)S(1)}, f16[96,2560]{1,0:T(8,128)(2,1)S(1)}, u32[]{:S(2)}, u32[]{:S(2)}) %collective-permute-start.16) | collective-permute-done | bytes 491552 | tf_op jit(solution)/shard_map/ppermute | solution.py:24
  101.0 1.5 %collective-permute-start.15 = (f16[96,2560]{1,0:T(8,128)(2,1)S(1)}, f16[96,2560]{1,0:T(8,128)(2,1)S(1)}, u32[]{:S(2)}, u32[]{:S(2)}) collective-permute-start(f16[96,2560]{1,0:T(8,128)(2,1)S(1)} %multiply_convert_fusion.5), channel_id=1, source_target_pairs={{0,2},{1,3},{2,0},{3,1},{4,6},{5,7},{6,4},{7,5},{8,10},{9,11},{10,... | collective-permute-start | bytes 1474568 | tf_op jit(solution)/shard_map/ppermute | solution.py:24
  104.8 1.6 %collective-permute-start.20 = (f16[96,2560]{1,0:T(8,128)(2,1)S(1)}, f16[96,2560]{1,0:T(8,128)(2,1)S(1)}, u32[]{:S(2)}, u32[]{:S(2)}) collective-permute-start(f16[96,2560]{1,0:T(8,128)(2,1)S(1)} %multiply_convert_fusion.2), channel_id=1, source_target_pairs={{0,16},{1,17},{2,18},{3,19},{4,20},{5,21},{6,22},{7,23},{8,24},{9,... | collective-permute-start | bytes 1474568 | tf_op jit(solution)/shard_map/ppermute | solution.py:24
  106.3 11.9 %collective-permute-done.23 = f16[96,2560]{1,0:T(8,128)(2,1)S(1)} collective-permute-done((f16[96,2560]{1,0:T(8,128)(2,1)S(1)}, f16[96,2560]{1,0:T(8,128)(2,1)S(1)}, u32[]{:S(2)}, u32[]{:S(2)}) %collective-permute-start.23) | collective-permute-done | bytes 491552 | tf_op jit(solution)/shard_map/ppermute | solution.py:24
  118.5 3.0 %collective-permute-start.24 = (f16[96,2560]{1,0:T(8,128)(2,1)S(1)}, f16[96,2560]{1,0:T(8,128)(2,1)S(1)}, u32[]{:S(2)}, u32[]{:S(2)}) collective-permute-start(f16[96,2560]{1,0:T(8,128)(2,1)S(1)} %multiply_convert_fusion), channel_id=1, source_target_pairs={{0,8},{1,9},{2,10},{3,11},{4,12},{5,13},{6,14},{7,15},{8,0},{9,1},... | collective-permute-start | bytes 1474568 | tf_op jit(solution)/shard_map/ppermute | solution.py:24
  122.7 4.2 %collective-permute-done.20 = f16[96,2560]{1,0:T(8,128)(2,1)S(1)} collective-permute-done((f16[96,2560]{1,0:T(8,128)(2,1)S(1)}, f16[96,2560]{1,0:T(8,128)(2,1)S(1)}, u32[]{:S(2)}, u32[]{:S(2)}) %collective-permute-start.20) | collective-permute-done | bytes 491552 | tf_op jit(solution)/shard_map/ppermute | solution.py:24
  126.9 12.8 %collective-permute-done.24 = f16[96,2560]{1,0:T(8,128)(2,1)S(1)} collective-permute-done((f16[96,2560]{1,0:T(8,128)(2,1)S(1)}, f16[96,2560]{1,0:T(8,128)(2,1)S(1)}, u32[]{:S(2)}, u32[]{:S(2)}) %collective-permute-start.24) | collective-permute-done | bytes 491552 | tf_op jit(solution)/shard_map/ppermute | solution.py:24
  139.7 1.2 add_bitcast_fusion
  (76 shorter events, 21.5 us)
Async XLA Ops:
  0.6 26.2 %collective-permute-start.4 = (bf16[96,2560]{1,0:T(8,128)(2,1)}, bf16[96,2560]{1,0:T(8,128)(2,1)S(1)}, u32[]{:S(2)}, u32[]{:S(2)}) collective-permute-start(bf16[96,2560]{1,0:T(8,128)(2,1)} %bitcast.30), channel_id=1, source_target_pairs={{0,8},{1,9},{2,10},{3,11},{4,12},{5,13},{6,14},{7,15},{8,0},{9,1},... | collective-permute-start | bytes 1474568 | tf_op jit(solution)/shard_map/ppermute | solution.py:24
  4.7 43.1 %collective-permute-start.6 = (bf16[96,2560]{1,0:T(8,128)(2,1)}, bf16[96,2560]{1,0:T(8,128)(2,1)S(1)}, u32[]{:S(2)}, u32[]{:S(2)}) collective-permute-start(bf16[96,2560]{1,0:T(8,128)(2,1)} %bitcast.31), channel_id=1, source_target_pairs={{0,16},{1,17},{2,18},{3,19},{4,20},{5,21},{6,22},{7,23},{8,24},{9,... | collective-permute-start | bytes 1474568 | tf_op jit(solution)/shard_map/ppermute | solution.py:24
  6.3 42.1 %collective-permute-start.3 = (bf16[96,2560]{1,0:T(8,128)(2,1)}, bf16[96,2560]{1,0:T(8,128)(2,1)S(1)}, u32[]{:S(2)}, u32[]{:S(2)}) collective-permute-start(bf16[96,2560]{1,0:T(8,128)(2,1)} %bitcast.32), channel_id=1, source_target_pairs={{0,1},{1,0},{2,3},{3,2},{4,5},{5,4},{6,7},{7,6},{8,9},{9,8},{10,11... | collective-permute-start | bytes 1474568 | tf_op jit(solution)/shard_map/ppermute | solution.py:24
  6.3 41.6 %collective-permute-start.1 = (bf16[96,2560]{1,0:T(8,128)(2,1)}, bf16[96,2560]{1,0:T(8,128)(2,1)S(1)}, u32[]{:S(2)}, u32[]{:S(2)}) collective-permute-start(bf16[96,2560]{1,0:T(8,128)(2,1)} %bitcast.27), channel_id=1, source_target_pairs={{0,4},{1,5},{2,6},{3,7},{4,0},{5,1},{6,2},{7,3},{8,12},{9,13},{10,... | collective-permute-start | bytes 1474568 | tf_op jit(solution)/shard_map/ppermute | solution.py:24
  26.8 22.1 %collective-permute-start.8 = (bf16[96,2560]{1,0:T(8,128)(2,1)S(1)}, bf16[96,2560]{1,0:T(8,128)(2,1)S(1)}, u32[]{:S(2)}, u32[]{:S(2)}) collective-permute-start(bf16[96,2560]{1,0:T(8,128)(2,1)S(1)} %collective-permute-done.4.refs_6_), channel_id=1, source_target_pairs={{0,16},{1,17},{2,18},{3,19},{4,20},{5,21},{6,22},{7,23},{8,24},{9,... | collective-permute-start | bytes 1474568 | tf_op jit(solution)/shard_map/ppermute | solution.py:24
  29.8 1.2 collective-permute-start.10
  31.0 3.6 %collective-permute-start.11 = (f32[3,128]{1,0:T(4,128)S(1)}, f32[3,128]{1,0:T(4,128)S(1)}, u32[]{:S(2)}, u32[]{:S(2)}) collective-permute-start(f32[3,128]{1,0:T(4,128)S(1)} %broadcast_maximum_fusion), channel_id=1, source_target_pairs={{0,2},{1,3},{2,0},{3,1},{4,6},{5,7},{6,4},{7,5},{8,10},{9,11},{10,... | collective-permute-start | bytes 4616 | tf_op jit(solution)/shard_map/ppermute | solution.py:24
  34.6 3.6 %collective-permute-start.12 = (f32[3,128]{1,0:T(4,128)S(1)}, f32[3,128]{1,0:T(4,128)S(1)}, u32[]{:S(2)}, u32[]{:S(2)}) collective-permute-start(f32[3,128]{1,0:T(4,128)S(1)} %fusion.9), channel_id=1, source_target_pairs={{0,4},{1,5},{2,6},{3,7},{4,0},{5,1},{6,2},{7,3},{8,12},{9,13},{10,... | collective-permute-start | bytes 4616 | tf_op jit(solution)/shard_map/ppermute | solution.py:24
  38.2 4.5 %collective-permute-start.13 = (f32[3,128]{1,0:T(4,128)S(1)}, f32[3,128]{1,0:T(4,128)S(1)}, u32[]{:S(2)}, u32[]{:S(2)}) collective-permute-start(f32[3,128]{1,0:T(4,128)S(1)} %max.25), channel_id=1, source_target_pairs={{0,8},{1,9},{2,10},{3,11},{4,12},{5,13},{6,14},{7,15},{8,0},{9,1},... | collective-permute-start | bytes 4616 | tf_op jit(solution)/shard_map/ppermute | solution.py:24
  42.7 3.6 %collective-permute-start.14 = (f32[3,128]{1,0:T(4,128)S(1)}, f32[3,128]{1,0:T(4,128)S(1)}, u32[]{:S(2)}, u32[]{:S(2)}) collective-permute-start(f32[3,128]{1,0:T(4,128)S(1)} %max.26), channel_id=1, source_target_pairs={{0,16},{1,17},{2,18},{3,19},{4,20},{5,21},{6,22},{7,23},{8,24},{9,... | collective-permute-start | bytes 4616 | tf_op jit(solution)/shard_map/ppermute | solution.py:24
  46.3 23.8 %collective-permute-start = (bf16[96,2560]{1,0:T(8,128)(2,1)}, bf16[96,2560]{1,0:T(8,128)(2,1)S(1)}, u32[]{:S(2)}, u32[]{:S(2)}) collective-permute-start(bf16[96,2560]{1,0:T(8,128)(2,1)} %bitcast.28), channel_id=1, source_target_pairs={{0,2},{1,3},{2,0},{3,1},{4,6},{5,7},{6,4},{7,5},{8,10},{9,11},{10,... | collective-permute-start | bytes 1474568 | tf_op jit(solution)/shard_map/ppermute | solution.py:24
  47.8 22.3 %collective-permute-start.5 = (bf16[96,2560]{1,0:T(8,128)(2,1)S(1)}, bf16[96,2560]{1,0:T(8,128)(2,1)}, u32[]{:S(2)}, u32[]{:S(2)}) collective-permute-start(bf16[96,2560]{1,0:T(8,128)(2,1)S(1)} %collective-permute-done.4.refs_6_), channel_id=1, source_target_pairs={{0,1},{1,0},{2,3},{3,2},{4,5},{5,4},{6,7},{7,6},{8,9},{9,8},{10,11... | collective-permute-start | bytes 1474568 | tf_op jit(solution)/shard_map/ppermute | solution.py:24
  47.8 22.3 %collective-permute-start.7 = (bf16[96,2560]{1,0:T(8,128)(2,1)S(1)}, bf16[96,2560]{1,0:T(8,128)(2,1)}, u32[]{:S(2)}, u32[]{:S(2)}) collective-permute-start(bf16[96,2560]{1,0:T(8,128)(2,1)S(1)} %collective-permute-done.6.refs_8_), channel_id=1, source_target_pairs={{0,1},{1,0},{2,3},{3,2},{4,5},{5,4},{6,7},{7,6},{8,9},{9,8},{10,11... | collective-permute-start | bytes 1474568 | tf_op jit(solution)/shard_map/ppermute | solution.py:24
  48.3 21.8 %collective-permute-start.2 = (bf16[96,2560]{1,0:T(8,128)(2,1)S(1)}, bf16[96,2560]{1,0:T(8,128)(2,1)}, u32[]{:S(2)}, u32[]{:S(2)}) collective-permute-start(bf16[96,2560]{1,0:T(8,128)(2,1)S(1)} %collective-permute-done.1.refs_2_), channel_id=1, source_target_pairs={{0,2},{1,3},{2,0},{3,1},{4,6},{5,7},{6,4},{7,5},{8,10},{9,11},{10,... | collective-permute-start | bytes 1474568 | tf_op jit(solution)/shard_map/ppermute | solution.py:24
  48.9 21.3 %collective-permute-start.9 = (bf16[96,2560]{1,0:T(8,128)(2,1)S(1)}, bf16[96,2560]{1,0:T(8,128)(2,1)}, u32[]{:S(2)}, u32[]{:S(2)}) collective-permute-start(bf16[96,2560]{1,0:T(8,128)(2,1)S(1)} %collective-permute-done.8.refs_10_), channel_id=1, source_target_pairs={{0,1},{1,0},{2,3},{3,2},{4,5},{5,4},{6,7},{7,6},{8,9},{9,8},{10,11... | collective-permute-start | bytes 1474568 | tf_op jit(solution)/shard_map/ppermute | solution.py:24
  70.1 1.0 copy-start
  71.2 1.0 copy-start.1
  81.7 22.3 %collective-permute-start.19 = (f32[96,2560]{1,0:T(8,128)}, f32[96,2560]{1,0:T(8,128)S(1)}, u32[]{:S(2)}, u32[]{:S(2)}) collective-permute-start(f32[96,2560]{1,0:T(8,128)} %get-tuple-element.25), channel_id=1, source_target_pairs={{0,1},{1,0},{2,3},{3,2},{4,5},{5,4},{6,7},{7,6},{8,9},{9,8},{10,11... | collective-permute-start | bytes 2949128 | tf_op jit(solution)/shard_map/ppermute | solution.py:24
  82.2 20.5 %collective-permute-start.22 = (f32[96,2560]{1,0:T(8,128)}, f32[96,2560]{1,0:T(8,128)S(1)}, u32[]{:S(2)}, u32[]{:S(2)}) collective-permute-start(f32[96,2560]{1,0:T(8,128)} %get-tuple-element.29), channel_id=1, source_target_pairs={{0,1},{1,0},{2,3},{3,2},{4,5},{5,4},{6,7},{7,6},{8,9},{9,8},{10,11... | collective-permute-start | bytes 2949128 | tf_op jit(solution)/shard_map/ppermute | solution.py:24
  82.2 22.5 %collective-permute-start.21 = (f32[96,2560]{1,0:T(8,128)}, f32[96,2560]{1,0:T(8,128)S(1)}, u32[]{:S(2)}, u32[]{:S(2)}) collective-permute-start(f32[96,2560]{1,0:T(8,128)} %get-tuple-element.27), channel_id=1, source_target_pairs={{0,1},{1,0},{2,3},{3,2},{4,5},{5,4},{6,7},{7,6},{8,9},{9,8},{10,11... | collective-permute-start | bytes 2949128 | tf_op jit(solution)/shard_map/ppermute | solution.py:24
  82.7 39.9 %collective-permute-start.18 = (f32[96,2560]{1,0:T(8,128)S(1)}, f32[96,2560]{1,0:T(8,128)S(1)}, u32[]{:S(2)}, u32[]{:S(2)}) collective-permute-start(f32[96,2560]{1,0:T(8,128)S(1)} %get-tuple-element.23), channel_id=1, source_target_pairs={{0,1},{1,0},{2,3},{3,2},{4,5},{5,4},{6,7},{7,6},{8,9},{9,8},{10,11... | collective-permute-start | bytes 2949128 | tf_op jit(solution)/shard_map/ppermute | solution.py:24
  82.7 2.1 %copy-start.2 = (bf16[768,2560]{1,0:T(8,128)(2,1)S(1)}, bf16[768,2560]{1,0:T(8,128)(2,1)}, u32[]{:S(2)}) copy-start(bf16[768,2560]{1,0:T(8,128)(2,1)} %get-tuple-element.17.bcat) | copy-start | bytes 11796484
  84.8 19.0 %copy-start.4 = (f32[96,2560]{1,0:T(8,128)S(1)}, f32[96,2560]{1,0:T(8,128)}, u32[]{:S(2)}) copy-start(f32[96,2560]{1,0:T(8,128)} %get-tuple-element.28) | copy-start | bytes 2949124
  87.2 17.4 %copy-start.3 = (f32[96,2560]{1,0:T(8,128)S(1)}, f32[96,2560]{1,0:T(8,128)}, u32[]{:S(2)}) copy-start(f32[96,2560]{1,0:T(8,128)} %get-tuple-element.24) | copy-start | bytes 2949124
  87.3 13.7 %collective-permute-start.16 = (f16[96,2560]{1,0:T(8,128)(2,1)S(1)}, f16[96,2560]{1,0:T(8,128)(2,1)S(1)}, u32[]{:S(2)}, u32[]{:S(2)}) collective-permute-start(f16[96,2560]{1,0:T(8,128)(2,1)S(1)} %multiply_convert_fusion.4), channel_id=1, source_target_pairs={{0,2},{1,3},{2,0},{3,1},{4,6},{5,7},{6,4},{7,5},{8,10},{9,11},{10,... | collective-permute-start | bytes 1474568 | tf_op jit(solution)/shard_map/ppermute | solution.py:24
  101.0 20.4 %collective-permute-start.15 = (f16[96,2560]{1,0:T(8,128)(2,1)S(1)}, f16[96,2560]{1,0:T(8,128)(2,1)S(1)}, u32[]{:S(2)}, u32[]{:S(2)}) collective-permute-start(f16[96,2560]{1,0:T(8,128)(2,1)S(1)} %multiply_convert_fusion.5), channel_id=1, source_target_pairs={{0,2},{1,3},{2,0},{3,1},{4,6},{5,7},{6,4},{7,5},{8,10},{9,11},{10,... | collective-permute-start | bytes 1474568 | tf_op jit(solution)/shard_map/ppermute | solution.py:24
  102.7 18.8 %collective-permute-start.17 = (f16[96,2560]{1,0:T(8,128)(2,1)S(1)}, f16[96,2560]{1,0:T(8,128)(2,1)S(1)}, u32[]{:S(2)}, u32[]{:S(2)}) collective-permute-start(f16[96,2560]{1,0:T(8,128)(2,1)S(1)} %multiply_convert_fusion.3), channel_id=1, source_target_pairs={{0,4},{1,5},{2,6},{3,7},{4,0},{5,1},{6,2},{7,3},{8,12},{9,13},{10,... | collective-permute-start | bytes 1474568 | tf_op jit(solution)/shard_map/ppermute | solution.py:24
  104.0 14.2 %collective-permute-start.23 = (f16[96,2560]{1,0:T(8,128)(2,1)S(1)}, f16[96,2560]{1,0:T(8,128)(2,1)S(1)}, u32[]{:S(2)}, u32[]{:S(2)}) collective-permute-start(f16[96,2560]{1,0:T(8,128)(2,1)S(1)} %multiply_convert_fusion.1), channel_id=1, source_target_pairs={{0,16},{1,17},{2,18},{3,19},{4,20},{5,21},{6,22},{7,23},{8,24},{9,... | collective-permute-start | bytes 1474568 | tf_op jit(solution)/shard_map/ppermute | solution.py:24
  104.8 22.1 %collective-permute-start.20 = (f16[96,2560]{1,0:T(8,128)(2,1)S(1)}, f16[96,2560]{1,0:T(8,128)(2,1)S(1)}, u32[]{:S(2)}, u32[]{:S(2)}) collective-permute-start(f16[96,2560]{1,0:T(8,128)(2,1)S(1)} %multiply_convert_fusion.2), channel_id=1, source_target_pairs={{0,16},{1,17},{2,18},{3,19},{4,20},{5,21},{6,22},{7,23},{8,24},{9,... | collective-permute-start | bytes 1474568 | tf_op jit(solution)/shard_map/ppermute | solution.py:24
  118.5 21.3 %collective-permute-start.24 = (f16[96,2560]{1,0:T(8,128)(2,1)S(1)}, f16[96,2560]{1,0:T(8,128)(2,1)S(1)}, u32[]{:S(2)}, u32[]{:S(2)}) collective-permute-start(f16[96,2560]{1,0:T(8,128)(2,1)S(1)} %multiply_convert_fusion), channel_id=1, source_target_pairs={{0,8},{1,9},{2,10},{3,11},{4,12},{5,13},{6,14},{7,15},{8,0},{9,1},... | collective-permute-start | bytes 1474568 | tf_op jit(solution)/shard_map/ppermute | solution.py:24

commit v2 on v1

v2 whole, which is shorter than its diff:
```python
import functools

import jax
import jax.numpy as jnp
from jax import lax
from jax.experimental import pallas as pl
from jax.experimental.pallas import tpu as pltpu
from jax.sharding import PartitionSpec as P

MIB = 1024 * 1024
together = lax.optimization_barrier


def bits_of(groups, slabs):
    slab_bits = slabs.bit_length() - 1
    total = (groups * slabs).bit_length() - 1
    shared = min(slab_bits - 1, total // 2)
    alpha = list(range(shared, 0, -1))
    beta = list(range(total - 1, slab_bits - 1, -1))
    beta = list(range(slab_bits - 1, shared, -1)) + beta + [0]
    return alpha, beta


def exchange(value, bit, devices):
    return lax.ppermute(value, ("grp", "slab"), [(d, d ^ (1 << bit)) for d in range(devices)])


def prepare(masks_a, masks_b, slabs, per, place, occ_a, occ_b, a_ref, b_ref, va_ref, vb_ref, stats, ninv):
    width = a_ref.shape[0]
    wide_a, wide_b = a_ref[...].astype(jnp.float32), b_ref[...].astype(jnp.float32)
    norm_a = jnp.max(jnp.sum(wide_a * wide_a, axis=1, keepdims=True), axis=0, keepdims=True)
    norm_b = jnp.max(jnp.sum(wide_b * wide_b, axis=1, keepdims=True), axis=0, keepdims=True)
    largest = jnp.maximum(jnp.abs(wide_a), jnp.abs(wide_b))
    largest = jnp.max(jnp.max(largest, axis=1, keepdims=True), axis=0, keepdims=True)
    row = lax.broadcasted_iota(jnp.int32, stats.shape, 0)
    stats[...] = jnp.where(row == 0, norm_a, jnp.where(row == 1, norm_b, largest))
    me = place[0]
    parts, occs = [], []
    for m in masks_b:
        other = jnp.bitwise_xor(me, m)
        for o in range(per):
            parts.append(vb_ref[pl.ds(other % slabs, 1), :])
            occs.append(jnp.full((1, width // per), occ_b[(other // slabs) * per + o], jnp.float32))
    vb, ob = jnp.concatenate(parts, axis=1), jnp.concatenate(occs, axis=1)
    for p, m in enumerate(masks_a):
        other = jnp.bitwise_xor(me, m)
        at = pl.multiple_of((other % slabs) * (width // per), 8)
        va = jnp.concatenate([va_ref[pl.ds(at, width // per), :]] * per, axis=0)
        oa = jnp.concatenate(
            [jnp.full((width // per, 1), occ_a[(other // slabs) * per + o], jnp.float32) for o in range(per)], axis=0
        )
        ninv[p * width:(p + 1) * width, :] = -1.0 / (((va + vb) - oa) - ob)


def contract_amplitudes(n_a, n_b, width, early, *refs):
    a_refs, b_refs, ninv = refs[:n_a], refs[n_a:n_a + n_b], refs[n_a + n_b]
    t_ref, tt, acat, bcat = refs[n_a + n_b + 1:n_a + n_b + 5]
    gb = refs[n_a + n_b + 5:]
    for p in range(n_a):
        acat[p * width:(p + 1) * width, :] = a_refs[p][...]
    for p in range(n_b):
        bcat[p * width:(p + 1) * width, :] = b_refs[p][...]
    cols = n_b * width
    step = 256 if cols % 256 == 0 else width
    for c in range(0, cols, step):
        integrals = lax.dot_general(
            acat[...], bcat[c:c + step, :], (((1,), (1,)), ((), ())), preferred_element_type=jnp.float32
        )
        amps = (integrals * ninv[:, c:c + step]).astype(jnp.bfloat16)
        t_ref[:, c:c + step] = amps
        tt[c:c + step, :] = amps.T
    rows_out(width, early, tt, acat, *gb)


def rows_out(width, span, left, right, *outs):
    aux = right.shape[1]
    tile = 512 if aux % 512 == 0 else 128
    rows = left[span[0] * width:span[1] * width, :]

    def one(k, _):
        at = pl.ds(pl.multiple_of(k * tile, tile), tile)
        acc = jnp.dot(rows, right[:, at], preferred_element_type=jnp.float32)
        for p, out in enumerate(outs):
            out[:, at] = acc[p * width:(p + 1) * width, :]
        return 0

    lax.fori_loop(0, aux // tile, one, 0)


def body(orbital_alpha, orbital_beta, occ_alpha, occ_beta, virt_alpha, virt_beta):
    groups, slabs = lax.axis_size("grp"), lax.axis_size("slab")
    devices = groups * slabs
    me = lax.axis_index("grp") * slabs + lax.axis_index("slab")
    per, block, aux = orbital_alpha.shape
    width = per * block
    own_a, own_b = orbital_alpha.reshape(width, aux), orbital_beta.reshape(width, aux)
    alpha_bits, beta_bits = bits_of(groups, slabs)

    def masks(bits):
        found = [0]
        for bit in bits[::-1]:
            found = found + [m | (1 << bit) for m in found]
        return found[::-1]

    masks_a, masks_b = masks(alpha_bits), masks(beta_bits)
    n_a, n_b = len(masks_a), len(masks_b)
    rows, cols = n_a * width, n_b * width

    pieces_a, pieces_b = {0: own_a}, {0: own_b}
    first_a, first_b = alpha_bits[0], beta_bits[0]
    near_b = exchange(own_b, first_b, devices)
    near_a = exchange(own_a, first_a, devices)
    for bit in alpha_bits[1:]:
        pieces_a.update({m | (1 << bit): exchange(v, bit, devices) for m, v in list(pieces_a.items())})
    for bit in beta_bits[1:-1]:
        pieces_b.update({m | (1 << bit): exchange(v, bit, devices) for m, v in list(pieces_b.items())})

    vmem = pl.BlockSpec(memory_space=pltpu.VMEM)
    smem = pl.BlockSpec(memory_space=pltpu.SMEM)
    stats, ninv = pl.pallas_call(
        functools.partial(prepare, masks_a, masks_b, slabs, per),
        out_shape=[jax.ShapeDtypeStruct((8, 128), jnp.float32), jax.ShapeDtypeStruct((rows, cols), jnp.float32)],
        in_specs=[smem] * 3 + [vmem] * 4,
        compiler_params=pltpu.CompilerParams(vmem_limit_bytes=12 * MIB),
        name="prepare",
    )(me.reshape(1), occ_alpha, occ_beta, own_a, own_b, virt_alpha[:, None], virt_beta.reshape(slabs, block))

    for bit in sorted(alpha_bits + beta_bits):
        stats = jnp.maximum(stats, exchange(stats, bit, devices))

    near_a, near_b, stats, pieces_a, pieces_b = together((near_a, near_b, stats, pieces_a, pieces_b))
    far_a, far_b = {1 << first_a: near_a}, {1 << first_b: near_b}
    for bit in alpha_bits[1:]:
        far_a.update({m | (1 << bit): exchange(v, bit, devices) for m, v in list(far_a.items())})
    for bit in beta_bits[1:-1]:
        far_b.update({m | (1 << bit): exchange(v, bit, devices) for m, v in list(far_b.items())})
    pieces_a.update(far_a)
    pieces_b.update(far_b)
    pieces_b.update({m | 1: exchange(v, 0, devices) for m, v in list(pieces_b.items())})

    smallest = jnp.min(virt_alpha) + jnp.min(virt_beta) - jnp.max(occ_alpha) - jnp.max(occ_beta)
    bound = jnp.sqrt(stats[0, 0]) * jnp.sqrt(stats[1, 0]) / smallest * stats[2, 0] * (devices * width)
    bound = jnp.maximum(bound, 2e-34)
    scale, unscale = 32768.0 / bound, bound / 32768.0

    piece = jax.ShapeDtypeStruct((width, aux), jnp.float32)
    early = min(2, n_b)
    first = pl.pallas_call(
        functools.partial(contract_amplitudes, n_a, n_b, width, (0, early)),
        out_shape=[
            jax.ShapeDtypeStruct((rows, cols), jnp.bfloat16),
            jax.ShapeDtypeStruct((cols, rows), jnp.bfloat16),
            jax.ShapeDtypeStruct((rows, aux), jnp.bfloat16),
            jax.ShapeDtypeStruct((cols, aux), jnp.bfloat16),
        ] + [piece] * early,
        compiler_params=pltpu.CompilerParams(vmem_limit_bytes=24 * MIB),
        cost_estimate=pl.CostEstimate(
            flops=3 * rows * cols * aux, bytes_accessed=2 * (rows + cols) * aux * 2, transcendentals=0
        ),
        name="amplitudes",
    )(*[pieces_a[m] for m in masks_a], *[pieces_b[m] for m in masks_b], ninv)
    t, tt, acat, bcat = first[:4]

    def contracted(left, right, start, stop, name):
        return pl.pallas_call(
            functools.partial(rows_out, width, (start, stop)),
            out_shape=[piece] * (stop - start),
            compiler_params=pltpu.CompilerParams(vmem_limit_bytes=24 * MIB),
            cost_estimate=pl.CostEstimate(
                flops=2 * (stop - start) * width * left.shape[1] * aux,
                bytes_accessed=(stop - start) * width * aux * 4 + right.size * 2, transcendentals=0,
            ),
            name=name,
        )(left, right)

    ga = dict(zip(masks_a, contracted(t, bcat, 0, n_a, "alpha")))
    gb = dict(zip(masks_b, list(first[4:]) + list(contracted(tt, acat, early, n_b, "beta"))))

    def narrow(value):
        return (value * scale).astype(jnp.float16)

    def wide(value):
        return value.astype(jnp.float32) * unscale

    gb = {m: v + exchange(gb[m | 1], 0, devices) for m, v in gb.items() if not m & 1}

    def scattered(parts_a, parts_b, bits_a, bits_b):
        for level in range(max(len(bits_a), len(bits_b))):
            jobs = []
            for parts, bits in ((parts_b, bits_b), (parts_a, bits_a)):
                if level < len(bits):
                    flag = 1 << bits[level]
                    jobs.append((parts, bits[level], [m for m in parts if m & flag]))
            ahead = [[m for m in ms if len(ms) == 1 or m & (1 << bits)] for (_, _, ms), bits in zip(
                jobs, [b[level + 1] if level + 1 < len(b) else 31 for b in (bits_b, bits_a) if level < len(b)])]
            sent = together([[narrow(parts[m]) for m in ms] for (parts, _, _), ms in zip(jobs, ahead)])
            got = [[exchange(v, bit, devices) for v in vs] for (_, bit, _), vs in zip(jobs, sent)]
            rest = [[narrow(parts[m]) for m in ms if m not in first] for (parts, _, ms), first in zip(jobs, ahead)]
            got, rest = together((got, rest))
            late = [[exchange(v, bit, devices) for v in vs] for (_, bit, _), vs in zip(jobs, rest)]
            for (parts, bit, ms), first, arrived, later in zip(jobs, ahead, got, late):
                others = [m for m in ms if m not in first]
                for m, v in list(zip(first, arrived)) + list(zip(others, later)):
                    parts[m ^ (1 << bit)] = parts[m ^ (1 << bit)] + wide(v)
                    del parts[m]
        return parts_a[0], parts_b[0]

    grad_alpha, grad_beta = scattered(ga, gb, alpha_bits[::-1], [b for b in beta_bits[::-1] if b])
    return (grad_alpha.reshape(orbital_alpha.shape), grad_beta.reshape(orbital_beta.shape))


def solution(mesh):
    in_specs = (P("grp", "slab", None), P("grp", "slab", None), P(), P(), P(), P())
    out_specs = (P("grp", "slab", None), P("grp", "slab", None))
    return jax.shard_map(body, mesh=mesh, in_specs=in_specs, out_specs=out_specs, check_vma=False)
```

time: 142 us -> 106 us (0.75)
  waiting for transfers between devices: 65.6 us -> 54.2 us
  local copies, waits for them, and re-layouts: 15.4 us -> 4.6 us
  other arithmetic: 14.9 us -> 5.57 us
  starting transfers between devices: 26.4 us -> 24.4 us
  between operations: 6.77 us -> 5.35 us
    ppermute x25, waiting for transfers between devices: 65.6 us -> 54.2 us  [exchange(): lax.ppermute(value, ('grp', 'slab'), [(d, d ^ 1 << bit) for d in range(de...]
    reshape x12 -> x1, local copies, waits for them, and re-layouts: 7.5 us -> 0.77 us  [body(): virt_beta.reshape(slabs, block)]
    reduce_sum x2 -> x0, other arithmetic: 3.52 us -> none  [the longest x1 1.78 us: body(): jnp.sum(wide_a * wide_a, axis=1)]
    dynamic_slice x2 -> x0, local copies, waits for them, and re-layouts: 2.74 us -> none  [the longest x1 1.66 us: energies(): o = lax.dynamic_slice_in_dim(occ, grp * own_occ, own_occ, 0)]
    ppermute x25, starting transfers between devices: 26.4 us -> 24.4 us  [exchange(): lax.ppermute(value, ('grp', 'slab'), [(d, d ^ 1 << bit) for d in range(de...]
    unnamed x10 -> x16, local copies, waits for them, and re-layouts: 4.18 us -> 2.36 us
    pallas_call x2 -> x4, Pallas kernels: 11.9 us -> 11.7 us  [the longest x1 5.2 us: body(): pl.pallas_call(functools.partial(contract_amplitudes, n_a, n_b, width, (0...]
  transfers between devices with their start and end apart: 25 -> 25, of which waited for: 10 -> 10; matrix products, arithmetic and copies ran while one was open for 18% -> 6% of each run, Pallas kernels for 2% -> 6%
where the time goes in v2:
time: 106 us
  waiting for transfers between devices  54.2 us (51%)
  starting transfers between devices  24.4 us (23%)
  Pallas kernels  11.7 us (11%)
  other arithmetic  5.57 us (5%)
  between operations  5.35 us (5%)
  local copies, waits for them, and re-layouts  4.6 us (4%)
    ppermute x25, waiting for transfers between devices, exchange(): lax.ppermute(value, ('grp', 'slab'), [(d, d ^ 1 << bit) for d in range(de...  54.2 us
    ppermute x25, starting transfers between devices, exchange(): lax.ppermute(value, ('grp', 'slab'), [(d, d ^ 1 << bit) for d in range(de...  24.4 us
    pallas_call x1, Pallas kernels, body(): pl.pallas_call(functools.partial(contract_amplitudes, n_a, n_b, width, (0...  5.2 us
    pallas_call x2, Pallas kernels, contracted(): pl.pallas_call(functools.partial(rows_out, width, (start, stop)), out_sha...  4.79 us
    unnamed x16, local copies, waits for them, and re-layouts  2.36 us
  transfers between devices with their start and end apart: 25, of which 10 were waited for; matrix products, arithmetic and copies ran while one was open for 6% of the time, Pallas kernels for 6%

profile of v2, /device:TPU:0, one launch (start us, length us, event | category | flops | bytes accessed | tf_op | source)
XLA Modules:
  0.0 105.8 jit_solution(274359405874754253)
XLA Ops:
  0.7 3.0 %collective-permute-start.7 = (bf16[96,2560]{1,0:T(8,128)(2,1)}, bf16[96,2560]{1,0:T(8,128)(2,1)S(1)}, u32[]{:S(2)}, u32[]{:S(2)}) collective-permute-start(bf16[96,2560]{1,0:T(8,128)(2,1)} %bitcast.9), channel_id=1, source_target_pairs={{0,2},{1,3},{2,0},{3,1},{4,6},{5,7},{6,4},{7,5},{8,10},{9,11},{10,... | collective-permute-start | bytes 1474568 | tf_op jit(solution)/shard_map/ppermute | solution.py:25
  3.7 1.6 %collective-permute-start = (bf16[96,2560]{1,0:T(8,128)(2,1)}, bf16[96,2560]{1,0:T(8,128)(2,1)S(1)}, u32[]{:S(2)}, u32[]{:S(2)}) collective-permute-start(bf16[96,2560]{1,0:T(8,128)(2,1)} %bitcast.10), channel_id=1, source_target_pairs={{0,4},{1,5},{2,6},{3,7},{4,0},{5,1},{6,2},{7,3},{8,12},{9,13},{10,... | collective-permute-start | bytes 1474568 | tf_op jit(solution)/shard_map/ppermute | solution.py:25
  5.3 1.5 %collective-permute-start.8 = (bf16[96,2560]{1,0:T(8,128)(2,1)}, bf16[96,2560]{1,0:T(8,128)(2,1)}, u32[]{:S(2)}, u32[]{:S(2)}) collective-permute-start(bf16[96,2560]{1,0:T(8,128)(2,1)} %bitcast.1.b_ref.refs_11_), channel_id=1, source_target_pairs={{0,16},{1,17},{2,18},{3,19},{4,20},{5,21},{6,22},{7,23},{8,24},{9,... | collective-permute-start | bytes 1474568 | tf_op jit(solution)/shard_map/ppermute | solution.py:25
  6.8 2.6 %collective-permute-start.1 = (bf16[96,2560]{1,0:T(8,128)(2,1)}, bf16[96,2560]{1,0:T(8,128)(2,1)}, u32[]{:S(2)}, u32[]{:S(2)}) collective-permute-start(bf16[96,2560]{1,0:T(8,128)(2,1)} %bitcast.1.b_ref.refs_11_), channel_id=1, source_target_pairs={{0,8},{1,9},{2,10},{3,11},{4,12},{5,13},{6,14},{7,15},{8,0},{9,1},... | collective-permute-start | bytes 1474568 | tf_op jit(solution)/shard_map/ppermute | solution.py:25
  9.4 0.8 reshape.28.vb_ref
  10.1 1.0 broadcast_in_dim.4.va_ref
  11.1 1.0 copy-done
  12.2 0.7 copy-done.2
  12.8 0.7 copy-done.4
  13.5 1.7 %prepare.1 = (f32[8,128]{1,0:T(8,128)S(1)}, f32[384,768]{1,0:T(8,128)S(1)}) custom-call(s32[1]{0:T(128)} %bitcast.2.place, f32[2]{0:T(128)S(1)} %copy-done.4, f32[2]{0:T(128)S(1)} %copy-done.2, bf16[96,2560]{1,0:T(8,128)(2,1)S(1)} %bitcast.11, bf16[96,2560]{1,0:T(8,128)(2,1)} %bitcast.1.b_ref.refs_11_, f32[1536,1]{1,0:T(8,128)S(1)} %broadcast_in_dim.4.va_ref, ...), custom_call_target="tpu_custom_call" | custom-call | tf_op jit(solution)/shard_map/prepare/pallas_call | solution.py:120
  15.2 1.2 %collective-permute-done.2 = f32[8,128]{1,0:T(8,128)S(1)} collective-permute-done((f32[8,128]{1,0:T(8,128)S(1)}, f32[8,128]{1,0:T(8,128)S(1)}, u32[]{:S(2)}, u32[]{:S(2)}) %collective-permute-start.2) | collective-permute-done | bytes 4128 | tf_op jit(solution)/shard_map/ppermute | solution.py:25
  16.9 3.1 %collective-permute-done.3 = f32[8,128]{1,0:T(8,128)S(1)} collective-permute-done((f32[8,128]{1,0:T(8,128)S(1)}, f32[8,128]{1,0:T(8,128)S(1)}, u32[]{:S(2)}, u32[]{:S(2)}) %collective-permute-start.3) | collective-permute-done | bytes 4128 | tf_op jit(solution)/shard_map/ppermute | solution.py:25
  20.4 6.0 %collective-permute-done.4 = f32[8,128]{1,0:T(8,128)S(1)} collective-permute-done((f32[8,128]{1,0:T(8,128)S(1)}, f32[8,128]{1,0:T(8,128)S(1)}, u32[]{:S(2)}, u32[]{:S(2)}) %collective-permute-start.4) | collective-permute-done | bytes 4128 | tf_op jit(solution)/shard_map/ppermute | solution.py:25
  26.4 3.4 %collective-permute-start.5 = (f32[8,128]{1,0:T(8,128)S(1)}, f32[8,128]{1,0:T(8,128)S(1)}, u32[]{:S(2)}, u32[]{:S(2)}) collective-permute-start(f32[8,128]{1,0:T(8,128)S(1)} %max.20), channel_id=1, source_target_pairs={{0,8},{1,9},{2,10},{3,11},{4,12},{5,13},{6,14},{7,15},{8,0},{9,1},... | collective-permute-start | bytes 12296 | tf_op jit(solution)/shard_map/ppermute | solution.py:25
  29.8 1.6 %collective-permute-done.5 = f32[8,128]{1,0:T(8,128)S(1)} collective-permute-done((f32[8,128]{1,0:T(8,128)S(1)}, f32[8,128]{1,0:T(8,128)S(1)}, u32[]{:S(2)}, u32[]{:S(2)}) %collective-permute-start.5) | collective-permute-done | bytes 4128 | tf_op jit(solution)/shard_map/ppermute | solution.py:25
  31.4 1.5 %collective-permute-start.6 = (f32[8,128]{1,0:T(8,128)S(1)}, f32[8,128]{1,0:T(8,128)S(1)}, u32[]{:S(2)}, u32[]{:S(2)}) collective-permute-start(f32[8,128]{1,0:T(8,128)S(1)} %max.21), channel_id=1, source_target_pairs={{0,16},{1,17},{2,18},{3,19},{4,20},{5,21},{6,22},{7,23},{8,24},{9,... | collective-permute-start | bytes 12296 | tf_op jit(solution)/shard_map/ppermute | solution.py:25
  33.0 2.1 %collective-permute-done.6 = f32[8,128]{1,0:T(8,128)S(1)} collective-permute-done((f32[8,128]{1,0:T(8,128)S(1)}, f32[8,128]{1,0:T(8,128)S(1)}, u32[]{:S(2)}, u32[]{:S(2)}) %collective-permute-start.6) | collective-permute-done | bytes 4128 | tf_op jit(solution)/shard_map/ppermute | solution.py:25
  35.1 1.6 %collective-permute-start.10 = (bf16[96,2560]{1,0:T(8,128)(2,1)}, bf16[96,2560]{1,0:T(8,128)(2,1)S(1)}, u32[]{:S(2)}, u32[]{:S(2)}) collective-permute-start(bf16[96,2560]{1,0:T(8,128)(2,1)} %collective-permute-done.1.refs_7_), channel_id=1, source_target_pairs={{0,16},{1,17},{2,18},{3,19},{4,20},{5,21},{6,22},{7,23},{8,24},{9,... | collective-permute-start | bytes 1474568 | tf_op jit(solution)/shard_map/ppermute | solution.py:25
  37.7 8.0 %collective-permute-done.10.refs_5_ = bf16[96,2560]{1,0:T(8,128)(2,1)S(1)} collective-permute-done((bf16[96,2560]{1,0:T(8,128)(2,1)}, bf16[96,2560]{1,0:T(8,128)(2,1)S(1)}, u32[]{:S(2)}, u32[]{:S(2)}) %collective-permute-start.10) | collective-permute-done | bytes 491552 | tf_op jit(solution)/shard_map/ppermute | solution.py:25
  45.7 0.6 reduce_min.19
  46.3 0.6 reduce_min.18
  47.5 0.7 reduce_max.18
  53.2 5.2 %amplitudes.1 = (bf16[384,768]{1,0:T(8,128)(2,1)S(1)}, bf16[768,384]{1,0:T(8,128)(2,1)S(1)}, bf16[384,2560]{1,0:T(8,128)(2,1)S(1)}, bf16[768,2560]{1,0:T(8,128)(...) custom-call(bf16[96,2560]{1,0:T(8,128)(2,1)} %collective-permute-done.9.refs_0_, ...), custom_call_target="tpu_custom_call" | custom-call | flops 2264924160 | bytes 11796480 | tf_op jit(solution)/shard_map/amplitudes/pallas_call | solution.py:148
  59.0 2.4 %beta.1 = (f32[96,2560]{1,0:T(8,128)S(1)}, f32[96,2560]{1,0:T(8,128)S(1)}, f32[96,2560]{1,0:T(8,128)S(1)}, f32[96,2560]{1,0:T(8,128)S(1)}, f32[96,2560]{1,0:T(8,128)S(1)}, /*index=5*/f32[96,2560]{1,0:T(8,128)S(1)}) custom-call(bf16[768,384]{1,0:T(8,128)(2,1)S(1)} %get-tuple-element.54.left, bf16[384,2560]{1,0:T(8,128)(2,1)S(1)} %get-tuple-element.55.right), custom_call_target="tpu_custom_call" | custom-call | flops 1132462080 | bytes 7864320 | tf_op jit(solution)/shard_map/beta/pallas_call | solution.py:165
  61.5 2.4 %alpha.1 = (f32[96,2560]{1,0:T(8,128)S(1)}, f32[96,2560]{1,0:T(8,128)S(1)}, f32[96,2560]{1,0:T(8,128)S(1)}, f32[96,2560]{1,0:T(8,128)S(1)}) custom-call(bf16[384,768]{1,0:T(8,128)(2,1)S(1)} %get-tuple-element.45.left, bf16[768,2560]{1,0:T(8,128)(2,1)S(1)} %get-tuple-element.46.right), custom_call_target="tpu_custom_call" | custom-call | flops 1509949440 | bytes 7864320 | tf_op jit(solution)/shard_map/alpha/pallas_call | solution.py:165
  64.8 1.6 %collective-permute-start.16 = (f16[96,2560]{1,0:T(8,128)(2,1)S(1)}, f16[96,2560]{1,0:T(8,128)(2,1)S(1)}, u32[]{:S(2)}, u32[]{:S(2)}) collective-permute-start(f16[96,2560]{1,0:T(8,128)(2,1)S(1)} %multiply_convert_fusion.5), channel_id=1, source_target_pairs={{0,16},{1,17},{2,18},{3,19},{4,20},{5,21},{6,22},{7,23},{8,24},{9,... | collective-permute-start | bytes 1474568 | tf_op jit(solution)/shard_map/ppermute | solution.py:25
  67.0 11.0 %collective-permute-done.16 = f16[96,2560]{1,0:T(8,128)(2,1)S(1)} collective-permute-done((f16[96,2560]{1,0:T(8,128)(2,1)S(1)}, f16[96,2560]{1,0:T(8,128)(2,1)S(1)}, u32[]{:S(2)}, u32[]{:S(2)}) %collective-permute-start.16) | collective-permute-done | bytes 491552 | tf_op jit(solution)/shard_map/ppermute | solution.py:25
  78.0 1.2 %collective-permute-done.17 = f16[96,2560]{1,0:T(8,128)(2,1)S(1)} collective-permute-done((f16[96,2560]{1,0:T(8,128)(2,1)S(1)}, f16[96,2560]{1,0:T(8,128)(2,1)S(1)}, u32[]{:S(2)}, u32[]{:S(2)}) %collective-permute-start.17) | collective-permute-done | bytes 491552 | tf_op jit(solution)/shard_map/ppermute | solution.py:25
  79.6 2.3 %collective-permute-start.21 = (f16[96,2560]{1,0:T(8,128)(2,1)S(1)}, f16[96,2560]{1,0:T(8,128)(2,1)S(1)}, u32[]{:S(2)}, u32[]{:S(2)}) collective-permute-start(f16[96,2560]{1,0:T(8,128)(2,1)S(1)} %multiply_convert_fusion.1), channel_id=1, source_target_pairs={{0,8},{1,9},{2,10},{3,11},{4,12},{5,13},{6,14},{7,15},{8,0},{9,1},... | collective-permute-start | bytes 1474568 | tf_op jit(solution)/shard_map/ppermute | solution.py:25
  83.4 19.9 %collective-permute-done.21 = f16[96,2560]{1,0:T(8,128)(2,1)S(1)} collective-permute-done((f16[96,2560]{1,0:T(8,128)(2,1)S(1)}, f16[96,2560]{1,0:T(8,128)(2,1)S(1)}, u32[]{:S(2)}, u32[]{:S(2)}) %collective-permute-start.21) | collective-permute-done | bytes 491552 | tf_op jit(solution)/shard_map/ppermute | solution.py:25
  103.4 1.1 %add_bitcast_fusion.1 = f32[1,96,2560]{2,1,0:T(8,128)} fusion(f16[96,2560]{1,0:T(8,128)(2,1)S(1)} %collective-permute-done.22, f32[96,2560]{1,0:T(8,128)S(1)} %get-tuple-element.47, f16[96,2560]{1,0:T(8,128)(2,1)S(1)} %collective-permute-done.19, f32[]{:T(128)S(6)} %div.11), kind=kLoop, calls=%fused_computation.1 | loop fusion | flops 1474560 | bytes 2949124 | tf_op jit(solution)/shard_map/reshape | solution.py:209
  104.6 1.2 %add_bitcast_fusion = f32[1,96,2560]{2,1,0:T(8,128)} fusion(f16[96,2560]{1,0:T(8,128)(2,1)S(1)} %collective-permute-done.21, f16[96,2560]{1,0:T(8,128)(2,1)S(1)} %collective-permute-done.24, f32[96,2560]{1,0:T(8,128)S(1)} %get-tuple-element.68, f32[96,2560]{1,0:T(8,128)S(1)} %collective-permute-done.23, f32[]{:T(128)S(6)} %div.11), kind=kLoop, calls=%fused_computation | loop fusion | flops 1720320 | bytes 3932164 | tf_op jit(solution)/shard_map/reshape | solution.py:209
  (58 shorter events, 7.4 us)
Async XLA Ops:
  0.6 52.6 %copy-start.1 = (bf16[1,96,2560]{2,1,0:T(8,128)(2,1)S(1)}, bf16[1,96,2560]{2,1,0:T(8,128)(2,1)}, u32[]{:S(2)}) copy-start(bf16[1,96,2560]{2,1,0:T(8,128)(2,1)} %param.6) | copy-start | bytes 1474564
  0.6 45.1 %copy-start.7 = (f32[1536]{0:T(1024)S(1)}, f32[1536]{0:T(1024)}, u32[]{:S(2)}) copy-start(f32[1536]{0:T(1024)} %param.11) | copy-start | bytes 18436
  0.7 45.7 %copy-start.6 = (f32[1536]{0:T(1024)S(1)}, f32[1536]{0:T(1024)}, u32[]{:S(2)}) copy-start(f32[1536]{0:T(1024)} %param.10) | copy-start | bytes 18436
  0.7 46.3 %copy-start.3 = (f32[2]{0:T(128)S(1)}, f32[2]{0:T(128)}, u32[]{:S(2)}) copy-start(f32[2]{0:T(128)} %occ_b.1) | copy-start | bytes 28
  0.7 46.8 %copy-start.5 = (f32[2]{0:T(128)S(1)}, f32[2]{0:T(128)}, u32[]{:S(2)}) copy-start(f32[2]{0:T(128)} %occ_a.1) | copy-start | bytes 28
  0.7 34.4 %collective-permute-start.7 = (bf16[96,2560]{1,0:T(8,128)(2,1)}, bf16[96,2560]{1,0:T(8,128)(2,1)S(1)}, u32[]{:S(2)}, u32[]{:S(2)}) collective-permute-start(bf16[96,2560]{1,0:T(8,128)(2,1)} %bitcast.9), channel_id=1, source_target_pairs={{0,2},{1,3},{2,0},{3,1},{4,6},{5,7},{6,4},{7,5},{8,10},{9,11},{10,... | collective-permute-start | bytes 1474568 | tf_op jit(solution)/shard_map/ppermute | solution.py:25
  3.7 31.4 %collective-permute-start = (bf16[96,2560]{1,0:T(8,128)(2,1)}, bf16[96,2560]{1,0:T(8,128)(2,1)S(1)}, u32[]{:S(2)}, u32[]{:S(2)}) collective-permute-start(bf16[96,2560]{1,0:T(8,128)(2,1)} %bitcast.10), channel_id=1, source_target_pairs={{0,4},{1,5},{2,6},{3,7},{4,0},{5,1},{6,2},{7,3},{8,12},{9,13},{10,... | collective-permute-start | bytes 1474568 | tf_op jit(solution)/shard_map/ppermute | solution.py:25
  5.3 29.8 %collective-permute-start.8 = (bf16[96,2560]{1,0:T(8,128)(2,1)}, bf16[96,2560]{1,0:T(8,128)(2,1)}, u32[]{:S(2)}, u32[]{:S(2)}) collective-permute-start(bf16[96,2560]{1,0:T(8,128)(2,1)} %bitcast.1.b_ref.refs_11_), channel_id=1, source_target_pairs={{0,16},{1,17},{2,18},{3,19},{4,20},{5,21},{6,22},{7,23},{8,24},{9,... | collective-permute-start | bytes 1474568 | tf_op jit(solution)/shard_map/ppermute | solution.py:25
  6.8 28.3 %collective-permute-start.1 = (bf16[96,2560]{1,0:T(8,128)(2,1)}, bf16[96,2560]{1,0:T(8,128)(2,1)}, u32[]{:S(2)}, u32[]{:S(2)}) collective-permute-start(bf16[96,2560]{1,0:T(8,128)(2,1)} %bitcast.1.b_ref.refs_11_), channel_id=1, source_target_pairs={{0,8},{1,9},{2,10},{3,11},{4,12},{5,13},{6,14},{7,15},{8,0},{9,1},... | collective-permute-start | bytes 1474568 | tf_op jit(solution)/shard_map/ppermute | solution.py:25
  11.1 1.0 copy-start
  12.1 0.7 copy-start.2
  15.1 1.2 %collective-permute-start.2 = (f32[8,128]{1,0:T(8,128)S(1)}, f32[8,128]{1,0:T(8,128)S(1)}, u32[]{:S(2)}, u32[]{:S(2)}) collective-permute-start(f32[8,128]{1,0:T(8,128)S(1)} %get-tuple-element.37), channel_id=1, source_target_pairs={{0,1},{1,0},{2,3},{3,2},{4,5},{5,4},{6,7},{7,6},{8,9},{9,8},{10,11... | collective-permute-start | bytes 12296 | tf_op jit(solution)/shard_map/ppermute | solution.py:25
  16.4 3.6 %collective-permute-start.3 = (f32[8,128]{1,0:T(8,128)S(1)}, f32[8,128]{1,0:T(8,128)S(1)}, u32[]{:S(2)}, u32[]{:S(2)}) collective-permute-start(f32[8,128]{1,0:T(8,128)S(1)} %max.18), channel_id=1, source_target_pairs={{0,2},{1,3},{2,0},{3,1},{4,6},{5,7},{6,4},{7,5},{8,10},{9,11},{10,... | collective-permute-start | bytes 12296 | tf_op jit(solution)/shard_map/ppermute | solution.py:25
  20.0 6.4 %collective-permute-start.4 = (f32[8,128]{1,0:T(8,128)S(1)}, f32[8,128]{1,0:T(8,128)S(1)}, u32[]{:S(2)}, u32[]{:S(2)}) collective-permute-start(f32[8,128]{1,0:T(8,128)S(1)} %max.19), channel_id=1, source_target_pairs={{0,4},{1,5},{2,6},{3,7},{4,0},{5,1},{6,2},{7,3},{8,12},{9,13},{10,... | collective-permute-start | bytes 12296 | tf_op jit(solution)/shard_map/ppermute | solution.py:25
  26.4 5.0 %collective-permute-start.5 = (f32[8,128]{1,0:T(8,128)S(1)}, f32[8,128]{1,0:T(8,128)S(1)}, u32[]{:S(2)}, u32[]{:S(2)}) collective-permute-start(f32[8,128]{1,0:T(8,128)S(1)} %max.20), channel_id=1, source_target_pairs={{0,8},{1,9},{2,10},{3,11},{4,12},{5,13},{6,14},{7,15},{8,0},{9,1},... | collective-permute-start | bytes 12296 | tf_op jit(solution)/shard_map/ppermute | solution.py:25
  31.4 3.6 %collective-permute-start.6 = (f32[8,128]{1,0:T(8,128)S(1)}, f32[8,128]{1,0:T(8,128)S(1)}, u32[]{:S(2)}, u32[]{:S(2)}) collective-permute-start(f32[8,128]{1,0:T(8,128)S(1)} %max.21), channel_id=1, source_target_pairs={{0,16},{1,17},{2,18},{3,19},{4,20},{5,21},{6,22},{7,23},{8,24},{9,... | collective-permute-start | bytes 12296 | tf_op jit(solution)/shard_map/ppermute | solution.py:25
  35.1 10.6 %collective-permute-start.10 = (bf16[96,2560]{1,0:T(8,128)(2,1)}, bf16[96,2560]{1,0:T(8,128)(2,1)S(1)}, u32[]{:S(2)}, u32[]{:S(2)}) collective-permute-start(bf16[96,2560]{1,0:T(8,128)(2,1)} %collective-permute-done.1.refs_7_), channel_id=1, source_target_pairs={{0,16},{1,17},{2,18},{3,19},{4,20},{5,21},{6,22},{7,23},{8,24},{9,... | collective-permute-start | bytes 1474568 | tf_op jit(solution)/shard_map/ppermute | solution.py:25
  36.7 16.5 %collective-permute-start.12 = (bf16[96,2560]{1,0:T(8,128)(2,1)}, bf16[96,2560]{1,0:T(8,128)(2,1)}, u32[]{:S(2)}, u32[]{:S(2)}) collective-permute-start(bf16[96,2560]{1,0:T(8,128)(2,1)} %collective-permute-done.1.refs_7_), channel_id=1, source_target_pairs={{0,1},{1,0},{2,3},{3,2},{4,5},{5,4},{6,7},{7,6},{8,9},{9,8},{10,11... | collective-permute-start | bytes 1474568 | tf_op jit(solution)/shard_map/ppermute | solution.py:25
  36.7 16.5 %collective-permute-start.9 = (bf16[96,2560]{1,0:T(8,128)(2,1)S(1)}, bf16[96,2560]{1,0:T(8,128)(2,1)}, u32[]{:S(2)}, u32[]{:S(2)}) collective-permute-start(bf16[96,2560]{1,0:T(8,128)(2,1)S(1)} %collective-permute-done.refs_1_), channel_id=1, source_target_pairs={{0,2},{1,3},{2,0},{3,1},{4,6},{5,7},{6,4},{7,5},{8,10},{9,11},{10,... | collective-permute-start | bytes 1474568 | tf_op jit(solution)/shard_map/ppermute | solution.py:25
  37.2 16.0 %collective-permute-start.13 = (bf16[96,2560]{1,0:T(8,128)(2,1)}, bf16[96,2560]{1,0:T(8,128)(2,1)}, u32[]{:S(2)}, u32[]{:S(2)}) collective-permute-start(bf16[96,2560]{1,0:T(8,128)(2,1)} %collective-permute-done.8.refs_9_), channel_id=1, source_target_pairs={{0,1},{1,0},{2,3},{3,2},{4,5},{5,4},{6,7},{7,6},{8,9},{9,8},{10,11... | collective-permute-start | bytes 1474568 | tf_op jit(solution)/shard_map/ppermute | solution.py:25
  37.4 15.8 %collective-permute-start.14 = (bf16[96,2560]{1,0:T(8,128)(2,1)}, bf16[96,2560]{1,0:T(8,128)(2,1)}, u32[]{:S(2)}, u32[]{:S(2)}) collective-permute-start(bf16[96,2560]{1,0:T(8,128)(2,1)} %bitcast.1.b_ref.refs_11_), channel_id=1, source_target_pairs={{0,1},{1,0},{2,3},{3,2},{4,5},{5,4},{6,7},{7,6},{8,9},{9,8},{10,11... | collective-permute-start | bytes 1474568 | tf_op jit(solution)/shard_map/ppermute | solution.py:25
  45.7 7.5 %collective-permute-start.11 = (bf16[96,2560]{1,0:T(8,128)(2,1)S(1)}, bf16[96,2560]{1,0:T(8,128)(2,1)}, u32[]{:S(2)}, u32[]{:S(2)}) collective-permute-start(bf16[96,2560]{1,0:T(8,128)(2,1)S(1)} %collective-permute-done.10.refs_5_), channel_id=1, source_target_pairs={{0,1},{1,0},{2,3},{3,2},{4,5},{5,4},{6,7},{7,6},{8,9},{9,8},{10,11... | collective-permute-start | bytes 1474568 | tf_op jit(solution)/shard_map/ppermute | solution.py:25
  58.4 6.2 %collective-permute-start.15 = (f32[96,2560]{1,0:T(8,128)S(1)}, f32[96,2560]{1,0:T(8,128)S(1)}, u32[]{:S(2)}, u32[]{:S(2)}) collective-permute-start(f32[96,2560]{1,0:T(8,128)S(1)} %get-tuple-element.49), channel_id=1, source_target_pairs={{0,1},{1,0},{2,3},{3,2},{4,5},{5,4},{6,7},{7,6},{8,9},{9,8},{10,11... | collective-permute-start | bytes 2949128 | tf_op jit(solution)/shard_map/ppermute | solution.py:25
  61.4 5.5 %collective-permute-start.18 = (f32[96,2560]{1,0:T(8,128)S(1)}, f32[96,2560]{1,0:T(8,128)S(1)}, u32[]{:S(2)}, u32[]{:S(2)}) collective-permute-start(f32[96,2560]{1,0:T(8,128)S(1)} %get-tuple-element.57), channel_id=1, source_target_pairs={{0,1},{1,0},{2,3},{3,2},{4,5},{5,4},{6,7},{7,6},{8,9},{9,8},{10,11... | collective-permute-start | bytes 2949128 | tf_op jit(solution)/shard_map/ppermute | solution.py:25
  64.1 15.3 %collective-permute-start.20 = (f32[96,2560]{1,0:T(8,128)S(1)}, f32[96,2560]{1,0:T(8,128)S(1)}, u32[]{:S(2)}, u32[]{:S(2)}) collective-permute-start(f32[96,2560]{1,0:T(8,128)S(1)} %get-tuple-element.61), channel_id=1, source_target_pairs={{0,1},{1,0},{2,3},{3,2},{4,5},{5,4},{6,7},{7,6},{8,9},{9,8},{10,11... | collective-permute-start | bytes 2949128 | tf_op jit(solution)/shard_map/ppermute | solution.py:25
  64.8 13.2 %collective-permute-start.16 = (f16[96,2560]{1,0:T(8,128)(2,1)S(1)}, f16[96,2560]{1,0:T(8,128)(2,1)S(1)}, u32[]{:S(2)}, u32[]{:S(2)}) collective-permute-start(f16[96,2560]{1,0:T(8,128)(2,1)S(1)} %multiply_convert_fusion.5), channel_id=1, source_target_pairs={{0,16},{1,17},{2,18},{3,19},{4,20},{5,21},{6,22},{7,23},{8,24},{9,... | collective-permute-start | bytes 1474568 | tf_op jit(solution)/shard_map/ppermute | solution.py:25
  66.4 12.9 %collective-permute-start.17 = (f16[96,2560]{1,0:T(8,128)(2,1)S(1)}, f16[96,2560]{1,0:T(8,128)(2,1)S(1)}, u32[]{:S(2)}, u32[]{:S(2)}) collective-permute-start(f16[96,2560]{1,0:T(8,128)(2,1)S(1)} %multiply_convert_fusion.4), channel_id=1, source_target_pairs={{0,2},{1,3},{2,0},{3,1},{4,6},{5,7},{6,4},{7,5},{8,10},{9,11},{10,... | collective-permute-start | bytes 1474568 | tf_op jit(solution)/shard_map/ppermute | solution.py:25
  79.6 23.6 %collective-permute-start.21 = (f16[96,2560]{1,0:T(8,128)(2,1)S(1)}, f16[96,2560]{1,0:T(8,128)(2,1)S(1)}, u32[]{:S(2)}, u32[]{:S(2)}) collective-permute-start(f16[96,2560]{1,0:T(8,128)(2,1)S(1)} %multiply_convert_fusion.1), channel_id=1, source_target_pairs={{0,8},{1,9},{2,10},{3,11},{4,12},{5,13},{6,14},{7,15},{8,0},{9,1},... | collective-permute-start | bytes 1474568 | tf_op jit(solution)/shard_map/ppermute | solution.py:25
  81.9 21.5 %collective-permute-start.22 = (f16[96,2560]{1,0:T(8,128)(2,1)S(1)}, f16[96,2560]{1,0:T(8,128)(2,1)S(1)}, u32[]{:S(2)}, u32[]{:S(2)}) collective-permute-start(f16[96,2560]{1,0:T(8,128)(2,1)S(1)} %multiply_convert_fusion), channel_id=1, source_target_pairs={{0,4},{1,5},{2,6},{3,7},{4,0},{5,1},{6,2},{7,3},{8,12},{9,13},{10,... | collective-permute-start | bytes 1474568 | tf_op jit(solution)/shard_map/ppermute | solution.py:25
  82.5 21.0 %collective-permute-start.19 = (f16[96,2560]{1,0:T(8,128)(2,1)S(1)}, f16[96,2560]{1,0:T(8,128)(2,1)S(1)}, u32[]{:S(2)}, u32[]{:S(2)}) collective-permute-start(f16[96,2560]{1,0:T(8,128)(2,1)S(1)} %multiply_convert_fusion.2), channel_id=1, source_target_pairs={{0,2},{1,3},{2,0},{3,1},{4,6},{5,7},{6,4},{7,5},{8,10},{9,11},{10,... | collective-permute-start | bytes 1474568 | tf_op jit(solution)/shard_map/ppermute | solution.py:25
  83.0 21.6 %collective-permute-start.23 = (f32[96,2560]{1,0:T(8,128)S(1)}, f32[96,2560]{1,0:T(8,128)S(1)}, u32[]{:S(2)}, u32[]{:S(2)}) collective-permute-start(f32[96,2560]{1,0:T(8,128)S(1)} %get-tuple-element.69), channel_id=1, source_target_pairs={{0,1},{1,0},{2,3},{3,2},{4,5},{5,4},{6,7},{7,6},{8,9},{9,8},{10,11... | collective-permute-start | bytes 2949128 | tf_op jit(solution)/shard_map/ppermute | solution.py:25
  83.0 21.6 %collective-permute-start.24 = (f16[96,2560]{1,0:T(8,128)(2,1)S(1)}, f16[96,2560]{1,0:T(8,128)(2,1)S(1)}, u32[]{:S(2)}, u32[]{:S(2)}) collective-permute-start(f16[96,2560]{1,0:T(8,128)(2,1)S(1)} %multiply_convert_fusion.3), channel_id=1, source_target_pairs={{0,16},{1,17},{2,18},{3,19},{4,20},{5,21},{6,22},{7,23},{8,24},{9,... | collective-permute-start | bytes 1474568 | tf_op jit(solution)/shard_map/ppermute | solution.py:25
  (1 other events, 0.7 us)

commit v3 on v2

v3 whole, which is shorter than its diff:
```python
import functools

import jax
import jax.numpy as jnp
from jax import lax
from jax.experimental import pallas as pl
from jax.experimental.pallas import tpu as pltpu
from jax.sharding import PartitionSpec as P

MIB = 1024 * 1024
together = lax.optimization_barrier


def bits_of(groups, slabs):
    slab_bits = slabs.bit_length() - 1
    total = (groups * slabs).bit_length() - 1
    shared = min(slab_bits - 1, total // 2)
    alpha = [slab_bits - 1] + list(range(shared - 1, 0, -1))
    beta = list(range(slab_bits - 2, shared - 1, -1)) + list(range(total - 1, slab_bits - 1, -1)) + [0]
    return alpha, beta


def exchange(value, bit, devices):
    return lax.ppermute(value, ("grp", "slab"), [(d, d ^ (1 << bit)) for d in range(devices)])


def magnitudes(a_ref, b_ref, stats):
    wide_a, wide_b = a_ref[...].astype(jnp.float32), b_ref[...].astype(jnp.float32)
    norm_a = jnp.max(jnp.sum(wide_a * wide_a, axis=1, keepdims=True), axis=0, keepdims=True)
    norm_b = jnp.max(jnp.sum(wide_b * wide_b, axis=1, keepdims=True), axis=0, keepdims=True)
    largest = jnp.maximum(jnp.abs(wide_a), jnp.abs(wide_b))
    largest = jnp.max(jnp.max(largest, axis=1, keepdims=True), axis=0, keepdims=True)
    row = lax.broadcasted_iota(jnp.int32, stats.shape, 0)
    stats[...] = jnp.where(row == 0, norm_a, jnp.where(row == 1, norm_b, largest))


def energies(masks_a, masks_b, slabs, per, place, occ_a, occ_b, va_ref, vb_ref, least, ninv):
    width = ninv.shape[0] // len(masks_a)
    me = place[0]

    def lowest(ref):
        return jnp.min(jnp.min(ref[...], axis=1, keepdims=True), axis=0, keepdims=True)

    highest_a, highest_b = occ_a[0], occ_b[0]
    for o in range(1, occ_a.shape[0]):
        highest_a = jnp.maximum(highest_a, occ_a[o])
        highest_b = jnp.maximum(highest_b, occ_b[o])
    least[...] = jnp.broadcast_to(lowest(va_ref) + lowest(vb_ref) - highest_a - highest_b, least.shape)
    parts, occs = [], []
    for m in masks_b:
        other = jnp.bitwise_xor(me, m)
        for o in range(per):
            parts.append(vb_ref[pl.ds(other % slabs, 1), :])
            occs.append(jnp.full((1, width // per), occ_b[(other // slabs) * per + o], jnp.float32))
    vb, ob = jnp.concatenate(parts, axis=1), jnp.concatenate(occs, axis=1)
    for p, m in enumerate(masks_a):
        other = jnp.bitwise_xor(me, m)
        at = pl.multiple_of((other % slabs) * (width // per), 8)
        va = jnp.concatenate([va_ref[pl.ds(at, width // per), :]] * per, axis=0)
        oa = jnp.concatenate(
            [jnp.full((width // per, 1), occ_a[(other // slabs) * per + o], jnp.float32) for o in range(per)], axis=0
        )
        ninv[p * width:(p + 1) * width, :] = -1.0 / (((va + vb) - oa) - ob)


def contract_amplitudes(n_a, n_b, width, summed, *refs):
    a_refs, b_refs = refs[:n_a], refs[n_a:n_a + n_b]
    ninv, stats, least = refs[n_a + n_b:n_a + n_b + 3]
    t_ref, tt, acat, bcat, factors = refs[n_a + n_b + 3:n_a + n_b + 8]
    early = refs[n_a + n_b + 8:]
    bound = jnp.sqrt(stats[0:1, :]) * jnp.sqrt(stats[1:2, :]) / least[0:1, :] * stats[2:3, :] * summed
    bound = jnp.maximum(bound, 2e-34)
    factors[0:1, :] = 32768.0 / bound
    factors[1:8, :] = jnp.broadcast_to(bound / 32768.0, (7, bound.shape[1]))
    for p in range(n_a):
        acat[p * width:(p + 1) * width, :] = a_refs[p][...]
    for p in range(n_b):
        bcat[p * width:(p + 1) * width, :] = b_refs[p][...]
    cols = n_b * width
    step = 256 if cols % 256 == 0 else width
    for c in range(0, cols, step):
        integrals = lax.dot_general(
            acat[...], bcat[c:c + step, :], (((1,), (1,)), ((), ())), preferred_element_type=jnp.float32
        )
        amps = (integrals * ninv[:, c:c + step]).astype(jnp.bfloat16)
        t_ref[:, c:c + step] = amps
        tt[c:c + step, :] = amps.T
    rows_out(width, 0, tt, acat, factors, *early)


def rows_out(width, start, left, right, factors, *outs):
    aux = right.shape[1]
    tile = 512 if aux % 512 == 0 else 128
    rows = left[start * width:(start + len(outs)) * width, :]

    def one(k, _):
        at = pl.ds(pl.multiple_of(k * tile, tile), tile)
        acc = jnp.dot(rows, right[:, at], preferred_element_type=jnp.float32) * factors[0:1, 0:1]
        for p, out in enumerate(outs):
            out[:, at] = acc[p * width:(p + 1) * width, :]
        return 0

    lax.fori_loop(0, aux // tile, one, 0)


def body(orbital_alpha, orbital_beta, occ_alpha, occ_beta, virt_alpha, virt_beta):
    groups, slabs = lax.axis_size("grp"), lax.axis_size("slab")
    devices = groups * slabs
    me = lax.axis_index("grp") * slabs + lax.axis_index("slab")
    per, block, aux = orbital_alpha.shape
    width = per * block
    own_a, own_b = orbital_alpha.reshape(width, aux), orbital_beta.reshape(width, aux)
    alpha_bits, beta_bits = bits_of(groups, slabs)

    def masks(bits):
        found = [0]
        for bit in bits:
            found = found + [m | (1 << bit) for m in found]
        return found[::-1]

    masks_a, masks_b = masks(alpha_bits), masks([0] + beta_bits[:-1])
    n_a, n_b = len(masks_a), len(masks_b)
    rows, cols = n_a * width, n_b * width

    vmem = pl.BlockSpec(memory_space=pltpu.VMEM)
    smem = pl.BlockSpec(memory_space=pltpu.SMEM)
    scalars = jax.ShapeDtypeStruct((8, 128), jnp.float32)
    first_a, first_b = alpha_bits[0], beta_bits[0]
    pieces_a, pieces_b = {0: own_a}, {0: own_b}
    for bit in alpha_bits[1:]:
        pieces_a.update({m | (1 << bit): exchange(v, bit, devices) for m, v in list(pieces_a.items())})
    for bit in beta_bits[1:-1]:
        pieces_b.update({m | (1 << bit): exchange(v, bit, devices) for m, v in list(pieces_b.items())})
    near_a = exchange(own_a, first_a, devices)
    near_b = exchange(own_b, first_b, devices)
    stats = pl.pallas_call(
        magnitudes, out_shape=scalars, in_specs=[vmem] * 2,
        compiler_params=pltpu.CompilerParams(vmem_limit_bytes=8 * MIB), name="magnitudes",
    )(own_a, own_b)

    order = alpha_bits[1:] + [b for b in beta_bits[1:] if b] + [first_b, first_a, 0]
    split = len(order) - 1
    for bit in order[:split]:
        stats = jnp.maximum(stats, exchange(stats, bit, devices))

    pieces_b, pieces_a, near_a, near_b, stats, virt_alpha, virt_beta = together(
        (pieces_b, pieces_a, near_a, near_b, stats, virt_alpha, virt_beta)
    )
    far_a, far_b = {1 << first_a: near_a}, {1 << first_b: near_b}
    for bit in alpha_bits[1:]:
        far_a.update({m | (1 << bit): exchange(v, bit, devices) for m, v in list(far_a.items())})
    for bit in beta_bits[1:-1]:
        far_b.update({m | (1 << bit): exchange(v, bit, devices) for m, v in list(far_b.items())})
    pieces_a.update(far_a)
    pieces_b.update(far_b)
    pieces_b.update({m | 1: exchange(v, 0, devices) for m, v in list(pieces_b.items())})

    least, ninv = pl.pallas_call(
        functools.partial(energies, masks_a, masks_b, slabs, per),
        out_shape=[scalars, jax.ShapeDtypeStruct((rows, cols), jnp.float32)],
        in_specs=[smem] * 3 + [vmem] * 2,
        compiler_params=pltpu.CompilerParams(vmem_limit_bytes=12 * MIB),
        name="energies",
    )(me.reshape(1), occ_alpha, occ_beta, virt_alpha[:, None], virt_beta.reshape(slabs, block))

    for bit in order[split:]:
        stats = jnp.maximum(stats, exchange(stats, bit, devices))

    piece = jax.ShapeDtypeStruct((width, aux), jnp.float32)
    early = max(n_b // 4, 2)
    opening = pl.pallas_call(
        functools.partial(contract_amplitudes, n_a, n_b, width, float(devices * width)),
        out_shape=[
            jax.ShapeDtypeStruct((rows, cols), jnp.bfloat16),
            jax.ShapeDtypeStruct((cols, rows), jnp.bfloat16),
            jax.ShapeDtypeStruct((rows, aux), jnp.bfloat16),
            jax.ShapeDtypeStruct((cols, aux), jnp.bfloat16),
            scalars,
        ] + [piece] * early,
        compiler_params=pltpu.CompilerParams(vmem_limit_bytes=28 * MIB),
        cost_estimate=pl.CostEstimate(
            flops=2 * rows * cols * aux, bytes_accessed=2 * (rows + cols) * aux * 2, transcendentals=0
        ),
        name="amplitudes",
    )(*[pieces_a[m] for m in masks_a], *[pieces_b[m] for m in masks_b], ninv, stats, least)
    t, tt, acat, bcat, factors = opening[:5]

    def contracted(left, right, start, names, name):
        outs = pl.pallas_call(
            functools.partial(rows_out, width, start),
            out_shape=[piece] * len(names),
            compiler_params=pltpu.CompilerParams(vmem_limit_bytes=28 * MIB),
            cost_estimate=pl.CostEstimate(
                flops=2 * len(names) * width * right.size, bytes_accessed=len(names) * width * aux * 4 + right.size * 2,
                transcendentals=0,
            ),
            name=name,
        )(left, right, factors)
        return dict(zip(names, outs))

    def narrow(parts, names):
        return [parts[m].astype(jnp.float16) for m in names]

    def passed_on(names, bits, level):
        flag = 1 << bits[level]
        gone = sum(1 << b for b in bits[:level])
        every = [m for m in names if m & flag and not m & gone]
        after = 1 << bits[level + 1] if level + 1 < len(bits) else flag
        ahead = [m for m in every if m & after]
        return ahead, [m for m in every if m not in ahead]

    def chips_sum(found):
        return {m: v + exchange(found[m | 1], 0, devices) for m, v in found.items() if not m & 1}

    bits_a, bits_b = alpha_bits[::-1], [b for b in beta_bits[::-1] if b]
    names_b = [m for m in masks_b if not m & 1]
    gb = chips_sum(dict(zip(masks_b, opening[5:])))
    ga = contracted(t, bcat, 0, masks_a, "alpha")
    for level in range(max(len(bits_a), len(bits_b))):
        jobs = [
            (parts, bits[level]) + passed_on(names, bits, level)
            for parts, names, bits in ((ga, masks_a, bits_a), (gb, names_b, bits_b)) if level < len(bits)
        ]
        sent, tt, acat = together(([narrow(parts, ahead) for parts, _, ahead, _ in jobs], tt, acat))
        got = [[exchange(v, bit, devices) for v in vs] for (_, bit, _, _), vs in zip(jobs, sent)]
        if level == 0:
            gb.update(chips_sum(contracted(tt, acat, early, masks_b[early:], "beta")))
        got, rest = together((got, [narrow(parts, others) for parts, _, _, others in jobs]))
        late = [[exchange(v, bit, devices) for v in vs] for (_, bit, _, _), vs in zip(jobs, rest)]
        for (parts, bit, ahead, others), arrived, later in zip(jobs, got, late):
            for m, v in zip(ahead + others, arrived + later):
                parts[m ^ (1 << bit)] = parts[m ^ (1 << bit)] + v.astype(jnp.float32)
    total_a, total_b = ga[0], gb[0]

    unscale = factors[1:2, 0:1]
    return ((total_a * unscale).reshape(orbital_alpha.shape), (total_b * unscale).reshape(orbital_beta.shape))


def solution(mesh):
    in_specs = (P("grp", "slab", None), P("grp", "slab", None), P(), P(), P(), P())
    out_specs = (P("grp", "slab", None), P("grp", "slab", None))
    return jax.shard_map(body, mesh=mesh, in_specs=in_specs, out_specs=out_specs, check_vma=False)
```

time: 106 us -> 102 us (0.962)
  between operations: 5.35 us -> 0.8 us
  other arithmetic: 5.57 us -> 4.26 us
  starting transfers between devices: 24.4 us -> 25.5 us
    reshape x2, other arithmetic: 2.32 us -> 3.57 us  [the longest x1 1.85 us: body(): (total_b * unscale).reshape(orbital_beta.shape)]
    reduce_max x2 -> x0, other arithmetic: 1.23 us -> none  [the longest x1 0.66 us: body(): jnp.max(occ_alpha)]
    reduce_min x2 -> x0, other arithmetic: 1.2 us -> none  [the longest x1 0.6 us: body(): jnp.min(virt_beta)]
    ppermute x25, starting transfers between devices: 24.4 us -> 25.5 us  [exchange(): lax.ppermute(value, ('grp', 'slab'), [(d, d ^ 1 << bit) for d in range(de...]
    unnamed x16 -> x12, local copies, waits for them, and re-layouts: 2.36 us -> 3.37 us
    pallas_call x4 -> x5, Pallas kernels: 11.7 us -> 10.9 us  [the longest x2 4.87 us: contracted(): pl.pallas_call(functools.partial(rows_out, width, start), out_shape=[piec...]
  transfers between devices with their start and end apart: 25 -> 25, of which waited for: 10 -> 11; matrix products, arithmetic and copies ran while one was open for 6% -> 4% of each run, Pallas kernels for 6% -> 4%
where the time goes in v3:
time: 102 us; the launch traced here: 101 us
  waiting for transfers between devices  54.2 us (53%)
  starting transfers between devices  25.5 us (25%)
  Pallas kernels  10.9 us (11%)
  local copies, waits for them, and re-layouts  5.64 us (6%)
  other arithmetic  4.26 us (4%)
    ppermute x25, waiting for transfers between devices, exchange(): lax.ppermute(value, ('grp', 'slab'), [(d, d ^ 1 << bit) for d in range(de...  54.2 us
    ppermute x25, starting transfers between devices, exchange(): lax.ppermute(value, ('grp', 'slab'), [(d, d ^ 1 << bit) for d in range(de...  25.5 us
    pallas_call x2, Pallas kernels, contracted(): pl.pallas_call(functools.partial(rows_out, width, start), out_shape=[piec...  4.87 us
    pallas_call x1, Pallas kernels, body(): pl.pallas_call(functools.partial(contract_amplitudes, n_a, n_b, width, fl...  4.8 us
    unnamed x12, local copies, waits for them, and re-layouts  3.37 us
  transfers between devices with their start and end apart: 25, of which 11 were waited for; matrix products, arithmetic and copies ran while one was open for 4% of the time, Pallas kernels for 4%

profile of v3, /device:TPU:0, one launch (start us, length us, event | category | flops | bytes accessed | tf_op | source)
XLA Modules:
  0.0 101.3 jit_solution(4041318199317952799)
XLA Ops:
  0.6 4.1 %collective-permute-start.2 = (bf16[96,2560]{1,0:T(8,128)(2,1)}, bf16[96,2560]{1,0:T(8,128)(2,1)S(1)}, u32[]{:S(2)}, u32[]{:S(2)}) collective-permute-start(bf16[96,2560]{1,0:T(8,128)(2,1)} %bitcast.8), channel_id=1, source_target_pairs={{0,8},{1,9},{2,10},{3,11},{4,12},{5,13},{6,14},{7,15},{8,0},{9,1},... | collective-permute-start | bytes 1474568 | tf_op jit(solution)/shard_map/ppermute | solution.py:24
  4.7 1.5 %collective-permute-start.1 = (bf16[96,2560]{1,0:T(8,128)(2,1)}, bf16[96,2560]{1,0:T(8,128)(2,1)S(1)}, u32[]{:S(2)}, u32[]{:S(2)}) collective-permute-start(bf16[96,2560]{1,0:T(8,128)(2,1)} %bitcast.9), channel_id=1, source_target_pairs={{0,2},{1,3},{2,0},{3,1},{4,6},{5,7},{6,4},{7,5},{8,10},{9,11},{10,... | collective-permute-start | bytes 1474568 | tf_op jit(solution)/shard_map/ppermute | solution.py:24
  6.2 1.6 %collective-permute-start.3 = (bf16[96,2560]{1,0:T(8,128)(2,1)}, bf16[96,2560]{1,0:T(8,128)(2,1)S(1)}, u32[]{:S(2)}, u32[]{:S(2)}) collective-permute-start(bf16[96,2560]{1,0:T(8,128)(2,1)} %bitcast.12), channel_id=1, source_target_pairs={{0,4},{1,5},{2,6},{3,7},{4,0},{5,1},{6,2},{7,3},{8,12},{9,13},{10,... | collective-permute-start | bytes 1474568 | tf_op jit(solution)/shard_map/ppermute | solution.py:24
  7.8 1.5 %collective-permute-start = (bf16[96,2560]{1,0:T(8,128)(2,1)}, bf16[96,2560]{1,0:T(8,128)(2,1)S(1)}, u32[]{:S(2)}, u32[]{:S(2)}) collective-permute-start(bf16[96,2560]{1,0:T(8,128)(2,1)} %bitcast.13), channel_id=1, source_target_pairs={{0,16},{1,17},{2,18},{3,19},{4,20},{5,21},{6,22},{7,23},{8,24},{9,... | collective-permute-start | bytes 1474568 | tf_op jit(solution)/shard_map/ppermute | solution.py:24
  9.3 1.0 %copy-done = bf16[1,96,2560]{2,1,0:T(8,128)(2,1)S(1)} copy-done((bf16[1,96,2560]{2,1,0:T(8,128)(2,1)S(1)}, bf16[1,96,2560]{2,1,0:T(8,128)(2,1)}, u32[]{:S(2)}) %copy-start) | copy-done | bytes 491544
  10.4 1.0 %copy-done.2 = bf16[1,96,2560]{2,1,0:T(8,128)(2,1)S(1)} copy-done((bf16[1,96,2560]{2,1,0:T(8,128)(2,1)S(1)}, bf16[1,96,2560]{2,1,0:T(8,128)(2,1)}, u32[]{:S(2)}) %copy-start.2) | copy-done | bytes 491544
  12.4 5.4 %collective-permute-done.4 = f32[8,128]{1,0:T(8,128)S(1)} collective-permute-done((f32[8,128]{1,0:T(8,128)S(1)}, f32[8,128]{1,0:T(8,128)S(1)}, u32[]{:S(2)}, u32[]{:S(2)}) %collective-permute-start.4) | collective-permute-done | bytes 4128 | tf_op jit(solution)/shard_map/ppermute | solution.py:24
  17.7 1.5 %collective-permute-start.5 = (f32[8,128]{1,0:T(8,128)S(1)}, f32[8,128]{1,0:T(8,128)S(1)}, u32[]{:S(2)}, u32[]{:S(2)}) collective-permute-start(f32[8,128]{1,0:T(8,128)S(1)} %max.15), channel_id=1, source_target_pairs={{0,16},{1,17},{2,18},{3,19},{4,20},{5,21},{6,22},{7,23},{8,24},{9,... | collective-permute-start | bytes 12296 | tf_op jit(solution)/shard_map/ppermute | solution.py:24
  19.2 2.1 %collective-permute-done.5 = f32[8,128]{1,0:T(8,128)S(1)} collective-permute-done((f32[8,128]{1,0:T(8,128)S(1)}, f32[8,128]{1,0:T(8,128)S(1)}, u32[]{:S(2)}, u32[]{:S(2)}) %collective-permute-start.5) | collective-permute-done | bytes 4128 | tf_op jit(solution)/shard_map/ppermute | solution.py:24
  21.3 1.6 %collective-permute-start.6 = (f32[8,128]{1,0:T(8,128)S(1)}, f32[8,128]{1,0:T(8,128)S(1)}, u32[]{:S(2)}, u32[]{:S(2)}) collective-permute-start(f32[8,128]{1,0:T(8,128)S(1)} %max.16), channel_id=1, source_target_pairs={{0,4},{1,5},{2,6},{3,7},{4,0},{5,1},{6,2},{7,3},{8,12},{9,13},{10,... | collective-permute-start | bytes 12296 | tf_op jit(solution)/shard_map/ppermute | solution.py:24
  22.9 5.4 %collective-permute-done.6 = f32[8,128]{1,0:T(8,128)S(1)} collective-permute-done((f32[8,128]{1,0:T(8,128)S(1)}, f32[8,128]{1,0:T(8,128)S(1)}, u32[]{:S(2)}, u32[]{:S(2)}) %collective-permute-start.6) | collective-permute-done | bytes 4128 | tf_op jit(solution)/shard_map/ppermute | solution.py:24
  28.3 0.7 collective-permute-start.7
  29.0 3.8 %collective-permute-done.7 = f32[8,128]{1,0:T(8,128)S(1)} collective-permute-done((f32[8,128]{1,0:T(8,128)S(1)}, f32[8,128]{1,0:T(8,128)S(1)}, u32[]{:S(2)}, u32[]{:S(2)}) %collective-permute-start.7) | collective-permute-done | bytes 4128 | tf_op jit(solution)/shard_map/ppermute | solution.py:24
  32.8 1.6 %collective-permute-start.9 = (bf16[96,2560]{1,0:T(8,128)(2,1)S(1)}, bf16[96,2560]{1,0:T(8,128)(2,1)S(1)}, u32[]{:S(2)}, u32[]{:S(2)}) collective-permute-start(bf16[96,2560]{1,0:T(8,128)(2,1)S(1)} %collective-permute-done.3.refs_9_), channel_id=1, source_target_pairs={{0,16},{1,17},{2,18},{3,19},{4,20},{5,21},{6,22},{7,23},{8,24},{9,... | collective-permute-start | bytes 1474568 | tf_op jit(solution)/shard_map/ppermute | solution.py:24
  36.0 7.6 %collective-permute-done.9.refs_5_ = bf16[96,2560]{1,0:T(8,128)(2,1)S(1)} collective-permute-done((bf16[96,2560]{1,0:T(8,128)(2,1)S(1)}, bf16[96,2560]{1,0:T(8,128)(2,1)S(1)}, u32[]{:S(2)}, u32[]{:S(2)}) %collective-permute-start.9) | collective-permute-done | bytes 491552 | tf_op jit(solution)/shard_map/ppermute | solution.py:24
  43.6 0.8 reshape.25.vb_ref
  44.4 1.0 broadcast_in_dim.4.va_ref
  46.0 0.7 copy-done.5
  46.7 0.8 energies.1
  48.3 4.8 %amplitudes.1 = (bf16[384,768]{1,0:T(8,128)(2,1)S(1)}, bf16[768,384]{1,0:T(8,128)(2,1)S(1)}, bf16[384,2560]{1,0:T(8,128)(2,1)S(1)}, bf16[768,2560]{1,0:T(8,128)(...) custom-call(bf16[96,2560]{1,0:T(8,128)(2,1)} %collective-permute-done.8.refs_0_, ...), custom_call_target="tpu_custom_call" | custom-call | flops 1509949440 | bytes 11796480 | tf_op jit(solution)/shard_map/amplitudes/pallas_call | solution.py:171
  53.1 2.4 %alpha.1 = (f32[96,2560]{1,0:T(8,128)S(1)}, f32[96,2560]{1,0:T(8,128)S(1)}, f32[96,2560]{1,0:T(8,128)S(1)}, f32[96,2560]{1,0:T(8,128)S(1)}) custom-call(bf16[384,768]{1,0:T(8,128)(2,1)S(1)} %get-tuple-element.53.left, bf16[768,2560]{1,0:T(8,128)(2,1)S(1)} %get-tuple-element.54.right, f32[8,128]{1,0:T(8,128)S(1)} %get-tuple-element.55.factors), custom_call_target="tpu_custom_call" | custom-call | flops 1509949440 | bytes 7864320 | tf_op jit(solution)/shard_map/alpha/pallas_call | solution.py:189
  55.8 2.4 %beta.1 = (f32[96,2560]{1,0:T(8,128)S(1)}, f32[96,2560]{1,0:T(8,128)S(1)}, f32[96,2560]{1,0:T(8,128)S(1)}, f32[96,2560]{1,0:T(8,128)S(1)}, f32[96,2560]{1,0:T(8,128)S(1)}, /*index=5*/f32[96,2560]{1,0:T(8,128)S(1)}) custom-call(bf16[768,384]{1,0:T(8,128)(2,1)S(1)} %get-tuple-element.65.left, bf16[384,2560]{1,0:T(8,128)(2,1)S(1)} %get-tuple-element.66.right, ...), custom_call_target="tpu_custom_call" | custom-call | flops 1132462080 | bytes 7864320 | tf_op jit(solution)/shard_map/beta/pallas_call | solution.py:189
  58.8 1.0 %collective-permute-start.16 = (f16[96,2560]{1,0:T(8,128)(2,1)S(1)}, f16[96,2560]{1,0:T(8,128)(2,1)S(1)}, u32[]{:S(2)}, u32[]{:S(2)}) collective-permute-start(f16[96,2560]{1,0:T(8,128)(2,1)S(1)} %convert_element_type.36), channel_id=1, source_target_pairs={{0,2},{1,3},{2,0},{3,1},{4,6},{5,7},{6,4},{7,5},{8,10},{9,11},{10,... | collective-permute-start | bytes 1474568 | tf_op jit(solution)/shard_map/ppermute | solution.py:24
  59.9 1.5 %collective-permute-start.17 = (f16[96,2560]{1,0:T(8,128)(2,1)S(1)}, f16[96,2560]{1,0:T(8,128)(2,1)S(1)}, u32[]{:S(2)}, u32[]{:S(2)}) collective-permute-start(f16[96,2560]{1,0:T(8,128)(2,1)S(1)} %add_convert_fusion.3), channel_id=1, source_target_pairs={{0,16},{1,17},{2,18},{3,19},{4,20},{5,21},{6,22},{7,23},{8,24},{9,... | collective-permute-start | bytes 1474568 | tf_op jit(solution)/shard_map/ppermute | solution.py:24
  61.5 10.6 %collective-permute-done.16 = f16[96,2560]{1,0:T(8,128)(2,1)S(1)} collective-permute-done((f16[96,2560]{1,0:T(8,128)(2,1)S(1)}, f16[96,2560]{1,0:T(8,128)(2,1)S(1)}, u32[]{:S(2)}, u32[]{:S(2)}) %collective-permute-start.16) | collective-permute-done | bytes 491552 | tf_op jit(solution)/shard_map/ppermute | solution.py:24
  72.1 1.1 %collective-permute-done.17 = f16[96,2560]{1,0:T(8,128)(2,1)S(1)} collective-permute-done((f16[96,2560]{1,0:T(8,128)(2,1)S(1)}, f16[96,2560]{1,0:T(8,128)(2,1)S(1)}, u32[]{:S(2)}, u32[]{:S(2)}) %collective-permute-start.17) | collective-permute-done | bytes 491552 | tf_op jit(solution)/shard_map/ppermute | solution.py:24
  74.0 2.6 %collective-permute-start.22 = (f16[96,2560]{1,0:T(8,128)(2,1)S(1)}, f16[96,2560]{1,0:T(8,128)(2,1)S(1)}, u32[]{:S(2)}, u32[]{:S(2)}) collective-permute-start(f16[96,2560]{1,0:T(8,128)(2,1)S(1)} %add_convert_fusion), channel_id=1, source_target_pairs={{0,4},{1,5},{2,6},{3,7},{4,0},{5,1},{6,2},{7,3},{8,12},{9,13},{10,... | collective-permute-start | bytes 1474568 | tf_op jit(solution)/shard_map/ppermute | solution.py:24
  76.5 1.7 %collective-permute-start.19 = (f16[96,2560]{1,0:T(8,128)(2,1)S(1)}, f16[96,2560]{1,0:T(8,128)(2,1)S(1)}, u32[]{:S(2)}, u32[]{:S(2)}) collective-permute-start(f16[96,2560]{1,0:T(8,128)(2,1)S(1)} %convert_element_type.38), channel_id=1, source_target_pairs={{0,2},{1,3},{2,0},{3,1},{4,6},{5,7},{6,4},{7,5},{8,10},{9,11},{10,... | collective-permute-start | bytes 1474568 | tf_op jit(solution)/shard_map/ppermute | solution.py:24
  78.7 1.5 %collective-permute-start.24 = (f16[96,2560]{1,0:T(8,128)(2,1)S(1)}, f16[96,2560]{1,0:T(8,128)(2,1)S(1)}, u32[]{:S(2)}, u32[]{:S(2)}) collective-permute-start(f16[96,2560]{1,0:T(8,128)(2,1)S(1)} %add_convert_fusion.2), channel_id=1, source_target_pairs={{0,16},{1,17},{2,18},{3,19},{4,20},{5,21},{6,22},{7,23},{8,24},{9,... | collective-permute-start | bytes 1474568 | tf_op jit(solution)/shard_map/ppermute | solution.py:24
  80.3 17.4 %collective-permute-done.21 = f16[96,2560]{1,0:T(8,128)(2,1)S(1)} collective-permute-done((f16[96,2560]{1,0:T(8,128)(2,1)S(1)}, f16[96,2560]{1,0:T(8,128)(2,1)S(1)}, u32[]{:S(2)}, u32[]{:S(2)}) %collective-permute-start.21) | collective-permute-done | bytes 491552 | tf_op jit(solution)/shard_map/ppermute | solution.py:24
  97.7 1.7 %multiply_bitcast_fusion.1 = f32[1,96,2560]{2,1,0:T(8,128)} fusion(f16[96,2560]{1,0:T(8,128)(2,1)S(1)} %collective-permute-done.21, f32[96,2560]{1,0:T(8,128)S(1)} %get-tuple-element.56, f16[96,2560]{1,0:T(8,128)(2,1)S(1)} %collective-permute-done.19, f32[]{:T(128)} %bitcast.3), kind=kLoop, calls=%fused_computation.1 | loop fusion | flops 1228800 | bytes 2949124 | tf_op jit(solution)/shard_map/reshape | solution.py:236
  99.4 1.9 %multiply_bitcast_fusion = f32[1,96,2560]{2,1,0:T(8,128)} fusion(f16[96,2560]{1,0:T(8,128)(2,1)S(1)} %collective-permute-done.22, f16[96,2560]{1,0:T(8,128)(2,1)S(1)} %collective-permute-done.24, f32[96,2560]{1,0:T(8,128)S(1)} %get-tuple-element.78, f32[96,2560]{1,0:T(8,128)S(1)} %collective-permute-done.23, f32[]{:T(128)} %bitcast.3), kind=kLoop, calls=%fused_computation | loop fusion | flops 1474560 | bytes 3932164 | tf_op jit(solution)/shard_map/reshape | solution.py:236
  (51 shorter events, 6.3 us)
Async XLA Ops:
  0.6 32.2 %collective-permute-start.2 = (bf16[96,2560]{1,0:T(8,128)(2,1)}, bf16[96,2560]{1,0:T(8,128)(2,1)S(1)}, u32[]{:S(2)}, u32[]{:S(2)}) collective-permute-start(bf16[96,2560]{1,0:T(8,128)(2,1)} %bitcast.8), channel_id=1, source_target_pairs={{0,8},{1,9},{2,10},{3,11},{4,12},{5,13},{6,14},{7,15},{8,0},{9,1},... | collective-permute-start | bytes 1474568 | tf_op jit(solution)/shard_map/ppermute | solution.py:24
  4.7 28.1 %collective-permute-start.1 = (bf16[96,2560]{1,0:T(8,128)(2,1)}, bf16[96,2560]{1,0:T(8,128)(2,1)S(1)}, u32[]{:S(2)}, u32[]{:S(2)}) collective-permute-start(bf16[96,2560]{1,0:T(8,128)(2,1)} %bitcast.9), channel_id=1, source_target_pairs={{0,2},{1,3},{2,0},{3,1},{4,6},{5,7},{6,4},{7,5},{8,10},{9,11},{10,... | collective-permute-start | bytes 1474568 | tf_op jit(solution)/shard_map/ppermute | solution.py:24
  6.2 26.6 %collective-permute-start.3 = (bf16[96,2560]{1,0:T(8,128)(2,1)}, bf16[96,2560]{1,0:T(8,128)(2,1)S(1)}, u32[]{:S(2)}, u32[]{:S(2)}) collective-permute-start(bf16[96,2560]{1,0:T(8,128)(2,1)} %bitcast.12), channel_id=1, source_target_pairs={{0,4},{1,5},{2,6},{3,7},{4,0},{5,1},{6,2},{7,3},{8,12},{9,13},{10,... | collective-permute-start | bytes 1474568 | tf_op jit(solution)/shard_map/ppermute | solution.py:24
  7.8 25.0 %collective-permute-start = (bf16[96,2560]{1,0:T(8,128)(2,1)}, bf16[96,2560]{1,0:T(8,128)(2,1)S(1)}, u32[]{:S(2)}, u32[]{:S(2)}) collective-permute-start(bf16[96,2560]{1,0:T(8,128)(2,1)} %bitcast.13), channel_id=1, source_target_pairs={{0,16},{1,17},{2,18},{3,19},{4,20},{5,21},{6,22},{7,23},{8,24},{9,... | collective-permute-start | bytes 1474568 | tf_op jit(solution)/shard_map/ppermute | solution.py:24
  9.3 1.0 %copy-start = (bf16[1,96,2560]{2,1,0:T(8,128)(2,1)S(1)}, bf16[1,96,2560]{2,1,0:T(8,128)(2,1)}, u32[]{:S(2)}) copy-start(bf16[1,96,2560]{2,1,0:T(8,128)(2,1)} %param.6) | copy-start | bytes 1474564
  10.3 1.0 %copy-start.2 = (bf16[1,96,2560]{2,1,0:T(8,128)(2,1)S(1)}, bf16[1,96,2560]{2,1,0:T(8,128)(2,1)}, u32[]{:S(2)}) copy-start(bf16[1,96,2560]{2,1,0:T(8,128)(2,1)} %param.7) | copy-start | bytes 1474564
  11.4 36.9 %copy-start.1 = (bf16[1,96,2560]{2,1,0:T(8,128)(2,1)S(1)}, bf16[1,96,2560]{2,1,0:T(8,128)(2,1)}, u32[]{:S(2)}) copy-start(bf16[1,96,2560]{2,1,0:T(8,128)(2,1)} %param.6) | copy-start | bytes 1474564
  11.4 36.9 %copy-start.3 = (bf16[1,96,2560]{2,1,0:T(8,128)(2,1)S(1)}, bf16[1,96,2560]{2,1,0:T(8,128)(2,1)}, u32[]{:S(2)}) copy-start(bf16[1,96,2560]{2,1,0:T(8,128)(2,1)} %param.7) | copy-start | bytes 1474564
  11.8 6.0 %collective-permute-start.4 = (f32[8,128]{1,0:T(8,128)S(1)}, f32[8,128]{1,0:T(8,128)S(1)}, u32[]{:S(2)}, u32[]{:S(2)}) collective-permute-start(f32[8,128]{1,0:T(8,128)S(1)} %magnitudes.1), channel_id=1, source_target_pairs={{0,2},{1,3},{2,0},{3,1},{4,6},{5,7},{6,4},{7,5},{8,10},{9,11},{10,... | collective-permute-start | bytes 12296 | tf_op jit(solution)/shard_map/ppermute | solution.py:24
  17.7 3.6 %collective-permute-start.5 = (f32[8,128]{1,0:T(8,128)S(1)}, f32[8,128]{1,0:T(8,128)S(1)}, u32[]{:S(2)}, u32[]{:S(2)}) collective-permute-start(f32[8,128]{1,0:T(8,128)S(1)} %max.15), channel_id=1, source_target_pairs={{0,16},{1,17},{2,18},{3,19},{4,20},{5,21},{6,22},{7,23},{8,24},{9,... | collective-permute-start | bytes 12296 | tf_op jit(solution)/shard_map/ppermute | solution.py:24
  21.3 7.0 %collective-permute-start.6 = (f32[8,128]{1,0:T(8,128)S(1)}, f32[8,128]{1,0:T(8,128)S(1)}, u32[]{:S(2)}, u32[]{:S(2)}) collective-permute-start(f32[8,128]{1,0:T(8,128)S(1)} %max.16), channel_id=1, source_target_pairs={{0,4},{1,5},{2,6},{3,7},{4,0},{5,1},{6,2},{7,3},{8,12},{9,13},{10,... | collective-permute-start | bytes 12296 | tf_op jit(solution)/shard_map/ppermute | solution.py:24
  28.3 4.5 %collective-permute-start.7 = (f32[8,128]{1,0:T(8,128)S(1)}, f32[8,128]{1,0:T(8,128)S(1)}, u32[]{:S(2)}, u32[]{:S(2)}) collective-permute-start(f32[8,128]{1,0:T(8,128)S(1)} %max.17), channel_id=1, source_target_pairs={{0,8},{1,9},{2,10},{3,11},{4,12},{5,13},{6,14},{7,15},{8,0},{9,1},... | collective-permute-start | bytes 12296 | tf_op jit(solution)/shard_map/ppermute | solution.py:24
  32.8 10.8 %collective-permute-start.9 = (bf16[96,2560]{1,0:T(8,128)(2,1)S(1)}, bf16[96,2560]{1,0:T(8,128)(2,1)S(1)}, u32[]{:S(2)}, u32[]{:S(2)}) collective-permute-start(bf16[96,2560]{1,0:T(8,128)(2,1)S(1)} %collective-permute-done.3.refs_9_), channel_id=1, source_target_pairs={{0,16},{1,17},{2,18},{3,19},{4,20},{5,21},{6,22},{7,23},{8,24},{9,... | collective-permute-start | bytes 1474568 | tf_op jit(solution)/shard_map/ppermute | solution.py:24
  34.5 1.2 %collective-permute-start.14 = (f32[8,128]{1,0:T(8,128)S(1)}, f32[8,128]{1,0:T(8,128)S(1)}, u32[]{:S(2)}, u32[]{:S(2)}) collective-permute-start(f32[8,128]{1,0:T(8,128)S(1)} %max.18), channel_id=1, source_target_pairs={{0,1},{1,0},{2,3},{3,2},{4,5},{5,4},{6,7},{7,6},{8,9},{9,8},{10,11... | collective-permute-start | bytes 12296 | tf_op jit(solution)/shard_map/ppermute | solution.py:24
  34.5 13.8 %collective-permute-start.12 = (bf16[96,2560]{1,0:T(8,128)(2,1)S(1)}, bf16[96,2560]{1,0:T(8,128)(2,1)}, u32[]{:S(2)}, u32[]{:S(2)}) collective-permute-start(bf16[96,2560]{1,0:T(8,128)(2,1)S(1)} %collective-permute-done.3.refs_9_), channel_id=1, source_target_pairs={{0,1},{1,0},{2,3},{3,2},{4,5},{5,4},{6,7},{7,6},{8,9},{9,8},{10,11... | collective-permute-start | bytes 1474568 | tf_op jit(solution)/shard_map/ppermute | solution.py:24
  35.0 13.2 %collective-permute-start.8 = (bf16[96,2560]{1,0:T(8,128)(2,1)S(1)}, bf16[96,2560]{1,0:T(8,128)(2,1)}, u32[]{:S(2)}, u32[]{:S(2)}) collective-permute-start(bf16[96,2560]{1,0:T(8,128)(2,1)S(1)} %collective-permute-done.2.refs_2_), channel_id=1, source_target_pairs={{0,2},{1,3},{2,0},{3,1},{4,6},{5,7},{6,4},{7,5},{8,10},{9,11},{10,... | collective-permute-start | bytes 1474568 | tf_op jit(solution)/shard_map/ppermute | solution.py:24
  35.5 12.7 %collective-permute-start.11 = (bf16[96,2560]{1,0:T(8,128)(2,1)S(1)}, bf16[96,2560]{1,0:T(8,128)(2,1)}, u32[]{:S(2)}, u32[]{:S(2)}) collective-permute-start(bf16[96,2560]{1,0:T(8,128)(2,1)S(1)} %collective-permute-done.refs_7_), channel_id=1, source_target_pairs={{0,1},{1,0},{2,3},{3,2},{4,5},{5,4},{6,7},{7,6},{8,9},{9,8},{10,11... | collective-permute-start | bytes 1474568 | tf_op jit(solution)/shard_map/ppermute | solution.py:24
  35.6 12.6 %collective-permute-start.13 = (bf16[96,2560]{1,0:T(8,128)(2,1)}, bf16[96,2560]{1,0:T(8,128)(2,1)}, u32[]{:S(2)}, u32[]{:S(2)}) collective-permute-start(bf16[96,2560]{1,0:T(8,128)(2,1)} %bitcast.14), channel_id=1, source_target_pairs={{0,1},{1,0},{2,3},{3,2},{4,5},{5,4},{6,7},{7,6},{8,9},{9,8},{10,11... | collective-permute-start | bytes 1474568 | tf_op jit(solution)/shard_map/ppermute | solution.py:24
  43.6 4.6 %collective-permute-start.10 = (bf16[96,2560]{1,0:T(8,128)(2,1)S(1)}, bf16[96,2560]{1,0:T(8,128)(2,1)}, u32[]{:S(2)}, u32[]{:S(2)}) collective-permute-start(bf16[96,2560]{1,0:T(8,128)(2,1)S(1)} %collective-permute-done.9.refs_5_), channel_id=1, source_target_pairs={{0,1},{1,0},{2,3},{3,2},{4,5},{5,4},{6,7},{7,6},{8,9},{9,8},{10,11... | collective-permute-start | bytes 1474568 | tf_op jit(solution)/shard_map/ppermute | solution.py:24
  45.4 0.7 copy-start.4
  46.0 0.7 copy-start.5
  53.1 2.6 %collective-permute-start.15 = (f32[96,2560]{1,0:T(8,128)S(1)}, f32[96,2560]{1,0:T(8,128)S(1)}, u32[]{:S(2)}, u32[]{:S(2)}) collective-permute-start(f32[96,2560]{1,0:T(8,128)S(1)} %get-tuple-element.59), channel_id=1, source_target_pairs={{0,1},{1,0},{2,3},{3,2},{4,5},{5,4},{6,7},{7,6},{8,9},{9,8},{10,11... | collective-permute-start | bytes 2949128 | tf_op jit(solution)/shard_map/ppermute | solution.py:24
  58.3 3.1 %collective-permute-start.18 = (f32[96,2560]{1,0:T(8,128)S(1)}, f32[96,2560]{1,0:T(8,128)S(1)}, u32[]{:S(2)}, u32[]{:S(2)}) collective-permute-start(f32[96,2560]{1,0:T(8,128)S(1)} %get-tuple-element.68), channel_id=1, source_target_pairs={{0,1},{1,0},{2,3},{3,2},{4,5},{5,4},{6,7},{7,6},{8,9},{9,8},{10,11... | collective-permute-start | bytes 2949128 | tf_op jit(solution)/shard_map/ppermute | solution.py:24
  58.8 13.3 %collective-permute-start.16 = (f16[96,2560]{1,0:T(8,128)(2,1)S(1)}, f16[96,2560]{1,0:T(8,128)(2,1)S(1)}, u32[]{:S(2)}, u32[]{:S(2)}) collective-permute-start(f16[96,2560]{1,0:T(8,128)(2,1)S(1)} %convert_element_type.36), channel_id=1, source_target_pairs={{0,2},{1,3},{2,0},{3,1},{4,6},{5,7},{6,4},{7,5},{8,10},{9,11},{10,... | collective-permute-start | bytes 1474568 | tf_op jit(solution)/shard_map/ppermute | solution.py:24
  59.9 13.3 %collective-permute-start.17 = (f16[96,2560]{1,0:T(8,128)(2,1)S(1)}, f16[96,2560]{1,0:T(8,128)(2,1)S(1)}, u32[]{:S(2)}, u32[]{:S(2)}) collective-permute-start(f16[96,2560]{1,0:T(8,128)(2,1)S(1)} %add_convert_fusion.3), channel_id=1, source_target_pairs={{0,16},{1,17},{2,18},{3,19},{4,20},{5,21},{6,22},{7,23},{8,24},{9,... | collective-permute-start | bytes 1474568 | tf_op jit(solution)/shard_map/ppermute | solution.py:24
  61.4 11.9 %collective-permute-start.20 = (f32[96,2560]{1,0:T(8,128)S(1)}, f32[96,2560]{1,0:T(8,128)S(1)}, u32[]{:S(2)}, u32[]{:S(2)}) collective-permute-start(f32[96,2560]{1,0:T(8,128)S(1)} %get-tuple-element.73), channel_id=1, source_target_pairs={{0,1},{1,0},{2,3},{3,2},{4,5},{5,4},{6,7},{7,6},{8,9},{9,8},{10,11... | collective-permute-start | bytes 2949128 | tf_op jit(solution)/shard_map/ppermute | solution.py:24
  73.5 24.1 %collective-permute-start.21 = (f16[96,2560]{1,0:T(8,128)(2,1)S(1)}, f16[96,2560]{1,0:T(8,128)(2,1)S(1)}, u32[]{:S(2)}, u32[]{:S(2)}) collective-permute-start(f16[96,2560]{1,0:T(8,128)(2,1)S(1)} %add_convert_fusion.1), channel_id=1, source_target_pairs={{0,8},{1,9},{2,10},{3,11},{4,12},{5,13},{6,14},{7,15},{8,0},{9,1},... | collective-permute-start | bytes 1474568 | tf_op jit(solution)/shard_map/ppermute | solution.py:24
  74.0 23.7 %collective-permute-start.22 = (f16[96,2560]{1,0:T(8,128)(2,1)S(1)}, f16[96,2560]{1,0:T(8,128)(2,1)S(1)}, u32[]{:S(2)}, u32[]{:S(2)}) collective-permute-start(f16[96,2560]{1,0:T(8,128)(2,1)S(1)} %add_convert_fusion), channel_id=1, source_target_pairs={{0,4},{1,5},{2,6},{3,7},{4,0},{5,1},{6,2},{7,3},{8,12},{9,13},{10,... | collective-permute-start | bytes 1474568 | tf_op jit(solution)/shard_map/ppermute | solution.py:24
  76.5 21.2 %collective-permute-start.19 = (f16[96,2560]{1,0:T(8,128)(2,1)S(1)}, f16[96,2560]{1,0:T(8,128)(2,1)S(1)}, u32[]{:S(2)}, u32[]{:S(2)}) collective-permute-start(f16[96,2560]{1,0:T(8,128)(2,1)S(1)} %convert_element_type.38), channel_id=1, source_target_pairs={{0,2},{1,3},{2,0},{3,1},{4,6},{5,7},{6,4},{7,5},{8,10},{9,11},{10,... | collective-permute-start | bytes 1474568 | tf_op jit(solution)/shard_map/ppermute | solution.py:24
  78.2 21.2 %collective-permute-start.23 = (f32[96,2560]{1,0:T(8,128)S(1)}, f32[96,2560]{1,0:T(8,128)S(1)}, u32[]{:S(2)}, u32[]{:S(2)}) collective-permute-start(f32[96,2560]{1,0:T(8,128)S(1)} %get-tuple-element.79), channel_id=1, source_target_pairs={{0,1},{1,0},{2,3},{3,2},{4,5},{5,4},{6,7},{7,6},{8,9},{9,8},{10,11... | collective-permute-start | bytes 2949128 | tf_op jit(solution)/shard_map/ppermute | solution.py:24
  78.7 20.7 %collective-permute-start.24 = (f16[96,2560]{1,0:T(8,128)(2,1)S(1)}, f16[96,2560]{1,0:T(8,128)(2,1)S(1)}, u32[]{:S(2)}, u32[]{:S(2)}) collective-permute-start(f16[96,2560]{1,0:T(8,128)(2,1)S(1)} %add_convert_fusion.2), channel_id=1, source_target_pairs={{0,16},{1,17},{2,18},{3,19},{4,20},{5,21},{6,22},{7,23},{8,24},{9,... | collective-permute-start | bytes 1474568 | tf_op jit(solution)/shard_map/ppermute | solution.py:24

commit v4 on v3

v4 whole, which is shorter than its diff:
```python
import functools

import jax
import jax.numpy as jnp
from jax import lax
from jax.experimental import pallas as pl
from jax.experimental.pallas import tpu as pltpu
from jax.sharding import PartitionSpec as P

MIB = 1024 * 1024
together = lax.optimization_barrier


def bits_of(groups, slabs):
    slab_bits = slabs.bit_length() - 1
    total = (groups * slabs).bit_length() - 1
    shared = min(slab_bits - 1, total // 2)
    alpha = [slab_bits - 1] + list(range(shared - 1, 0, -1))
    beta = list(range(slab_bits - 2, shared - 1, -1)) + list(range(total - 1, slab_bits - 1, -1)) + [0]
    return alpha, beta


def exchange(value, bit, devices):
    return lax.ppermute(value, ("grp", "slab"), [(d, d ^ (1 << bit)) for d in range(devices)])


def energies(masks_a, masks_b, slabs, per, place, occ_a, occ_b, va_ref, vb_ref, ninv):
    width = ninv.shape[0] // len(masks_a)
    me = place[0]
    parts, occs = [], []
    for m in masks_b:
        other = jnp.bitwise_xor(me, m)
        for o in range(per):
            parts.append(vb_ref[pl.ds(other % slabs, 1), :])
            occs.append(jnp.full((1, width // per), occ_b[(other // slabs) * per + o], jnp.float32))
    vb, ob = jnp.concatenate(parts, axis=1), jnp.concatenate(occs, axis=1)
    for p, m in enumerate(masks_a):
        other = jnp.bitwise_xor(me, m)
        at = pl.multiple_of((other % slabs) * (width // per), 8)
        va = jnp.concatenate([va_ref[pl.ds(at, width // per), :]] * per, axis=0)
        oa = jnp.concatenate(
            [jnp.full((width // per, 1), occ_a[(other // slabs) * per + o], jnp.float32) for o in range(per)], axis=0
        )
        ninv[p * width:(p + 1) * width, :] = -1.0 / (((va + vb) - oa) - ob)


def magnitude(value):
    return jnp.max(jnp.max(jnp.abs(value), axis=1, keepdims=True), axis=0, keepdims=True).astype(jnp.float32)


def contract_amplitudes(n_a, n_b, early, spans, *refs):
    a_refs, b_refs, ninv = refs[:n_a], refs[n_a:n_a + n_b], refs[n_a + n_b]
    t_ref, tt, acat, bcat, scale_a, unit_a, unit_b = refs[n_a + n_b + 1:n_a + n_b + 8]
    outs = refs[n_a + n_b + 8:]
    largest = []
    for sources, joined in ((a_refs, acat), (b_refs, bcat)):
        at, top = 0, None
        for ref in sources:
            value = ref[...]
            joined[at:at + ref.shape[0], :] = value
            at += ref.shape[0]
            top = magnitude(value) if top is None else jnp.maximum(top, magnitude(value))
        largest.append(top)
    rows, cols = t_ref.shape
    step = 256 if cols % 256 == 0 else cols // 2
    top = None
    for c in range(0, cols, step):
        integrals = lax.dot_general(
            acat[...], bcat[c:c + step, :], (((1,), (1,)), ((), ())), preferred_element_type=jnp.float32
        )
        amps = integrals * ninv[:, c:c + step]
        top = magnitude(amps) if top is None else jnp.maximum(top, magnitude(amps))
        amps = amps.astype(jnp.bfloat16)
        t_ref[:, c:c + step] = amps
        tt[c:c + step, :] = amps.T
    unit = top * largest[1] * (float(cols) / 32768.0) + 1e-36
    unit_a[...] = jnp.broadcast_to(unit, unit_a.shape)
    scale_a[...] = jnp.broadcast_to(1.0 / unit, scale_a.shape)
    unit_b[...] = jnp.broadcast_to(top * largest[0] * (float(rows) / 32768.0) + 1e-36, unit_b.shape)
    rows_out(0, spans, tt, acat, *outs)


def rows_out(start, spans, left, right, *outs):
    aux = right.shape[1]
    tile = 512 if aux % 512 == 0 else 128
    rows = left[start:start + sum(spans), :]

    def one(k, _):
        at = pl.ds(pl.multiple_of(k * tile, tile), tile)
        acc = jnp.dot(rows, right[:, at], preferred_element_type=jnp.float32)
        low = 0
        for span, out in zip(spans, outs):
            out[:, at] = acc[low:low + span, :]
            low += span
        return 0

    lax.fori_loop(0, aux // tile, one, 0)


def body(orbital_alpha, orbital_beta, occ_alpha, occ_beta, virt_alpha, virt_beta):
    groups, slabs = lax.axis_size("grp"), lax.axis_size("slab")
    devices = groups * slabs
    me = lax.axis_index("grp") * slabs + lax.axis_index("slab")
    per, block, aux = orbital_alpha.shape
    width = per * block
    own_a, own_b = orbital_alpha.reshape(width, aux), orbital_beta.reshape(width, aux)
    alpha_bits, beta_bits = bits_of(groups, slabs)

    def masks(bits):
        found = [0]
        for bit in bits:
            found = found + [m | (1 << bit) for m in found]
        return found[::-1]

    masks_a, masks_b = masks(alpha_bits), masks([0] + beta_bits[:-1])
    n_a, n_b = len(masks_a), len(masks_b)
    rows, cols = n_a * width, n_b * width

    cut = [width]

    def sent_on(pieces, bits):
        for bit in bits:
            pieces = dict(pieces)
            pieces.update({m | (1 << bit): [exchange(v, bit, devices) for v in vs] for m, vs in list(pieces.items())})
        return pieces

    first_a, first_b = alpha_bits[0], beta_bits[0]
    pieces_a, pieces_b = sent_on({0: [own_a]}, alpha_bits[1:]), sent_on({0: [own_b]}, beta_bits[1:-1])
    near_a, near_b = exchange(own_a, first_a, devices), exchange(own_b, first_b, devices)
    vmem = pl.BlockSpec(memory_space=pltpu.VMEM)
    smem = pl.BlockSpec(memory_space=pltpu.SMEM)
    ninv = pl.pallas_call(
        functools.partial(energies, masks_a, masks_b, slabs, per),
        out_shape=jax.ShapeDtypeStruct((rows, cols), jnp.float32),
        in_specs=[smem] * 3 + [vmem] * 2,
        compiler_params=pltpu.CompilerParams(vmem_limit_bytes=12 * MIB),
        name="energies",
    )(me.reshape(1), occ_alpha, occ_beta, virt_alpha[:, None], virt_beta.reshape(slabs, block))
    pieces_b, pieces_a, near_a, near_b, ninv = together((pieces_b, pieces_a, near_a, near_b, ninv))
    pieces_a.update(sent_on({1 << first_a: [near_a]}, alpha_bits[1:]))
    pieces_b.update(sent_on({1 << first_b: [near_b]}, beta_bits[1:-1]))
    pieces_b = sent_on(pieces_b, [0])

    def blocks(count):
        return [jax.ShapeDtypeStruct((n, aux), jnp.float32) for n in cut * count]

    def pairs(names, outs):
        return {m: [out] for m, out in zip(names, outs)}

    early = max(n_b // 4, 2)
    list_a = [v for m in masks_a for v in pieces_a[m]]
    list_b = [v for m in masks_b for v in pieces_b[m]]
    opening = pl.pallas_call(
        functools.partial(contract_amplitudes, len(list_a), len(list_b), early, cut * early),
        out_shape=[
            jax.ShapeDtypeStruct((rows, cols), jnp.bfloat16),
            jax.ShapeDtypeStruct((cols, rows), jnp.bfloat16),
            jax.ShapeDtypeStruct((rows, aux), jnp.bfloat16),
            jax.ShapeDtypeStruct((cols, aux), jnp.bfloat16),
        ] + [jax.ShapeDtypeStruct((1, aux), jnp.float32)] * 3 + blocks(early),
        compiler_params=pltpu.CompilerParams(vmem_limit_bytes=28 * MIB),
        cost_estimate=pl.CostEstimate(
            flops=2 * rows * cols * aux, bytes_accessed=2 * (rows + cols) * aux * 2, transcendentals=0
        ),
        name="amplitudes",
    )(*list_a, *list_b, ninv)
    t, tt, acat, bcat, scale_a, unit_a, unit_b = opening[:7]

    def contracted(left, right, start, names, name):
        outs = pl.pallas_call(
            functools.partial(rows_out, start * width, cut * len(names)),
            out_shape=blocks(len(names)),
            compiler_params=pltpu.CompilerParams(vmem_limit_bytes=28 * MIB),
            cost_estimate=pl.CostEstimate(
                flops=2 * len(names) * width * right.size, bytes_accessed=len(names) * width * aux * 4 + right.size * 2,
                transcendentals=0,
            ),
            name=name,
        )(left, right)
        return pairs(names, outs)

    def narrow(value, scale):
        return (value * scale).astype(jnp.float16)

    def wide(value, unit):
        return value.astype(jnp.float32) * unit

    def passed_on(names, bits, level):
        flag = 1 << bits[level]
        gone = sum(1 << b for b in bits[:level])
        every = [m for m in names if m & flag and not m & gone]
        after = 1 << bits[level + 1] if level + 1 < len(bits) else flag
        ahead = [m for m in every if m & after]
        return ahead, [m for m in every if m not in ahead]

    def chips_sum(found):
        return {
            m: [v + exchange(w, 0, devices) for v, w in zip(vs, found[m | 1])] for m, vs in found.items() if not m & 1
        }

    bits_a, bits_b = alpha_bits[::-1], [b for b in beta_bits[::-1] if b]
    names_b = [m for m in masks_b if not m & 1]
    unit_b = unit_b + exchange(unit_b, 0, devices)
    units, scales = [unit_a, unit_b], [scale_a, 1.0 / unit_b]
    gb = chips_sum(pairs(masks_b, opening[7:]))
    ga = contracted(t, bcat, 0, masks_a, "alpha")
    for level in range(max(len(bits_a), len(bits_b))):
        jobs = [
            (which, parts, bits[level]) + passed_on(names, bits, level)
            for which, parts, names, bits in ((0, ga, masks_a, bits_a), (1, gb, names_b, bits_b)) if level < len(bits)
        ]

        def made(names_at):
            return [[narrow(job[1][m][0], scales[job[0]]) for m in job[names_at]] for job in jobs]

        def moved(values):
            return [[exchange(v, job[2], devices) for v in vs] for job, vs in zip(jobs, values)]

        def added(names_at, values):
            for job, vs in zip(jobs, values):
                for m, v in zip(job[names_at], vs):
                    job[1][m ^ (1 << job[2])][0] += wide(v, partner[job[0]])

        if level == 0:
            sent, units, tt, acat = together((made(3), units, tt, acat))
        else:
            sent = made(3)
        got = moved(sent)
        partner = {job[0]: exchange(units[job[0]], job[2], devices) for job in jobs}
        if level == 0:
            gb.update(chips_sum(contracted(tt, acat, early, masks_b[early:], "beta")))
        got, rest = together((got, made(4)))
        rest = moved(rest)
        added(3, got)
        added(4, rest)
        units = [units[w] + partner[w] if w in partner else units[w] for w in range(2)]
        scales = [1.0 / unit for unit in units]

    def whole(parts):
        return parts[0].reshape(orbital_alpha.shape)

    return whole(ga[0]), whole(gb[0])


def solution(mesh):
    in_specs = (P("grp", "slab", None), P("grp", "slab", None), P(), P(), P(), P())
    out_specs = (P("grp", "slab", None), P("grp", "slab", None))
    return jax.shard_map(body, mesh=mesh, in_specs=in_specs, out_specs=out_specs, check_vma=False)
```

time: 102 us -> 123 us (1.21)
  waiting for transfers between devices: 54.2 us -> 65.9 us
  other arithmetic: 4.26 us -> 10.9 us
  local copies, waits for them, and re-layouts: 5.64 us -> 8.88 us
  starting transfers between devices: 25.5 us -> 23.6 us
  Pallas kernels: 10.9 us -> 12.3 us
    ppermute x25, waiting for transfers between devices: 54.2 us -> 65.9 us  [exchange(): lax.ppermute(value, ('grp', 'slab'), [(d, d ^ 1 << bit) for d in range(de...]
    convert_element_type x6 -> x5, other arithmetic: 0.67 us -> 6.04 us  [narrow(): return (value * scale).astype(jnp.float16)]
    unnamed x12 -> x28, local copies, waits for them, and re-layouts: 3.37 us -> 7.16 us
    ppermute x25, starting transfers between devices: 25.5 us -> 23.6 us  [exchange(): lax.ppermute(value, ('grp', 'slab'), [(d, d ^ 1 << bit) for d in range(de...]
    pallas_call x4 -> x3, Pallas kernels: 10 us -> 11.5 us  [the longest x1 5.78 us: body(): pl.pallas_call(functools.partial(contract_amplitudes, len(list_a), len(li...]
  transfers between devices with their start and end apart: 25 -> 25, of which waited for: 11 -> 10; matrix products, arithmetic and copies ran while one was open for 4% -> 7% of each run, Pallas kernels for 4% -> 3%
where the time goes in v4:
time: 123 us; the launch traced here: 122 us
  waiting for transfers between devices  65.9 us (54%)
  starting transfers between devices  23.6 us (19%)
  Pallas kernels  12.3 us (10%)
  other arithmetic  10.9 us (9%)
  local copies, waits for them, and re-layouts  8.88 us (7%)
    ppermute x25, waiting for transfers between devices, exchange(): lax.ppermute(value, ('grp', 'slab'), [(d, d ^ 1 << bit) for d in range(de...  65.9 us
    ppermute x25, starting transfers between devices, exchange(): lax.ppermute(value, ('grp', 'slab'), [(d, d ^ 1 << bit) for d in range(de...  23.6 us
    unnamed x28, local copies, waits for them, and re-layouts  7.16 us
    convert_element_type x5, other arithmetic, narrow(): return (value * scale).astype(jnp.float16)  6.04 us
    pallas_call x1, Pallas kernels, body(): pl.pallas_call(functools.partial(contract_amplitudes, len(list_a), len(li...  5.78 us
    pallas_call x2, Pallas kernels, contracted(): pl.pallas_call(functools.partial(rows_out, start * width, cut * len(names...  5.72 us
    reshape x2, other arithmetic, whole(): return parts[0].reshape(orbital_alpha.shape)  4.57 us
  transfers between devices with their start and end apart: 25, of which 10 were waited for; matrix products, arithmetic and copies ran while one was open for 7% of the time, Pallas kernels for 3%

profile of v4, /device:TPU:0, one launch (start us, length us, event | category | flops | bytes accessed | tf_op | source)
XLA Modules:
  0.0 122.5 jit_solution(1605165952558750303)
XLA Ops:
  0.6 4.1 %collective-permute-start.2 = (bf16[96,2560]{1,0:T(8,128)(2,1)}, bf16[96,2560]{1,0:T(8,128)(2,1)S(1)}, u32[]{:S(2)}, u32[]{:S(2)}) collective-permute-start(bf16[96,2560]{1,0:T(8,128)(2,1)} %bitcast.7), channel_id=1, source_target_pairs={{0,8},{1,9},{2,10},{3,11},{4,12},{5,13},{6,14},{7,15},{8,0},{9,1},... | collective-permute-start | bytes 1474568 | tf_op jit(solution)/shard_map/ppermute | solution.py:24
  4.8 1.5 %collective-permute-start.1 = (bf16[96,2560]{1,0:T(8,128)(2,1)}, bf16[96,2560]{1,0:T(8,128)(2,1)S(1)}, u32[]{:S(2)}, u32[]{:S(2)}) collective-permute-start(bf16[96,2560]{1,0:T(8,128)(2,1)} %bitcast.8), channel_id=1, source_target_pairs={{0,2},{1,3},{2,0},{3,1},{4,6},{5,7},{6,4},{7,5},{8,10},{9,11},{10,... | collective-permute-start | bytes 1474568 | tf_op jit(solution)/shard_map/ppermute | solution.py:24
  6.2 1.6 %collective-permute-start.3 = (bf16[96,2560]{1,0:T(8,128)(2,1)}, bf16[96,2560]{1,0:T(8,128)(2,1)S(1)}, u32[]{:S(2)}, u32[]{:S(2)}) collective-permute-start(bf16[96,2560]{1,0:T(8,128)(2,1)} %bitcast.10), channel_id=1, source_target_pairs={{0,4},{1,5},{2,6},{3,7},{4,0},{5,1},{6,2},{7,3},{8,12},{9,13},{10,... | collective-permute-start | bytes 1474568 | tf_op jit(solution)/shard_map/ppermute | solution.py:24
  7.8 1.5 %collective-permute-start = (bf16[96,2560]{1,0:T(8,128)(2,1)}, bf16[96,2560]{1,0:T(8,128)(2,1)}, u32[]{:S(2)}, u32[]{:S(2)}) collective-permute-start(bf16[96,2560]{1,0:T(8,128)(2,1)} %bitcast.11), channel_id=1, source_target_pairs={{0,16},{1,17},{2,18},{3,19},{4,20},{5,21},{6,22},{7,23},{8,24},{9,... | collective-permute-start | bytes 1474568 | tf_op jit(solution)/shard_map/ppermute | solution.py:24
  10.1 1.0 broadcast_in_dim.4.va_ref
  13.2 13.6 %collective-permute-done.2.refs_2_ = bf16[96,2560]{1,0:T(8,128)(2,1)S(1)} collective-permute-done((bf16[96,2560]{1,0:T(8,128)(2,1)}, bf16[96,2560]{1,0:T(8,128)(2,1)S(1)}, u32[]{:S(2)}, u32[]{:S(2)}) %collective-permute-start.2) | collective-permute-done | bytes 491552 | tf_op jit(solution)/shard_map/ppermute | solution.py:24
  28.2 1.6 %collective-permute-start.5 = (bf16[96,2560]{1,0:T(8,128)(2,1)S(1)}, bf16[96,2560]{1,0:T(8,128)(2,1)S(1)}, u32[]{:S(2)}, u32[]{:S(2)}) collective-permute-start(bf16[96,2560]{1,0:T(8,128)(2,1)S(1)} %collective-permute-done.3.refs_9_), channel_id=1, source_target_pairs={{0,16},{1,17},{2,18},{3,19},{4,20},{5,21},{6,22},{7,23},{8,24},{9,... | collective-permute-start | bytes 1474568 | tf_op jit(solution)/shard_map/ppermute | solution.py:24
  32.0 8.0 %collective-permute-done.5.refs_5_ = bf16[96,2560]{1,0:T(8,128)(2,1)S(1)} collective-permute-done((bf16[96,2560]{1,0:T(8,128)(2,1)S(1)}, bf16[96,2560]{1,0:T(8,128)(2,1)S(1)}, u32[]{:S(2)}, u32[]{:S(2)}) %collective-permute-start.5) | collective-permute-done | bytes 491552 | tf_op jit(solution)/shard_map/ppermute | solution.py:24
  40.0 4.3 %collective-permute-done.4.refs_0_ = bf16[96,2560]{1,0:T(8,128)(2,1)S(1)} collective-permute-done((bf16[96,2560]{1,0:T(8,128)(2,1)S(1)}, bf16[96,2560]{1,0:T(8,128)(2,1)S(1)}, u32[]{:S(2)}, u32[]{:S(2)}) %collective-permute-start.4) | collective-permute-done | bytes 491552 | tf_op jit(solution)/shard_map/ppermute | solution.py:24
  44.3 1.0 copy-done.5
  45.3 1.0 copy-done.7
  46.3 5.8 %amplitudes.1 = (bf16[384,768]{1,0:T(8,128)(2,1)S(1)}, bf16[768,384]{1,0:T(8,128)(2,1)S(1)}, bf16[384,2560]{1,0:T(8,128)(2,1)S(1)}, bf16[768,2560]{1,0:T(8,128)(...) custom-call(bf16[96,2560]{1,0:T(8,128)(2,1)S(1)} %collective-permute, ...), custom_call_target="tpu_custom_call" | custom-call | flops 1509949440 | bytes 11796480 | tf_op jit(solution)/shard_map/amplitudes/pallas_call | solution.py:153
  52.6 2.4 %alpha.1 = (f32[96,2560]{1,0:T(8,128)S(1)}, f32[96,2560]{1,0:T(8,128)S(1)}, f32[96,2560]{1,0:T(8,128)S(1)}, f32[96,2560]{1,0:T(8,128)S(1)}) custom-call(bf16[384,768]{1,0:T(8,128)(2,1)S(1)} %get-tuple-element.47.left, bf16[768,2560]{1,0:T(8,128)(2,1)S(1)} %get-tuple-element.48.right), custom_call_target="tpu_custom_call" | custom-call | flops 1509949440 | bytes 7864320 | tf_op jit(solution)/shard_map/alpha/pallas_call | solution.py:170
  55.0 1.0 copy-done
  56.0 0.9 copy-done.1
  57.0 2.5 %multiply_convert_fusion.3 = (f16[96,2560]{1,0:T(8,128)(2,1)}, f16[96,2560]{1,0:T(8,128)(2,1)S(1)}) fusion(f32[96,2560]{1,0:T(8,128)} %copy-done.1, f32[2560]{0:T(1024)S(1)} %reduce, f32[96,2560]{1,0:T(8,128)} %copy-done), kind=kLoop, calls=%fused_computation.5 | loop fusion | flops 983040 | bytes 2959360 | tf_op jit(solution)/shard_map/convert_element_type | solution.py:183
  59.5 1.5 %multiply_convert_fusion.4 = f16[96,2560]{1,0:T(8,128)(2,1)S(1)} fusion(f32[96,2560]{1,0:T(8,128)S(1)} %get-tuple-element.52, f32[96,2560]{1,0:T(8,128)} %collective-permute-done.10, f32[2560]{0:T(1024)S(1)} %get-tuple-element.82), kind=kLoop, calls=%fused_computation.6 | loop fusion | flops 737280 | bytes 2467840 | tf_op jit(solution)/shard_map/convert_element_type | solution.py:183
  61.3 3.3 %beta.1 = (f32[96,2560]{1,0:T(8,128)S(1)}, f32[96,2560]{1,0:T(8,128)S(1)}, f32[96,2560]{1,0:T(8,128)S(1)}, f32[96,2560]{1,0:T(8,128)S(1)}, f32[96,2560]{1,0:T(8,128)}, /*index=5*/f32[96,2560]{1,0:T(8,128)S(1)}) custom-call(bf16[768,384]{1,0:T(8,128)(2,1)S(1)} %copy-done.13, bf16[384,2560]{1,0:T(8,128)(2,1)S(1)} %copy-done.11), custom_call_target="tpu_custom_call" | custom-call | flops 1132462080 | bytes 7864320 | tf_op jit(solution)/shard_map/beta/pallas_call | solution.py:170
  64.7 0.9 collective-permute-start.16
  66.1 1.1 collective-permute-start.12
  67.2 1.6 %collective-permute-start.13 = (f16[96,2560]{1,0:T(8,128)(2,1)S(1)}, f16[96,2560]{1,0:T(8,128)(2,1)S(1)}, u32[]{:S(2)}, u32[]{:S(2)}) collective-permute-start(f16[96,2560]{1,0:T(8,128)(2,1)S(1)} %multiply_convert_fusion.4), channel_id=1, source_target_pairs={{0,16},{1,17},{2,18},{3,19},{4,20},{5,21},{6,22},{7,23},{8,24},{9,... | collective-permute-start | bytes 1474568 | tf_op jit(solution)/shard_map/ppermute | solution.py:24
  69.5 9.6 %collective-permute-done.12 = f16[96,2560]{1,0:T(8,128)(2,1)S(1)} collective-permute-done((f16[96,2560]{1,0:T(8,128)(2,1)S(1)}, f16[96,2560]{1,0:T(8,128)(2,1)S(1)}, u32[]{:S(2)}, u32[]{:S(2)}) %collective-permute-start.12) | collective-permute-done | bytes 491552 | tf_op jit(solution)/shard_map/ppermute | solution.py:24
  79.9 1.0 multiply_convert_fusion.1
  81.6 1.0 multiply_convert_fusion
  82.6 2.9 %collective-permute-start.20 = (f16[96,2560]{1,0:T(8,128)(2,1)}, f16[96,2560]{1,0:T(8,128)(2,1)}, u32[]{:S(2)}, u32[]{:S(2)}) collective-permute-start(f16[96,2560]{1,0:T(8,128)(2,1)} %multiply_convert_fusion), channel_id=1, source_target_pairs={{0,4},{1,5},{2,6},{3,7},{4,0},{5,1},{6,2},{7,3},{8,12},{9,13},{10,... | collective-permute-start | bytes 1474568 | tf_op jit(solution)/shard_map/ppermute | solution.py:24
  85.5 1.3 %collective-permute-start.15 = (f16[96,2560]{1,0:T(8,128)(2,1)}, f16[96,2560]{1,0:T(8,128)(2,1)}, u32[]{:S(2)}, u32[]{:S(2)}) collective-permute-start(f16[96,2560]{1,0:T(8,128)(2,1)} %get-tuple-element.65), channel_id=1, source_target_pairs={{0,2},{1,3},{2,0},{3,1},{4,6},{5,7},{6,4},{7,5},{8,10},{9,11},{10,... | collective-permute-start | bytes 1474568 | tf_op jit(solution)/shard_map/ppermute | solution.py:24
  86.8 18.0 %collective-permute-done.21 = f32[1,2560]{1,0:T(1,128)S(1)} collective-permute-done((f32[1,2560]{1,0:T(1,128)S(1)}, f32[1,2560]{1,0:T(1,128)S(1)}, u32[]{:S(2)}, u32[]{:S(2)}) %collective-permute-start.21) | collective-permute-done | bytes 10272 | tf_op jit(solution)/shard_map/ppermute | solution.py:24
  105.6 2.8 %collective-permute-done.24 = f32[1,2560]{1,0:T(1,128)S(1)} collective-permute-done((f32[1,2560]{1,0:T(1,128)S(1)}, f32[1,2560]{1,0:T(1,128)S(1)}, u32[]{:S(2)}, u32[]{:S(2)}) %collective-permute-start.24) | collective-permute-done | bytes 10272 | tf_op jit(solution)/shard_map/ppermute | solution.py:24
  108.5 1.6 %collective-permute-start.23 = (f16[96,2560]{1,0:T(8,128)(2,1)S(1)}, f16[96,2560]{1,0:T(8,128)(2,1)S(1)}, u32[]{:S(2)}, u32[]{:S(2)}) collective-permute-start(f16[96,2560]{1,0:T(8,128)(2,1)S(1)} %multiply_convert_fusion.2), channel_id=1, source_target_pairs={{0,16},{1,17},{2,18},{3,19},{4,20},{5,21},{6,22},{7,23},{8,24},{9,... | collective-permute-start | bytes 1474568 | tf_op jit(solution)/shard_map/ppermute | solution.py:24
  110.2 2.3 %add_bitcast_fusion.1 = f32[1,96,2560]{2,1,0:T(8,128)} fusion(f16[96,2560]{1,0:T(8,128)(2,1)} %collective-permute-done.17, f32[96,2560]{1,0:T(8,128)S(1)} %get-tuple-element.49, f16[96,2560]{1,0:T(8,128)(2,1)} %collective-permute-done.15, f32[2560]{0:T(1024)S(1)} %reduce.6, f32[2560]{0:T(1024)S(1)} %get-tuple-element.87), kind=kLoop, calls=%fused_computation.1 | loop fusion | flops 1474560 | bytes 2969600 | tf_op jit(solution)/shard_map/reshape | solution.py:240
  112.5 7.7 %collective-permute-done.23 = f16[96,2560]{1,0:T(8,128)(2,1)S(1)} collective-permute-done((f16[96,2560]{1,0:T(8,128)(2,1)S(1)}, f16[96,2560]{1,0:T(8,128)(2,1)S(1)}, u32[]{:S(2)}, u32[]{:S(2)}) %collective-permute-start.23) | collective-permute-done | bytes 491552 | tf_op jit(solution)/shard_map/ppermute | solution.py:24
  120.2 2.2 %add_bitcast_fusion = f32[1,96,2560]{2,1,0:T(8,128)} fusion(f16[96,2560]{1,0:T(8,128)(2,1)} %collective-permute-done.20, f16[96,2560]{1,0:T(8,128)(2,1)S(1)} %collective-permute-done.23, f32[96,2560]{1,0:T(8,128)S(1)} %get-tuple-element.74, f32[96,2560]{1,0:T(8,128)S(1)} %collective-permute-done.22, f32[2560]{0:T(1024)S(1)} %reduce.7, ...), kind=kLoop, calls=%fused_computation | loop fusion | flops 1720320 | bytes 3952640 | tf_op jit(solution)/shard_map/reshape | solution.py:240
  (65 shorter events, 11.1 us)
Async XLA Ops:
  0.6 43.6 %copy-start.2 = (bf16[1,96,2560]{2,1,0:T(8,128)(2,1)S(1)}, bf16[1,96,2560]{2,1,0:T(8,128)(2,1)}, u32[]{:S(2)}) copy-start(bf16[1,96,2560]{2,1,0:T(8,128)(2,1)} %param.6) | copy-start | bytes 1474564
  0.6 31.0 %copy-start.3 = (bf16[1,96,2560]{2,1,0:T(8,128)(2,1)S(1)}, bf16[1,96,2560]{2,1,0:T(8,128)(2,1)}, u32[]{:S(2)}) copy-start(bf16[1,96,2560]{2,1,0:T(8,128)(2,1)} %param.7) | copy-start | bytes 1474564
  0.6 26.2 %collective-permute-start.2 = (bf16[96,2560]{1,0:T(8,128)(2,1)}, bf16[96,2560]{1,0:T(8,128)(2,1)S(1)}, u32[]{:S(2)}, u32[]{:S(2)}) collective-permute-start(bf16[96,2560]{1,0:T(8,128)(2,1)} %bitcast.7), channel_id=1, source_target_pairs={{0,8},{1,9},{2,10},{3,11},{4,12},{5,13},{6,14},{7,15},{8,0},{9,1},... | collective-permute-start | bytes 1474568 | tf_op jit(solution)/shard_map/ppermute | solution.py:24
  4.8 22.1 %collective-permute-start.1 = (bf16[96,2560]{1,0:T(8,128)(2,1)}, bf16[96,2560]{1,0:T(8,128)(2,1)S(1)}, u32[]{:S(2)}, u32[]{:S(2)}) collective-permute-start(bf16[96,2560]{1,0:T(8,128)(2,1)} %bitcast.8), channel_id=1, source_target_pairs={{0,2},{1,3},{2,0},{3,1},{4,6},{5,7},{6,4},{7,5},{8,10},{9,11},{10,... | collective-permute-start | bytes 1474568 | tf_op jit(solution)/shard_map/ppermute | solution.py:24
  6.2 22.0 %collective-permute-start.3 = (bf16[96,2560]{1,0:T(8,128)(2,1)}, bf16[96,2560]{1,0:T(8,128)(2,1)S(1)}, u32[]{:S(2)}, u32[]{:S(2)}) collective-permute-start(bf16[96,2560]{1,0:T(8,128)(2,1)} %bitcast.10), channel_id=1, source_target_pairs={{0,4},{1,5},{2,6},{3,7},{4,0},{5,1},{6,2},{7,3},{8,12},{9,13},{10,... | collective-permute-start | bytes 1474568 | tf_op jit(solution)/shard_map/ppermute | solution.py:24
  7.8 20.4 %collective-permute-start = (bf16[96,2560]{1,0:T(8,128)(2,1)}, bf16[96,2560]{1,0:T(8,128)(2,1)}, u32[]{:S(2)}, u32[]{:S(2)}) collective-permute-start(bf16[96,2560]{1,0:T(8,128)(2,1)} %bitcast.11), channel_id=1, source_target_pairs={{0,16},{1,17},{2,18},{3,19},{4,20},{5,21},{6,22},{7,23},{8,24},{9,... | collective-permute-start | bytes 1474568 | tf_op jit(solution)/shard_map/ppermute | solution.py:24
  28.2 11.7 %collective-permute-start.5 = (bf16[96,2560]{1,0:T(8,128)(2,1)S(1)}, bf16[96,2560]{1,0:T(8,128)(2,1)S(1)}, u32[]{:S(2)}, u32[]{:S(2)}) collective-permute-start(bf16[96,2560]{1,0:T(8,128)(2,1)S(1)} %collective-permute-done.3.refs_9_), channel_id=1, source_target_pairs={{0,16},{1,17},{2,18},{3,19},{4,20},{5,21},{6,22},{7,23},{8,24},{9,... | collective-permute-start | bytes 1474568 | tf_op jit(solution)/shard_map/ppermute | solution.py:24
  29.8 14.4 %collective-permute-start.8 = (bf16[96,2560]{1,0:T(8,128)(2,1)S(1)}, bf16[96,2560]{1,0:T(8,128)(2,1)S(1)}, u32[]{:S(2)}, u32[]{:S(2)}) collective-permute-start(bf16[96,2560]{1,0:T(8,128)(2,1)S(1)} %collective-permute-done.3.refs_9_), channel_id=1, source_target_pairs={{0,1},{1,0},{2,3},{3,2},{4,5},{5,4},{6,7},{7,6},{8,9},{9,8},{10,11... | collective-permute-start | bytes 1474568 | tf_op jit(solution)/shard_map/ppermute | solution.py:24
  30.6 13.6 %collective-permute-start.4 = (bf16[96,2560]{1,0:T(8,128)(2,1)S(1)}, bf16[96,2560]{1,0:T(8,128)(2,1)S(1)}, u32[]{:S(2)}, u32[]{:S(2)}) collective-permute-start(bf16[96,2560]{1,0:T(8,128)(2,1)S(1)} %collective-permute-done.2.refs_2_), channel_id=1, source_target_pairs={{0,2},{1,3},{2,0},{3,1},{4,6},{5,7},{6,4},{7,5},{8,10},{9,11},{10,... | collective-permute-start | bytes 1474568 | tf_op jit(solution)/shard_map/ppermute | solution.py:24
  31.5 12.8 %collective-permute-start.7 = (bf16[96,2560]{1,0:T(8,128)(2,1)}, bf16[96,2560]{1,0:T(8,128)(2,1)S(1)}, u32[]{:S(2)}, u32[]{:S(2)}) collective-permute-start(bf16[96,2560]{1,0:T(8,128)(2,1)} %collective-permute-done.refs_7_), channel_id=1, source_target_pairs={{0,1},{1,0},{2,3},{3,2},{4,5},{5,4},{6,7},{7,6},{8,9},{9,8},{10,11... | collective-permute-start | bytes 1474568 | tf_op jit(solution)/shard_map/ppermute | solution.py:24
  31.7 12.5 %collective-permute-start.9 = (bf16[96,2560]{1,0:T(8,128)(2,1)S(1)}, bf16[96,2560]{1,0:T(8,128)(2,1)S(1)}, u32[]{:S(2)}, u32[]{:S(2)}) collective-permute-start(bf16[96,2560]{1,0:T(8,128)(2,1)S(1)} %bitcast.12), channel_id=1, source_target_pairs={{0,1},{1,0},{2,3},{3,2},{4,5},{5,4},{6,7},{7,6},{8,9},{9,8},{10,11... | collective-permute-start | bytes 1474568 | tf_op jit(solution)/shard_map/ppermute | solution.py:24
  40.0 4.3 %collective-permute-start.6 = (bf16[96,2560]{1,0:T(8,128)(2,1)S(1)}, bf16[96,2560]{1,0:T(8,128)(2,1)S(1)}, u32[]{:S(2)}, u32[]{:S(2)}) collective-permute-start(bf16[96,2560]{1,0:T(8,128)(2,1)S(1)} %collective-permute-done.5.refs_5_), channel_id=1, source_target_pairs={{0,1},{1,0},{2,3},{3,2},{4,5},{5,4},{6,7},{7,6},{8,9},{9,8},{10,11... | collective-permute-start | bytes 1474568 | tf_op jit(solution)/shard_map/ppermute | solution.py:24
  44.2 1.0 copy-start.5
  52.1 2.9 %copy-start.10 = (bf16[384,2560]{1,0:T(8,128)(2,1)}, bf16[384,2560]{1,0:T(8,128)(2,1)S(1)}, u32[]{:S(2)}) copy-start(bf16[384,2560]{1,0:T(8,128)(2,1)S(1)} %get-tuple-element.62.right) | copy-start | bytes 5898244
  52.1 2.9 %copy-start.12 = (bf16[768,384]{1,0:T(8,128)(2,1)}, bf16[768,384]{1,0:T(8,128)(2,1)S(1)}, u32[]{:S(2)}) copy-start(bf16[768,384]{1,0:T(8,128)(2,1)S(1)} %get-tuple-element.61.left) | copy-start | bytes 1769476
  52.1 7.4 %collective-permute-start.11 = (f32[1,2560]{1,0:T(1,128)S(1)}, f32[1,2560]{1,0:T(1,128)S(1)}, u32[]{:S(2)}, u32[]{:S(2)}) collective-permute-start(f32[1,2560]{1,0:T(1,128)S(1)} %get-tuple-element.54), channel_id=1, source_target_pairs={{0,1},{1,0},{2,3},{3,2},{4,5},{5,4},{6,7},{7,6},{8,9},{9,8},{10,11... | collective-permute-start | bytes 30728 | tf_op jit(solution)/shard_map/ppermute | solution.py:24
  52.1 7.4 %collective-permute-start.10 = (f32[96,2560]{1,0:T(8,128)}, f32[96,2560]{1,0:T(8,128)}, u32[]{:S(2)}, u32[]{:S(2)}) collective-permute-start(f32[96,2560]{1,0:T(8,128)} %get-tuple-element.53), channel_id=1, source_target_pairs={{0,1},{1,0},{2,3},{3,2},{4,5},{5,4},{6,7},{7,6},{8,9},{9,8},{10,11... | collective-permute-start | bytes 2949128 | tf_op jit(solution)/shard_map/ppermute | solution.py:24
  57.0 4.0 %copy-start.13 = (bf16[768,384]{1,0:T(8,128)(2,1)S(1)}, bf16[768,384]{1,0:T(8,128)(2,1)}, u32[]{:S(2)}) copy-start(bf16[768,384]{1,0:T(8,128)(2,1)} %copy-done.12) | copy-start | bytes 1769476
  59.5 1.8 %copy-start.11 = (bf16[384,2560]{1,0:T(8,128)(2,1)S(1)}, bf16[384,2560]{1,0:T(8,128)(2,1)}, u32[]{:S(2)}) copy-start(bf16[384,2560]{1,0:T(8,128)(2,1)} %copy-done.10) | copy-start | bytes 5898244
  64.7 4.7 %collective-permute-start.14 = (f32[96,2560]{1,0:T(8,128)S(1)}, f32[96,2560]{1,0:T(8,128)S(1)}, u32[]{:S(2)}, u32[]{:S(2)}) collective-permute-start(f32[96,2560]{1,0:T(8,128)S(1)} %get-tuple-element.64), channel_id=1, source_target_pairs={{0,1},{1,0},{2,3},{3,2},{4,5},{5,4},{6,7},{7,6},{8,9},{9,8},{10,11... | collective-permute-start | bytes 2949128 | tf_op jit(solution)/shard_map/ppermute | solution.py:24
  64.7 4.1 %collective-permute-start.16 = (f32[1,2560]{1,0:T(1,128)S(1)}, f32[1,2560]{1,0:T(1,128)S(1)}, u32[]{:S(2)}, u32[]{:S(2)}) collective-permute-start(f32[1,2560]{1,0:T(1,128)S(1)} %get-tuple-element.66), channel_id=1, source_target_pairs={{0,2},{1,3},{2,0},{3,1},{4,6},{5,7},{6,4},{7,5},{8,10},{9,11},{10,... | collective-permute-start | bytes 30728 | tf_op jit(solution)/shard_map/ppermute | solution.py:24
  65.6 3.7 %collective-permute-start.19 = (f32[1,2560]{1,0:T(1,128)S(1)}, f32[1,2560]{1,0:T(1,128)S(1)}, u32[]{:S(2)}, u32[]{:S(2)}) collective-permute-start(f32[1,2560]{1,0:T(1,128)S(1)} %get-tuple-element.72), channel_id=1, source_target_pairs={{0,16},{1,17},{2,18},{3,19},{4,20},{5,21},{6,22},{7,23},{8,24},{9,... | collective-permute-start | bytes 30728 | tf_op jit(solution)/shard_map/ppermute | solution.py:24
  66.1 13.0 %collective-permute-start.12 = (f16[96,2560]{1,0:T(8,128)(2,1)S(1)}, f16[96,2560]{1,0:T(8,128)(2,1)S(1)}, u32[]{:S(2)}, u32[]{:S(2)}) collective-permute-start(f16[96,2560]{1,0:T(8,128)(2,1)S(1)} %get-tuple-element.58), channel_id=1, source_target_pairs={{0,2},{1,3},{2,0},{3,1},{4,6},{5,7},{6,4},{7,5},{8,10},{9,11},{10,... | collective-permute-start | bytes 1474568 | tf_op jit(solution)/shard_map/ppermute | solution.py:24
  67.2 12.7 %collective-permute-start.13 = (f16[96,2560]{1,0:T(8,128)(2,1)S(1)}, f16[96,2560]{1,0:T(8,128)(2,1)S(1)}, u32[]{:S(2)}, u32[]{:S(2)}) collective-permute-start(f16[96,2560]{1,0:T(8,128)(2,1)S(1)} %multiply_convert_fusion.4), channel_id=1, source_target_pairs={{0,16},{1,17},{2,18},{3,19},{4,20},{5,21},{6,22},{7,23},{8,24},{9,... | collective-permute-start | bytes 1474568 | tf_op jit(solution)/shard_map/ppermute | solution.py:24
  68.8 12.9 %collective-permute-start.18 = (f32[96,2560]{1,0:T(8,128)S(1)}, f32[96,2560]{1,0:T(8,128)S(1)}, u32[]{:S(2)}, u32[]{:S(2)}) collective-permute-start(f32[96,2560]{1,0:T(8,128)S(1)} %get-tuple-element.70), channel_id=1, source_target_pairs={{0,1},{1,0},{2,3},{3,2},{4,5},{5,4},{6,7},{7,6},{8,9},{9,8},{10,11... | collective-permute-start | bytes 2949128 | tf_op jit(solution)/shard_map/ppermute | solution.py:24
  80.9 29.2 %collective-permute-start.17 = (f16[96,2560]{1,0:T(8,128)(2,1)}, f16[96,2560]{1,0:T(8,128)(2,1)}, u32[]{:S(2)}, u32[]{:S(2)}) collective-permute-start(f16[96,2560]{1,0:T(8,128)(2,1)} %multiply_convert_fusion.1), channel_id=1, source_target_pairs={{0,8},{1,9},{2,10},{3,11},{4,12},{5,13},{6,14},{7,15},{8,0},{9,1},... | collective-permute-start | bytes 1474568 | tf_op jit(solution)/shard_map/ppermute | solution.py:24
  82.6 27.5 %collective-permute-start.20 = (f16[96,2560]{1,0:T(8,128)(2,1)}, f16[96,2560]{1,0:T(8,128)(2,1)}, u32[]{:S(2)}, u32[]{:S(2)}) collective-permute-start(f16[96,2560]{1,0:T(8,128)(2,1)} %multiply_convert_fusion), channel_id=1, source_target_pairs={{0,4},{1,5},{2,6},{3,7},{4,0},{5,1},{6,2},{7,3},{8,12},{9,13},{10,... | collective-permute-start | bytes 1474568 | tf_op jit(solution)/shard_map/ppermute | solution.py:24
  85.5 24.6 %collective-permute-start.15 = (f16[96,2560]{1,0:T(8,128)(2,1)}, f16[96,2560]{1,0:T(8,128)(2,1)}, u32[]{:S(2)}, u32[]{:S(2)}) collective-permute-start(f16[96,2560]{1,0:T(8,128)(2,1)} %get-tuple-element.65), channel_id=1, source_target_pairs={{0,2},{1,3},{2,0},{3,1},{4,6},{5,7},{6,4},{7,5},{8,10},{9,11},{10,... | collective-permute-start | bytes 1474568 | tf_op jit(solution)/shard_map/ppermute | solution.py:24
  86.8 25.6 %collective-permute-start.22 = (f32[96,2560]{1,0:T(8,128)}, f32[96,2560]{1,0:T(8,128)S(1)}, u32[]{:S(2)}, u32[]{:S(2)}) collective-permute-start(f32[96,2560]{1,0:T(8,128)} %get-tuple-element.75), channel_id=1, source_target_pairs={{0,1},{1,0},{2,3},{3,2},{4,5},{5,4},{6,7},{7,6},{8,9},{9,8},{10,11... | collective-permute-start | bytes 2949128 | tf_op jit(solution)/shard_map/ppermute | solution.py:24
  86.8 18.0 %collective-permute-start.21 = (f32[1,2560]{1,0:T(1,128)S(1)}, f32[1,2560]{1,0:T(1,128)S(1)}, u32[]{:S(2)}, u32[]{:S(2)}) collective-permute-start(f32[1,2560]{1,0:T(1,128)S(1)} %get-tuple-element.81), channel_id=1, source_target_pairs={{0,8},{1,9},{2,10},{3,11},{4,12},{5,13},{6,14},{7,15},{8,0},{9,1},... | collective-permute-start | bytes 30728 | tf_op jit(solution)/shard_map/ppermute | solution.py:24
  104.8 3.7 %collective-permute-start.24 = (f32[1,2560]{1,0:T(1,128)S(1)}, f32[1,2560]{1,0:T(1,128)S(1)}, u32[]{:S(2)}, u32[]{:S(2)}) collective-permute-start(f32[1,2560]{1,0:T(1,128)S(1)} %get-tuple-element.79), channel_id=1, source_target_pairs={{0,4},{1,5},{2,6},{3,7},{4,0},{5,1},{6,2},{7,3},{8,12},{9,13},{10,... | collective-permute-start | bytes 30728 | tf_op jit(solution)/shard_map/ppermute | solution.py:24
  108.5 11.7 %collective-permute-start.23 = (f16[96,2560]{1,0:T(8,128)(2,1)S(1)}, f16[96,2560]{1,0:T(8,128)(2,1)S(1)}, u32[]{:S(2)}, u32[]{:S(2)}) collective-permute-start(f16[96,2560]{1,0:T(8,128)(2,1)S(1)} %multiply_convert_fusion.2), channel_id=1, source_target_pairs={{0,16},{1,17},{2,18},{3,19},{4,20},{5,21},{6,22},{7,23},{8,24},{9,... | collective-permute-start | bytes 1474568 | tf_op jit(solution)/shard_map/ppermute | solution.py:24
  (7 other events, 5.8 us)

commit v5 on v4

--- a/solution.py
+++ b/solution.py
@@ -74,9 +74,9 @@
         t_ref[:, c:c + step] = amps
         tt[c:c + step, :] = amps.T
     unit = top * largest[1] * (float(cols) / 32768.0) + 1e-36
-    unit_a[...] = jnp.broadcast_to(unit, unit_a.shape)
-    scale_a[...] = jnp.broadcast_to(1.0 / unit, scale_a.shape)
-    unit_b[...] = jnp.broadcast_to(top * largest[0] * (float(rows) / 32768.0) + 1e-36, unit_b.shape)
+    unit_a[...] = jnp.broadcast_to(unit[0, 0], unit_a.shape)
+    scale_a[...] = jnp.broadcast_to((1.0 / unit)[0, 0], scale_a.shape)
+    unit_b[...] = jnp.broadcast_to((top * largest[0] * (float(rows) / 32768.0) + 1e-36)[0, 0], unit_b.shape)
     rows_out(0, spans, tt, acat, *outs)
 
 
@@ -133,7 +133,7 @@
         functools.partial(energies, masks_a, masks_b, slabs, per),
         out_shape=jax.ShapeDtypeStruct((rows, cols), jnp.float32),
         in_specs=[smem] * 3 + [vmem] * 2,
-        compiler_params=pltpu.CompilerParams(vmem_limit_bytes=12 * MIB),
+        compiler_params=pltpu.CompilerParams(vmem_limit_bytes=6 * MIB),
         name="energies",
     )(me.reshape(1), occ_alpha, occ_beta, virt_alpha[:, None], virt_beta.reshape(slabs, block))
     pieces_b, pieces_a, near_a, near_b, ninv = together((pieces_b, pieces_a, near_a, near_b, ninv))
@@ -157,8 +157,8 @@
             jax.ShapeDtypeStruct((cols, rows), jnp.bfloat16),
             jax.ShapeDtypeStruct((rows, aux), jnp.bfloat16),
             jax.ShapeDtypeStruct((cols, aux), jnp.bfloat16),
-        ] + [jax.ShapeDtypeStruct((1, aux), jnp.float32)] * 3 + blocks(early),
-        compiler_params=pltpu.CompilerParams(vmem_limit_bytes=28 * MIB),
+        ] + [jax.ShapeDtypeStruct((aux,), jnp.float32)] * 3 + blocks(early),
+        compiler_params=pltpu.CompilerParams(vmem_limit_bytes=20 * MIB),
         cost_estimate=pl.CostEstimate(
             flops=2 * rows * cols * aux, bytes_accessed=2 * (rows + cols) * aux * 2, transcendentals=0
         ),
@@ -170,7 +170,7 @@
         outs = pl.pallas_call(
             functools.partial(rows_out, start * width, cut * len(names)),
             out_shape=blocks(len(names)),
-            compiler_params=pltpu.CompilerParams(vmem_limit_bytes=28 * MIB),
+            compiler_params=pltpu.CompilerParams(vmem_limit_bytes=14 * MIB),
             cost_estimate=pl.CostEstimate(
                 flops=2 * len(names) * width * right.size, bytes_accessed=len(names) * width * aux * 4 + right.size * 2,
                 transcendentals=0,
@@ -210,8 +210,10 @@
             for which, parts, names, bits in ((0, ga, masks_a, bits_a), (1, gb, names_b, bits_b)) if level < len(bits)
         ]
 
-        def made(names_at):
-            return [[narrow(job[1][m][0], scales[job[0]]) for m in job[names_at]] for job in jobs]
+        before = scales
+
+        def made(names_at, by):
+            return [[narrow(job[1][m][0], by[job[0]]) for m in job[names_at]] for job in jobs]
 
         def moved(values):
             return [[exchange(v, job[2], devices) for v in vs] for job, vs in zip(jobs, values)]
@@ -222,19 +224,24 @@
                     job[1][m ^ (1 << job[2])][0] += wide(v, partner[job[0]])
 
         if level == 0:
-            sent, units, tt, acat = together((made(3), units, tt, acat))
+            sent, units, tt, acat = together((made(3, before), units, tt, acat))
+            coming = {job[0]: exchange(units[job[0]], job[2], devices) for job in jobs}
         else:
-            sent = made(3)
+            sent = made(3, before)
+        partner = coming
         got = moved(sent)
-        partner = {job[0]: exchange(units[job[0]], job[2], devices) for job in jobs}
         if level == 0:
             gb.update(chips_sum(contracted(tt, acat, early, masks_b[early:], "beta")))
-        got, rest = together((got, made(4)))
+        units = [units[w] + partner[w] if w in partner else units[w] for w in range(2)]
+        scales = [1.0 / unit for unit in units]
+        coming = {
+            w: exchange(units[w], bits[level + 1], devices)
+            for w, bits in ((0, bits_a), (1, bits_b)) if level + 1 < len(bits)
+        }
+        got, rest, coming, scales = together((got, made(4, before), coming, scales))
         rest = moved(rest)
         added(3, got)
         added(4, rest)
-        units = [units[w] + partner[w] if w in partner else units[w] for w in range(2)]
-        scales = [1.0 / unit for unit in units]
 
     def whole(parts):
         return parts[0].reshape(orbital_alpha.shape)

time: 123 us -> 96.1 us (0.78)
  waiting for transfers between devices: 65.9 us -> 52.7 us
  other arithmetic: 10.9 us -> 3.25 us
  local copies, waits for them, and re-layouts: 8.88 us -> 3.03 us
  starting transfers between devices: 23.6 us -> 25.5 us
  Pallas kernels: 12.3 us -> 10.5 us
    ppermute x25, waiting for transfers between devices: 65.9 us -> 52.7 us  [exchange(): lax.ppermute(value, ('grp', 'slab'), [(d, d ^ 1 << bit) for d in range(de...]
    unnamed x28 -> x8, local copies, waits for them, and re-layouts: 7.16 us -> 1.31 us
    convert_element_type x5, other arithmetic: 6.04 us -> 0.85 us  [narrow(): return (value * scale).astype(jnp.float16)]
    reshape x2, other arithmetic: 4.57 us -> 2.38 us  [whole(): return parts[0].reshape(orbital_alpha.shape)]
    ppermute x25, starting transfers between devices: 23.6 us -> 25.5 us  [exchange(): lax.ppermute(value, ('grp', 'slab'), [(d, d ^ 1 << bit) for d in range(de...]
  transfers between devices with their start and end apart: 25 -> 25, of which waited for: 10 -> 11; matrix products, arithmetic and copies ran while one was open for 7% -> 4% of each run, Pallas kernels for 3% -> 3%
where the time goes in v5:
time: 96.1 us; the launch traced here: 95.8 us
  waiting for transfers between devices  52.7 us (55%)
  starting transfers between devices  25.5 us (27%)
  Pallas kernels  10.5 us (11%)
  other arithmetic  3.25 us (3%)
  local copies, waits for them, and re-layouts  3.03 us (3%)
    ppermute x25, waiting for transfers between devices, exchange(): lax.ppermute(value, ('grp', 'slab'), [(d, d ^ 1 << bit) for d in range(de...  52.7 us
    ppermute x25, starting transfers between devices, exchange(): lax.ppermute(value, ('grp', 'slab'), [(d, d ^ 1 << bit) for d in range(de...  25.5 us
    pallas_call x1, Pallas kernels, body(): pl.pallas_call(functools.partial(contract_amplitudes, len(list_a), len(li...  4.87 us
    pallas_call x2, Pallas kernels, contracted(): pl.pallas_call(functools.partial(rows_out, start * width, cut * len(names...  4.8 us
    reshape x2, other arithmetic, whole(): return parts[0].reshape(orbital_alpha.shape)  2.38 us
  transfers between devices with their start and end apart: 25, of which 11 were waited for; matrix products, arithmetic and copies ran while one was open for 4% of the time, Pallas kernels for 3%

profile of v5, /device:TPU:0, one launch (start us, length us, event | category | flops | bytes accessed | tf_op | source)
XLA Modules:
  0.0 95.8 jit_solution(10503562597636545833)
XLA Ops:
  0.6 4.1 %collective-permute-start.2 = (bf16[96,2560]{1,0:T(8,128)(2,1)}, bf16[96,2560]{1,0:T(8,128)(2,1)S(1)}, u32[]{:S(2)}, u32[]{:S(2)}) collective-permute-start(bf16[96,2560]{1,0:T(8,128)(2,1)} %bitcast.7), channel_id=1, source_target_pairs={{0,8},{1,9},{2,10},{3,11},{4,12},{5,13},{6,14},{7,15},{8,0},{9,1},... | collective-permute-start | bytes 1474568 | tf_op jit(solution)/shard_map/ppermute | solution.py:24
  4.8 1.5 %collective-permute-start.1 = (bf16[96,2560]{1,0:T(8,128)(2,1)}, bf16[96,2560]{1,0:T(8,128)(2,1)S(1)}, u32[]{:S(2)}, u32[]{:S(2)}) collective-permute-start(bf16[96,2560]{1,0:T(8,128)(2,1)} %bitcast.8), channel_id=1, source_target_pairs={{0,2},{1,3},{2,0},{3,1},{4,6},{5,7},{6,4},{7,5},{8,10},{9,11},{10,... | collective-permute-start | bytes 1474568 | tf_op jit(solution)/shard_map/ppermute | solution.py:24
  6.2 1.6 %collective-permute-start.3 = (bf16[96,2560]{1,0:T(8,128)(2,1)}, bf16[96,2560]{1,0:T(8,128)(2,1)S(1)}, u32[]{:S(2)}, u32[]{:S(2)}) collective-permute-start(bf16[96,2560]{1,0:T(8,128)(2,1)} %bitcast.10), channel_id=1, source_target_pairs={{0,4},{1,5},{2,6},{3,7},{4,0},{5,1},{6,2},{7,3},{8,12},{9,13},{10,... | collective-permute-start | bytes 1474568 | tf_op jit(solution)/shard_map/ppermute | solution.py:24
  7.8 1.5 %collective-permute-start = (bf16[96,2560]{1,0:T(8,128)(2,1)}, bf16[96,2560]{1,0:T(8,128)(2,1)}, u32[]{:S(2)}, u32[]{:S(2)}) collective-permute-start(bf16[96,2560]{1,0:T(8,128)(2,1)} %bitcast.11), channel_id=1, source_target_pairs={{0,16},{1,17},{2,18},{3,19},{4,20},{5,21},{6,22},{7,23},{8,24},{9,... | collective-permute-start | bytes 1474568 | tf_op jit(solution)/shard_map/ppermute | solution.py:24
  9.3 0.8 reshape.33.vb_ref
  10.1 1.0 broadcast_in_dim.3.va_ref
  11.1 0.6 copy-done.2
  11.7 0.7 copy-done.3
  12.4 0.8 energies.1.refs_12_
  13.2 13.6 %collective-permute-done.2.refs_2_ = bf16[96,2560]{1,0:T(8,128)(2,1)S(1)} collective-permute-done((bf16[96,2560]{1,0:T(8,128)(2,1)}, bf16[96,2560]{1,0:T(8,128)(2,1)S(1)}, u32[]{:S(2)}, u32[]{:S(2)}) %collective-permute-start.2) | collective-permute-done | bytes 491552 | tf_op jit(solution)/shard_map/ppermute | solution.py:24
  26.8 1.4 %collective-permute-done.3.refs_9_ = bf16[96,2560]{1,0:T(8,128)(2,1)S(1)} collective-permute-done((bf16[96,2560]{1,0:T(8,128)(2,1)}, bf16[96,2560]{1,0:T(8,128)(2,1)S(1)}, u32[]{:S(2)}, u32[]{:S(2)}) %collective-permute-start.3) | collective-permute-done | bytes 491552 | tf_op jit(solution)/shard_map/ppermute | solution.py:24
  28.2 1.6 %collective-permute-start.5 = (bf16[96,2560]{1,0:T(8,128)(2,1)S(1)}, bf16[96,2560]{1,0:T(8,128)(2,1)S(1)}, u32[]{:S(2)}, u32[]{:S(2)}) collective-permute-start(bf16[96,2560]{1,0:T(8,128)(2,1)S(1)} %collective-permute-done.3.refs_9_), channel_id=1, source_target_pairs={{0,16},{1,17},{2,18},{3,19},{4,20},{5,21},{6,22},{7,23},{8,24},{9,... | collective-permute-start | bytes 1474568 | tf_op jit(solution)/shard_map/ppermute | solution.py:24
  30.9 8.4 %collective-permute-done.5.refs_5_ = bf16[96,2560]{1,0:T(8,128)(2,1)S(1)} collective-permute-done((bf16[96,2560]{1,0:T(8,128)(2,1)S(1)}, bf16[96,2560]{1,0:T(8,128)(2,1)S(1)}, u32[]{:S(2)}, u32[]{:S(2)}) %collective-permute-start.5) | collective-permute-done | bytes 491552 | tf_op jit(solution)/shard_map/ppermute | solution.py:24
  39.2 4.2 %collective-permute-done.4.refs_0_ = bf16[96,2560]{1,0:T(8,128)(2,1)S(1)} collective-permute-done((bf16[96,2560]{1,0:T(8,128)(2,1)S(1)}, bf16[96,2560]{1,0:T(8,128)(2,1)S(1)}, u32[]{:S(2)}, u32[]{:S(2)}) %collective-permute-start.4) | collective-permute-done | bytes 491552 | tf_op jit(solution)/shard_map/ppermute | solution.py:24
  43.5 4.9 %amplitudes.1 = (bf16[384,768]{1,0:T(8,128)(2,1)S(1)}, bf16[768,384]{1,0:T(8,128)(2,1)S(1)}, bf16[384,2560]{1,0:T(8,128)(2,1)S(1)}, bf16[768,2560]{1,0:T(8,128)(...) custom-call(bf16[96,2560]{1,0:T(8,128)(2,1)S(1)} %collective-permute, ...), custom_call_target="tpu_custom_call" | custom-call | flops 1509949440 | bytes 11796480 | tf_op jit(solution)/shard_map/amplitudes/pallas_call | solution.py:153
  48.9 2.4 %alpha.1 = (f32[96,2560]{1,0:T(8,128)S(1)}, f32[96,2560]{1,0:T(8,128)S(1)}, f32[96,2560]{1,0:T(8,128)S(1)}, f32[96,2560]{1,0:T(8,128)S(1)}) custom-call(bf16[384,768]{1,0:T(8,128)(2,1)S(1)} %get-tuple-element.51.left, bf16[768,2560]{1,0:T(8,128)(2,1)S(1)} %get-tuple-element.52.right), custom_call_target="tpu_custom_call" | custom-call | flops 1509949440 | bytes 7864320 | tf_op jit(solution)/shard_map/alpha/pallas_call | solution.py:170
  51.7 2.4 %beta.1 = (f32[96,2560]{1,0:T(8,128)S(1)}, f32[96,2560]{1,0:T(8,128)S(1)}, f32[96,2560]{1,0:T(8,128)S(1)}, f32[96,2560]{1,0:T(8,128)S(1)}, f32[96,2560]{1,0:T(8,128)S(1)}, /*index=5*/f32[96,2560]{1,0:T(8,128)S(1)}) custom-call(bf16[768,384]{1,0:T(8,128)(2,1)S(1)} %get-tuple-element.65.left, bf16[384,2560]{1,0:T(8,128)(2,1)S(1)} %get-tuple-element.66.right), custom_call_target="tpu_custom_call" | custom-call | flops 1132462080 | bytes 7864320 | tf_op jit(solution)/shard_map/beta/pallas_call | solution.py:170
  55.3 1.4 %collective-permute-start.12 = (f16[96,2560]{1,0:T(8,128)(2,1)S(1)}, f16[96,2560]{1,0:T(8,128)(2,1)S(1)}, u32[]{:S(2)}, u32[]{:S(2)}) collective-permute-start(f16[96,2560]{1,0:T(8,128)(2,1)S(1)} %get-tuple-element.62), channel_id=1, source_target_pairs={{0,2},{1,3},{2,0},{3,1},{4,6},{5,7},{6,4},{7,5},{8,10},{9,11},{10,... | collective-permute-start | bytes 1474568 | tf_op jit(solution)/shard_map/ppermute | solution.py:24
  56.7 1.6 %collective-permute-start.13 = (f16[96,2560]{1,0:T(8,128)(2,1)S(1)}, f16[96,2560]{1,0:T(8,128)(2,1)S(1)}, u32[]{:S(2)}, u32[]{:S(2)}) collective-permute-start(f16[96,2560]{1,0:T(8,128)(2,1)S(1)} %multiply_convert_fusion.4), channel_id=1, source_target_pairs={{0,16},{1,17},{2,18},{3,19},{4,20},{5,21},{6,22},{7,23},{8,24},{9,... | collective-permute-start | bytes 1474568 | tf_op jit(solution)/shard_map/ppermute | solution.py:24
  58.5 1.1 %collective-permute-start.16 = (f32[2560]{0:T(1024)S(1)}, f32[2560]{0:T(1024)S(1)}, u32[]{:S(2)}, u32[]{:S(2)}) collective-permute-start(f32[2560]{0:T(1024)S(1)} %get-tuple-element.89), channel_id=1, source_target_pairs={{0,8},{1,9},{2,10},{3,11},{4,12},{5,13},{6,14},{7,15},{8,0},{9,1},... | collective-permute-start | bytes 30728 | tf_op jit(solution)/shard_map/ppermute | solution.py:24
  59.6 2.6 %collective-permute-start.18 = (f32[2560]{0:T(1024)S(1)}, f32[2560]{0:T(1024)S(1)}, u32[]{:S(2)}, u32[]{:S(2)}) collective-permute-start(f32[2560]{0:T(1024)S(1)} %get-tuple-element.87), channel_id=1, source_target_pairs={{0,4},{1,5},{2,6},{3,7},{4,0},{5,1},{6,2},{7,3},{8,12},{9,13},{10,... | collective-permute-start | bytes 30728 | tf_op jit(solution)/shard_map/ppermute | solution.py:24
  62.3 0.8 collective-permute-done.16
  63.1 0.7 collective-permute-done.18
  63.8 4.6 %collective-permute-done.12 = f16[96,2560]{1,0:T(8,128)(2,1)S(1)} collective-permute-done((f16[96,2560]{1,0:T(8,128)(2,1)S(1)}, f16[96,2560]{1,0:T(8,128)(2,1)S(1)}, u32[]{:S(2)}, u32[]{:S(2)}) %collective-permute-start.12) | collective-permute-done | bytes 491552 | tf_op jit(solution)/shard_map/ppermute | solution.py:24
  68.4 1.0 %collective-permute-done.13 = f16[96,2560]{1,0:T(8,128)(2,1)S(1)} collective-permute-done((f16[96,2560]{1,0:T(8,128)(2,1)S(1)}, f16[96,2560]{1,0:T(8,128)(2,1)S(1)}, u32[]{:S(2)}, u32[]{:S(2)}) %collective-permute-start.13) | collective-permute-done | bytes 491552 | tf_op jit(solution)/shard_map/ppermute | solution.py:24
  69.7 0.8 collective-permute-start.20
  70.7 2.9 %collective-permute-start.22 = (f16[96,2560]{1,0:T(8,128)(2,1)S(1)}, f16[96,2560]{1,0:T(8,128)(2,1)S(1)}, u32[]{:S(2)}, u32[]{:S(2)}) collective-permute-start(f16[96,2560]{1,0:T(8,128)(2,1)S(1)} %multiply_convert_fusion), channel_id=1, source_target_pairs={{0,4},{1,5},{2,6},{3,7},{4,0},{5,1},{6,2},{7,3},{8,12},{9,13},{10,... | collective-permute-start | bytes 1474568 | tf_op jit(solution)/shard_map/ppermute | solution.py:24
  73.5 1.5 %collective-permute-start.19 = (f16[96,2560]{1,0:T(8,128)(2,1)S(1)}, f16[96,2560]{1,0:T(8,128)(2,1)S(1)}, u32[]{:S(2)}, u32[]{:S(2)}) collective-permute-start(f16[96,2560]{1,0:T(8,128)(2,1)S(1)} %get-tuple-element.71), channel_id=1, source_target_pairs={{0,2},{1,3},{2,0},{3,1},{4,6},{5,7},{6,4},{7,5},{8,10},{9,11},{10,... | collective-permute-start | bytes 1474568 | tf_op jit(solution)/shard_map/ppermute | solution.py:24
  75.0 0.7 collective-permute-start.24
  75.7 17.4 %collective-permute-done.20 = f16[96,2560]{1,0:T(8,128)(2,1)S(1)} collective-permute-done((f16[96,2560]{1,0:T(8,128)(2,1)S(1)}, f16[96,2560]{1,0:T(8,128)(2,1)S(1)}, u32[]{:S(2)}, u32[]{:S(2)}) %collective-permute-start.20) | collective-permute-done | bytes 491552 | tf_op jit(solution)/shard_map/ppermute | solution.py:24
  93.5 1.1 %add_bitcast_fusion.1 = f32[1,96,2560]{2,1,0:T(8,128)} fusion(f16[96,2560]{1,0:T(8,128)(2,1)S(1)} %collective-permute-done.20, f32[96,2560]{1,0:T(8,128)S(1)} %get-tuple-element.53, f16[96,2560]{1,0:T(8,128)(2,1)S(1)} %collective-permute-done.19, f32[2560]{0:T(1024)S(1)} %collective-permute-done.16, f32[2560]{0:T(1024)S(1)} %collective-permute-done.15), kind=kLoop, calls=%fused_computation.1 | loop fusion | flops 1474560 | bytes 2969600 | tf_op jit(solution)/shard_map/reshape | solution.py:247
  94.6 1.2 %add_bitcast_fusion = f32[1,96,2560]{2,1,0:T(8,128)} fusion(f16[96,2560]{1,0:T(8,128)(2,1)S(1)} %collective-permute-done.22, f16[96,2560]{1,0:T(8,128)(2,1)S(1)} %collective-permute-done.24, f32[96,2560]{1,0:T(8,128)S(1)} %get-tuple-element.81, f32[96,2560]{1,0:T(8,128)S(1)} %collective-permute-done.23, f32[2560]{0:T(1024)S(1)} %collective-permute-done.18, ...), kind=kLoop, calls=%fused_computation | loop fusion | flops 1720320 | bytes 3952640 | tf_op jit(solution)/shard_map/reshape | solution.py:247
  (42 shorter events, 4.3 us)
Async XLA Ops:
  0.6 42.8 %copy-start = (bf16[1,96,2560]{2,1,0:T(8,128)(2,1)S(1)}, bf16[1,96,2560]{2,1,0:T(8,128)(2,1)}, u32[]{:S(2)}) copy-start(bf16[1,96,2560]{2,1,0:T(8,128)(2,1)} %param.6) | copy-start | bytes 1474564
  0.6 29.9 %copy-start.1 = (bf16[1,96,2560]{2,1,0:T(8,128)(2,1)S(1)}, bf16[1,96,2560]{2,1,0:T(8,128)(2,1)}, u32[]{:S(2)}) copy-start(bf16[1,96,2560]{2,1,0:T(8,128)(2,1)} %param.7) | copy-start | bytes 1474564
  0.6 26.2 %collective-permute-start.2 = (bf16[96,2560]{1,0:T(8,128)(2,1)}, bf16[96,2560]{1,0:T(8,128)(2,1)S(1)}, u32[]{:S(2)}, u32[]{:S(2)}) collective-permute-start(bf16[96,2560]{1,0:T(8,128)(2,1)} %bitcast.7), channel_id=1, source_target_pairs={{0,8},{1,9},{2,10},{3,11},{4,12},{5,13},{6,14},{7,15},{8,0},{9,1},... | collective-permute-start | bytes 1474568 | tf_op jit(solution)/shard_map/ppermute | solution.py:24
  4.8 22.1 %collective-permute-start.1 = (bf16[96,2560]{1,0:T(8,128)(2,1)}, bf16[96,2560]{1,0:T(8,128)(2,1)S(1)}, u32[]{:S(2)}, u32[]{:S(2)}) collective-permute-start(bf16[96,2560]{1,0:T(8,128)(2,1)} %bitcast.8), channel_id=1, source_target_pairs={{0,2},{1,3},{2,0},{3,1},{4,6},{5,7},{6,4},{7,5},{8,10},{9,11},{10,... | collective-permute-start | bytes 1474568 | tf_op jit(solution)/shard_map/ppermute | solution.py:24
  6.2 22.0 %collective-permute-start.3 = (bf16[96,2560]{1,0:T(8,128)(2,1)}, bf16[96,2560]{1,0:T(8,128)(2,1)S(1)}, u32[]{:S(2)}, u32[]{:S(2)}) collective-permute-start(bf16[96,2560]{1,0:T(8,128)(2,1)} %bitcast.10), channel_id=1, source_target_pairs={{0,4},{1,5},{2,6},{3,7},{4,0},{5,1},{6,2},{7,3},{8,12},{9,13},{10,... | collective-permute-start | bytes 1474568 | tf_op jit(solution)/shard_map/ppermute | solution.py:24
  7.8 20.4 %collective-permute-start = (bf16[96,2560]{1,0:T(8,128)(2,1)}, bf16[96,2560]{1,0:T(8,128)(2,1)}, u32[]{:S(2)}, u32[]{:S(2)}) collective-permute-start(bf16[96,2560]{1,0:T(8,128)(2,1)} %bitcast.11), channel_id=1, source_target_pairs={{0,16},{1,17},{2,18},{3,19},{4,20},{5,21},{6,22},{7,23},{8,24},{9,... | collective-permute-start | bytes 1474568 | tf_op jit(solution)/shard_map/ppermute | solution.py:24
  11.1 0.7 copy-start.2
  11.7 0.7 copy-start.3
  28.2 11.0 %collective-permute-start.5 = (bf16[96,2560]{1,0:T(8,128)(2,1)S(1)}, bf16[96,2560]{1,0:T(8,128)(2,1)S(1)}, u32[]{:S(2)}, u32[]{:S(2)}) collective-permute-start(bf16[96,2560]{1,0:T(8,128)(2,1)S(1)} %collective-permute-done.3.refs_9_), channel_id=1, source_target_pairs={{0,16},{1,17},{2,18},{3,19},{4,20},{5,21},{6,22},{7,23},{8,24},{9,... | collective-permute-start | bytes 1474568 | tf_op jit(solution)/shard_map/ppermute | solution.py:24
  29.8 13.6 %collective-permute-start.8 = (bf16[96,2560]{1,0:T(8,128)(2,1)S(1)}, bf16[96,2560]{1,0:T(8,128)(2,1)S(1)}, u32[]{:S(2)}, u32[]{:S(2)}) collective-permute-start(bf16[96,2560]{1,0:T(8,128)(2,1)S(1)} %collective-permute-done.3.refs_9_), channel_id=1, source_target_pairs={{0,1},{1,0},{2,3},{3,2},{4,5},{5,4},{6,7},{7,6},{8,9},{9,8},{10,11... | collective-permute-start | bytes 1474568 | tf_op jit(solution)/shard_map/ppermute | solution.py:24
  29.8 13.6 %collective-permute-start.4 = (bf16[96,2560]{1,0:T(8,128)(2,1)S(1)}, bf16[96,2560]{1,0:T(8,128)(2,1)S(1)}, u32[]{:S(2)}, u32[]{:S(2)}) collective-permute-start(bf16[96,2560]{1,0:T(8,128)(2,1)S(1)} %collective-permute-done.2.refs_2_), channel_id=1, source_target_pairs={{0,2},{1,3},{2,0},{3,1},{4,6},{5,7},{6,4},{7,5},{8,10},{9,11},{10,... | collective-permute-start | bytes 1474568 | tf_op jit(solution)/shard_map/ppermute | solution.py:24
  30.3 13.1 %collective-permute-start.7 = (bf16[96,2560]{1,0:T(8,128)(2,1)}, bf16[96,2560]{1,0:T(8,128)(2,1)S(1)}, u32[]{:S(2)}, u32[]{:S(2)}) collective-permute-start(bf16[96,2560]{1,0:T(8,128)(2,1)} %collective-permute-done.refs_7_), channel_id=1, source_target_pairs={{0,1},{1,0},{2,3},{3,2},{4,5},{5,4},{6,7},{7,6},{8,9},{9,8},{10,11... | collective-permute-start | bytes 1474568 | tf_op jit(solution)/shard_map/ppermute | solution.py:24
  30.6 12.9 %collective-permute-start.9 = (bf16[96,2560]{1,0:T(8,128)(2,1)S(1)}, bf16[96,2560]{1,0:T(8,128)(2,1)S(1)}, u32[]{:S(2)}, u32[]{:S(2)}) collective-permute-start(bf16[96,2560]{1,0:T(8,128)(2,1)S(1)} %bitcast.12), channel_id=1, source_target_pairs={{0,1},{1,0},{2,3},{3,2},{4,5},{5,4},{6,7},{7,6},{8,9},{9,8},{10,11... | collective-permute-start | bytes 1474568 | tf_op jit(solution)/shard_map/ppermute | solution.py:24
  39.2 4.2 %collective-permute-start.6 = (bf16[96,2560]{1,0:T(8,128)(2,1)S(1)}, bf16[96,2560]{1,0:T(8,128)(2,1)S(1)}, u32[]{:S(2)}, u32[]{:S(2)}) collective-permute-start(bf16[96,2560]{1,0:T(8,128)(2,1)S(1)} %collective-permute-done.5.refs_5_), channel_id=1, source_target_pairs={{0,1},{1,0},{2,3},{3,2},{4,5},{5,4},{6,7},{7,6},{8,9},{9,8},{10,11... | collective-permute-start | bytes 1474568 | tf_op jit(solution)/shard_map/ppermute | solution.py:24
  48.4 3.2 %collective-permute-start.11 = (f32[2560]{0:T(1024)S(1)}, f32[2560]{0:T(1024)S(1)}, u32[]{:S(2)}, u32[]{:S(2)}) collective-permute-start(f32[2560]{0:T(1024)S(1)} %get-tuple-element.58), channel_id=1, source_target_pairs={{0,1},{1,0},{2,3},{3,2},{4,5},{5,4},{6,7},{7,6},{8,9},{9,8},{10,11... | collective-permute-start | bytes 30728 | tf_op jit(solution)/shard_map/ppermute | solution.py:24
  48.4 3.1 %collective-permute-start.10 = (f32[96,2560]{1,0:T(8,128)S(1)}, f32[96,2560]{1,0:T(8,128)S(1)}, u32[]{:S(2)}, u32[]{:S(2)}) collective-permute-start(f32[96,2560]{1,0:T(8,128)S(1)} %get-tuple-element.57), channel_id=1, source_target_pairs={{0,1},{1,0},{2,3},{3,2},{4,5},{5,4},{6,7},{7,6},{8,9},{9,8},{10,11... | collective-permute-start | bytes 2949128 | tf_op jit(solution)/shard_map/ppermute | solution.py:24
  54.1 5.5 %collective-permute-start.14 = (f32[96,2560]{1,0:T(8,128)S(1)}, f32[96,2560]{1,0:T(8,128)S(1)}, u32[]{:S(2)}, u32[]{:S(2)}) collective-permute-start(f32[96,2560]{1,0:T(8,128)S(1)} %get-tuple-element.68), channel_id=1, source_target_pairs={{0,1},{1,0},{2,3},{3,2},{4,5},{5,4},{6,7},{7,6},{8,9},{9,8},{10,11... | collective-permute-start | bytes 2949128 | tf_op jit(solution)/shard_map/ppermute | solution.py:24
  54.3 4.1 %collective-permute-start.15 = (f32[2560]{0:T(1024)S(1)}, f32[2560]{0:T(1024)S(1)}, u32[]{:S(2)}, u32[]{:S(2)}) collective-permute-start(f32[2560]{0:T(1024)S(1)} %get-tuple-element.69), channel_id=1, source_target_pairs={{0,2},{1,3},{2,0},{3,1},{4,6},{5,7},{6,4},{7,5},{8,10},{9,11},{10,... | collective-permute-start | bytes 30728 | tf_op jit(solution)/shard_map/ppermute | solution.py:24
  54.8 3.7 %collective-permute-start.17 = (f32[2560]{0:T(1024)S(1)}, f32[2560]{0:T(1024)S(1)}, u32[]{:S(2)}, u32[]{:S(2)}) collective-permute-start(f32[2560]{0:T(1024)S(1)} %get-tuple-element.70), channel_id=1, source_target_pairs={{0,16},{1,17},{2,18},{3,19},{4,20},{5,21},{6,22},{7,23},{8,24},{9,... | collective-permute-start | bytes 30728 | tf_op jit(solution)/shard_map/ppermute | solution.py:24
  55.3 13.1 %collective-permute-start.12 = (f16[96,2560]{1,0:T(8,128)(2,1)S(1)}, f16[96,2560]{1,0:T(8,128)(2,1)S(1)}, u32[]{:S(2)}, u32[]{:S(2)}) collective-permute-start(f16[96,2560]{1,0:T(8,128)(2,1)S(1)} %get-tuple-element.62), channel_id=1, source_target_pairs={{0,2},{1,3},{2,0},{3,1},{4,6},{5,7},{6,4},{7,5},{8,10},{9,11},{10,... | collective-permute-start | bytes 1474568 | tf_op jit(solution)/shard_map/ppermute | solution.py:24
  56.7 12.7 %collective-permute-start.13 = (f16[96,2560]{1,0:T(8,128)(2,1)S(1)}, f16[96,2560]{1,0:T(8,128)(2,1)S(1)}, u32[]{:S(2)}, u32[]{:S(2)}) collective-permute-start(f16[96,2560]{1,0:T(8,128)(2,1)S(1)} %multiply_convert_fusion.4), channel_id=1, source_target_pairs={{0,16},{1,17},{2,18},{3,19},{4,20},{5,21},{6,22},{7,23},{8,24},{9,... | collective-permute-start | bytes 1474568 | tf_op jit(solution)/shard_map/ppermute | solution.py:24
  58.3 12.1 %collective-permute-start.21 = (f32[96,2560]{1,0:T(8,128)S(1)}, f32[96,2560]{1,0:T(8,128)S(1)}, u32[]{:S(2)}, u32[]{:S(2)}) collective-permute-start(f32[96,2560]{1,0:T(8,128)S(1)} %get-tuple-element.76), channel_id=1, source_target_pairs={{0,1},{1,0},{2,3},{3,2},{4,5},{5,4},{6,7},{7,6},{8,9},{9,8},{10,11... | collective-permute-start | bytes 2949128 | tf_op jit(solution)/shard_map/ppermute | solution.py:24
  58.5 4.6 %collective-permute-start.16 = (f32[2560]{0:T(1024)S(1)}, f32[2560]{0:T(1024)S(1)}, u32[]{:S(2)}, u32[]{:S(2)}) collective-permute-start(f32[2560]{0:T(1024)S(1)} %get-tuple-element.89), channel_id=1, source_target_pairs={{0,8},{1,9},{2,10},{3,11},{4,12},{5,13},{6,14},{7,15},{8,0},{9,1},... | collective-permute-start | bytes 30728 | tf_op jit(solution)/shard_map/ppermute | solution.py:24
  59.6 4.2 %collective-permute-start.18 = (f32[2560]{0:T(1024)S(1)}, f32[2560]{0:T(1024)S(1)}, u32[]{:S(2)}, u32[]{:S(2)}) collective-permute-start(f32[2560]{0:T(1024)S(1)} %get-tuple-element.87), channel_id=1, source_target_pairs={{0,4},{1,5},{2,6},{3,7},{4,0},{5,1},{6,2},{7,3},{8,12},{9,13},{10,... | collective-permute-start | bytes 30728 | tf_op jit(solution)/shard_map/ppermute | solution.py:24
  69.7 23.4 %collective-permute-start.20 = (f16[96,2560]{1,0:T(8,128)(2,1)S(1)}, f16[96,2560]{1,0:T(8,128)(2,1)S(1)}, u32[]{:S(2)}, u32[]{:S(2)}) collective-permute-start(f16[96,2560]{1,0:T(8,128)(2,1)S(1)} %multiply_convert_fusion.1), channel_id=1, source_target_pairs={{0,8},{1,9},{2,10},{3,11},{4,12},{5,13},{6,14},{7,15},{8,0},{9,1},... | collective-permute-start | bytes 1474568 | tf_op jit(solution)/shard_map/ppermute | solution.py:24
  70.7 22.8 %collective-permute-start.22 = (f16[96,2560]{1,0:T(8,128)(2,1)S(1)}, f16[96,2560]{1,0:T(8,128)(2,1)S(1)}, u32[]{:S(2)}, u32[]{:S(2)}) collective-permute-start(f16[96,2560]{1,0:T(8,128)(2,1)S(1)} %multiply_convert_fusion), channel_id=1, source_target_pairs={{0,4},{1,5},{2,6},{3,7},{4,0},{5,1},{6,2},{7,3},{8,12},{9,13},{10,... | collective-permute-start | bytes 1474568 | tf_op jit(solution)/shard_map/ppermute | solution.py:24
  73.5 19.9 %collective-permute-start.19 = (f16[96,2560]{1,0:T(8,128)(2,1)S(1)}, f16[96,2560]{1,0:T(8,128)(2,1)S(1)}, u32[]{:S(2)}, u32[]{:S(2)}) collective-permute-start(f16[96,2560]{1,0:T(8,128)(2,1)S(1)} %get-tuple-element.71), channel_id=1, source_target_pairs={{0,2},{1,3},{2,0},{3,1},{4,6},{5,7},{6,4},{7,5},{8,10},{9,11},{10,... | collective-permute-start | bytes 1474568 | tf_op jit(solution)/shard_map/ppermute | solution.py:24
  75.0 19.6 %collective-permute-start.23 = (f32[96,2560]{1,0:T(8,128)S(1)}, f32[96,2560]{1,0:T(8,128)S(1)}, u32[]{:S(2)}, u32[]{:S(2)}) collective-permute-start(f32[96,2560]{1,0:T(8,128)S(1)} %get-tuple-element.82), channel_id=1, source_target_pairs={{0,1},{1,0},{2,3},{3,2},{4,5},{5,4},{6,7},{7,6},{8,9},{9,8},{10,11... | collective-permute-start | bytes 2949128 | tf_op jit(solution)/shard_map/ppermute | solution.py:24
  75.0 19.6 %collective-permute-start.24 = (f16[96,2560]{1,0:T(8,128)(2,1)S(1)}, f16[96,2560]{1,0:T(8,128)(2,1)S(1)}, u32[]{:S(2)}, u32[]{:S(2)}) collective-permute-start(f16[96,2560]{1,0:T(8,128)(2,1)S(1)} %multiply_convert_fusion.2), channel_id=1, source_target_pairs={{0,16},{1,17},{2,18},{3,19},{4,20},{5,21},{6,22},{7,23},{8,24},{9,... | collective-permute-start | bytes 1474568 | tf_op jit(solution)/shard_map/ppermute | solution.py:24

commit v6 on v5

--- a/solution.py
+++ b/solution.py
@@ -50,8 +50,8 @@
 
 def contract_amplitudes(n_a, n_b, early, spans, *refs):
     a_refs, b_refs, ninv = refs[:n_a], refs[n_a:n_a + n_b], refs[n_a + n_b]
-    t_ref, tt, acat, bcat, scale_a, unit_a, unit_b = refs[n_a + n_b + 1:n_a + n_b + 8]
-    outs = refs[n_a + n_b + 8:]
+    t_ref, tt, acat, bcat, scale_a, scale_b, unit_a, unit_b = refs[n_a + n_b + 1:n_a + n_b + 9]
+    outs = refs[n_a + n_b + 9:]
     largest = []
     for sources, joined in ((a_refs, acat), (b_refs, bcat)):
         at, top = 0, None
@@ -73,10 +73,12 @@
         amps = amps.astype(jnp.bfloat16)
         t_ref[:, c:c + step] = amps
         tt[c:c + step, :] = amps.T
-    unit = top * largest[1] * (float(cols) / 32768.0) + 1e-36
-    unit_a[...] = jnp.broadcast_to(unit[0, 0], unit_a.shape)
-    scale_a[...] = jnp.broadcast_to((1.0 / unit)[0, 0], scale_a.shape)
-    unit_b[...] = jnp.broadcast_to((top * largest[0] * (float(rows) / 32768.0) + 1e-36)[0, 0], unit_b.shape)
+    for largest_right, count, unit, scale in (
+        (largest[1], cols, unit_a, scale_a), (largest[0], rows, unit_b, scale_b)
+    ):
+        value = top * largest_right * (count / 32768.0) + 1e-36
+        unit[...] = jnp.broadcast_to(value[0, 0], unit.shape)
+        scale[...] = jnp.broadcast_to((1.0 / value)[0, 0], scale.shape)
     rows_out(0, spans, tt, acat, *outs)
 
 
@@ -157,14 +159,14 @@
             jax.ShapeDtypeStruct((cols, rows), jnp.bfloat16),
             jax.ShapeDtypeStruct((rows, aux), jnp.bfloat16),
             jax.ShapeDtypeStruct((cols, aux), jnp.bfloat16),
-        ] + [jax.ShapeDtypeStruct((aux,), jnp.float32)] * 3 + blocks(early),
+        ] + [jax.ShapeDtypeStruct((aux,), jnp.float32)] * 4 + blocks(early),
         compiler_params=pltpu.CompilerParams(vmem_limit_bytes=20 * MIB),
         cost_estimate=pl.CostEstimate(
             flops=2 * rows * cols * aux, bytes_accessed=2 * (rows + cols) * aux * 2, transcendentals=0
         ),
         name="amplitudes",
     )(*list_a, *list_b, ninv)
-    t, tt, acat, bcat, scale_a, unit_a, unit_b = opening[:7]
+    t, tt, acat, bcat, scale_a, scale_b, unit_a, unit_b = opening[:8]
 
     def contracted(left, right, start, names, name):
         outs = pl.pallas_call(
@@ -200,9 +202,17 @@
 
     bits_a, bits_b = alpha_bits[::-1], [b for b in beta_bits[::-1] if b]
     names_b = [m for m in masks_b if not m & 1]
-    unit_b = unit_b + exchange(unit_b, 0, devices)
+    unit_other = exchange(unit_b, 0, devices)
+
+    def chips_sum_narrow(found):
+        return {
+            m: [v + wide(exchange(narrow(w, scale_b), 0, devices), unit_other) for v, w in zip(vs, found[m | 1])]
+            for m, vs in found.items() if not m & 1
+        }
+
+    unit_b = unit_b + unit_other
     units, scales = [unit_a, unit_b], [scale_a, 1.0 / unit_b]
-    gb = chips_sum(pairs(masks_b, opening[7:]))
+    gb = chips_sum(pairs(masks_b, opening[8:]))
     ga = contracted(t, bcat, 0, masks_a, "alpha")
     for level in range(max(len(bits_a), len(bits_b))):
         jobs = [
@@ -231,14 +241,15 @@
         partner = coming
         got = moved(sent)
         if level == 0:
-            gb.update(chips_sum(contracted(tt, acat, early, masks_b[early:], "beta")))
+            gb.update(chips_sum_narrow(contracted(tt, acat, early, masks_b[early:], "beta")))
         units = [units[w] + partner[w] if w in partner else units[w] for w in range(2)]
         scales = [1.0 / unit for unit in units]
         coming = {
             w: exchange(units[w], bits[level + 1], devices)
             for w, bits in ((0, bits_a), (1, bits_b)) if level + 1 < len(bits)
         }
-        got, rest, coming, scales = together((got, made(4, before), coming, scales))
+        rest = made(4, before)
+        got, rest[0], coming, scales = together((got, rest[0], coming, scales))
         rest = moved(rest)
         added(3, got)
         added(4, rest)

time: 96.1 us -> 93.2 us (0.970)
  waiting for transfers between devices: 52.7 us -> 49.8 us
    ppermute x25, waiting for transfers between devices: 52.7 us -> 49.8 us  [exchange(): lax.ppermute(value, ('grp', 'slab'), [(d, d ^ 1 << bit) for d in range(de...]
  transfers between devices with their start and end apart: 25 -> 25, of which waited for: 11 -> 10; matrix products, arithmetic and copies ran while one was open for 4% -> 4% of each run, Pallas kernels for 3% -> 6%
where the time goes in v6:
time: 93.2 us; the launch traced here: 93 us
  waiting for transfers between devices  49.8 us (53%)
  starting transfers between devices  25 us (27%)
  Pallas kernels  10.5 us (11%)
  other arithmetic  3.73 us (4%)
  local copies, waits for them, and re-layouts  3.03 us (3%)
    ppermute x25, waiting for transfers between devices, exchange(): lax.ppermute(value, ('grp', 'slab'), [(d, d ^ 1 << bit) for d in range(de...  49.8 us
    ppermute x25, starting transfers between devices, exchange(): lax.ppermute(value, ('grp', 'slab'), [(d, d ^ 1 << bit) for d in range(de...  25 us
    pallas_call x1, Pallas kernels, body(): pl.pallas_call(functools.partial(contract_amplitudes, len(list_a), len(li...  4.87 us
    pallas_call x2, Pallas kernels, contracted(): pl.pallas_call(functools.partial(rows_out, start * width, cut * len(names...  4.79 us
    reshape x2, other arithmetic, whole(): return parts[0].reshape(orbital_alpha.shape)  2.44 us
  transfers between devices with their start and end apart: 25, of which 10 were waited for; matrix products, arithmetic and copies ran while one was open for 4% of the time, Pallas kernels for 6%

profile of v6, /device:TPU:0, one launch (start us, length us, event | category | flops | bytes accessed | tf_op | source)
XLA Modules:
  0.0 93.0 jit_solution(11988026390524037445)
XLA Ops:
  0.6 4.1 %collective-permute-start.2 = (bf16[96,2560]{1,0:T(8,128)(2,1)}, bf16[96,2560]{1,0:T(8,128)(2,1)S(1)}, u32[]{:S(2)}, u32[]{:S(2)}) collective-permute-start(bf16[96,2560]{1,0:T(8,128)(2,1)} %bitcast.7), channel_id=1, source_target_pairs={{0,8},{1,9},{2,10},{3,11},{4,12},{5,13},{6,14},{7,15},{8,0},{9,1},... | collective-permute-start | bytes 1474568 | tf_op jit(solution)/shard_map/ppermute | solution.py:24
  4.8 1.5 %collective-permute-start.1 = (bf16[96,2560]{1,0:T(8,128)(2,1)}, bf16[96,2560]{1,0:T(8,128)(2,1)S(1)}, u32[]{:S(2)}, u32[]{:S(2)}) collective-permute-start(bf16[96,2560]{1,0:T(8,128)(2,1)} %bitcast.8), channel_id=1, source_target_pairs={{0,2},{1,3},{2,0},{3,1},{4,6},{5,7},{6,4},{7,5},{8,10},{9,11},{10,... | collective-permute-start | bytes 1474568 | tf_op jit(solution)/shard_map/ppermute | solution.py:24
  6.2 1.6 %collective-permute-start.3 = (bf16[96,2560]{1,0:T(8,128)(2,1)}, bf16[96,2560]{1,0:T(8,128)(2,1)S(1)}, u32[]{:S(2)}, u32[]{:S(2)}) collective-permute-start(bf16[96,2560]{1,0:T(8,128)(2,1)} %bitcast.10), channel_id=1, source_target_pairs={{0,4},{1,5},{2,6},{3,7},{4,0},{5,1},{6,2},{7,3},{8,12},{9,13},{10,... | collective-permute-start | bytes 1474568 | tf_op jit(solution)/shard_map/ppermute | solution.py:24
  7.8 1.5 %collective-permute-start = (bf16[96,2560]{1,0:T(8,128)(2,1)}, bf16[96,2560]{1,0:T(8,128)(2,1)}, u32[]{:S(2)}, u32[]{:S(2)}) collective-permute-start(bf16[96,2560]{1,0:T(8,128)(2,1)} %bitcast.11), channel_id=1, source_target_pairs={{0,16},{1,17},{2,18},{3,19},{4,20},{5,21},{6,22},{7,23},{8,24},{9,... | collective-permute-start | bytes 1474568 | tf_op jit(solution)/shard_map/ppermute | solution.py:24
  9.3 0.8 reshape.35.vb_ref
  10.1 1.0 %broadcast_in_dim.3.va_ref = f32[1536,1]{1,0:T(8,128)S(1)} reshape(f32[1536]{0:T(1024)} %param.10) | data formatting | bytes 12288 | tf_op jit(solution)/shard_map/broadcast_in_dim | solution.py:140
  11.1 0.6 copy-done.2
  11.7 0.7 copy-done.3
  12.4 0.8 energies.1.refs_12_
  13.2 13.6 %collective-permute-done.2.refs_2_ = bf16[96,2560]{1,0:T(8,128)(2,1)S(1)} collective-permute-done((bf16[96,2560]{1,0:T(8,128)(2,1)}, bf16[96,2560]{1,0:T(8,128)(2,1)S(1)}, u32[]{:S(2)}, u32[]{:S(2)}) %collective-permute-start.2) | collective-permute-done | bytes 491552 | tf_op jit(solution)/shard_map/ppermute | solution.py:24
  26.8 1.4 %collective-permute-done.3.refs_9_ = bf16[96,2560]{1,0:T(8,128)(2,1)S(1)} collective-permute-done((bf16[96,2560]{1,0:T(8,128)(2,1)}, bf16[96,2560]{1,0:T(8,128)(2,1)S(1)}, u32[]{:S(2)}, u32[]{:S(2)}) %collective-permute-start.3) | collective-permute-done | bytes 491552 | tf_op jit(solution)/shard_map/ppermute | solution.py:24
  28.2 1.6 %collective-permute-start.5 = (bf16[96,2560]{1,0:T(8,128)(2,1)S(1)}, bf16[96,2560]{1,0:T(8,128)(2,1)S(1)}, u32[]{:S(2)}, u32[]{:S(2)}) collective-permute-start(bf16[96,2560]{1,0:T(8,128)(2,1)S(1)} %collective-permute-done.3.refs_9_), channel_id=1, source_target_pairs={{0,16},{1,17},{2,18},{3,19},{4,20},{5,21},{6,22},{7,23},{8,24},{9,... | collective-permute-start | bytes 1474568 | tf_op jit(solution)/shard_map/ppermute | solution.py:24
  30.9 8.4 %collective-permute-done.5.refs_5_ = bf16[96,2560]{1,0:T(8,128)(2,1)S(1)} collective-permute-done((bf16[96,2560]{1,0:T(8,128)(2,1)S(1)}, bf16[96,2560]{1,0:T(8,128)(2,1)S(1)}, u32[]{:S(2)}, u32[]{:S(2)}) %collective-permute-start.5) | collective-permute-done | bytes 491552 | tf_op jit(solution)/shard_map/ppermute | solution.py:24
  39.2 4.2 %collective-permute-done.4.refs_0_ = bf16[96,2560]{1,0:T(8,128)(2,1)S(1)} collective-permute-done((bf16[96,2560]{1,0:T(8,128)(2,1)S(1)}, bf16[96,2560]{1,0:T(8,128)(2,1)S(1)}, u32[]{:S(2)}, u32[]{:S(2)}) %collective-permute-start.4) | collective-permute-done | bytes 491552 | tf_op jit(solution)/shard_map/ppermute | solution.py:24
  43.5 4.9 %amplitudes.1 = (bf16[384,768]{1,0:T(8,128)(2,1)S(1)}, bf16[768,384]{1,0:T(8,128)(2,1)S(1)}, bf16[384,2560]{1,0:T(8,128)(2,1)S(1)}, bf16[768,2560]{1,0:T(8,128)(...) custom-call(bf16[96,2560]{1,0:T(8,128)(2,1)S(1)} %collective-permute, ...), custom_call_target="tpu_custom_call" | custom-call | flops 1509949440 | bytes 11796480 | tf_op jit(solution)/shard_map/amplitudes/pallas_call | solution.py:155
  48.9 2.4 %alpha.1 = (f32[96,2560]{1,0:T(8,128)S(1)}, f32[96,2560]{1,0:T(8,128)S(1)}, f32[96,2560]{1,0:T(8,128)S(1)}, f32[96,2560]{1,0:T(8,128)S(1)}) custom-call(bf16[384,768]{1,0:T(8,128)(2,1)S(1)} %get-tuple-element.51.left, bf16[768,2560]{1,0:T(8,128)(2,1)S(1)} %get-tuple-element.52.right), custom_call_target="tpu_custom_call" | custom-call | flops 1509949440 | bytes 7864320 | tf_op jit(solution)/shard_map/alpha/pallas_call | solution.py:172
  52.8 1.4 %collective-permute-start.12 = (f16[96,2560]{1,0:T(8,128)(2,1)S(1)}, f16[96,2560]{1,0:T(8,128)(2,1)S(1)}, u32[]{:S(2)}, u32[]{:S(2)}) collective-permute-start(f16[96,2560]{1,0:T(8,128)(2,1)S(1)} %get-tuple-element.62), channel_id=1, source_target_pairs={{0,2},{1,3},{2,0},{3,1},{4,6},{5,7},{6,4},{7,5},{8,10},{9,11},{10,... | collective-permute-start | bytes 1474568 | tf_op jit(solution)/shard_map/ppermute | solution.py:24
  54.2 1.6 %collective-permute-start.13 = (f16[96,2560]{1,0:T(8,128)(2,1)S(1)}, f16[96,2560]{1,0:T(8,128)(2,1)S(1)}, u32[]{:S(2)}, u32[]{:S(2)}) collective-permute-start(f16[96,2560]{1,0:T(8,128)(2,1)S(1)} %multiply_convert_fusion.7), channel_id=1, source_target_pairs={{0,16},{1,17},{2,18},{3,19},{4,20},{5,21},{6,22},{7,23},{8,24},{9,... | collective-permute-start | bytes 1474568 | tf_op jit(solution)/shard_map/ppermute | solution.py:24
  55.8 2.4 %beta.1 = (f32[96,2560]{1,0:T(8,128)S(1)}, f32[96,2560]{1,0:T(8,128)S(1)}, f32[96,2560]{1,0:T(8,128)S(1)}, f32[96,2560]{1,0:T(8,128)S(1)}, f32[96,2560]{1,0:T(8,128)S(1)}, /*index=5*/f32[96,2560]{1,0:T(8,128)S(1)}) custom-call(bf16[768,384]{1,0:T(8,128)(2,1)S(1)} %get-tuple-element.71.left, bf16[384,2560]{1,0:T(8,128)(2,1)S(1)} %get-tuple-element.72.right), custom_call_target="tpu_custom_call" | custom-call | flops 1132462080 | bytes 7864320 | tf_op jit(solution)/shard_map/beta/pallas_call | solution.py:172
  58.2 0.7 collective-permute-start.15
  59.0 2.4 %collective-permute-start.17 = (f32[2560]{0:T(1024)S(1)}, f32[2560]{0:T(1024)S(1)}, u32[]{:S(2)}, u32[]{:S(2)}) collective-permute-start(f32[2560]{0:T(1024)S(1)} %get-tuple-element.87), channel_id=1, source_target_pairs={{0,4},{1,5},{2,6},{3,7},{4,0},{5,1},{6,2},{7,3},{8,12},{9,13},{10,... | collective-permute-start | bytes 30728 | tf_op jit(solution)/shard_map/ppermute | solution.py:24
  61.7 1.2 %collective-permute-done.15 = f32[2560]{0:T(1024)S(1)} collective-permute-done((f32[2560]{0:T(1024)S(1)}, f32[2560]{0:T(1024)S(1)}, u32[]{:S(2)}, u32[]{:S(2)}) %collective-permute-start.15) | collective-permute-done | bytes 10272 | tf_op jit(solution)/shard_map/ppermute | solution.py:24
  63.0 2.5 %collective-permute-done.12 = f16[96,2560]{1,0:T(8,128)(2,1)S(1)} collective-permute-done((f16[96,2560]{1,0:T(8,128)(2,1)S(1)}, f16[96,2560]{1,0:T(8,128)(2,1)S(1)}, u32[]{:S(2)}, u32[]{:S(2)}) %collective-permute-start.12) | collective-permute-done | bytes 491552 | tf_op jit(solution)/shard_map/ppermute | solution.py:24
  65.6 1.0 %collective-permute-done.13 = f16[96,2560]{1,0:T(8,128)(2,1)S(1)} collective-permute-done((f16[96,2560]{1,0:T(8,128)(2,1)S(1)}, f16[96,2560]{1,0:T(8,128)(2,1)S(1)}, u32[]{:S(2)}, u32[]{:S(2)}) %collective-permute-start.13) | collective-permute-done | bytes 491552 | tf_op jit(solution)/shard_map/ppermute | solution.py:24
  66.8 0.9 collective-permute-start.19
  68.2 2.8 %collective-permute-start.21 = (f16[96,2560]{1,0:T(8,128)(2,1)S(1)}, f16[96,2560]{1,0:T(8,128)(2,1)S(1)}, u32[]{:S(2)}, u32[]{:S(2)}) collective-permute-start(f16[96,2560]{1,0:T(8,128)(2,1)S(1)} %get-tuple-element.96), channel_id=1, source_target_pairs={{0,4},{1,5},{2,6},{3,7},{4,0},{5,1},{6,2},{7,3},{8,12},{9,13},{10,... | collective-permute-start | bytes 1474568 | tf_op jit(solution)/shard_map/ppermute | solution.py:24
  71.1 1.4 %collective-permute-start.18 = (f16[96,2560]{1,0:T(8,128)(2,1)S(1)}, f16[96,2560]{1,0:T(8,128)(2,1)S(1)}, u32[]{:S(2)}, u32[]{:S(2)}) collective-permute-start(f16[96,2560]{1,0:T(8,128)(2,1)S(1)} %get-tuple-element.67), channel_id=1, source_target_pairs={{0,2},{1,3},{2,0},{3,1},{4,6},{5,7},{6,4},{7,5},{8,10},{9,11},{10,... | collective-permute-start | bytes 1474568 | tf_op jit(solution)/shard_map/ppermute | solution.py:24
  72.5 0.6 collective-permute-start.24
  73.1 16.7 %collective-permute-done.19 = f16[96,2560]{1,0:T(8,128)(2,1)S(1)} collective-permute-done((f16[96,2560]{1,0:T(8,128)(2,1)S(1)}, f16[96,2560]{1,0:T(8,128)(2,1)S(1)}, u32[]{:S(2)}, u32[]{:S(2)}) %collective-permute-start.19) | collective-permute-done | bytes 491552 | tf_op jit(solution)/shard_map/ppermute | solution.py:24
  89.8 0.7 collective-permute-done.21
  90.5 1.2 %add_bitcast_fusion.1 = f32[1,96,2560]{2,1,0:T(8,128)} fusion(f16[96,2560]{1,0:T(8,128)(2,1)S(1)} %collective-permute-done.19, f32[96,2560]{1,0:T(8,128)S(1)} %get-tuple-element.53, f16[96,2560]{1,0:T(8,128)(2,1)S(1)} %collective-permute-done.18, f32[2560]{0:T(1024)S(1)} %collective-permute-done.15, f32[2560]{0:T(1024)S(1)} %collective-permute-done.14), kind=kLoop, calls=%fused_computation.4 | loop fusion | flops 1474560 | bytes 2969600 | tf_op jit(solution)/shard_map/reshape | solution.py:258
  91.7 1.2 %add_bitcast_fusion = f32[1,96,2560]{2,1,0:T(8,128)} fusion(f16[96,2560]{1,0:T(8,128)(2,1)S(1)} %collective-permute-done.21, f16[96,2560]{1,0:T(8,128)(2,1)S(1)} %collective-permute-done.24, f32[96,2560]{1,0:T(8,128)S(1)} %get-tuple-element.80, f16[96,2560]{1,0:T(8,128)(2,1)S(1)} %collective-permute-done.22, f32[2560]{0:T(1024)S(1)} %collective-permute-done.17, ...), kind=kLoop, calls=%fused_computation | loop fusion | flops 2211840 | bytes 3471360 | tf_op jit(solution)/shard_map/reshape | solution.py:258
  (42 shorter events, 4.3 us)
Async XLA Ops:
  0.6 42.8 %copy-start = (bf16[1,96,2560]{2,1,0:T(8,128)(2,1)S(1)}, bf16[1,96,2560]{2,1,0:T(8,128)(2,1)}, u32[]{:S(2)}) copy-start(bf16[1,96,2560]{2,1,0:T(8,128)(2,1)} %param.6) | copy-start | bytes 1474564
  0.6 29.9 %copy-start.1 = (bf16[1,96,2560]{2,1,0:T(8,128)(2,1)S(1)}, bf16[1,96,2560]{2,1,0:T(8,128)(2,1)}, u32[]{:S(2)}) copy-start(bf16[1,96,2560]{2,1,0:T(8,128)(2,1)} %param.7) | copy-start | bytes 1474564
  0.6 26.2 %collective-permute-start.2 = (bf16[96,2560]{1,0:T(8,128)(2,1)}, bf16[96,2560]{1,0:T(8,128)(2,1)S(1)}, u32[]{:S(2)}, u32[]{:S(2)}) collective-permute-start(bf16[96,2560]{1,0:T(8,128)(2,1)} %bitcast.7), channel_id=1, source_target_pairs={{0,8},{1,9},{2,10},{3,11},{4,12},{5,13},{6,14},{7,15},{8,0},{9,1},... | collective-permute-start | bytes 1474568 | tf_op jit(solution)/shard_map/ppermute | solution.py:24
  4.8 22.1 %collective-permute-start.1 = (bf16[96,2560]{1,0:T(8,128)(2,1)}, bf16[96,2560]{1,0:T(8,128)(2,1)S(1)}, u32[]{:S(2)}, u32[]{:S(2)}) collective-permute-start(bf16[96,2560]{1,0:T(8,128)(2,1)} %bitcast.8), channel_id=1, source_target_pairs={{0,2},{1,3},{2,0},{3,1},{4,6},{5,7},{6,4},{7,5},{8,10},{9,11},{10,... | collective-permute-start | bytes 1474568 | tf_op jit(solution)/shard_map/ppermute | solution.py:24
  6.2 22.0 %collective-permute-start.3 = (bf16[96,2560]{1,0:T(8,128)(2,1)}, bf16[96,2560]{1,0:T(8,128)(2,1)S(1)}, u32[]{:S(2)}, u32[]{:S(2)}) collective-permute-start(bf16[96,2560]{1,0:T(8,128)(2,1)} %bitcast.10), channel_id=1, source_target_pairs={{0,4},{1,5},{2,6},{3,7},{4,0},{5,1},{6,2},{7,3},{8,12},{9,13},{10,... | collective-permute-start | bytes 1474568 | tf_op jit(solution)/shard_map/ppermute | solution.py:24
  7.8 20.4 %collective-permute-start = (bf16[96,2560]{1,0:T(8,128)(2,1)}, bf16[96,2560]{1,0:T(8,128)(2,1)}, u32[]{:S(2)}, u32[]{:S(2)}) collective-permute-start(bf16[96,2560]{1,0:T(8,128)(2,1)} %bitcast.11), channel_id=1, source_target_pairs={{0,16},{1,17},{2,18},{3,19},{4,20},{5,21},{6,22},{7,23},{8,24},{9,... | collective-permute-start | bytes 1474568 | tf_op jit(solution)/shard_map/ppermute | solution.py:24
  11.1 0.7 copy-start.2
  11.7 0.7 copy-start.3
  28.2 11.0 %collective-permute-start.5 = (bf16[96,2560]{1,0:T(8,128)(2,1)S(1)}, bf16[96,2560]{1,0:T(8,128)(2,1)S(1)}, u32[]{:S(2)}, u32[]{:S(2)}) collective-permute-start(bf16[96,2560]{1,0:T(8,128)(2,1)S(1)} %collective-permute-done.3.refs_9_), channel_id=1, source_target_pairs={{0,16},{1,17},{2,18},{3,19},{4,20},{5,21},{6,22},{7,23},{8,24},{9,... | collective-permute-start | bytes 1474568 | tf_op jit(solution)/shard_map/ppermute | solution.py:24
  29.8 13.6 %collective-permute-start.8 = (bf16[96,2560]{1,0:T(8,128)(2,1)S(1)}, bf16[96,2560]{1,0:T(8,128)(2,1)S(1)}, u32[]{:S(2)}, u32[]{:S(2)}) collective-permute-start(bf16[96,2560]{1,0:T(8,128)(2,1)S(1)} %collective-permute-done.3.refs_9_), channel_id=1, source_target_pairs={{0,1},{1,0},{2,3},{3,2},{4,5},{5,4},{6,7},{7,6},{8,9},{9,8},{10,11... | collective-permute-start | bytes 1474568 | tf_op jit(solution)/shard_map/ppermute | solution.py:24
  29.8 13.6 %collective-permute-start.4 = (bf16[96,2560]{1,0:T(8,128)(2,1)S(1)}, bf16[96,2560]{1,0:T(8,128)(2,1)S(1)}, u32[]{:S(2)}, u32[]{:S(2)}) collective-permute-start(bf16[96,2560]{1,0:T(8,128)(2,1)S(1)} %collective-permute-done.2.refs_2_), channel_id=1, source_target_pairs={{0,2},{1,3},{2,0},{3,1},{4,6},{5,7},{6,4},{7,5},{8,10},{9,11},{10,... | collective-permute-start | bytes 1474568 | tf_op jit(solution)/shard_map/ppermute | solution.py:24
  30.3 13.1 %collective-permute-start.7 = (bf16[96,2560]{1,0:T(8,128)(2,1)}, bf16[96,2560]{1,0:T(8,128)(2,1)S(1)}, u32[]{:S(2)}, u32[]{:S(2)}) collective-permute-start(bf16[96,2560]{1,0:T(8,128)(2,1)} %collective-permute-done.refs_7_), channel_id=1, source_target_pairs={{0,1},{1,0},{2,3},{3,2},{4,5},{5,4},{6,7},{7,6},{8,9},{9,8},{10,11... | collective-permute-start | bytes 1474568 | tf_op jit(solution)/shard_map/ppermute | solution.py:24
  30.6 12.9 %collective-permute-start.9 = (bf16[96,2560]{1,0:T(8,128)(2,1)S(1)}, bf16[96,2560]{1,0:T(8,128)(2,1)S(1)}, u32[]{:S(2)}, u32[]{:S(2)}) collective-permute-start(bf16[96,2560]{1,0:T(8,128)(2,1)S(1)} %bitcast.12), channel_id=1, source_target_pairs={{0,1},{1,0},{2,3},{3,2},{4,5},{5,4},{6,7},{7,6},{8,9},{9,8},{10,11... | collective-permute-start | bytes 1474568 | tf_op jit(solution)/shard_map/ppermute | solution.py:24
  39.2 4.2 %collective-permute-start.6 = (bf16[96,2560]{1,0:T(8,128)(2,1)S(1)}, bf16[96,2560]{1,0:T(8,128)(2,1)S(1)}, u32[]{:S(2)}, u32[]{:S(2)}) collective-permute-start(bf16[96,2560]{1,0:T(8,128)(2,1)S(1)} %collective-permute-done.5.refs_5_), channel_id=1, source_target_pairs={{0,1},{1,0},{2,3},{3,2},{4,5},{5,4},{6,7},{7,6},{8,9},{9,8},{10,11... | collective-permute-start | bytes 1474568 | tf_op jit(solution)/shard_map/ppermute | solution.py:24
  48.4 3.2 %collective-permute-start.11 = (f32[2560]{0:T(1024)S(1)}, f32[2560]{0:T(1024)S(1)}, u32[]{:S(2)}, u32[]{:S(2)}) collective-permute-start(f32[2560]{0:T(1024)S(1)} %get-tuple-element.58), channel_id=1, source_target_pairs={{0,1},{1,0},{2,3},{3,2},{4,5},{5,4},{6,7},{7,6},{8,9},{9,8},{10,11... | collective-permute-start | bytes 30728 | tf_op jit(solution)/shard_map/ppermute | solution.py:24
  48.4 3.1 %collective-permute-start.10 = (f32[96,2560]{1,0:T(8,128)S(1)}, f32[96,2560]{1,0:T(8,128)S(1)}, u32[]{:S(2)}, u32[]{:S(2)}) collective-permute-start(f32[96,2560]{1,0:T(8,128)S(1)} %get-tuple-element.57), channel_id=1, source_target_pairs={{0,1},{1,0},{2,3},{3,2},{4,5},{5,4},{6,7},{7,6},{8,9},{9,8},{10,11... | collective-permute-start | bytes 2949128 | tf_op jit(solution)/shard_map/ppermute | solution.py:24
  51.7 6.5 %collective-permute-start.14 = (f32[2560]{0:T(1024)S(1)}, f32[2560]{0:T(1024)S(1)}, u32[]{:S(2)}, u32[]{:S(2)}) collective-permute-start(f32[2560]{0:T(1024)S(1)} %get-tuple-element.65), channel_id=1, source_target_pairs={{0,2},{1,3},{2,0},{3,1},{4,6},{5,7},{6,4},{7,5},{8,10},{9,11},{10,... | collective-permute-start | bytes 30728 | tf_op jit(solution)/shard_map/ppermute | solution.py:24
  52.3 6.7 %collective-permute-start.16 = (f32[2560]{0:T(1024)S(1)}, f32[2560]{0:T(1024)S(1)}, u32[]{:S(2)}, u32[]{:S(2)}) collective-permute-start(f32[2560]{0:T(1024)S(1)} %get-tuple-element.66), channel_id=1, source_target_pairs={{0,16},{1,17},{2,18},{3,19},{4,20},{5,21},{6,22},{7,23},{8,24},{9,... | collective-permute-start | bytes 30728 | tf_op jit(solution)/shard_map/ppermute | solution.py:24
  52.8 12.8 %collective-permute-start.12 = (f16[96,2560]{1,0:T(8,128)(2,1)S(1)}, f16[96,2560]{1,0:T(8,128)(2,1)S(1)}, u32[]{:S(2)}, u32[]{:S(2)}) collective-permute-start(f16[96,2560]{1,0:T(8,128)(2,1)S(1)} %get-tuple-element.62), channel_id=1, source_target_pairs={{0,2},{1,3},{2,0},{3,1},{4,6},{5,7},{6,4},{7,5},{8,10},{9,11},{10,... | collective-permute-start | bytes 1474568 | tf_op jit(solution)/shard_map/ppermute | solution.py:24
  54.2 12.4 %collective-permute-start.13 = (f16[96,2560]{1,0:T(8,128)(2,1)S(1)}, f16[96,2560]{1,0:T(8,128)(2,1)S(1)}, u32[]{:S(2)}, u32[]{:S(2)}) collective-permute-start(f16[96,2560]{1,0:T(8,128)(2,1)S(1)} %multiply_convert_fusion.7), channel_id=1, source_target_pairs={{0,16},{1,17},{2,18},{3,19},{4,20},{5,21},{6,22},{7,23},{8,24},{9,... | collective-permute-start | bytes 1474568 | tf_op jit(solution)/shard_map/ppermute | solution.py:24
  58.2 4.7 %collective-permute-start.15 = (f32[2560]{0:T(1024)S(1)}, f32[2560]{0:T(1024)S(1)}, u32[]{:S(2)}, u32[]{:S(2)}) collective-permute-start(f32[2560]{0:T(1024)S(1)} %get-tuple-element.89), channel_id=1, source_target_pairs={{0,8},{1,9},{2,10},{3,11},{4,12},{5,13},{6,14},{7,15},{8,0},{9,1},... | collective-permute-start | bytes 30728 | tf_op jit(solution)/shard_map/ppermute | solution.py:24
  59.0 4.1 %collective-permute-start.17 = (f32[2560]{0:T(1024)S(1)}, f32[2560]{0:T(1024)S(1)}, u32[]{:S(2)}, u32[]{:S(2)}) collective-permute-start(f32[2560]{0:T(1024)S(1)} %get-tuple-element.87), channel_id=1, source_target_pairs={{0,4},{1,5},{2,6},{3,7},{4,0},{5,1},{6,2},{7,3},{8,12},{9,13},{10,... | collective-permute-start | bytes 30728 | tf_op jit(solution)/shard_map/ppermute | solution.py:24
  61.6 6.1 %collective-permute-start.23 = (f16[96,2560]{1,0:T(8,128)(2,1)S(1)}, f16[96,2560]{1,0:T(8,128)(2,1)S(1)}, u32[]{:S(2)}, u32[]{:S(2)}) collective-permute-start(f16[96,2560]{1,0:T(8,128)(2,1)S(1)} %get-tuple-element.93), channel_id=1, source_target_pairs={{0,1},{1,0},{2,3},{3,2},{4,5},{5,4},{6,7},{7,6},{8,9},{9,8},{10,11... | collective-permute-start | bytes 1474568 | tf_op jit(solution)/shard_map/ppermute | solution.py:24
  62.9 4.8 %collective-permute-start.20 = (f16[96,2560]{1,0:T(8,128)(2,1)S(1)}, f16[96,2560]{1,0:T(8,128)(2,1)S(1)}, u32[]{:S(2)}, u32[]{:S(2)}) collective-permute-start(f16[96,2560]{1,0:T(8,128)(2,1)S(1)} %get-tuple-element.94), channel_id=1, source_target_pairs={{0,1},{1,0},{2,3},{3,2},{4,5},{5,4},{6,7},{7,6},{8,9},{9,8},{10,11... | collective-permute-start | bytes 1474568 | tf_op jit(solution)/shard_map/ppermute | solution.py:24
  66.8 23.0 %collective-permute-start.19 = (f16[96,2560]{1,0:T(8,128)(2,1)S(1)}, f16[96,2560]{1,0:T(8,128)(2,1)S(1)}, u32[]{:S(2)}, u32[]{:S(2)}) collective-permute-start(f16[96,2560]{1,0:T(8,128)(2,1)S(1)} %multiply_convert_fusion.5), channel_id=1, source_target_pairs={{0,8},{1,9},{2,10},{3,11},{4,12},{5,13},{6,14},{7,15},{8,0},{9,1},... | collective-permute-start | bytes 1474568 | tf_op jit(solution)/shard_map/ppermute | solution.py:24
  68.2 22.3 %collective-permute-start.21 = (f16[96,2560]{1,0:T(8,128)(2,1)S(1)}, f16[96,2560]{1,0:T(8,128)(2,1)S(1)}, u32[]{:S(2)}, u32[]{:S(2)}) collective-permute-start(f16[96,2560]{1,0:T(8,128)(2,1)S(1)} %get-tuple-element.96), channel_id=1, source_target_pairs={{0,4},{1,5},{2,6},{3,7},{4,0},{5,1},{6,2},{7,3},{8,12},{9,13},{10,... | collective-permute-start | bytes 1474568 | tf_op jit(solution)/shard_map/ppermute | solution.py:24
  71.1 19.4 %collective-permute-start.18 = (f16[96,2560]{1,0:T(8,128)(2,1)S(1)}, f16[96,2560]{1,0:T(8,128)(2,1)S(1)}, u32[]{:S(2)}, u32[]{:S(2)}) collective-permute-start(f16[96,2560]{1,0:T(8,128)(2,1)S(1)} %get-tuple-element.67), channel_id=1, source_target_pairs={{0,2},{1,3},{2,0},{3,1},{4,6},{5,7},{6,4},{7,5},{8,10},{9,11},{10,... | collective-permute-start | bytes 1474568 | tf_op jit(solution)/shard_map/ppermute | solution.py:24
  72.5 19.2 %collective-permute-start.22 = (f16[96,2560]{1,0:T(8,128)(2,1)S(1)}, f16[96,2560]{1,0:T(8,128)(2,1)S(1)}, u32[]{:S(2)}, u32[]{:S(2)}) collective-permute-start(f16[96,2560]{1,0:T(8,128)(2,1)S(1)} %get-tuple-element.92), channel_id=1, source_target_pairs={{0,1},{1,0},{2,3},{3,2},{4,5},{5,4},{6,7},{7,6},{8,9},{9,8},{10,11... | collective-permute-start | bytes 1474568 | tf_op jit(solution)/shard_map/ppermute | solution.py:24
  72.5 19.2 %collective-permute-start.24 = (f16[96,2560]{1,0:T(8,128)(2,1)S(1)}, f16[96,2560]{1,0:T(8,128)(2,1)S(1)}, u32[]{:S(2)}, u32[]{:S(2)}) collective-permute-start(f16[96,2560]{1,0:T(8,128)(2,1)S(1)} %get-tuple-element.95), channel_id=1, source_target_pairs={{0,16},{1,17},{2,18},{3,19},{4,20},{5,21},{6,22},{7,23},{8,24},{9,... | collective-permute-start | bytes 1474568 | tf_op jit(solution)/shard_map/ppermute | solution.py:24

commit v7 on v6

--- a/solution.py
+++ b/solution.py
@@ -48,34 +48,56 @@
     return jnp.max(jnp.max(jnp.abs(value), axis=1, keepdims=True), axis=0, keepdims=True).astype(jnp.float32)
 
 
-def contract_amplitudes(n_a, n_b, early, spans, *refs):
+def amplitudes_of(rows, cols, acat, bcat, ninv, t_ref, tt):
+    top = jnp.zeros((1, 1), jnp.float32)
+    step = 256 if (cols[1] - cols[0]) % 256 == 0 else cols[1] - cols[0]
+    for c in range(cols[0], cols[1], step):
+        integrals = lax.dot_general(
+            acat[rows[0]:rows[1], :], bcat[c:c + step, :], (((1,), (1,)), ((), ())), preferred_element_type=jnp.float32
+        )
+        amps = integrals * ninv[rows[0]:rows[1], c:c + step]
+        top = jnp.maximum(top, magnitude(amps))
+        amps = amps.astype(jnp.bfloat16)
+        t_ref[rows[0]:rows[1], c:c + step] = amps
+        tt[c:c + step, rows[0]:rows[1]] = amps.T
+    return top
+
+
+def joined(sources, places, target):
+    top = jnp.zeros((1, 1), jnp.float32)
+    for ref, at in zip(sources, places):
+        value = ref[...]
+        target[at:at + ref.shape[0], :] = value
+        top = jnp.maximum(top, magnitude(value))
+    return top
+
+
+def begin_amplitudes(places_a, places_b, corner, *refs):
+    n_a, n_b = len(places_a), len(places_b)
     a_refs, b_refs, ninv = refs[:n_a], refs[n_a:n_a + n_b], refs[n_a + n_b]
-    t_ref, tt, acat, bcat, scale_a, scale_b, unit_a, unit_b = refs[n_a + n_b + 1:n_a + n_b + 9]
-    outs = refs[n_a + n_b + 9:]
-    largest = []
-    for sources, joined in ((a_refs, acat), (b_refs, bcat)):
-        at, top = 0, None
-        for ref in sources:
-            value = ref[...]
-            joined[at:at + ref.shape[0], :] = value
-            at += ref.shape[0]
-            top = magnitude(value) if top is None else jnp.maximum(top, magnitude(value))
-        largest.append(top)
+    t_ref, tt, acat, bcat, tops = refs[n_a + n_b + 1:]
+    top_a, top_b = joined(a_refs, places_a, acat), joined(b_refs, places_b, bcat)
     rows, cols = t_ref.shape
-    step = 256 if cols % 256 == 0 else cols // 2
-    top = None
-    for c in range(0, cols, step):
-        integrals = lax.dot_general(
-            acat[...], bcat[c:c + step, :], (((1,), (1,)), ((), ())), preferred_element_type=jnp.float32
-        )
-        amps = integrals * ninv[:, c:c + step]
-        top = magnitude(amps) if top is None else jnp.maximum(top, magnitude(amps))
-        amps = amps.astype(jnp.bfloat16)
-        t_ref[:, c:c + step] = amps
-        tt[c:c + step, :] = amps.T
-    for largest_right, count, unit, scale in (
-        (largest[1], cols, unit_a, scale_a), (largest[0], rows, unit_b, scale_b)
-    ):
+    top = jnp.zeros((1, 1), jnp.float32)
+    if corner[0] < rows and corner[1] < cols:
+        top = amplitudes_of((corner[0], rows), (corner[1], cols), acat, bcat, ninv, t_ref, tt)
+    row = lax.broadcasted_iota(jnp.int32, tops.shape, 0)
+    tops[...] = jnp.where(row == 0, top, jnp.where(row == 1, top_a, top_b))
+
+
+def end_amplitudes(places_a, places_b, corner, spans, *refs):
+    n_a, n_b = len(places_a), len(places_b)
+    a_refs, b_refs, ninv = refs[:n_a], refs[n_a:n_a + n_b], refs[n_a + n_b]
+    tops = refs[n_a + n_b + 5]
+    t_ref, tt, acat, bcat, scale_a, scale_b, unit_a, unit_b = refs[n_a + n_b + 6:n_a + n_b + 14]
+    outs = refs[n_a + n_b + 14:]
+    rows, cols = t_ref.shape
+    top_a = jnp.maximum(tops[1:2, 0:1], joined(a_refs, places_a, acat))
+    top_b = jnp.maximum(tops[2:3, 0:1], joined(b_refs, places_b, bcat))
+    top = jnp.maximum(tops[0:1, 0:1], amplitudes_of((0, corner[0]), (0, cols), acat, bcat, ninv, t_ref, tt))
+    if corner[0] < rows:
+        top = jnp.maximum(top, amplitudes_of((corner[0], rows), (0, corner[1]), acat, bcat, ninv, t_ref, tt))
+    for largest_right, count, unit, scale in ((top_b, cols, unit_a, scale_a), (top_a, rows, unit_b, scale_b)):
         value = top * largest_right * (count / 32768.0) + 1e-36
         unit[...] = jnp.broadcast_to(value[0, 0], unit.shape)
         scale[...] = jnp.broadcast_to((1.0 / value)[0, 0], scale.shape)
@@ -150,22 +172,45 @@
         return {m: [out] for m, out in zip(names, outs)}
 
     early = max(n_b // 4, 2)
-    list_a = [v for m in masks_a for v in pieces_a[m]]
-    list_b = [v for m in masks_b for v in pieces_b[m]]
+
+    def late_first(names, first):
+        late = [m for m in names if m & (1 << first) and m & ~(1 << first) & ~1]
+        return len(late) if names[:len(late)] == late else len(names)
+
+    late_a, late_b = late_first(masks_a, first_a), late_first(masks_b, first_b)
+    corner = (min(-(-late_a * width // 128) * 128, rows), min(-(-late_b * width // 256) * 256, cols))
+    all_a = [(v, k * width) for k, m in enumerate(masks_a) for v in pieces_a[m]]
+    all_b = [(v, k * width) for k, m in enumerate(masks_b) for v in pieces_b[m]]
+    shared = [
+        jax.ShapeDtypeStruct((rows, cols), jnp.bfloat16),
+        jax.ShapeDtypeStruct((cols, rows), jnp.bfloat16),
+        jax.ShapeDtypeStruct((rows, aux), jnp.bfloat16),
+        jax.ShapeDtypeStruct((cols, aux), jnp.bfloat16),
+    ]
+
+    def estimate(part):
+        return pl.CostEstimate(
+            flops=2 * part * aux, bytes_accessed=2 * (rows + cols) * aux * 2, transcendentals=0
+        )
+
+    begun = pl.pallas_call(
+        functools.partial(begin_amplitudes, [p for _, p in all_a[late_a:]], [p for _, p in all_b[late_b:]], corner),
+        out_shape=shared + [jax.ShapeDtypeStruct((8, 128), jnp.float32)],
+        compiler_params=pltpu.CompilerParams(vmem_limit_bytes=18 * MIB),
+        cost_estimate=estimate((rows - corner[0]) * (cols - corner[1])),
+        name="amplitudes_early",
+    )(*[v for v, _ in all_a[late_a:] + all_b[late_b:]], ninv)
+    count = late_a + late_b + 1
     opening = pl.pallas_call(
-        functools.partial(contract_amplitudes, len(list_a), len(list_b), early, cut * early),
-        out_shape=[
-            jax.ShapeDtypeStruct((rows, cols), jnp.bfloat16),
-            jax.ShapeDtypeStruct((cols, rows), jnp.bfloat16),
-            jax.ShapeDtypeStruct((rows, aux), jnp.bfloat16),
-            jax.ShapeDtypeStruct((cols, aux), jnp.bfloat16),
-        ] + [jax.ShapeDtypeStruct((aux,), jnp.float32)] * 4 + blocks(early),
-        compiler_params=pltpu.CompilerParams(vmem_limit_bytes=20 * MIB),
-        cost_estimate=pl.CostEstimate(
-            flops=2 * rows * cols * aux, bytes_accessed=2 * (rows + cols) * aux * 2, transcendentals=0
+        functools.partial(
+            end_amplitudes, [p for _, p in all_a[:late_a]], [p for _, p in all_b[:late_b]], corner, cut * early
         ),
-        name="amplitudes",
-    )(*list_a, *list_b, ninv)
+        out_shape=shared + [jax.ShapeDtypeStruct((aux,), jnp.float32)] * 4 + blocks(early),
+        input_output_aliases={count + k: k for k in range(4)},
+        compiler_params=pltpu.CompilerParams(vmem_limit_bytes=24 * MIB),
+        cost_estimate=estimate(rows * cols),
+        name="amplitudes_late",
+    )(*[v for v, _ in all_a[:late_a] + all_b[:late_b]], ninv, *begun)
     t, tt, acat, bcat, scale_a, scale_b, unit_a, unit_b = opening[:8]
 
     def contracted(left, right, start, names, name):

time: 93.2 us -> 92.1 us (0.988)
  waiting for transfers between devices: 49.8 us -> 47.5 us
    ppermute x25, waiting for transfers between devices: 49.8 us -> 47.5 us  [exchange(): lax.ppermute(value, ('grp', 'slab'), [(d, d ^ 1 << bit) for d in range(de...]
    pallas_call x1 -> x2, Pallas kernels: 4.87 us -> 5.71 us  [the longest x1 3.28 us: body(): pl.pallas_call(functools.partial(end_amplitudes, [p for _, p in all_a[:la...]
  transfers between devices with their start and end apart: 25 -> 25, of which waited for: 10 -> 10; matrix products, arithmetic and copies ran while one was open for 4% -> 4% of each run, Pallas kernels for 6% -> 9%
where the time goes in v7:
time: 92.1 us; the launch traced here: 91.9 us
  waiting for transfers between devices  47.5 us (52%)
  starting transfers between devices  25.4 us (28%)
  Pallas kernels  11.4 us (12%)
  other arithmetic  3.74 us (4%)
  local copies, waits for them, and re-layouts  3.03 us (3%)
    ppermute x25, waiting for transfers between devices, exchange(): lax.ppermute(value, ('grp', 'slab'), [(d, d ^ 1 << bit) for d in range(de...  47.5 us
    ppermute x25, starting transfers between devices, exchange(): lax.ppermute(value, ('grp', 'slab'), [(d, d ^ 1 << bit) for d in range(de...  25.4 us
    pallas_call x2, Pallas kernels, contracted(): pl.pallas_call(functools.partial(rows_out, start * width, cut * len(names...  4.8 us
    pallas_call x1, Pallas kernels, body(): pl.pallas_call(functools.partial(end_amplitudes, [p for _, p in all_a[:la...  3.28 us
    pallas_call x1, Pallas kernels, body(): pl.pallas_call(functools.partial(begin_amplitudes, [p for _, p in all_a[l...  2.43 us
    reshape x2, other arithmetic, whole(): return parts[0].reshape(orbital_alpha.shape)  2.41 us
  transfers between devices with their start and end apart: 25, of which 10 were waited for; matrix products, arithmetic and copies ran while one was open for 4% of the time, Pallas kernels for 9%

profile of v7, /device:TPU:0, one launch (start us, length us, event | category | flops | bytes accessed | tf_op | source)
XLA Modules:
  0.0 91.9 jit_solution(10812861664583506902)
XLA Ops:
  0.6 4.1 %collective-permute-start.2 = (bf16[96,2560]{1,0:T(8,128)(2,1)}, bf16[96,2560]{1,0:T(8,128)(2,1)S(1)}, u32[]{:S(2)}, u32[]{:S(2)}) collective-permute-start(bf16[96,2560]{1,0:T(8,128)(2,1)} %bitcast.7), channel_id=1, source_target_pairs={{0,8},{1,9},{2,10},{3,11},{4,12},{5,13},{6,14},{7,15},{8,0},{9,1},... | collective-permute-start | bytes 1474568 | tf_op jit(solution)/shard_map/ppermute | solution.py:24
  4.8 1.5 %collective-permute-start.1 = (bf16[96,2560]{1,0:T(8,128)(2,1)}, bf16[96,2560]{1,0:T(8,128)(2,1)S(1)}, u32[]{:S(2)}, u32[]{:S(2)}) collective-permute-start(bf16[96,2560]{1,0:T(8,128)(2,1)} %bitcast.8), channel_id=1, source_target_pairs={{0,2},{1,3},{2,0},{3,1},{4,6},{5,7},{6,4},{7,5},{8,10},{9,11},{10,... | collective-permute-start | bytes 1474568 | tf_op jit(solution)/shard_map/ppermute | solution.py:24
  6.2 1.6 %collective-permute-start.3 = (bf16[96,2560]{1,0:T(8,128)(2,1)}, bf16[96,2560]{1,0:T(8,128)(2,1)S(1)}, u32[]{:S(2)}, u32[]{:S(2)}) collective-permute-start(bf16[96,2560]{1,0:T(8,128)(2,1)} %bitcast.10), channel_id=1, source_target_pairs={{0,4},{1,5},{2,6},{3,7},{4,0},{5,1},{6,2},{7,3},{8,12},{9,13},{10,... | collective-permute-start | bytes 1474568 | tf_op jit(solution)/shard_map/ppermute | solution.py:24
  7.8 1.5 %collective-permute-start = (bf16[96,2560]{1,0:T(8,128)(2,1)}, bf16[96,2560]{1,0:T(8,128)(2,1)}, u32[]{:S(2)}, u32[]{:S(2)}) collective-permute-start(bf16[96,2560]{1,0:T(8,128)(2,1)} %bitcast.11), channel_id=1, source_target_pairs={{0,16},{1,17},{2,18},{3,19},{4,20},{5,21},{6,22},{7,23},{8,24},{9,... | collective-permute-start | bytes 1474568 | tf_op jit(solution)/shard_map/ppermute | solution.py:24
  9.3 0.8 reshape.35.vb_ref
  10.1 1.0 %broadcast_in_dim.3.va_ref = f32[1536,1]{1,0:T(8,128)S(1)} reshape(f32[1536]{0:T(1024)} %param.10) | data formatting | bytes 12288 | tf_op jit(solution)/shard_map/broadcast_in_dim | solution.py:162
  11.1 0.6 copy-done.2
  11.7 0.7 copy-done.3
  12.4 0.8 energies.1.refs_9_.refs_3_
  13.2 13.6 %collective-permute-done.2.refs_1_ = bf16[96,2560]{1,0:T(8,128)(2,1)S(1)} collective-permute-done((bf16[96,2560]{1,0:T(8,128)(2,1)}, bf16[96,2560]{1,0:T(8,128)(2,1)S(1)}, u32[]{:S(2)}, u32[]{:S(2)}) %collective-permute-start.2) | collective-permute-done | bytes 491552 | tf_op jit(solution)/shard_map/ppermute | solution.py:24
  26.8 1.4 %collective-permute-done.3.refs_6_ = bf16[96,2560]{1,0:T(8,128)(2,1)S(1)} collective-permute-done((bf16[96,2560]{1,0:T(8,128)(2,1)}, bf16[96,2560]{1,0:T(8,128)(2,1)S(1)}, u32[]{:S(2)}, u32[]{:S(2)}) %collective-permute-start.3) | collective-permute-done | bytes 491552 | tf_op jit(solution)/shard_map/ppermute | solution.py:24
  28.2 1.6 %collective-permute-start.5 = (bf16[96,2560]{1,0:T(8,128)(2,1)S(1)}, bf16[96,2560]{1,0:T(8,128)(2,1)S(1)}, u32[]{:S(2)}, u32[]{:S(2)}) collective-permute-start(bf16[96,2560]{1,0:T(8,128)(2,1)S(1)} %collective-permute-done.3.refs_6_), channel_id=1, source_target_pairs={{0,16},{1,17},{2,18},{3,19},{4,20},{5,21},{6,22},{7,23},{8,24},{9,... | collective-permute-start | bytes 1474568 | tf_op jit(solution)/shard_map/ppermute | solution.py:24
  30.9 8.4 %collective-permute-done.5.refs_2_ = bf16[96,2560]{1,0:T(8,128)(2,1)S(1)} collective-permute-done((bf16[96,2560]{1,0:T(8,128)(2,1)S(1)}, bf16[96,2560]{1,0:T(8,128)(2,1)S(1)}, u32[]{:S(2)}, u32[]{:S(2)}) %collective-permute-start.5) | collective-permute-done | bytes 491552 | tf_op jit(solution)/shard_map/ppermute | solution.py:24
  39.3 2.4 %amplitudes_early.1 = (bf16[384,768]{1,0:T(8,128)(2,1)S(1)}, bf16[768,384]{1,0:T(8,128)(2,1)S(1)}, bf16[384,2560]{1,0:T(8,128)(2,1)S(1)}, bf16[768,2560]{1,0:T(8,128)(2,1)S(1)}, f32[8,128]{1,0:T(8,128)S(1)}) custom-call(bf16[96,2560]{1,0:T(8,128)(2,1)S(1)} %collective-permute-done.1.refs_0_, bf16[96,2560]{1,0:T(8,128)(2,1)S(1)} %collective-permute-done.2.refs_1_, ...), custom_call_target="tpu_custom_call" | custom-call | flops 671088640 | bytes 11796480 | tf_op jit(solution)/shard_map/amplitudes_early/pallas_call | solution.py:196
  41.7 2.2 %collective-permute-done.4.refs_0_ = bf16[96,2560]{1,0:T(8,128)(2,1)S(1)} collective-permute-done((bf16[96,2560]{1,0:T(8,128)(2,1)S(1)}, bf16[96,2560]{1,0:T(8,128)(2,1)S(1)}, u32[]{:S(2)}, u32[]{:S(2)}) %collective-permute-start.4) | collective-permute-done | bytes 491552 | tf_op jit(solution)/shard_map/ppermute | solution.py:24
  44.0 3.3 %amplitudes_late.1 = (bf16[384,768]{1,0:T(8,128)(2,1)S(1)}, bf16[768,384]{1,0:T(8,128)(2,1)S(1)}, bf16[384,2560]{1,0:T(8,128)(2,1)S(1)}, bf16[768,2560]{1,0:T(8,...) custom-call(bf16[96,2560]{1,0:T(8,128)(2,1)S(1)} %collective-permute, ...), custom_call_target="tpu_custom_call", output_to_operand_aliasing={{0}: (4, {}), {1}: (5, {}), {2}: (6, {}), {3}: (7, {})} | custom-call | flops 1509949440 | bytes 11796480 | tf_op jit(solution)/shard_map/amplitudes_late/pallas_call | solution.py:204
  47.8 2.4 %alpha.1 = (f32[96,2560]{1,0:T(8,128)S(1)}, f32[96,2560]{1,0:T(8,128)S(1)}, f32[96,2560]{1,0:T(8,128)S(1)}, f32[96,2560]{1,0:T(8,128)S(1)}) custom-call(bf16[384,768]{1,0:T(8,128)(2,1)S(1)} %get-tuple-element.61.left, bf16[768,2560]{1,0:T(8,128)(2,1)S(1)} %get-tuple-element.62.right), custom_call_target="tpu_custom_call" | custom-call | flops 1509949440 | bytes 7864320 | tf_op jit(solution)/shard_map/alpha/pallas_call | solution.py:217
  51.7 1.4 %collective-permute-start.12 = (f16[96,2560]{1,0:T(8,128)(2,1)S(1)}, f16[96,2560]{1,0:T(8,128)(2,1)S(1)}, u32[]{:S(2)}, u32[]{:S(2)}) collective-permute-start(f16[96,2560]{1,0:T(8,128)(2,1)S(1)} %get-tuple-element.72), channel_id=1, source_target_pairs={{0,2},{1,3},{2,0},{3,1},{4,6},{5,7},{6,4},{7,5},{8,10},{9,11},{10,... | collective-permute-start | bytes 1474568 | tf_op jit(solution)/shard_map/ppermute | solution.py:24
  53.2 1.6 %collective-permute-start.13 = (f16[96,2560]{1,0:T(8,128)(2,1)S(1)}, f16[96,2560]{1,0:T(8,128)(2,1)S(1)}, u32[]{:S(2)}, u32[]{:S(2)}) collective-permute-start(f16[96,2560]{1,0:T(8,128)(2,1)S(1)} %multiply_convert_fusion.7), channel_id=1, source_target_pairs={{0,16},{1,17},{2,18},{3,19},{4,20},{5,21},{6,22},{7,23},{8,24},{9,... | collective-permute-start | bytes 1474568 | tf_op jit(solution)/shard_map/ppermute | solution.py:24
  54.7 2.4 %beta.1 = (f32[96,2560]{1,0:T(8,128)S(1)}, f32[96,2560]{1,0:T(8,128)S(1)}, f32[96,2560]{1,0:T(8,128)S(1)}, f32[96,2560]{1,0:T(8,128)S(1)}, f32[96,2560]{1,0:T(8,128)S(1)}, /*index=5*/f32[96,2560]{1,0:T(8,128)S(1)}) custom-call(bf16[768,384]{1,0:T(8,128)(2,1)S(1)} %get-tuple-element.81.left, bf16[384,2560]{1,0:T(8,128)(2,1)S(1)} %get-tuple-element.82.right), custom_call_target="tpu_custom_call" | custom-call | flops 1132462080 | bytes 7864320 | tf_op jit(solution)/shard_map/beta/pallas_call | solution.py:217
  57.1 0.7 collective-permute-start.15
  57.9 2.4 %collective-permute-start.17 = (f32[2560]{0:T(1024)S(1)}, f32[2560]{0:T(1024)S(1)}, u32[]{:S(2)}, u32[]{:S(2)}) collective-permute-start(f32[2560]{0:T(1024)S(1)} %get-tuple-element.97), channel_id=1, source_target_pairs={{0,4},{1,5},{2,6},{3,7},{4,0},{5,1},{6,2},{7,3},{8,12},{9,13},{10,... | collective-permute-start | bytes 30728 | tf_op jit(solution)/shard_map/ppermute | solution.py:24
  60.6 1.2 %collective-permute-done.15 = f32[2560]{0:T(1024)S(1)} collective-permute-done((f32[2560]{0:T(1024)S(1)}, f32[2560]{0:T(1024)S(1)}, u32[]{:S(2)}, u32[]{:S(2)}) %collective-permute-start.15) | collective-permute-done | bytes 10272 | tf_op jit(solution)/shard_map/ppermute | solution.py:24
  62.0 2.5 %collective-permute-done.12 = f16[96,2560]{1,0:T(8,128)(2,1)S(1)} collective-permute-done((f16[96,2560]{1,0:T(8,128)(2,1)S(1)}, f16[96,2560]{1,0:T(8,128)(2,1)S(1)}, u32[]{:S(2)}, u32[]{:S(2)}) %collective-permute-start.12) | collective-permute-done | bytes 491552 | tf_op jit(solution)/shard_map/ppermute | solution.py:24
  64.5 1.0 %collective-permute-done.13 = f16[96,2560]{1,0:T(8,128)(2,1)S(1)} collective-permute-done((f16[96,2560]{1,0:T(8,128)(2,1)S(1)}, f16[96,2560]{1,0:T(8,128)(2,1)S(1)}, u32[]{:S(2)}, u32[]{:S(2)}) %collective-permute-start.13) | collective-permute-done | bytes 491552 | tf_op jit(solution)/shard_map/ppermute | solution.py:24
  65.7 0.9 collective-permute-start.19
  67.2 3.3 %collective-permute-start.21 = (f16[96,2560]{1,0:T(8,128)(2,1)S(1)}, f16[96,2560]{1,0:T(8,128)(2,1)S(1)}, u32[]{:S(2)}, u32[]{:S(2)}) collective-permute-start(f16[96,2560]{1,0:T(8,128)(2,1)S(1)} %get-tuple-element.106), channel_id=1, source_target_pairs={{0,4},{1,5},{2,6},{3,7},{4,0},{5,1},{6,2},{7,3},{8,12},{9,13},{10,... | collective-permute-start | bytes 1474568 | tf_op jit(solution)/shard_map/ppermute | solution.py:24
  70.5 1.4 %collective-permute-start.18 = (f16[96,2560]{1,0:T(8,128)(2,1)S(1)}, f16[96,2560]{1,0:T(8,128)(2,1)S(1)}, u32[]{:S(2)}, u32[]{:S(2)}) collective-permute-start(f16[96,2560]{1,0:T(8,128)(2,1)S(1)} %get-tuple-element.77), channel_id=1, source_target_pairs={{0,2},{1,3},{2,0},{3,1},{4,6},{5,7},{6,4},{7,5},{8,10},{9,11},{10,... | collective-permute-start | bytes 1474568 | tf_op jit(solution)/shard_map/ppermute | solution.py:24
  72.5 16.3 %collective-permute-done.19 = f16[96,2560]{1,0:T(8,128)(2,1)S(1)} collective-permute-done((f16[96,2560]{1,0:T(8,128)(2,1)S(1)}, f16[96,2560]{1,0:T(8,128)(2,1)S(1)}, u32[]{:S(2)}, u32[]{:S(2)}) %collective-permute-start.19) | collective-permute-done | bytes 491552 | tf_op jit(solution)/shard_map/ppermute | solution.py:24
  88.8 0.7 collective-permute-done.21
  89.4 1.2 %add_bitcast_fusion.1 = f32[1,96,2560]{2,1,0:T(8,128)} fusion(f16[96,2560]{1,0:T(8,128)(2,1)S(1)} %collective-permute-done.19, f32[96,2560]{1,0:T(8,128)S(1)} %get-tuple-element.63, f16[96,2560]{1,0:T(8,128)(2,1)S(1)} %collective-permute-done.18, f32[2560]{0:T(1024)S(1)} %collective-permute-done.15, f32[2560]{0:T(1024)S(1)} %collective-permute-done.14), kind=kLoop, calls=%fused_computation.4 | loop fusion | flops 1474560 | bytes 2969600 | tf_op jit(solution)/shard_map/reshape | solution.py:303
  90.6 1.2 %add_bitcast_fusion = f32[1,96,2560]{2,1,0:T(8,128)} fusion(f16[96,2560]{1,0:T(8,128)(2,1)S(1)} %collective-permute-done.21, f16[96,2560]{1,0:T(8,128)(2,1)S(1)} %collective-permute-done.24, f32[96,2560]{1,0:T(8,128)S(1)} %get-tuple-element.90, f16[96,2560]{1,0:T(8,128)(2,1)S(1)} %collective-permute-done.22, f32[2560]{0:T(1024)S(1)} %collective-permute-done.17, ...), kind=kLoop, calls=%fused_computation | loop fusion | flops 2211840 | bytes 3471360 | tf_op jit(solution)/shard_map/reshape | solution.py:303
  (43 shorter events, 4.9 us)
Async XLA Ops:
  0.6 38.6 %copy-start = (bf16[1,96,2560]{2,1,0:T(8,128)(2,1)S(1)}, bf16[1,96,2560]{2,1,0:T(8,128)(2,1)}, u32[]{:S(2)}) copy-start(bf16[1,96,2560]{2,1,0:T(8,128)(2,1)} %param.6) | copy-start | bytes 1474564
  0.6 29.2 %copy-start.1 = (bf16[1,96,2560]{2,1,0:T(8,128)(2,1)S(1)}, bf16[1,96,2560]{2,1,0:T(8,128)(2,1)}, u32[]{:S(2)}) copy-start(bf16[1,96,2560]{2,1,0:T(8,128)(2,1)} %param.7) | copy-start | bytes 1474564
  0.6 26.2 %collective-permute-start.2 = (bf16[96,2560]{1,0:T(8,128)(2,1)}, bf16[96,2560]{1,0:T(8,128)(2,1)S(1)}, u32[]{:S(2)}, u32[]{:S(2)}) collective-permute-start(bf16[96,2560]{1,0:T(8,128)(2,1)} %bitcast.7), channel_id=1, source_target_pairs={{0,8},{1,9},{2,10},{3,11},{4,12},{5,13},{6,14},{7,15},{8,0},{9,1},... | collective-permute-start | bytes 1474568 | tf_op jit(solution)/shard_map/ppermute | solution.py:24
  4.8 22.1 %collective-permute-start.1 = (bf16[96,2560]{1,0:T(8,128)(2,1)}, bf16[96,2560]{1,0:T(8,128)(2,1)S(1)}, u32[]{:S(2)}, u32[]{:S(2)}) collective-permute-start(bf16[96,2560]{1,0:T(8,128)(2,1)} %bitcast.8), channel_id=1, source_target_pairs={{0,2},{1,3},{2,0},{3,1},{4,6},{5,7},{6,4},{7,5},{8,10},{9,11},{10,... | collective-permute-start | bytes 1474568 | tf_op jit(solution)/shard_map/ppermute | solution.py:24
  6.2 22.0 %collective-permute-start.3 = (bf16[96,2560]{1,0:T(8,128)(2,1)}, bf16[96,2560]{1,0:T(8,128)(2,1)S(1)}, u32[]{:S(2)}, u32[]{:S(2)}) collective-permute-start(bf16[96,2560]{1,0:T(8,128)(2,1)} %bitcast.10), channel_id=1, source_target_pairs={{0,4},{1,5},{2,6},{3,7},{4,0},{5,1},{6,2},{7,3},{8,12},{9,13},{10,... | collective-permute-start | bytes 1474568 | tf_op jit(solution)/shard_map/ppermute | solution.py:24
  7.8 20.4 %collective-permute-start = (bf16[96,2560]{1,0:T(8,128)(2,1)}, bf16[96,2560]{1,0:T(8,128)(2,1)}, u32[]{:S(2)}, u32[]{:S(2)}) collective-permute-start(bf16[96,2560]{1,0:T(8,128)(2,1)} %bitcast.11), channel_id=1, source_target_pairs={{0,16},{1,17},{2,18},{3,19},{4,20},{5,21},{6,22},{7,23},{8,24},{9,... | collective-permute-start | bytes 1474568 | tf_op jit(solution)/shard_map/ppermute | solution.py:24
  11.1 0.7 copy-start.2
  11.7 0.7 copy-start.3
  28.2 11.0 %collective-permute-start.5 = (bf16[96,2560]{1,0:T(8,128)(2,1)S(1)}, bf16[96,2560]{1,0:T(8,128)(2,1)S(1)}, u32[]{:S(2)}, u32[]{:S(2)}) collective-permute-start(bf16[96,2560]{1,0:T(8,128)(2,1)S(1)} %collective-permute-done.3.refs_6_), channel_id=1, source_target_pairs={{0,16},{1,17},{2,18},{3,19},{4,20},{5,21},{6,22},{7,23},{8,24},{9,... | collective-permute-start | bytes 1474568 | tf_op jit(solution)/shard_map/ppermute | solution.py:24
  29.8 9.5 %collective-permute-start.7 = (bf16[96,2560]{1,0:T(8,128)(2,1)}, bf16[96,2560]{1,0:T(8,128)(2,1)S(1)}, u32[]{:S(2)}, u32[]{:S(2)}) collective-permute-start(bf16[96,2560]{1,0:T(8,128)(2,1)} %collective-permute-done.refs_4_), channel_id=1, source_target_pairs={{0,1},{1,0},{2,3},{3,2},{4,5},{5,4},{6,7},{7,6},{8,9},{9,8},{10,11... | collective-permute-start | bytes 1474568 | tf_op jit(solution)/shard_map/ppermute | solution.py:24
  29.8 9.5 %collective-permute-start.9 = (bf16[96,2560]{1,0:T(8,128)(2,1)S(1)}, bf16[96,2560]{1,0:T(8,128)(2,1)S(1)}, u32[]{:S(2)}, u32[]{:S(2)}) collective-permute-start(bf16[96,2560]{1,0:T(8,128)(2,1)S(1)} %bitcast.12), channel_id=1, source_target_pairs={{0,1},{1,0},{2,3},{3,2},{4,5},{5,4},{6,7},{7,6},{8,9},{9,8},{10,11... | collective-permute-start | bytes 1474568 | tf_op jit(solution)/shard_map/ppermute | solution.py:24
  30.3 8.9 %collective-permute-start.8 = (bf16[96,2560]{1,0:T(8,128)(2,1)S(1)}, bf16[96,2560]{1,0:T(8,128)(2,1)S(1)}, u32[]{:S(2)}, u32[]{:S(2)}) collective-permute-start(bf16[96,2560]{1,0:T(8,128)(2,1)S(1)} %collective-permute-done.3.refs_6_), channel_id=1, source_target_pairs={{0,1},{1,0},{2,3},{3,2},{4,5},{5,4},{6,7},{7,6},{8,9},{9,8},{10,11... | collective-permute-start | bytes 1474568 | tf_op jit(solution)/shard_map/ppermute | solution.py:24
  30.3 13.6 %collective-permute-start.4 = (bf16[96,2560]{1,0:T(8,128)(2,1)S(1)}, bf16[96,2560]{1,0:T(8,128)(2,1)S(1)}, u32[]{:S(2)}, u32[]{:S(2)}) collective-permute-start(bf16[96,2560]{1,0:T(8,128)(2,1)S(1)} %collective-permute-done.2.refs_1_), channel_id=1, source_target_pairs={{0,2},{1,3},{2,0},{3,1},{4,6},{5,7},{6,4},{7,5},{8,10},{9,11},{10,... | collective-permute-start | bytes 1474568 | tf_op jit(solution)/shard_map/ppermute | solution.py:24
  39.2 4.7 %collective-permute-start.6 = (bf16[96,2560]{1,0:T(8,128)(2,1)S(1)}, bf16[96,2560]{1,0:T(8,128)(2,1)S(1)}, u32[]{:S(2)}, u32[]{:S(2)}) collective-permute-start(bf16[96,2560]{1,0:T(8,128)(2,1)S(1)} %collective-permute-done.5.refs_2_), channel_id=1, source_target_pairs={{0,1},{1,0},{2,3},{3,2},{4,5},{5,4},{6,7},{7,6},{8,9},{9,8},{10,11... | collective-permute-start | bytes 1474568 | tf_op jit(solution)/shard_map/ppermute | solution.py:24
  47.2 3.2 %collective-permute-start.11 = (f32[2560]{0:T(1024)S(1)}, f32[2560]{0:T(1024)S(1)}, u32[]{:S(2)}, u32[]{:S(2)}) collective-permute-start(f32[2560]{0:T(1024)S(1)} %get-tuple-element.68), channel_id=1, source_target_pairs={{0,1},{1,0},{2,3},{3,2},{4,5},{5,4},{6,7},{7,6},{8,9},{9,8},{10,11... | collective-permute-start | bytes 30728 | tf_op jit(solution)/shard_map/ppermute | solution.py:24
  47.3 3.1 %collective-permute-start.10 = (f32[96,2560]{1,0:T(8,128)S(1)}, f32[96,2560]{1,0:T(8,128)S(1)}, u32[]{:S(2)}, u32[]{:S(2)}) collective-permute-start(f32[96,2560]{1,0:T(8,128)S(1)} %get-tuple-element.67), channel_id=1, source_target_pairs={{0,1},{1,0},{2,3},{3,2},{4,5},{5,4},{6,7},{7,6},{8,9},{9,8},{10,11... | collective-permute-start | bytes 2949128 | tf_op jit(solution)/shard_map/ppermute | solution.py:24
  50.6 6.5 %collective-permute-start.14 = (f32[2560]{0:T(1024)S(1)}, f32[2560]{0:T(1024)S(1)}, u32[]{:S(2)}, u32[]{:S(2)}) collective-permute-start(f32[2560]{0:T(1024)S(1)} %get-tuple-element.75), channel_id=1, source_target_pairs={{0,2},{1,3},{2,0},{3,1},{4,6},{5,7},{6,4},{7,5},{8,10},{9,11},{10,... | collective-permute-start | bytes 30728 | tf_op jit(solution)/shard_map/ppermute | solution.py:24
  51.2 6.7 %collective-permute-start.16 = (f32[2560]{0:T(1024)S(1)}, f32[2560]{0:T(1024)S(1)}, u32[]{:S(2)}, u32[]{:S(2)}) collective-permute-start(f32[2560]{0:T(1024)S(1)} %get-tuple-element.76), channel_id=1, source_target_pairs={{0,16},{1,17},{2,18},{3,19},{4,20},{5,21},{6,22},{7,23},{8,24},{9,... | collective-permute-start | bytes 30728 | tf_op jit(solution)/shard_map/ppermute | solution.py:24
  51.7 12.8 %collective-permute-start.12 = (f16[96,2560]{1,0:T(8,128)(2,1)S(1)}, f16[96,2560]{1,0:T(8,128)(2,1)S(1)}, u32[]{:S(2)}, u32[]{:S(2)}) collective-permute-start(f16[96,2560]{1,0:T(8,128)(2,1)S(1)} %get-tuple-element.72), channel_id=1, source_target_pairs={{0,2},{1,3},{2,0},{3,1},{4,6},{5,7},{6,4},{7,5},{8,10},{9,11},{10,... | collective-permute-start | bytes 1474568 | tf_op jit(solution)/shard_map/ppermute | solution.py:24
  53.2 12.4 %collective-permute-start.13 = (f16[96,2560]{1,0:T(8,128)(2,1)S(1)}, f16[96,2560]{1,0:T(8,128)(2,1)S(1)}, u32[]{:S(2)}, u32[]{:S(2)}) collective-permute-start(f16[96,2560]{1,0:T(8,128)(2,1)S(1)} %multiply_convert_fusion.7), channel_id=1, source_target_pairs={{0,16},{1,17},{2,18},{3,19},{4,20},{5,21},{6,22},{7,23},{8,24},{9,... | collective-permute-start | bytes 1474568 | tf_op jit(solution)/shard_map/ppermute | solution.py:24
  57.1 4.7 %collective-permute-start.15 = (f32[2560]{0:T(1024)S(1)}, f32[2560]{0:T(1024)S(1)}, u32[]{:S(2)}, u32[]{:S(2)}) collective-permute-start(f32[2560]{0:T(1024)S(1)} %get-tuple-element.99), channel_id=1, source_target_pairs={{0,8},{1,9},{2,10},{3,11},{4,12},{5,13},{6,14},{7,15},{8,0},{9,1},... | collective-permute-start | bytes 30728 | tf_op jit(solution)/shard_map/ppermute | solution.py:24
  57.9 4.1 %collective-permute-start.17 = (f32[2560]{0:T(1024)S(1)}, f32[2560]{0:T(1024)S(1)}, u32[]{:S(2)}, u32[]{:S(2)}) collective-permute-start(f32[2560]{0:T(1024)S(1)} %get-tuple-element.97), channel_id=1, source_target_pairs={{0,4},{1,5},{2,6},{3,7},{4,0},{5,1},{6,2},{7,3},{8,12},{9,13},{10,... | collective-permute-start | bytes 30728 | tf_op jit(solution)/shard_map/ppermute | solution.py:24
  60.6 6.1 %collective-permute-start.23 = (f16[96,2560]{1,0:T(8,128)(2,1)S(1)}, f16[96,2560]{1,0:T(8,128)(2,1)S(1)}, u32[]{:S(2)}, u32[]{:S(2)}) collective-permute-start(f16[96,2560]{1,0:T(8,128)(2,1)S(1)} %get-tuple-element.103), channel_id=1, source_target_pairs={{0,1},{1,0},{2,3},{3,2},{4,5},{5,4},{6,7},{7,6},{8,9},{9,8},{10,11... | collective-permute-start | bytes 1474568 | tf_op jit(solution)/shard_map/ppermute | solution.py:24
  61.8 4.8 %collective-permute-start.20 = (f16[96,2560]{1,0:T(8,128)(2,1)S(1)}, f16[96,2560]{1,0:T(8,128)(2,1)S(1)}, u32[]{:S(2)}, u32[]{:S(2)}) collective-permute-start(f16[96,2560]{1,0:T(8,128)(2,1)S(1)} %get-tuple-element.104), channel_id=1, source_target_pairs={{0,1},{1,0},{2,3},{3,2},{4,5},{5,4},{6,7},{7,6},{8,9},{9,8},{10,11... | collective-permute-start | bytes 1474568 | tf_op jit(solution)/shard_map/ppermute | solution.py:24
  65.7 23.0 %collective-permute-start.19 = (f16[96,2560]{1,0:T(8,128)(2,1)S(1)}, f16[96,2560]{1,0:T(8,128)(2,1)S(1)}, u32[]{:S(2)}, u32[]{:S(2)}) collective-permute-start(f16[96,2560]{1,0:T(8,128)(2,1)S(1)} %multiply_convert_fusion.5), channel_id=1, source_target_pairs={{0,8},{1,9},{2,10},{3,11},{4,12},{5,13},{6,14},{7,15},{8,0},{9,1},... | collective-permute-start | bytes 1474568 | tf_op jit(solution)/shard_map/ppermute | solution.py:24
  67.2 22.3 %collective-permute-start.21 = (f16[96,2560]{1,0:T(8,128)(2,1)S(1)}, f16[96,2560]{1,0:T(8,128)(2,1)S(1)}, u32[]{:S(2)}, u32[]{:S(2)}) collective-permute-start(f16[96,2560]{1,0:T(8,128)(2,1)S(1)} %get-tuple-element.106), channel_id=1, source_target_pairs={{0,4},{1,5},{2,6},{3,7},{4,0},{5,1},{6,2},{7,3},{8,12},{9,13},{10,... | collective-permute-start | bytes 1474568 | tf_op jit(solution)/shard_map/ppermute | solution.py:24
  70.5 18.9 %collective-permute-start.18 = (f16[96,2560]{1,0:T(8,128)(2,1)S(1)}, f16[96,2560]{1,0:T(8,128)(2,1)S(1)}, u32[]{:S(2)}, u32[]{:S(2)}) collective-permute-start(f16[96,2560]{1,0:T(8,128)(2,1)S(1)} %get-tuple-element.77), channel_id=1, source_target_pairs={{0,2},{1,3},{2,0},{3,1},{4,6},{5,7},{6,4},{7,5},{8,10},{9,11},{10,... | collective-permute-start | bytes 1474568 | tf_op jit(solution)/shard_map/ppermute | solution.py:24
  72.0 18.7 %collective-permute-start.22 = (f16[96,2560]{1,0:T(8,128)(2,1)S(1)}, f16[96,2560]{1,0:T(8,128)(2,1)S(1)}, u32[]{:S(2)}, u32[]{:S(2)}) collective-permute-start(f16[96,2560]{1,0:T(8,128)(2,1)S(1)} %get-tuple-element.102), channel_id=1, source_target_pairs={{0,1},{1,0},{2,3},{3,2},{4,5},{5,4},{6,7},{7,6},{8,9},{9,8},{10,11... | collective-permute-start | bytes 1474568 | tf_op jit(solution)/shard_map/ppermute | solution.py:24
  72.0 18.7 %collective-permute-start.24 = (f16[96,2560]{1,0:T(8,128)(2,1)S(1)}, f16[96,2560]{1,0:T(8,128)(2,1)S(1)}, u32[]{:S(2)}, u32[]{:S(2)}) collective-permute-start(f16[96,2560]{1,0:T(8,128)(2,1)S(1)} %get-tuple-element.105), channel_id=1, source_target_pairs={{0,16},{1,17},{2,18},{3,19},{4,20},{5,21},{6,22},{7,23},{8,24},{9,... | collective-permute-start | bytes 1474568 | tf_op jit(solution)/shard_map/ppermute | solution.py:24

commit v8 on v7

--- a/solution.py
+++ b/solution.py
@@ -85,7 +85,7 @@
     tops[...] = jnp.where(row == 0, top, jnp.where(row == 1, top_a, top_b))
 
 
-def end_amplitudes(places_a, places_b, corner, spans, *refs):
+def end_amplitudes(places_a, places_b, corner, spans_a, spans_b, *refs):
     n_a, n_b = len(places_a), len(places_b)
     a_refs, b_refs, ninv = refs[:n_a], refs[n_a:n_a + n_b], refs[n_a + n_b]
     tops = refs[n_a + n_b + 5]
@@ -101,7 +101,8 @@
         value = top * largest_right * (count / 32768.0) + 1e-36
         unit[...] = jnp.broadcast_to(value[0, 0], unit.shape)
         scale[...] = jnp.broadcast_to((1.0 / value)[0, 0], scale.shape)
-    rows_out(0, spans, tt, acat, *outs)
+    rows_out(0, spans_b, tt, acat, *outs[:len(spans_b)])
+    rows_out(0, spans_a, t_ref, bcat, *outs[len(spans_b):])
 
 
 def rows_out(start, spans, left, right, *outs):
@@ -171,7 +172,7 @@
     def pairs(names, outs):
         return {m: [out] for m, out in zip(names, outs)}
 
-    early = max(n_b // 4, 2)
+    early_a, early_b = max(n_a // 4, 1), max(n_b // 4, 2)
 
     def late_first(names, first):
         late = [m for m in names if m & (1 << first) and m & ~(1 << first) & ~1]
@@ -203,9 +204,10 @@
     count = late_a + late_b + 1
     opening = pl.pallas_call(
         functools.partial(
-            end_amplitudes, [p for _, p in all_a[:late_a]], [p for _, p in all_b[:late_b]], corner, cut * early
+            end_amplitudes, [p for _, p in all_a[:late_a]], [p for _, p in all_b[:late_b]], corner,
+            cut * early_a, cut * early_b,
         ),
-        out_shape=shared + [jax.ShapeDtypeStruct((aux,), jnp.float32)] * 4 + blocks(early),
+        out_shape=shared + [jax.ShapeDtypeStruct((aux,), jnp.float32)] * 4 + blocks(early_a + early_b),
         input_output_aliases={count + k: k for k in range(4)},
         compiler_params=pltpu.CompilerParams(vmem_limit_bytes=24 * MIB),
         cost_estimate=estimate(rows * cols),
@@ -240,16 +242,11 @@
         ahead = [m for m in every if m & after]
         return ahead, [m for m in every if m not in ahead]
 
-    def chips_sum(found):
-        return {
-            m: [v + exchange(w, 0, devices) for v, w in zip(vs, found[m | 1])] for m, vs in found.items() if not m & 1
-        }
-
     bits_a, bits_b = alpha_bits[::-1], [b for b in beta_bits[::-1] if b]
     names_b = [m for m in masks_b if not m & 1]
     unit_other = exchange(unit_b, 0, devices)
 
-    def chips_sum_narrow(found):
+    def chips_sum(found):
         return {
             m: [v + wide(exchange(narrow(w, scale_b), 0, devices), unit_other) for v, w in zip(vs, found[m | 1])]
             for m, vs in found.items() if not m & 1
@@ -257,8 +254,8 @@
 
     unit_b = unit_b + unit_other
     units, scales = [unit_a, unit_b], [scale_a, 1.0 / unit_b]
-    gb = chips_sum(pairs(masks_b, opening[8:]))
-    ga = contracted(t, bcat, 0, masks_a, "alpha")
+    gb = chips_sum(pairs(masks_b, opening[8:8 + early_b]))
+    ga = pairs(masks_a, opening[8 + early_b:])
     for level in range(max(len(bits_a), len(bits_b))):
         jobs = [
             (which, parts, bits[level]) + passed_on(names, bits, level)
@@ -279,14 +276,15 @@
                     job[1][m ^ (1 << job[2])][0] += wide(v, partner[job[0]])
 
         if level == 0:
-            sent, units, tt, acat = together((made(3, before), units, tt, acat))
+            sent, units, t, tt, acat, bcat = together((made(3, before), units, t, tt, acat, bcat))
             coming = {job[0]: exchange(units[job[0]], job[2], devices) for job in jobs}
         else:
             sent = made(3, before)
         partner = coming
         got = moved(sent)
         if level == 0:
-            gb.update(chips_sum_narrow(contracted(tt, acat, early, masks_b[early:], "beta")))
+            gb.update(chips_sum(contracted(tt, acat, early_b, masks_b[early_b:], "beta")))
+            ga.update(contracted(t, bcat, early_a, masks_a[early_a:], "alpha"))
         units = [units[w] + partner[w] if w in partner else units[w] for w in range(2)]
         scales = [1.0 / unit for unit in units]
         coming = {

time: 92.1 us -> 93.3 us (1.013)
    pallas_call x1, Pallas kernels: 3.28 us -> 4.6 us  [body(): pl.pallas_call(functools.partial(end_amplitudes, [p for _, p in all_a[:la...]
  transfers between devices with their start and end apart: 25 -> 25, of which waited for: 10 -> 12; matrix products, arithmetic and copies ran while one was open for 4% -> 4% of each run, Pallas kernels for 9% -> 8%
where the time goes in v8:
time: 93.3 us; the launch traced here: 93.1 us
  waiting for transfers between devices  47.9 us (51%)
  starting transfers between devices  25.2 us (27%)
  Pallas kernels  12.3 us (13%)
  other arithmetic  3.91 us (4%)
  local copies, waits for them, and re-layouts  3.03 us (3%)
    ppermute x25, waiting for transfers between devices, exchange(): lax.ppermute(value, ('grp', 'slab'), [(d, d ^ 1 << bit) for d in range(de...  47.9 us
    ppermute x25, starting transfers between devices, exchange(): lax.ppermute(value, ('grp', 'slab'), [(d, d ^ 1 << bit) for d in range(de...  25.2 us
    pallas_call x1, Pallas kernels, body(): pl.pallas_call(functools.partial(end_amplitudes, [p for _, p in all_a[:la...  4.6 us
    pallas_call x2, Pallas kernels, contracted(): pl.pallas_call(functools.partial(rows_out, start * width, cut * len(names...  4.4 us
    reshape x2, other arithmetic, whole(): return parts[0].reshape(orbital_alpha.shape)  2.46 us
    pallas_call x1, Pallas kernels, body(): pl.pallas_call(functools.partial(begin_amplitudes, [p for _, p in all_a[l...  2.43 us
  transfers between devices with their start and end apart: 25, of which 12 were waited for; matrix products, arithmetic and copies ran while one was open for 4% of the time, Pallas kernels for 8%

profile of v8, /device:TPU:0, one launch (start us, length us, event | category | flops | bytes accessed | tf_op | source)
XLA Modules:
  0.0 93.1 jit_solution(6636201312298220211)
XLA Ops:
  0.6 4.1 %collective-permute-start.2 = (bf16[96,2560]{1,0:T(8,128)(2,1)}, bf16[96,2560]{1,0:T(8,128)(2,1)S(1)}, u32[]{:S(2)}, u32[]{:S(2)}) collective-permute-start(bf16[96,2560]{1,0:T(8,128)(2,1)} %bitcast.7), channel_id=1, source_target_pairs={{0,8},{1,9},{2,10},{3,11},{4,12},{5,13},{6,14},{7,15},{8,0},{9,1},... | collective-permute-start | bytes 1474568 | tf_op jit(solution)/shard_map/ppermute | solution.py:24
  4.8 1.5 %collective-permute-start.1 = (bf16[96,2560]{1,0:T(8,128)(2,1)}, bf16[96,2560]{1,0:T(8,128)(2,1)S(1)}, u32[]{:S(2)}, u32[]{:S(2)}) collective-permute-start(bf16[96,2560]{1,0:T(8,128)(2,1)} %bitcast.8), channel_id=1, source_target_pairs={{0,2},{1,3},{2,0},{3,1},{4,6},{5,7},{6,4},{7,5},{8,10},{9,11},{10,... | collective-permute-start | bytes 1474568 | tf_op jit(solution)/shard_map/ppermute | solution.py:24
  6.2 1.6 %collective-permute-start.3 = (bf16[96,2560]{1,0:T(8,128)(2,1)}, bf16[96,2560]{1,0:T(8,128)(2,1)S(1)}, u32[]{:S(2)}, u32[]{:S(2)}) collective-permute-start(bf16[96,2560]{1,0:T(8,128)(2,1)} %bitcast.10), channel_id=1, source_target_pairs={{0,4},{1,5},{2,6},{3,7},{4,0},{5,1},{6,2},{7,3},{8,12},{9,13},{10,... | collective-permute-start | bytes 1474568 | tf_op jit(solution)/shard_map/ppermute | solution.py:24
  7.8 1.5 %collective-permute-start = (bf16[96,2560]{1,0:T(8,128)(2,1)}, bf16[96,2560]{1,0:T(8,128)(2,1)}, u32[]{:S(2)}, u32[]{:S(2)}) collective-permute-start(bf16[96,2560]{1,0:T(8,128)(2,1)} %bitcast.11), channel_id=1, source_target_pairs={{0,16},{1,17},{2,18},{3,19},{4,20},{5,21},{6,22},{7,23},{8,24},{9,... | collective-permute-start | bytes 1474568 | tf_op jit(solution)/shard_map/ppermute | solution.py:24
  9.3 0.8 reshape.35.vb_ref
  10.1 1.0 %broadcast_in_dim.3.va_ref = f32[1536,1]{1,0:T(8,128)S(1)} reshape(f32[1536]{0:T(1024)} %param.10) | data formatting | bytes 12288 | tf_op jit(solution)/shard_map/broadcast_in_dim | solution.py:163
  11.1 0.6 copy-done.2
  11.7 0.7 copy-done.3
  12.4 0.8 energies.1.refs_9_.refs_3_
  13.2 13.6 %collective-permute-done.2.refs_1_ = bf16[96,2560]{1,0:T(8,128)(2,1)S(1)} collective-permute-done((bf16[96,2560]{1,0:T(8,128)(2,1)}, bf16[96,2560]{1,0:T(8,128)(2,1)S(1)}, u32[]{:S(2)}, u32[]{:S(2)}) %collective-permute-start.2) | collective-permute-done | bytes 491552 | tf_op jit(solution)/shard_map/ppermute | solution.py:24
  26.8 1.4 %collective-permute-done.3.refs_6_ = bf16[96,2560]{1,0:T(8,128)(2,1)S(1)} collective-permute-done((bf16[96,2560]{1,0:T(8,128)(2,1)}, bf16[96,2560]{1,0:T(8,128)(2,1)S(1)}, u32[]{:S(2)}, u32[]{:S(2)}) %collective-permute-start.3) | collective-permute-done | bytes 491552 | tf_op jit(solution)/shard_map/ppermute | solution.py:24
  28.2 1.6 %collective-permute-start.5 = (bf16[96,2560]{1,0:T(8,128)(2,1)S(1)}, bf16[96,2560]{1,0:T(8,128)(2,1)S(1)}, u32[]{:S(2)}, u32[]{:S(2)}) collective-permute-start(bf16[96,2560]{1,0:T(8,128)(2,1)S(1)} %collective-permute-done.3.refs_6_), channel_id=1, source_target_pairs={{0,16},{1,17},{2,18},{3,19},{4,20},{5,21},{6,22},{7,23},{8,24},{9,... | collective-permute-start | bytes 1474568 | tf_op jit(solution)/shard_map/ppermute | solution.py:24
  30.9 8.4 %collective-permute-done.5.refs_2_ = bf16[96,2560]{1,0:T(8,128)(2,1)S(1)} collective-permute-done((bf16[96,2560]{1,0:T(8,128)(2,1)S(1)}, bf16[96,2560]{1,0:T(8,128)(2,1)S(1)}, u32[]{:S(2)}, u32[]{:S(2)}) %collective-permute-start.5) | collective-permute-done | bytes 491552 | tf_op jit(solution)/shard_map/ppermute | solution.py:24
  39.3 2.4 %amplitudes_early.1 = (bf16[384,768]{1,0:T(8,128)(2,1)S(1)}, bf16[768,384]{1,0:T(8,128)(2,1)S(1)}, bf16[384,2560]{1,0:T(8,128)(2,1)S(1)}, bf16[768,2560]{1,0:T(8,128)(2,1)S(1)}, f32[8,128]{1,0:T(8,128)S(1)}) custom-call(bf16[96,2560]{1,0:T(8,128)(2,1)S(1)} %collective-permute-done.1.refs_0_, bf16[96,2560]{1,0:T(8,128)(2,1)S(1)} %collective-permute-done.2.refs_1_, ...), custom_call_target="tpu_custom_call" | custom-call | flops 671088640 | bytes 11796480 | tf_op jit(solution)/shard_map/amplitudes_early/pallas_call | solution.py:197
  41.7 2.2 %collective-permute-done.4.refs_0_ = bf16[96,2560]{1,0:T(8,128)(2,1)S(1)} collective-permute-done((bf16[96,2560]{1,0:T(8,128)(2,1)S(1)}, bf16[96,2560]{1,0:T(8,128)(2,1)S(1)}, u32[]{:S(2)}, u32[]{:S(2)}) %collective-permute-start.4) | collective-permute-done | bytes 491552 | tf_op jit(solution)/shard_map/ppermute | solution.py:24
  44.0 4.6 %amplitudes_late.1 = (bf16[384,768]{1,0:T(8,128)(2,1)S(1)}, bf16[768,384]{1,0:T(8,128)(2,1)S(1)}, bf16[384,2560]{1,0:T(8,128)(2,1)S(1)}, bf16[768,2560]{1,0:T(8,...) custom-call(bf16[96,2560]{1,0:T(8,128)(2,1)S(1)} %collective-permute, ...), custom_call_target="tpu_custom_call", output_to_operand_aliasing={{0}: (4, {}), {1}: (5, {}), {2}: (6, {}), {3}: (7, {})} | custom-call | flops 1509949440 | bytes 11796480 | tf_op jit(solution)/shard_map/amplitudes_late/pallas_call | solution.py:205
  49.8 1.0 %collective-permute-done.10 = f16[96,2560]{1,0:T(8,128)(2,1)S(1)} collective-permute-done((f16[96,2560]{1,0:T(8,128)(2,1)S(1)}, f16[96,2560]{1,0:T(8,128)(2,1)S(1)}, u32[]{:S(2)}, u32[]{:S(2)}) %collective-permute-start.10) | collective-permute-done | bytes 491552 | tf_op jit(solution)/shard_map/ppermute | solution.py:24
  52.1 1.4 %collective-permute-start.12 = (f16[96,2560]{1,0:T(8,128)(2,1)S(1)}, f16[96,2560]{1,0:T(8,128)(2,1)S(1)}, u32[]{:S(2)}, u32[]{:S(2)}) collective-permute-start(f16[96,2560]{1,0:T(8,128)(2,1)S(1)} %multiply_convert_fusion.9), channel_id=1, source_target_pairs={{0,2},{1,3},{2,0},{3,1},{4,6},{5,7},{6,4},{7,5},{8,10},{9,11},{10,... | collective-permute-start | bytes 1474568 | tf_op jit(solution)/shard_map/ppermute | solution.py:24
  53.6 1.6 %collective-permute-start.13 = (f16[96,2560]{1,0:T(8,128)(2,1)S(1)}, f16[96,2560]{1,0:T(8,128)(2,1)S(1)}, u32[]{:S(2)}, u32[]{:S(2)}) collective-permute-start(f16[96,2560]{1,0:T(8,128)(2,1)S(1)} %multiply_convert_fusion.7), channel_id=1, source_target_pairs={{0,16},{1,17},{2,18},{3,19},{4,20},{5,21},{6,22},{7,23},{8,24},{9,... | collective-permute-start | bytes 1474568 | tf_op jit(solution)/shard_map/ppermute | solution.py:24
  55.1 2.4 %beta.1 = (f32[96,2560]{1,0:T(8,128)S(1)}, f32[96,2560]{1,0:T(8,128)S(1)}, f32[96,2560]{1,0:T(8,128)S(1)}, f32[96,2560]{1,0:T(8,128)S(1)}, f32[96,2560]{1,0:T(8,128)S(1)}, /*index=5*/f32[96,2560]{1,0:T(8,128)S(1)}) custom-call(bf16[768,384]{1,0:T(8,128)(2,1)S(1)} %get-tuple-element.86.left, bf16[384,2560]{1,0:T(8,128)(2,1)S(1)} %get-tuple-element.87.right), custom_call_target="tpu_custom_call" | custom-call | flops 1132462080 | bytes 7864320 | tf_op jit(solution)/shard_map/beta/pallas_call | solution.py:219
  57.8 2.0 %alpha.1 = (f32[96,2560]{1,0:T(8,128)S(1)}, f32[96,2560]{1,0:T(8,128)S(1)}, f32[96,2560]{1,0:T(8,128)S(1)}) custom-call(bf16[384,768]{1,0:T(8,128)(2,1)S(1)} %get-tuple-element.74.left, bf16[768,2560]{1,0:T(8,128)(2,1)S(1)} %get-tuple-element.75.right), custom_call_target="tpu_custom_call" | custom-call | flops 1132462080 | bytes 6881280 | tf_op jit(solution)/shard_map/alpha/pallas_call | solution.py:219
  59.8 0.7 collective-permute-start.15
  60.6 2.4 %collective-permute-start.17 = (f32[2560]{0:T(1024)S(1)}, f32[2560]{0:T(1024)S(1)}, u32[]{:S(2)}, u32[]{:S(2)}) collective-permute-start(f32[2560]{0:T(1024)S(1)} %get-tuple-element.101), channel_id=1, source_target_pairs={{0,4},{1,5},{2,6},{3,7},{4,0},{5,1},{6,2},{7,3},{8,12},{9,13},{10,... | collective-permute-start | bytes 30728 | tf_op jit(solution)/shard_map/ppermute | solution.py:24
  63.2 1.3 %collective-permute-done.15 = f32[2560]{0:T(1024)S(1)} collective-permute-done((f32[2560]{0:T(1024)S(1)}, f32[2560]{0:T(1024)S(1)}, u32[]{:S(2)}, u32[]{:S(2)}) %collective-permute-start.15) | collective-permute-done | bytes 10272 | tf_op jit(solution)/shard_map/ppermute | solution.py:24
  65.2 1.0 %collective-permute-done.13 = f16[96,2560]{1,0:T(8,128)(2,1)S(1)} collective-permute-done((f16[96,2560]{1,0:T(8,128)(2,1)S(1)}, f16[96,2560]{1,0:T(8,128)(2,1)S(1)}, u32[]{:S(2)}, u32[]{:S(2)}) %collective-permute-start.13) | collective-permute-done | bytes 491552 | tf_op jit(solution)/shard_map/ppermute | solution.py:24
  66.4 0.8 collective-permute-start.19
  67.7 3.2 %collective-permute-start.21 = (f16[96,2560]{1,0:T(8,128)(2,1)S(1)}, f16[96,2560]{1,0:T(8,128)(2,1)S(1)}, u32[]{:S(2)}, u32[]{:S(2)}) collective-permute-start(f16[96,2560]{1,0:T(8,128)(2,1)S(1)} %get-tuple-element.110), channel_id=1, source_target_pairs={{0,4},{1,5},{2,6},{3,7},{4,0},{5,1},{6,2},{7,3},{8,12},{9,13},{10,... | collective-permute-start | bytes 1474568 | tf_op jit(solution)/shard_map/ppermute | solution.py:24
  70.9 1.4 %collective-permute-start.18 = (f16[96,2560]{1,0:T(8,128)(2,1)S(1)}, f16[96,2560]{1,0:T(8,128)(2,1)S(1)}, u32[]{:S(2)}, u32[]{:S(2)}) collective-permute-start(f16[96,2560]{1,0:T(8,128)(2,1)S(1)} %multiply_convert_fusion.6), channel_id=1, source_target_pairs={{0,2},{1,3},{2,0},{3,1},{4,6},{5,7},{6,4},{7,5},{8,10},{9,11},{10,... | collective-permute-start | bytes 1474568 | tf_op jit(solution)/shard_map/ppermute | solution.py:24
  72.8 17.1 %collective-permute-done.19 = f16[96,2560]{1,0:T(8,128)(2,1)S(1)} collective-permute-done((f16[96,2560]{1,0:T(8,128)(2,1)S(1)}, f16[96,2560]{1,0:T(8,128)(2,1)S(1)}, u32[]{:S(2)}, u32[]{:S(2)}) %collective-permute-start.19) | collective-permute-done | bytes 491552 | tf_op jit(solution)/shard_map/ppermute | solution.py:24
  90.0 0.6 collective-permute-done.21
  90.6 1.2 %add_bitcast_fusion.1 = f32[1,96,2560]{2,1,0:T(8,128)} fusion(f16[96,2560]{1,0:T(8,128)(2,1)S(1)} %collective-permute-done.19, f32[96,2560]{1,0:T(8,128)S(1)} %get-tuple-element.76, f16[96,2560]{1,0:T(8,128)(2,1)S(1)} %collective-permute-done.18, f32[2560]{0:T(1024)S(1)} %collective-permute-done.15, f32[2560]{0:T(1024)S(1)} %collective-permute-done.14), kind=kLoop, calls=%fused_computation.4 | loop fusion | flops 1474560 | bytes 2969600 | tf_op jit(solution)/shard_map/reshape | solution.py:301
  91.8 1.3 %add_bitcast_fusion = f32[1,96,2560]{2,1,0:T(8,128)} fusion(f16[96,2560]{1,0:T(8,128)(2,1)S(1)} %collective-permute-done.21, f16[96,2560]{1,0:T(8,128)(2,1)S(1)} %collective-permute-done.24, f32[96,2560]{1,0:T(8,128)S(1)} %get-tuple-element.94, f16[96,2560]{1,0:T(8,128)(2,1)S(1)} %collective-permute-done.22, f32[2560]{0:T(1024)S(1)} %collective-permute-done.17, ...), kind=kLoop, calls=%fused_computation | loop fusion | flops 2211840 | bytes 3471360 | tf_op jit(solution)/shard_map/reshape | solution.py:301
  (45 shorter events, 6.0 us)
Async XLA Ops:
  0.6 38.6 %copy-start = (bf16[1,96,2560]{2,1,0:T(8,128)(2,1)S(1)}, bf16[1,96,2560]{2,1,0:T(8,128)(2,1)}, u32[]{:S(2)}) copy-start(bf16[1,96,2560]{2,1,0:T(8,128)(2,1)} %param.6) | copy-start | bytes 1474564
  0.6 29.2 %copy-start.1 = (bf16[1,96,2560]{2,1,0:T(8,128)(2,1)S(1)}, bf16[1,96,2560]{2,1,0:T(8,128)(2,1)}, u32[]{:S(2)}) copy-start(bf16[1,96,2560]{2,1,0:T(8,128)(2,1)} %param.7) | copy-start | bytes 1474564
  0.6 26.2 %collective-permute-start.2 = (bf16[96,2560]{1,0:T(8,128)(2,1)}, bf16[96,2560]{1,0:T(8,128)(2,1)S(1)}, u32[]{:S(2)}, u32[]{:S(2)}) collective-permute-start(bf16[96,2560]{1,0:T(8,128)(2,1)} %bitcast.7), channel_id=1, source_target_pairs={{0,8},{1,9},{2,10},{3,11},{4,12},{5,13},{6,14},{7,15},{8,0},{9,1},... | collective-permute-start | bytes 1474568 | tf_op jit(solution)/shard_map/ppermute | solution.py:24
  4.8 22.1 %collective-permute-start.1 = (bf16[96,2560]{1,0:T(8,128)(2,1)}, bf16[96,2560]{1,0:T(8,128)(2,1)S(1)}, u32[]{:S(2)}, u32[]{:S(2)}) collective-permute-start(bf16[96,2560]{1,0:T(8,128)(2,1)} %bitcast.8), channel_id=1, source_target_pairs={{0,2},{1,3},{2,0},{3,1},{4,6},{5,7},{6,4},{7,5},{8,10},{9,11},{10,... | collective-permute-start | bytes 1474568 | tf_op jit(solution)/shard_map/ppermute | solution.py:24
  6.2 22.0 %collective-permute-start.3 = (bf16[96,2560]{1,0:T(8,128)(2,1)}, bf16[96,2560]{1,0:T(8,128)(2,1)S(1)}, u32[]{:S(2)}, u32[]{:S(2)}) collective-permute-start(bf16[96,2560]{1,0:T(8,128)(2,1)} %bitcast.10), channel_id=1, source_target_pairs={{0,4},{1,5},{2,6},{3,7},{4,0},{5,1},{6,2},{7,3},{8,12},{9,13},{10,... | collective-permute-start | bytes 1474568 | tf_op jit(solution)/shard_map/ppermute | solution.py:24
  7.8 20.4 %collective-permute-start = (bf16[96,2560]{1,0:T(8,128)(2,1)}, bf16[96,2560]{1,0:T(8,128)(2,1)}, u32[]{:S(2)}, u32[]{:S(2)}) collective-permute-start(bf16[96,2560]{1,0:T(8,128)(2,1)} %bitcast.11), channel_id=1, source_target_pairs={{0,16},{1,17},{2,18},{3,19},{4,20},{5,21},{6,22},{7,23},{8,24},{9,... | collective-permute-start | bytes 1474568 | tf_op jit(solution)/shard_map/ppermute | solution.py:24
  11.1 0.7 copy-start.2
  11.7 0.7 copy-start.3
  28.2 11.0 %collective-permute-start.5 = (bf16[96,2560]{1,0:T(8,128)(2,1)S(1)}, bf16[96,2560]{1,0:T(8,128)(2,1)S(1)}, u32[]{:S(2)}, u32[]{:S(2)}) collective-permute-start(bf16[96,2560]{1,0:T(8,128)(2,1)S(1)} %collective-permute-done.3.refs_6_), channel_id=1, source_target_pairs={{0,16},{1,17},{2,18},{3,19},{4,20},{5,21},{6,22},{7,23},{8,24},{9,... | collective-permute-start | bytes 1474568 | tf_op jit(solution)/shard_map/ppermute | solution.py:24
  29.8 9.5 %collective-permute-start.7 = (bf16[96,2560]{1,0:T(8,128)(2,1)}, bf16[96,2560]{1,0:T(8,128)(2,1)S(1)}, u32[]{:S(2)}, u32[]{:S(2)}) collective-permute-start(bf16[96,2560]{1,0:T(8,128)(2,1)} %collective-permute-done.refs_4_), channel_id=1, source_target_pairs={{0,1},{1,0},{2,3},{3,2},{4,5},{5,4},{6,7},{7,6},{8,9},{9,8},{10,11... | collective-permute-start | bytes 1474568 | tf_op jit(solution)/shard_map/ppermute | solution.py:24
  29.8 9.5 %collective-permute-start.9 = (bf16[96,2560]{1,0:T(8,128)(2,1)S(1)}, bf16[96,2560]{1,0:T(8,128)(2,1)S(1)}, u32[]{:S(2)}, u32[]{:S(2)}) collective-permute-start(bf16[96,2560]{1,0:T(8,128)(2,1)S(1)} %bitcast.12), channel_id=1, source_target_pairs={{0,1},{1,0},{2,3},{3,2},{4,5},{5,4},{6,7},{7,6},{8,9},{9,8},{10,11... | collective-permute-start | bytes 1474568 | tf_op jit(solution)/shard_map/ppermute | solution.py:24
  30.3 8.9 %collective-permute-start.8 = (bf16[96,2560]{1,0:T(8,128)(2,1)S(1)}, bf16[96,2560]{1,0:T(8,128)(2,1)S(1)}, u32[]{:S(2)}, u32[]{:S(2)}) collective-permute-start(bf16[96,2560]{1,0:T(8,128)(2,1)S(1)} %collective-permute-done.3.refs_6_), channel_id=1, source_target_pairs={{0,1},{1,0},{2,3},{3,2},{4,5},{5,4},{6,7},{7,6},{8,9},{9,8},{10,11... | collective-permute-start | bytes 1474568 | tf_op jit(solution)/shard_map/ppermute | solution.py:24
  30.3 13.6 %collective-permute-start.4 = (bf16[96,2560]{1,0:T(8,128)(2,1)S(1)}, bf16[96,2560]{1,0:T(8,128)(2,1)S(1)}, u32[]{:S(2)}, u32[]{:S(2)}) collective-permute-start(bf16[96,2560]{1,0:T(8,128)(2,1)S(1)} %collective-permute-done.2.refs_1_), channel_id=1, source_target_pairs={{0,2},{1,3},{2,0},{3,1},{4,6},{5,7},{6,4},{7,5},{8,10},{9,11},{10,... | collective-permute-start | bytes 1474568 | tf_op jit(solution)/shard_map/ppermute | solution.py:24
  39.2 4.7 %collective-permute-start.6 = (bf16[96,2560]{1,0:T(8,128)(2,1)S(1)}, bf16[96,2560]{1,0:T(8,128)(2,1)S(1)}, u32[]{:S(2)}, u32[]{:S(2)}) collective-permute-start(bf16[96,2560]{1,0:T(8,128)(2,1)S(1)} %collective-permute-done.5.refs_2_), channel_id=1, source_target_pairs={{0,1},{1,0},{2,3},{3,2},{4,5},{5,4},{6,7},{7,6},{8,9},{9,8},{10,11... | collective-permute-start | bytes 1474568 | tf_op jit(solution)/shard_map/ppermute | solution.py:24
  48.6 1.2 %collective-permute-start.11 = (f32[2560]{0:T(1024)S(1)}, f32[2560]{0:T(1024)S(1)}, u32[]{:S(2)}, u32[]{:S(2)}) collective-permute-start(f32[2560]{0:T(1024)S(1)} %get-tuple-element.68), channel_id=1, source_target_pairs={{0,1},{1,0},{2,3},{3,2},{4,5},{5,4},{6,7},{7,6},{8,9},{9,8},{10,11... | collective-permute-start | bytes 30728 | tf_op jit(solution)/shard_map/ppermute | solution.py:24
  48.7 2.0 %collective-permute-start.10 = (f16[96,2560]{1,0:T(8,128)(2,1)S(1)}, f16[96,2560]{1,0:T(8,128)(2,1)S(1)}, u32[]{:S(2)}, u32[]{:S(2)}) collective-permute-start(f16[96,2560]{1,0:T(8,128)(2,1)S(1)} %multiply_convert_fusion.8), channel_id=1, source_target_pairs={{0,1},{1,0},{2,3},{3,2},{4,5},{5,4},{6,7},{7,6},{8,9},{9,8},{10,11... | collective-permute-start | bytes 1474568 | tf_op jit(solution)/shard_map/ppermute | solution.py:24
  51.0 8.8 %collective-permute-start.14 = (f32[2560]{0:T(1024)S(1)}, f32[2560]{0:T(1024)S(1)}, u32[]{:S(2)}, u32[]{:S(2)}) collective-permute-start(f32[2560]{0:T(1024)S(1)} %get-tuple-element.80), channel_id=1, source_target_pairs={{0,2},{1,3},{2,0},{3,1},{4,6},{5,7},{6,4},{7,5},{8,10},{9,11},{10,... | collective-permute-start | bytes 30728 | tf_op jit(solution)/shard_map/ppermute | solution.py:24
  51.6 9.0 %collective-permute-start.16 = (f32[2560]{0:T(1024)S(1)}, f32[2560]{0:T(1024)S(1)}, u32[]{:S(2)}, u32[]{:S(2)}) collective-permute-start(f32[2560]{0:T(1024)S(1)} %get-tuple-element.81), channel_id=1, source_target_pairs={{0,16},{1,17},{2,18},{3,19},{4,20},{5,21},{6,22},{7,23},{8,24},{9,... | collective-permute-start | bytes 30728 | tf_op jit(solution)/shard_map/ppermute | solution.py:24
  52.1 13.1 %collective-permute-start.12 = (f16[96,2560]{1,0:T(8,128)(2,1)S(1)}, f16[96,2560]{1,0:T(8,128)(2,1)S(1)}, u32[]{:S(2)}, u32[]{:S(2)}) collective-permute-start(f16[96,2560]{1,0:T(8,128)(2,1)S(1)} %multiply_convert_fusion.9), channel_id=1, source_target_pairs={{0,2},{1,3},{2,0},{3,1},{4,6},{5,7},{6,4},{7,5},{8,10},{9,11},{10,... | collective-permute-start | bytes 1474568 | tf_op jit(solution)/shard_map/ppermute | solution.py:24
  53.6 12.6 %collective-permute-start.13 = (f16[96,2560]{1,0:T(8,128)(2,1)S(1)}, f16[96,2560]{1,0:T(8,128)(2,1)S(1)}, u32[]{:S(2)}, u32[]{:S(2)}) collective-permute-start(f16[96,2560]{1,0:T(8,128)(2,1)S(1)} %multiply_convert_fusion.7), channel_id=1, source_target_pairs={{0,16},{1,17},{2,18},{3,19},{4,20},{5,21},{6,22},{7,23},{8,24},{9,... | collective-permute-start | bytes 1474568 | tf_op jit(solution)/shard_map/ppermute | solution.py:24
  59.8 4.7 %collective-permute-start.15 = (f32[2560]{0:T(1024)S(1)}, f32[2560]{0:T(1024)S(1)}, u32[]{:S(2)}, u32[]{:S(2)}) collective-permute-start(f32[2560]{0:T(1024)S(1)} %get-tuple-element.103), channel_id=1, source_target_pairs={{0,8},{1,9},{2,10},{3,11},{4,12},{5,13},{6,14},{7,15},{8,0},{9,1},... | collective-permute-start | bytes 30728 | tf_op jit(solution)/shard_map/ppermute | solution.py:24
  60.6 4.1 %collective-permute-start.17 = (f32[2560]{0:T(1024)S(1)}, f32[2560]{0:T(1024)S(1)}, u32[]{:S(2)}, u32[]{:S(2)}) collective-permute-start(f32[2560]{0:T(1024)S(1)} %get-tuple-element.101), channel_id=1, source_target_pairs={{0,4},{1,5},{2,6},{3,7},{4,0},{5,1},{6,2},{7,3},{8,12},{9,13},{10,... | collective-permute-start | bytes 30728 | tf_op jit(solution)/shard_map/ppermute | solution.py:24
  63.1 4.1 %collective-permute-start.20 = (f16[96,2560]{1,0:T(8,128)(2,1)S(1)}, f16[96,2560]{1,0:T(8,128)(2,1)S(1)}, u32[]{:S(2)}, u32[]{:S(2)}) collective-permute-start(f16[96,2560]{1,0:T(8,128)(2,1)S(1)} %get-tuple-element.107), channel_id=1, source_target_pairs={{0,1},{1,0},{2,3},{3,2},{4,5},{5,4},{6,7},{7,6},{8,9},{9,8},{10,11... | collective-permute-start | bytes 1474568 | tf_op jit(solution)/shard_map/ppermute | solution.py:24
  64.5 2.7 %collective-permute-start.23 = (f16[96,2560]{1,0:T(8,128)(2,1)S(1)}, f16[96,2560]{1,0:T(8,128)(2,1)S(1)}, u32[]{:S(2)}, u32[]{:S(2)}) collective-permute-start(f16[96,2560]{1,0:T(8,128)(2,1)S(1)} %get-tuple-element.108), channel_id=1, source_target_pairs={{0,1},{1,0},{2,3},{3,2},{4,5},{5,4},{6,7},{7,6},{8,9},{9,8},{10,11... | collective-permute-start | bytes 1474568 | tf_op jit(solution)/shard_map/ppermute | solution.py:24
  66.4 23.6 %collective-permute-start.19 = (f16[96,2560]{1,0:T(8,128)(2,1)S(1)}, f16[96,2560]{1,0:T(8,128)(2,1)S(1)}, u32[]{:S(2)}, u32[]{:S(2)}) collective-permute-start(f16[96,2560]{1,0:T(8,128)(2,1)S(1)} %multiply_convert_fusion.5), channel_id=1, source_target_pairs={{0,8},{1,9},{2,10},{3,11},{4,12},{5,13},{6,14},{7,15},{8,0},{9,1},... | collective-permute-start | bytes 1474568 | tf_op jit(solution)/shard_map/ppermute | solution.py:24
  67.7 22.9 %collective-permute-start.21 = (f16[96,2560]{1,0:T(8,128)(2,1)S(1)}, f16[96,2560]{1,0:T(8,128)(2,1)S(1)}, u32[]{:S(2)}, u32[]{:S(2)}) collective-permute-start(f16[96,2560]{1,0:T(8,128)(2,1)S(1)} %get-tuple-element.110), channel_id=1, source_target_pairs={{0,4},{1,5},{2,6},{3,7},{4,0},{5,1},{6,2},{7,3},{8,12},{9,13},{10,... | collective-permute-start | bytes 1474568 | tf_op jit(solution)/shard_map/ppermute | solution.py:24
  70.9 19.7 %collective-permute-start.18 = (f16[96,2560]{1,0:T(8,128)(2,1)S(1)}, f16[96,2560]{1,0:T(8,128)(2,1)S(1)}, u32[]{:S(2)}, u32[]{:S(2)}) collective-permute-start(f16[96,2560]{1,0:T(8,128)(2,1)S(1)} %multiply_convert_fusion.6), channel_id=1, source_target_pairs={{0,2},{1,3},{2,0},{3,1},{4,6},{5,7},{6,4},{7,5},{8,10},{9,11},{10,... | collective-permute-start | bytes 1474568 | tf_op jit(solution)/shard_map/ppermute | solution.py:24
  72.3 19.5 %collective-permute-start.22 = (f16[96,2560]{1,0:T(8,128)(2,1)S(1)}, f16[96,2560]{1,0:T(8,128)(2,1)S(1)}, u32[]{:S(2)}, u32[]{:S(2)}) collective-permute-start(f16[96,2560]{1,0:T(8,128)(2,1)S(1)} %get-tuple-element.106), channel_id=1, source_target_pairs={{0,1},{1,0},{2,3},{3,2},{4,5},{5,4},{6,7},{7,6},{8,9},{9,8},{10,11... | collective-permute-start | bytes 1474568 | tf_op jit(solution)/shard_map/ppermute | solution.py:24
  72.3 19.5 %collective-permute-start.24 = (f16[96,2560]{1,0:T(8,128)(2,1)S(1)}, f16[96,2560]{1,0:T(8,128)(2,1)S(1)}, u32[]{:S(2)}, u32[]{:S(2)}) collective-permute-start(f16[96,2560]{1,0:T(8,128)(2,1)S(1)} %get-tuple-element.109), channel_id=1, source_target_pairs={{0,16},{1,17},{2,18},{3,19},{4,20},{5,21},{6,22},{7,23},{8,24},{9,... | collective-permute-start | bytes 1474568 | tf_op jit(solution)/shard_map/ppermute | solution.py:24

commit v9 on v8

--- a/solution.py
+++ b/solution.py
@@ -85,7 +85,7 @@
     tops[...] = jnp.where(row == 0, top, jnp.where(row == 1, top_a, top_b))
 
 
-def end_amplitudes(places_a, places_b, corner, spans_a, spans_b, *refs):
+def end_amplitudes(places_a, places_b, corner, spans, *refs):
     n_a, n_b = len(places_a), len(places_b)
     a_refs, b_refs, ninv = refs[:n_a], refs[n_a:n_a + n_b], refs[n_a + n_b]
     tops = refs[n_a + n_b + 5]
@@ -101,8 +101,7 @@
         value = top * largest_right * (count / 32768.0) + 1e-36
         unit[...] = jnp.broadcast_to(value[0, 0], unit.shape)
         scale[...] = jnp.broadcast_to((1.0 / value)[0, 0], scale.shape)
-    rows_out(0, spans_b, tt, acat, *outs[:len(spans_b)])
-    rows_out(0, spans_a, t_ref, bcat, *outs[len(spans_b):])
+    rows_out(0, spans, tt, acat, *outs)
 
 
 def rows_out(start, spans, left, right, *outs):
@@ -204,10 +203,9 @@
     count = late_a + late_b + 1
     opening = pl.pallas_call(
         functools.partial(
-            end_amplitudes, [p for _, p in all_a[:late_a]], [p for _, p in all_b[:late_b]], corner,
-            cut * early_a, cut * early_b,
+            end_amplitudes, [p for _, p in all_a[:late_a]], [p for _, p in all_b[:late_b]], corner, cut * early_b
         ),
-        out_shape=shared + [jax.ShapeDtypeStruct((aux,), jnp.float32)] * 4 + blocks(early_a + early_b),
+        out_shape=shared + [jax.ShapeDtypeStruct((aux,), jnp.float32)] * 4 + blocks(early_b),
         input_output_aliases={count + k: k for k in range(4)},
         compiler_params=pltpu.CompilerParams(vmem_limit_bytes=24 * MIB),
         cost_estimate=estimate(rows * cols),
@@ -254,8 +252,8 @@
 
     unit_b = unit_b + unit_other
     units, scales = [unit_a, unit_b], [scale_a, 1.0 / unit_b]
-    gb = chips_sum(pairs(masks_b, opening[8:8 + early_b]))
-    ga = pairs(masks_a, opening[8 + early_b:])
+    gb = chips_sum(pairs(masks_b, opening[8:]))
+    ga = contracted(t, bcat, 0, masks_a[:early_a], "alpha_first")
     for level in range(max(len(bits_a), len(bits_b))):
         jobs = [
             (which, parts, bits[level]) + passed_on(names, bits, level)

time: 93.3 us -> 92 us (0.986)
  waiting for transfers between devices: 47.9 us -> 46.5 us
    ppermute x25, waiting for transfers between devices: 47.9 us -> 46.5 us  [exchange(): lax.ppermute(value, ('grp', 'slab'), [(d, d ^ 1 << bit) for d in range(de...]
    pallas_call x1, Pallas kernels: 4.6 us -> 3.28 us  [body(): pl.pallas_call(functools.partial(end_amplitudes, [p for _, p in all_a[:la...]
    pallas_call x2 -> x3, Pallas kernels: 4.4 us -> 5.73 us  [contracted(): pl.pallas_call(functools.partial(rows_out, start * width, cut * len(names...]
  transfers between devices with their start and end apart: 25 -> 25, of which waited for: 12 -> 10; matrix products, arithmetic and copies ran while one was open for 4% -> 5% of each run, Pallas kernels for 8% -> 10%
where the time goes in v9:
time: 92 us; the launch traced here: 91.8 us
  waiting for transfers between devices  46.5 us (51%)
  starting transfers between devices  25.2 us (27%)
  Pallas kernels  12.3 us (13%)
  other arithmetic  3.93 us (4%)
  local copies, waits for them, and re-layouts  3.03 us (3%)
    ppermute x25, waiting for transfers between devices, exchange(): lax.ppermute(value, ('grp', 'slab'), [(d, d ^ 1 << bit) for d in range(de...  46.5 us
    ppermute x25, starting transfers between devices, exchange(): lax.ppermute(value, ('grp', 'slab'), [(d, d ^ 1 << bit) for d in range(de...  25.2 us
    pallas_call x3, Pallas kernels, contracted(): pl.pallas_call(functools.partial(rows_out, start * width, cut * len(names...  5.73 us
    pallas_call x1, Pallas kernels, body(): pl.pallas_call(functools.partial(end_amplitudes, [p for _, p in all_a[:la...  3.28 us
    reshape x2, other arithmetic, whole(): return parts[0].reshape(orbital_alpha.shape)  2.46 us
    pallas_call x1, Pallas kernels, body(): pl.pallas_call(functools.partial(begin_amplitudes, [p for _, p in all_a[l...  2.43 us
  transfers between devices with their start and end apart: 25, of which 10 were waited for; matrix products, arithmetic and copies ran while one was open for 5% of the time, Pallas kernels for 10%

profile of v9, /device:TPU:0, one launch (start us, length us, event | category | flops | bytes accessed | tf_op | source)
XLA Modules:
  0.0 91.8 jit_solution(1652967068947037655)
XLA Ops:
  0.6 4.1 %collective-permute-start.2 = (bf16[96,2560]{1,0:T(8,128)(2,1)}, bf16[96,2560]{1,0:T(8,128)(2,1)S(1)}, u32[]{:S(2)}, u32[]{:S(2)}) collective-permute-start(bf16[96,2560]{1,0:T(8,128)(2,1)} %bitcast.7), channel_id=1, source_target_pairs={{0,8},{1,9},{2,10},{3,11},{4,12},{5,13},{6,14},{7,15},{8,0},{9,1},... | collective-permute-start | bytes 1474568 | tf_op jit(solution)/shard_map/ppermute | solution.py:24
  4.8 1.5 %collective-permute-start.1 = (bf16[96,2560]{1,0:T(8,128)(2,1)}, bf16[96,2560]{1,0:T(8,128)(2,1)S(1)}, u32[]{:S(2)}, u32[]{:S(2)}) collective-permute-start(bf16[96,2560]{1,0:T(8,128)(2,1)} %bitcast.8), channel_id=1, source_target_pairs={{0,2},{1,3},{2,0},{3,1},{4,6},{5,7},{6,4},{7,5},{8,10},{9,11},{10,... | collective-permute-start | bytes 1474568 | tf_op jit(solution)/shard_map/ppermute | solution.py:24
  6.2 1.6 %collective-permute-start.3 = (bf16[96,2560]{1,0:T(8,128)(2,1)}, bf16[96,2560]{1,0:T(8,128)(2,1)S(1)}, u32[]{:S(2)}, u32[]{:S(2)}) collective-permute-start(bf16[96,2560]{1,0:T(8,128)(2,1)} %bitcast.10), channel_id=1, source_target_pairs={{0,4},{1,5},{2,6},{3,7},{4,0},{5,1},{6,2},{7,3},{8,12},{9,13},{10,... | collective-permute-start | bytes 1474568 | tf_op jit(solution)/shard_map/ppermute | solution.py:24
  7.8 1.5 %collective-permute-start = (bf16[96,2560]{1,0:T(8,128)(2,1)}, bf16[96,2560]{1,0:T(8,128)(2,1)}, u32[]{:S(2)}, u32[]{:S(2)}) collective-permute-start(bf16[96,2560]{1,0:T(8,128)(2,1)} %bitcast.11), channel_id=1, source_target_pairs={{0,16},{1,17},{2,18},{3,19},{4,20},{5,21},{6,22},{7,23},{8,24},{9,... | collective-permute-start | bytes 1474568 | tf_op jit(solution)/shard_map/ppermute | solution.py:24
  9.3 0.8 reshape.35.vb_ref
  10.1 1.0 %broadcast_in_dim.3.va_ref = f32[1536,1]{1,0:T(8,128)S(1)} reshape(f32[1536]{0:T(1024)} %param.10) | data formatting | bytes 12288 | tf_op jit(solution)/shard_map/broadcast_in_dim | solution.py:162
  11.1 0.6 copy-done.2
  11.7 0.7 copy-done.3
  12.4 0.8 energies.1.refs_9_.refs_3_
  13.2 13.6 %collective-permute-done.2.refs_1_ = bf16[96,2560]{1,0:T(8,128)(2,1)S(1)} collective-permute-done((bf16[96,2560]{1,0:T(8,128)(2,1)}, bf16[96,2560]{1,0:T(8,128)(2,1)S(1)}, u32[]{:S(2)}, u32[]{:S(2)}) %collective-permute-start.2) | collective-permute-done | bytes 491552 | tf_op jit(solution)/shard_map/ppermute | solution.py:24
  26.8 1.4 %collective-permute-done.3.refs_6_ = bf16[96,2560]{1,0:T(8,128)(2,1)S(1)} collective-permute-done((bf16[96,2560]{1,0:T(8,128)(2,1)}, bf16[96,2560]{1,0:T(8,128)(2,1)S(1)}, u32[]{:S(2)}, u32[]{:S(2)}) %collective-permute-start.3) | collective-permute-done | bytes 491552 | tf_op jit(solution)/shard_map/ppermute | solution.py:24
  28.2 1.6 %collective-permute-start.5 = (bf16[96,2560]{1,0:T(8,128)(2,1)S(1)}, bf16[96,2560]{1,0:T(8,128)(2,1)S(1)}, u32[]{:S(2)}, u32[]{:S(2)}) collective-permute-start(bf16[96,2560]{1,0:T(8,128)(2,1)S(1)} %collective-permute-done.3.refs_6_), channel_id=1, source_target_pairs={{0,16},{1,17},{2,18},{3,19},{4,20},{5,21},{6,22},{7,23},{8,24},{9,... | collective-permute-start | bytes 1474568 | tf_op jit(solution)/shard_map/ppermute | solution.py:24
  30.9 8.4 %collective-permute-done.5.refs_2_ = bf16[96,2560]{1,0:T(8,128)(2,1)S(1)} collective-permute-done((bf16[96,2560]{1,0:T(8,128)(2,1)S(1)}, bf16[96,2560]{1,0:T(8,128)(2,1)S(1)}, u32[]{:S(2)}, u32[]{:S(2)}) %collective-permute-start.5) | collective-permute-done | bytes 491552 | tf_op jit(solution)/shard_map/ppermute | solution.py:24
  39.3 2.4 %amplitudes_early.1 = (bf16[384,768]{1,0:T(8,128)(2,1)S(1)}, bf16[768,384]{1,0:T(8,128)(2,1)S(1)}, bf16[384,2560]{1,0:T(8,128)(2,1)S(1)}, bf16[768,2560]{1,0:T(8,128)(2,1)S(1)}, f32[8,128]{1,0:T(8,128)S(1)}) custom-call(bf16[96,2560]{1,0:T(8,128)(2,1)S(1)} %collective-permute-done.1.refs_0_, bf16[96,2560]{1,0:T(8,128)(2,1)S(1)} %collective-permute-done.2.refs_1_, ...), custom_call_target="tpu_custom_call" | custom-call | flops 671088640 | bytes 11796480 | tf_op jit(solution)/shard_map/amplitudes_early/pallas_call | solution.py:196
  41.7 2.2 %collective-permute-done.4.refs_0_ = bf16[96,2560]{1,0:T(8,128)(2,1)S(1)} collective-permute-done((bf16[96,2560]{1,0:T(8,128)(2,1)S(1)}, bf16[96,2560]{1,0:T(8,128)(2,1)S(1)}, u32[]{:S(2)}, u32[]{:S(2)}) %collective-permute-start.4) | collective-permute-done | bytes 491552 | tf_op jit(solution)/shard_map/ppermute | solution.py:24
  44.0 3.3 %amplitudes_late.1 = (bf16[384,768]{1,0:T(8,128)(2,1)S(1)}, bf16[768,384]{1,0:T(8,128)(2,1)S(1)}, bf16[384,2560]{1,0:T(8,128)(2,1)S(1)}, bf16[768,2560]{1,0:T(8,...) custom-call(bf16[96,2560]{1,0:T(8,128)(2,1)S(1)} %collective-permute, ...), custom_call_target="tpu_custom_call", output_to_operand_aliasing={{0}: (4, {}), {1}: (5, {}), {2}: (6, {}), {3}: (7, {})} | custom-call | flops 1509949440 | bytes 11796480 | tf_op jit(solution)/shard_map/amplitudes_late/pallas_call | solution.py:204
  48.0 1.3 %alpha_first.1 = f32[96,2560]{1,0:T(8,128)S(1)} custom-call(bf16[384,768]{1,0:T(8,128)(2,1)S(1)} %get-tuple-element.72.left, bf16[768,2560]{1,0:T(8,128)(2,1)S(1)} %get-tuple-element.73.right), custom_call_target="tpu_custom_call" | custom-call | flops 377487360 | bytes 4915200 | tf_op jit(solution)/shard_map/alpha_first/pallas_call | solution.py:217
  50.8 1.4 %collective-permute-start.12 = (f16[96,2560]{1,0:T(8,128)(2,1)S(1)}, f16[96,2560]{1,0:T(8,128)(2,1)S(1)}, u32[]{:S(2)}, u32[]{:S(2)}) collective-permute-start(f16[96,2560]{1,0:T(8,128)(2,1)S(1)} %multiply_convert_fusion.9), channel_id=1, source_target_pairs={{0,2},{1,3},{2,0},{3,1},{4,6},{5,7},{6,4},{7,5},{8,10},{9,11},{10,... | collective-permute-start | bytes 1474568 | tf_op jit(solution)/shard_map/ppermute | solution.py:24
  52.2 1.6 %collective-permute-start.13 = (f16[96,2560]{1,0:T(8,128)(2,1)S(1)}, f16[96,2560]{1,0:T(8,128)(2,1)S(1)}, u32[]{:S(2)}, u32[]{:S(2)}) collective-permute-start(f16[96,2560]{1,0:T(8,128)(2,1)S(1)} %multiply_convert_fusion.7), channel_id=1, source_target_pairs={{0,16},{1,17},{2,18},{3,19},{4,20},{5,21},{6,22},{7,23},{8,24},{9,... | collective-permute-start | bytes 1474568 | tf_op jit(solution)/shard_map/ppermute | solution.py:24
  53.8 2.4 %beta.1 = (f32[96,2560]{1,0:T(8,128)S(1)}, f32[96,2560]{1,0:T(8,128)S(1)}, f32[96,2560]{1,0:T(8,128)S(1)}, f32[96,2560]{1,0:T(8,128)S(1)}, f32[96,2560]{1,0:T(8,128)S(1)}, /*index=5*/f32[96,2560]{1,0:T(8,128)S(1)}) custom-call(bf16[768,384]{1,0:T(8,128)(2,1)S(1)} %get-tuple-element.84.left, bf16[384,2560]{1,0:T(8,128)(2,1)S(1)} %get-tuple-element.85.right), custom_call_target="tpu_custom_call" | custom-call | flops 1132462080 | bytes 7864320 | tf_op jit(solution)/shard_map/beta/pallas_call | solution.py:217
  56.5 2.0 %alpha.1 = (f32[96,2560]{1,0:T(8,128)S(1)}, f32[96,2560]{1,0:T(8,128)S(1)}, f32[96,2560]{1,0:T(8,128)S(1)}) custom-call(bf16[384,768]{1,0:T(8,128)(2,1)S(1)} %get-tuple-element.72.left, bf16[768,2560]{1,0:T(8,128)(2,1)S(1)} %get-tuple-element.73.right), custom_call_target="tpu_custom_call" | custom-call | flops 1132462080 | bytes 6881280 | tf_op jit(solution)/shard_map/alpha/pallas_call | solution.py:217
  58.5 0.7 collective-permute-start.15
  59.3 2.4 %collective-permute-start.17 = (f32[2560]{0:T(1024)S(1)}, f32[2560]{0:T(1024)S(1)}, u32[]{:S(2)}, u32[]{:S(2)}) collective-permute-start(f32[2560]{0:T(1024)S(1)} %get-tuple-element.99), channel_id=1, source_target_pairs={{0,4},{1,5},{2,6},{3,7},{4,0},{5,1},{6,2},{7,3},{8,12},{9,13},{10,... | collective-permute-start | bytes 30728 | tf_op jit(solution)/shard_map/ppermute | solution.py:24
  61.8 1.3 %collective-permute-done.15 = f32[2560]{0:T(1024)S(1)} collective-permute-done((f32[2560]{0:T(1024)S(1)}, f32[2560]{0:T(1024)S(1)}, u32[]{:S(2)}, u32[]{:S(2)}) %collective-permute-start.15) | collective-permute-done | bytes 10272 | tf_op jit(solution)/shard_map/ppermute | solution.py:24
  63.9 1.0 %collective-permute-done.13 = f16[96,2560]{1,0:T(8,128)(2,1)S(1)} collective-permute-done((f16[96,2560]{1,0:T(8,128)(2,1)S(1)}, f16[96,2560]{1,0:T(8,128)(2,1)S(1)}, u32[]{:S(2)}, u32[]{:S(2)}) %collective-permute-start.13) | collective-permute-done | bytes 491552 | tf_op jit(solution)/shard_map/ppermute | solution.py:24
  65.1 0.8 collective-permute-start.19
  66.4 3.2 %collective-permute-start.21 = (f16[96,2560]{1,0:T(8,128)(2,1)S(1)}, f16[96,2560]{1,0:T(8,128)(2,1)S(1)}, u32[]{:S(2)}, u32[]{:S(2)}) collective-permute-start(f16[96,2560]{1,0:T(8,128)(2,1)S(1)} %get-tuple-element.108), channel_id=1, source_target_pairs={{0,4},{1,5},{2,6},{3,7},{4,0},{5,1},{6,2},{7,3},{8,12},{9,13},{10,... | collective-permute-start | bytes 1474568 | tf_op jit(solution)/shard_map/ppermute | solution.py:24
  69.6 1.4 %collective-permute-start.18 = (f16[96,2560]{1,0:T(8,128)(2,1)S(1)}, f16[96,2560]{1,0:T(8,128)(2,1)S(1)}, u32[]{:S(2)}, u32[]{:S(2)}) collective-permute-start(f16[96,2560]{1,0:T(8,128)(2,1)S(1)} %multiply_convert_fusion.6), channel_id=1, source_target_pairs={{0,2},{1,3},{2,0},{3,1},{4,6},{5,7},{6,4},{7,5},{8,10},{9,11},{10,... | collective-permute-start | bytes 1474568 | tf_op jit(solution)/shard_map/ppermute | solution.py:24
  71.5 17.1 %collective-permute-done.19 = f16[96,2560]{1,0:T(8,128)(2,1)S(1)} collective-permute-done((f16[96,2560]{1,0:T(8,128)(2,1)S(1)}, f16[96,2560]{1,0:T(8,128)(2,1)S(1)}, u32[]{:S(2)}, u32[]{:S(2)}) %collective-permute-start.19) | collective-permute-done | bytes 491552 | tf_op jit(solution)/shard_map/ppermute | solution.py:24
  88.6 0.7 collective-permute-done.21
  89.3 1.2 %add_bitcast_fusion.1 = f32[1,96,2560]{2,1,0:T(8,128)} fusion(f16[96,2560]{1,0:T(8,128)(2,1)S(1)} %collective-permute-done.19, f32[96,2560]{1,0:T(8,128)S(1)} %get-tuple-element.74, f16[96,2560]{1,0:T(8,128)(2,1)S(1)} %collective-permute-done.18, f32[2560]{0:T(1024)S(1)} %collective-permute-done.15, f32[2560]{0:T(1024)S(1)} %collective-permute-done.14), kind=kLoop, calls=%fused_computation.4 | loop fusion | flops 1474560 | bytes 2969600 | tf_op jit(solution)/shard_map/reshape | solution.py:299
  90.5 1.3 %add_bitcast_fusion = f32[1,96,2560]{2,1,0:T(8,128)} fusion(f16[96,2560]{1,0:T(8,128)(2,1)S(1)} %collective-permute-done.21, f16[96,2560]{1,0:T(8,128)(2,1)S(1)} %collective-permute-done.24, f32[96,2560]{1,0:T(8,128)S(1)} %get-tuple-element.92, f16[96,2560]{1,0:T(8,128)(2,1)S(1)} %collective-permute-done.22, f32[2560]{0:T(1024)S(1)} %collective-permute-done.17, ...), kind=kLoop, calls=%fused_computation | loop fusion | flops 2211840 | bytes 3471360 | tf_op jit(solution)/shard_map/reshape | solution.py:299
  (46 shorter events, 5.6 us)
Async XLA Ops:
  0.6 38.6 %copy-start = (bf16[1,96,2560]{2,1,0:T(8,128)(2,1)S(1)}, bf16[1,96,2560]{2,1,0:T(8,128)(2,1)}, u32[]{:S(2)}) copy-start(bf16[1,96,2560]{2,1,0:T(8,128)(2,1)} %param.6) | copy-start | bytes 1474564
  0.6 29.2 %copy-start.1 = (bf16[1,96,2560]{2,1,0:T(8,128)(2,1)S(1)}, bf16[1,96,2560]{2,1,0:T(8,128)(2,1)}, u32[]{:S(2)}) copy-start(bf16[1,96,2560]{2,1,0:T(8,128)(2,1)} %param.7) | copy-start | bytes 1474564
  0.6 26.2 %collective-permute-start.2 = (bf16[96,2560]{1,0:T(8,128)(2,1)}, bf16[96,2560]{1,0:T(8,128)(2,1)S(1)}, u32[]{:S(2)}, u32[]{:S(2)}) collective-permute-start(bf16[96,2560]{1,0:T(8,128)(2,1)} %bitcast.7), channel_id=1, source_target_pairs={{0,8},{1,9},{2,10},{3,11},{4,12},{5,13},{6,14},{7,15},{8,0},{9,1},... | collective-permute-start | bytes 1474568 | tf_op jit(solution)/shard_map/ppermute | solution.py:24
  4.8 22.1 %collective-permute-start.1 = (bf16[96,2560]{1,0:T(8,128)(2,1)}, bf16[96,2560]{1,0:T(8,128)(2,1)S(1)}, u32[]{:S(2)}, u32[]{:S(2)}) collective-permute-start(bf16[96,2560]{1,0:T(8,128)(2,1)} %bitcast.8), channel_id=1, source_target_pairs={{0,2},{1,3},{2,0},{3,1},{4,6},{5,7},{6,4},{7,5},{8,10},{9,11},{10,... | collective-permute-start | bytes 1474568 | tf_op jit(solution)/shard_map/ppermute | solution.py:24
  6.2 22.0 %collective-permute-start.3 = (bf16[96,2560]{1,0:T(8,128)(2,1)}, bf16[96,2560]{1,0:T(8,128)(2,1)S(1)}, u32[]{:S(2)}, u32[]{:S(2)}) collective-permute-start(bf16[96,2560]{1,0:T(8,128)(2,1)} %bitcast.10), channel_id=1, source_target_pairs={{0,4},{1,5},{2,6},{3,7},{4,0},{5,1},{6,2},{7,3},{8,12},{9,13},{10,... | collective-permute-start | bytes 1474568 | tf_op jit(solution)/shard_map/ppermute | solution.py:24
  7.8 20.4 %collective-permute-start = (bf16[96,2560]{1,0:T(8,128)(2,1)}, bf16[96,2560]{1,0:T(8,128)(2,1)}, u32[]{:S(2)}, u32[]{:S(2)}) collective-permute-start(bf16[96,2560]{1,0:T(8,128)(2,1)} %bitcast.11), channel_id=1, source_target_pairs={{0,16},{1,17},{2,18},{3,19},{4,20},{5,21},{6,22},{7,23},{8,24},{9,... | collective-permute-start | bytes 1474568 | tf_op jit(solution)/shard_map/ppermute | solution.py:24
  11.1 0.7 copy-start.2
  11.7 0.7 copy-start.3
  28.2 11.0 %collective-permute-start.5 = (bf16[96,2560]{1,0:T(8,128)(2,1)S(1)}, bf16[96,2560]{1,0:T(8,128)(2,1)S(1)}, u32[]{:S(2)}, u32[]{:S(2)}) collective-permute-start(bf16[96,2560]{1,0:T(8,128)(2,1)S(1)} %collective-permute-done.3.refs_6_), channel_id=1, source_target_pairs={{0,16},{1,17},{2,18},{3,19},{4,20},{5,21},{6,22},{7,23},{8,24},{9,... | collective-permute-start | bytes 1474568 | tf_op jit(solution)/shard_map/ppermute | solution.py:24
  29.8 9.5 %collective-permute-start.7 = (bf16[96,2560]{1,0:T(8,128)(2,1)}, bf16[96,2560]{1,0:T(8,128)(2,1)S(1)}, u32[]{:S(2)}, u32[]{:S(2)}) collective-permute-start(bf16[96,2560]{1,0:T(8,128)(2,1)} %collective-permute-done.refs_4_), channel_id=1, source_target_pairs={{0,1},{1,0},{2,3},{3,2},{4,5},{5,4},{6,7},{7,6},{8,9},{9,8},{10,11... | collective-permute-start | bytes 1474568 | tf_op jit(solution)/shard_map/ppermute | solution.py:24
  29.8 9.5 %collective-permute-start.9 = (bf16[96,2560]{1,0:T(8,128)(2,1)S(1)}, bf16[96,2560]{1,0:T(8,128)(2,1)S(1)}, u32[]{:S(2)}, u32[]{:S(2)}) collective-permute-start(bf16[96,2560]{1,0:T(8,128)(2,1)S(1)} %bitcast.12), channel_id=1, source_target_pairs={{0,1},{1,0},{2,3},{3,2},{4,5},{5,4},{6,7},{7,6},{8,9},{9,8},{10,11... | collective-permute-start | bytes 1474568 | tf_op jit(solution)/shard_map/ppermute | solution.py:24
  30.3 8.9 %collective-permute-start.8 = (bf16[96,2560]{1,0:T(8,128)(2,1)S(1)}, bf16[96,2560]{1,0:T(8,128)(2,1)S(1)}, u32[]{:S(2)}, u32[]{:S(2)}) collective-permute-start(bf16[96,2560]{1,0:T(8,128)(2,1)S(1)} %collective-permute-done.3.refs_6_), channel_id=1, source_target_pairs={{0,1},{1,0},{2,3},{3,2},{4,5},{5,4},{6,7},{7,6},{8,9},{9,8},{10,11... | collective-permute-start | bytes 1474568 | tf_op jit(solution)/shard_map/ppermute | solution.py:24
  30.3 13.6 %collective-permute-start.4 = (bf16[96,2560]{1,0:T(8,128)(2,1)S(1)}, bf16[96,2560]{1,0:T(8,128)(2,1)S(1)}, u32[]{:S(2)}, u32[]{:S(2)}) collective-permute-start(bf16[96,2560]{1,0:T(8,128)(2,1)S(1)} %collective-permute-done.2.refs_1_), channel_id=1, source_target_pairs={{0,2},{1,3},{2,0},{3,1},{4,6},{5,7},{6,4},{7,5},{8,10},{9,11},{10,... | collective-permute-start | bytes 1474568 | tf_op jit(solution)/shard_map/ppermute | solution.py:24
  39.2 4.7 %collective-permute-start.6 = (bf16[96,2560]{1,0:T(8,128)(2,1)S(1)}, bf16[96,2560]{1,0:T(8,128)(2,1)S(1)}, u32[]{:S(2)}, u32[]{:S(2)}) collective-permute-start(bf16[96,2560]{1,0:T(8,128)(2,1)S(1)} %collective-permute-done.5.refs_2_), channel_id=1, source_target_pairs={{0,1},{1,0},{2,3},{3,2},{4,5},{5,4},{6,7},{7,6},{8,9},{9,8},{10,11... | collective-permute-start | bytes 1474568 | tf_op jit(solution)/shard_map/ppermute | solution.py:24
  47.2 2.2 %collective-permute-start.11 = (f32[2560]{0:T(1024)S(1)}, f32[2560]{0:T(1024)S(1)}, u32[]{:S(2)}, u32[]{:S(2)}) collective-permute-start(f32[2560]{0:T(1024)S(1)} %get-tuple-element.68), channel_id=1, source_target_pairs={{0,1},{1,0},{2,3},{3,2},{4,5},{5,4},{6,7},{7,6},{8,9},{9,8},{10,11... | collective-permute-start | bytes 30728 | tf_op jit(solution)/shard_map/ppermute | solution.py:24
  47.4 2.1 %collective-permute-start.10 = (f16[96,2560]{1,0:T(8,128)(2,1)S(1)}, f16[96,2560]{1,0:T(8,128)(2,1)S(1)}, u32[]{:S(2)}, u32[]{:S(2)}) collective-permute-start(f16[96,2560]{1,0:T(8,128)(2,1)S(1)} %multiply_convert_fusion.8), channel_id=1, source_target_pairs={{0,1},{1,0},{2,3},{3,2},{4,5},{5,4},{6,7},{7,6},{8,9},{9,8},{10,11... | collective-permute-start | bytes 1474568 | tf_op jit(solution)/shard_map/ppermute | solution.py:24
  49.7 8.8 %collective-permute-start.14 = (f32[2560]{0:T(1024)S(1)}, f32[2560]{0:T(1024)S(1)}, u32[]{:S(2)}, u32[]{:S(2)}) collective-permute-start(f32[2560]{0:T(1024)S(1)} %get-tuple-element.78), channel_id=1, source_target_pairs={{0,2},{1,3},{2,0},{3,1},{4,6},{5,7},{6,4},{7,5},{8,10},{9,11},{10,... | collective-permute-start | bytes 30728 | tf_op jit(solution)/shard_map/ppermute | solution.py:24
  50.3 9.0 %collective-permute-start.16 = (f32[2560]{0:T(1024)S(1)}, f32[2560]{0:T(1024)S(1)}, u32[]{:S(2)}, u32[]{:S(2)}) collective-permute-start(f32[2560]{0:T(1024)S(1)} %get-tuple-element.79), channel_id=1, source_target_pairs={{0,16},{1,17},{2,18},{3,19},{4,20},{5,21},{6,22},{7,23},{8,24},{9,... | collective-permute-start | bytes 30728 | tf_op jit(solution)/shard_map/ppermute | solution.py:24
  50.8 13.1 %collective-permute-start.12 = (f16[96,2560]{1,0:T(8,128)(2,1)S(1)}, f16[96,2560]{1,0:T(8,128)(2,1)S(1)}, u32[]{:S(2)}, u32[]{:S(2)}) collective-permute-start(f16[96,2560]{1,0:T(8,128)(2,1)S(1)} %multiply_convert_fusion.9), channel_id=1, source_target_pairs={{0,2},{1,3},{2,0},{3,1},{4,6},{5,7},{6,4},{7,5},{8,10},{9,11},{10,... | collective-permute-start | bytes 1474568 | tf_op jit(solution)/shard_map/ppermute | solution.py:24
  52.2 12.6 %collective-permute-start.13 = (f16[96,2560]{1,0:T(8,128)(2,1)S(1)}, f16[96,2560]{1,0:T(8,128)(2,1)S(1)}, u32[]{:S(2)}, u32[]{:S(2)}) collective-permute-start(f16[96,2560]{1,0:T(8,128)(2,1)S(1)} %multiply_convert_fusion.7), channel_id=1, source_target_pairs={{0,16},{1,17},{2,18},{3,19},{4,20},{5,21},{6,22},{7,23},{8,24},{9,... | collective-permute-start | bytes 1474568 | tf_op jit(solution)/shard_map/ppermute | solution.py:24
  58.5 4.7 %collective-permute-start.15 = (f32[2560]{0:T(1024)S(1)}, f32[2560]{0:T(1024)S(1)}, u32[]{:S(2)}, u32[]{:S(2)}) collective-permute-start(f32[2560]{0:T(1024)S(1)} %get-tuple-element.101), channel_id=1, source_target_pairs={{0,8},{1,9},{2,10},{3,11},{4,12},{5,13},{6,14},{7,15},{8,0},{9,1},... | collective-permute-start | bytes 30728 | tf_op jit(solution)/shard_map/ppermute | solution.py:24
  59.3 4.1 %collective-permute-start.17 = (f32[2560]{0:T(1024)S(1)}, f32[2560]{0:T(1024)S(1)}, u32[]{:S(2)}, u32[]{:S(2)}) collective-permute-start(f32[2560]{0:T(1024)S(1)} %get-tuple-element.99), channel_id=1, source_target_pairs={{0,4},{1,5},{2,6},{3,7},{4,0},{5,1},{6,2},{7,3},{8,12},{9,13},{10,... | collective-permute-start | bytes 30728 | tf_op jit(solution)/shard_map/ppermute | solution.py:24
  61.8 4.1 %collective-permute-start.20 = (f16[96,2560]{1,0:T(8,128)(2,1)S(1)}, f16[96,2560]{1,0:T(8,128)(2,1)S(1)}, u32[]{:S(2)}, u32[]{:S(2)}) collective-permute-start(f16[96,2560]{1,0:T(8,128)(2,1)S(1)} %get-tuple-element.105), channel_id=1, source_target_pairs={{0,1},{1,0},{2,3},{3,2},{4,5},{5,4},{6,7},{7,6},{8,9},{9,8},{10,11... | collective-permute-start | bytes 1474568 | tf_op jit(solution)/shard_map/ppermute | solution.py:24
  63.2 2.7 %collective-permute-start.23 = (f16[96,2560]{1,0:T(8,128)(2,1)S(1)}, f16[96,2560]{1,0:T(8,128)(2,1)S(1)}, u32[]{:S(2)}, u32[]{:S(2)}) collective-permute-start(f16[96,2560]{1,0:T(8,128)(2,1)S(1)} %get-tuple-element.106), channel_id=1, source_target_pairs={{0,1},{1,0},{2,3},{3,2},{4,5},{5,4},{6,7},{7,6},{8,9},{9,8},{10,11... | collective-permute-start | bytes 1474568 | tf_op jit(solution)/shard_map/ppermute | solution.py:24
  65.1 23.6 %collective-permute-start.19 = (f16[96,2560]{1,0:T(8,128)(2,1)S(1)}, f16[96,2560]{1,0:T(8,128)(2,1)S(1)}, u32[]{:S(2)}, u32[]{:S(2)}) collective-permute-start(f16[96,2560]{1,0:T(8,128)(2,1)S(1)} %multiply_convert_fusion.5), channel_id=1, source_target_pairs={{0,8},{1,9},{2,10},{3,11},{4,12},{5,13},{6,14},{7,15},{8,0},{9,1},... | collective-permute-start | bytes 1474568 | tf_op jit(solution)/shard_map/ppermute | solution.py:24
  66.4 22.9 %collective-permute-start.21 = (f16[96,2560]{1,0:T(8,128)(2,1)S(1)}, f16[96,2560]{1,0:T(8,128)(2,1)S(1)}, u32[]{:S(2)}, u32[]{:S(2)}) collective-permute-start(f16[96,2560]{1,0:T(8,128)(2,1)S(1)} %get-tuple-element.108), channel_id=1, source_target_pairs={{0,4},{1,5},{2,6},{3,7},{4,0},{5,1},{6,2},{7,3},{8,12},{9,13},{10,... | collective-permute-start | bytes 1474568 | tf_op jit(solution)/shard_map/ppermute | solution.py:24
  69.6 19.7 %collective-permute-start.18 = (f16[96,2560]{1,0:T(8,128)(2,1)S(1)}, f16[96,2560]{1,0:T(8,128)(2,1)S(1)}, u32[]{:S(2)}, u32[]{:S(2)}) collective-permute-start(f16[96,2560]{1,0:T(8,128)(2,1)S(1)} %multiply_convert_fusion.6), channel_id=1, source_target_pairs={{0,2},{1,3},{2,0},{3,1},{4,6},{5,7},{6,4},{7,5},{8,10},{9,11},{10,... | collective-permute-start | bytes 1474568 | tf_op jit(solution)/shard_map/ppermute | solution.py:24
  71.0 19.5 %collective-permute-start.22 = (f16[96,2560]{1,0:T(8,128)(2,1)S(1)}, f16[96,2560]{1,0:T(8,128)(2,1)S(1)}, u32[]{:S(2)}, u32[]{:S(2)}) collective-permute-start(f16[96,2560]{1,0:T(8,128)(2,1)S(1)} %get-tuple-element.104), channel_id=1, source_target_pairs={{0,1},{1,0},{2,3},{3,2},{4,5},{5,4},{6,7},{7,6},{8,9},{9,8},{10,11... | collective-permute-start | bytes 1474568 | tf_op jit(solution)/shard_map/ppermute | solution.py:24
  71.0 19.5 %collective-permute-start.24 = (f16[96,2560]{1,0:T(8,128)(2,1)S(1)}, f16[96,2560]{1,0:T(8,128)(2,1)S(1)}, u32[]{:S(2)}, u32[]{:S(2)}) collective-permute-start(f16[96,2560]{1,0:T(8,128)(2,1)S(1)} %get-tuple-element.107), channel_id=1, source_target_pairs={{0,16},{1,17},{2,18},{3,19},{4,20},{5,21},{6,22},{7,23},{8,24},{9,... | collective-permute-start | bytes 1474568 | tf_op jit(solution)/shard_map/ppermute | solution.py:24

commit v10 on v9

--- a/solution.py
+++ b/solution.py
@@ -109,16 +109,12 @@
     tile = 512 if aux % 512 == 0 else 128
     rows = left[start:start + sum(spans), :]
 
-    def one(k, _):
-        at = pl.ds(pl.multiple_of(k * tile, tile), tile)
-        acc = jnp.dot(rows, right[:, at], preferred_element_type=jnp.float32)
+    for at in range(0, aux, tile):
+        acc = jnp.dot(rows, right[:, at:at + tile], preferred_element_type=jnp.float32)
         low = 0
         for span, out in zip(spans, outs):
-            out[:, at] = acc[low:low + span, :]
+            out[:, at:at + tile] = acc[low:low + span, :]
             low += span
-        return 0
-
-    lax.fori_loop(0, aux // tile, one, 0)
 
 
 def body(orbital_alpha, orbital_beta, occ_alpha, occ_beta, virt_alpha, virt_beta):
@@ -160,10 +156,12 @@
         compiler_params=pltpu.CompilerParams(vmem_limit_bytes=6 * MIB),
         name="energies",
     )(me.reshape(1), occ_alpha, occ_beta, virt_alpha[:, None], virt_beta.reshape(slabs, block))
-    pieces_b, pieces_a, near_a, near_b, ninv = together((pieces_b, pieces_a, near_a, near_b, ninv))
+    beside = exchange(own_b, 0, devices)
+    pieces_b, pieces_a, near_a, near_b, beside, ninv = together((pieces_b, pieces_a, near_a, near_b, beside, ninv))
     pieces_a.update(sent_on({1 << first_a: [near_a]}, alpha_bits[1:]))
     pieces_b.update(sent_on({1 << first_b: [near_b]}, beta_bits[1:-1]))
-    pieces_b = sent_on(pieces_b, [0])
+    pieces_b.update({m | 1: [exchange(v, 0, devices) for v in vs] for m, vs in list(pieces_b.items()) if m})
+    pieces_b[1] = [beside]
 
     def blocks(count):
         return [jax.ShapeDtypeStruct((n, aux), jnp.float32) for n in cut * count]

time: 92 us -> 93.2 us (1.013)
  waiting for transfers between devices: 46.5 us -> 51.9 us
  Pallas kernels: 12.3 us -> 9.72 us
  starting transfers between devices: 25.2 us -> 23.6 us
    ppermute x25, waiting for transfers between devices: 46.5 us -> 51.9 us  [exchange(): lax.ppermute(value, ('grp', 'slab'), [(d, d ^ 1 << bit) for d in range(de...]
    pallas_call x3, Pallas kernels: 5.73 us -> 3.75 us  [contracted(): pl.pallas_call(functools.partial(rows_out, start * width, cut * len(names...]
    ppermute x25, starting transfers between devices: 25.2 us -> 23.6 us  [exchange(): lax.ppermute(value, ('grp', 'slab'), [(d, d ^ 1 << bit) for d in range(de...]
  transfers between devices with their start and end apart: 25 -> 25, of which waited for: 10 -> 10; matrix products, arithmetic and copies ran while one was open for 5% -> 4% of each run, Pallas kernels for 10% -> 8%
where the time goes in v10:
time: 93.2 us; the launch traced here: 92.9 us
  waiting for transfers between devices  51.9 us (56%)
  starting transfers between devices  23.6 us (25%)
  Pallas kernels  9.72 us (10%)
  other arithmetic  3.93 us (4%)
  local copies, waits for them, and re-layouts  3.03 us (3%)
    ppermute x25, waiting for transfers between devices, exchange(): lax.ppermute(value, ('grp', 'slab'), [(d, d ^ 1 << bit) for d in range(de...  51.9 us
    ppermute x25, starting transfers between devices, exchange(): lax.ppermute(value, ('grp', 'slab'), [(d, d ^ 1 << bit) for d in range(de...  23.6 us
    pallas_call x3, Pallas kernels, contracted(): pl.pallas_call(functools.partial(rows_out, start * width, cut * len(names...  3.75 us
    pallas_call x1, Pallas kernels, body(): pl.pallas_call(functools.partial(begin_amplitudes, [p for _, p in all_a[l...  2.57 us
    pallas_call x1, Pallas kernels, body(): pl.pallas_call(functools.partial(end_amplitudes, [p for _, p in all_a[:la...  2.56 us
    reshape x2, other arithmetic, whole(): return parts[0].reshape(orbital_alpha.shape)  2.46 us
  transfers between devices with their start and end apart: 25, of which 10 were waited for; matrix products, arithmetic and copies ran while one was open for 4% of the time, Pallas kernels for 8%

profile of v10, /device:TPU:0, one launch (start us, length us, event | category | flops | bytes accessed | tf_op | source)
XLA Modules:
  0.0 92.9 jit_solution(17727216587078134258)
XLA Ops:
  0.6 4.1 %collective-permute-start.2 = (bf16[96,2560]{1,0:T(8,128)(2,1)}, bf16[96,2560]{1,0:T(8,128)(2,1)S(1)}, u32[]{:S(2)}, u32[]{:S(2)}) collective-permute-start(bf16[96,2560]{1,0:T(8,128)(2,1)} %bitcast.7), channel_id=1, source_target_pairs={{0,8},{1,9},{2,10},{3,11},{4,12},{5,13},{6,14},{7,15},{8,0},{9,1},... | collective-permute-start | bytes 1474568 | tf_op jit(solution)/shard_map/ppermute | solution.py:24
  4.8 1.5 %collective-permute-start.1 = (bf16[96,2560]{1,0:T(8,128)(2,1)}, bf16[96,2560]{1,0:T(8,128)(2,1)S(1)}, u32[]{:S(2)}, u32[]{:S(2)}) collective-permute-start(bf16[96,2560]{1,0:T(8,128)(2,1)} %bitcast.8), channel_id=1, source_target_pairs={{0,2},{1,3},{2,0},{3,1},{4,6},{5,7},{6,4},{7,5},{8,10},{9,11},{10,... | collective-permute-start | bytes 1474568 | tf_op jit(solution)/shard_map/ppermute | solution.py:24
  6.2 1.6 %collective-permute-start.3 = (bf16[96,2560]{1,0:T(8,128)(2,1)}, bf16[96,2560]{1,0:T(8,128)(2,1)}, u32[]{:S(2)}, u32[]{:S(2)}) collective-permute-start(bf16[96,2560]{1,0:T(8,128)(2,1)} %bitcast.11), channel_id=1, source_target_pairs={{0,4},{1,5},{2,6},{3,7},{4,0},{5,1},{6,2},{7,3},{8,12},{9,13},{10,... | collective-permute-start | bytes 1474568 | tf_op jit(solution)/shard_map/ppermute | solution.py:24
  7.8 1.5 %collective-permute-start = (bf16[96,2560]{1,0:T(8,128)(2,1)}, bf16[96,2560]{1,0:T(8,128)(2,1)}, u32[]{:S(2)}, u32[]{:S(2)}) collective-permute-start(bf16[96,2560]{1,0:T(8,128)(2,1)} %bitcast.12), channel_id=1, source_target_pairs={{0,16},{1,17},{2,18},{3,19},{4,20},{5,21},{6,22},{7,23},{8,24},{9,... | collective-permute-start | bytes 1474568 | tf_op jit(solution)/shard_map/ppermute | solution.py:24
  9.3 0.8 reshape.35.vb_ref
  10.1 1.0 %broadcast_in_dim.3.va_ref = f32[1536,1]{1,0:T(8,128)S(1)} reshape(f32[1536]{0:T(1024)} %param.10) | data formatting | bytes 12288 | tf_op jit(solution)/shard_map/broadcast_in_dim | solution.py:158
  11.1 0.6 copy-done.2
  11.7 0.7 copy-done.3
  12.4 0.8 energies.1.refs_9_.refs_3_
  13.2 13.6 %collective-permute-done.2.refs_1_ = bf16[96,2560]{1,0:T(8,128)(2,1)S(1)} collective-permute-done((bf16[96,2560]{1,0:T(8,128)(2,1)}, bf16[96,2560]{1,0:T(8,128)(2,1)S(1)}, u32[]{:S(2)}, u32[]{:S(2)}) %collective-permute-start.2) | collective-permute-done | bytes 491552 | tf_op jit(solution)/shard_map/ppermute | solution.py:24
  26.8 2.7 %collective-permute-done.3.refs_6_ = bf16[96,2560]{1,0:T(8,128)(2,1)} collective-permute-done((bf16[96,2560]{1,0:T(8,128)(2,1)}, bf16[96,2560]{1,0:T(8,128)(2,1)}, u32[]{:S(2)}, u32[]{:S(2)}) %collective-permute-start.3) | collective-permute-done | bytes 491552 | tf_op jit(solution)/shard_map/ppermute | solution.py:24
  29.6 1.6 %collective-permute-start.6 = (bf16[96,2560]{1,0:T(8,128)(2,1)}, bf16[96,2560]{1,0:T(8,128)(2,1)S(1)}, u32[]{:S(2)}, u32[]{:S(2)}) collective-permute-start(bf16[96,2560]{1,0:T(8,128)(2,1)} %collective-permute-done.3.refs_6_), channel_id=1, source_target_pairs={{0,16},{1,17},{2,18},{3,19},{4,20},{5,21},{6,22},{7,23},{8,24},{9,... | collective-permute-start | bytes 1474568 | tf_op jit(solution)/shard_map/ppermute | solution.py:24
  32.2 10.4 %collective-permute-done.6.refs_2_ = bf16[96,2560]{1,0:T(8,128)(2,1)S(1)} collective-permute-done((bf16[96,2560]{1,0:T(8,128)(2,1)}, bf16[96,2560]{1,0:T(8,128)(2,1)S(1)}, u32[]{:S(2)}, u32[]{:S(2)}) %collective-permute-start.6) | collective-permute-done | bytes 491552 | tf_op jit(solution)/shard_map/ppermute | solution.py:24
  42.7 2.6 %amplitudes_early.1 = (bf16[384,768]{1,0:T(8,128)(2,1)S(1)}, bf16[768,384]{1,0:T(8,128)(2,1)S(1)}, bf16[384,2560]{1,0:T(8,128)(2,1)S(1)}, bf16[768,2560]{1,0:T(8,128)(2,1)S(1)}, f32[8,128]{1,0:T(8,128)S(1)}) custom-call(bf16[96,2560]{1,0:T(8,128)(2,1)S(1)} %collective-permute-done.1.refs_0_, bf16[96,2560]{1,0:T(8,128)(2,1)S(1)} %collective-permute-done.2.refs_1_, ...), custom_call_target="tpu_custom_call" | custom-call | flops 671088640 | bytes 11796480 | tf_op jit(solution)/shard_map/amplitudes_early/pallas_call | solution.py:194
  45.3 2.6 %amplitudes_late.1 = (bf16[384,768]{1,0:T(8,128)(2,1)S(1)}, bf16[768,384]{1,0:T(8,128)(2,1)S(1)}, bf16[384,2560]{1,0:T(8,128)(2,1)S(1)}, bf16[768,2560]{1,0:T(8,...) custom-call(bf16[96,2560]{1,0:T(8,128)(2,1)S(1)} %collective-permute, ...), custom_call_target="tpu_custom_call", output_to_operand_aliasing={{0}: (4, {}), {1}: (5, {}), {2}: (6, {}), {3}: (7, {})} | custom-call | flops 1509949440 | bytes 11796480 | tf_op jit(solution)/shard_map/amplitudes_late/pallas_call | solution.py:202
  48.6 0.8 alpha_first.1
  49.5 1.0 %collective-permute-done.10 = f16[96,2560]{1,0:T(8,128)(2,1)S(1)} collective-permute-done((f16[96,2560]{1,0:T(8,128)(2,1)S(1)}, f16[96,2560]{1,0:T(8,128)(2,1)S(1)}, u32[]{:S(2)}, u32[]{:S(2)}) %collective-permute-start.10) | collective-permute-done | bytes 491552 | tf_op jit(solution)/shard_map/ppermute | solution.py:24
  50.6 0.6 collective-permute-start.14
  51.3 1.5 %collective-permute-start.16 = (f32[2560]{0:T(1024)S(1)}, f32[2560]{0:T(1024)S(1)}, u32[]{:S(2)}, u32[]{:S(2)}) collective-permute-start(f32[2560]{0:T(1024)S(1)} %get-tuple-element.81), channel_id=1, source_target_pairs={{0,16},{1,17},{2,18},{3,19},{4,20},{5,21},{6,22},{7,23},{8,24},{9,... | collective-permute-start | bytes 30728 | tf_op jit(solution)/shard_map/ppermute | solution.py:24
  52.8 1.5 %collective-permute-start.12 = (f16[96,2560]{1,0:T(8,128)(2,1)S(1)}, f16[96,2560]{1,0:T(8,128)(2,1)S(1)}, u32[]{:S(2)}, u32[]{:S(2)}) collective-permute-start(f16[96,2560]{1,0:T(8,128)(2,1)S(1)} %multiply_convert_fusion.9), channel_id=1, source_target_pairs={{0,2},{1,3},{2,0},{3,1},{4,6},{5,7},{6,4},{7,5},{8,10},{9,11},{10,... | collective-permute-start | bytes 1474568 | tf_op jit(solution)/shard_map/ppermute | solution.py:24
  54.8 1.7 %beta.1 = (f32[96,2560]{1,0:T(8,128)S(1)}, f32[96,2560]{1,0:T(8,128)S(1)}, f32[96,2560]{1,0:T(8,128)S(1)}, f32[96,2560]{1,0:T(8,128)S(1)}, f32[96,2560]{1,0:T(8,128)S(1)}, /*index=5*/f32[96,2560]{1,0:T(8,128)S(1)}) custom-call(bf16[768,384]{1,0:T(8,128)(2,1)S(1)} %get-tuple-element.86.left, bf16[384,2560]{1,0:T(8,128)(2,1)S(1)} %get-tuple-element.87.right), custom_call_target="tpu_custom_call" | custom-call | flops 1132462080 | bytes 7864320 | tf_op jit(solution)/shard_map/beta/pallas_call | solution.py:215
  56.7 1.3 %alpha.1 = (f32[96,2560]{1,0:T(8,128)S(1)}, f32[96,2560]{1,0:T(8,128)S(1)}, f32[96,2560]{1,0:T(8,128)S(1)}) custom-call(bf16[384,768]{1,0:T(8,128)(2,1)S(1)} %get-tuple-element.74.left, bf16[768,2560]{1,0:T(8,128)(2,1)S(1)} %get-tuple-element.75.right), custom_call_target="tpu_custom_call" | custom-call | flops 1132462080 | bytes 6881280 | tf_op jit(solution)/shard_map/alpha/pallas_call | solution.py:215
  58.6 2.5 %collective-permute-start.17 = (f32[2560]{0:T(1024)S(1)}, f32[2560]{0:T(1024)S(1)}, u32[]{:S(2)}, u32[]{:S(2)}) collective-permute-start(f32[2560]{0:T(1024)S(1)} %get-tuple-element.101), channel_id=1, source_target_pairs={{0,4},{1,5},{2,6},{3,7},{4,0},{5,1},{6,2},{7,3},{8,12},{9,13},{10,... | collective-permute-start | bytes 30728 | tf_op jit(solution)/shard_map/ppermute | solution.py:24
  61.3 1.4 %collective-permute-done.15 = f32[2560]{0:T(1024)S(1)} collective-permute-done((f32[2560]{0:T(1024)S(1)}, f32[2560]{0:T(1024)S(1)}, u32[]{:S(2)}, u32[]{:S(2)}) %collective-permute-start.15) | collective-permute-done | bytes 10272 | tf_op jit(solution)/shard_map/ppermute | solution.py:24
  62.8 2.7 %collective-permute-done.12 = f16[96,2560]{1,0:T(8,128)(2,1)S(1)} collective-permute-done((f16[96,2560]{1,0:T(8,128)(2,1)S(1)}, f16[96,2560]{1,0:T(8,128)(2,1)S(1)}, u32[]{:S(2)}, u32[]{:S(2)}) %collective-permute-start.12) | collective-permute-done | bytes 491552 | tf_op jit(solution)/shard_map/ppermute | solution.py:24
  65.5 1.2 %collective-permute-done.13 = f16[96,2560]{1,0:T(8,128)(2,1)S(1)} collective-permute-done((f16[96,2560]{1,0:T(8,128)(2,1)S(1)}, f16[96,2560]{1,0:T(8,128)(2,1)S(1)}, u32[]{:S(2)}, u32[]{:S(2)}) %collective-permute-start.13) | collective-permute-done | bytes 491552 | tf_op jit(solution)/shard_map/ppermute | solution.py:24
  68.0 2.6 %collective-permute-start.21 = (f16[96,2560]{1,0:T(8,128)(2,1)S(1)}, f16[96,2560]{1,0:T(8,128)(2,1)S(1)}, u32[]{:S(2)}, u32[]{:S(2)}) collective-permute-start(f16[96,2560]{1,0:T(8,128)(2,1)S(1)} %get-tuple-element.110), channel_id=1, source_target_pairs={{0,4},{1,5},{2,6},{3,7},{4,0},{5,1},{6,2},{7,3},{8,12},{9,13},{10,... | collective-permute-start | bytes 1474568 | tf_op jit(solution)/shard_map/ppermute | solution.py:24
  71.1 0.7 collective-permute-start.24
  71.8 18.0 %collective-permute-done.19 = f16[96,2560]{1,0:T(8,128)(2,1)S(1)} collective-permute-done((f16[96,2560]{1,0:T(8,128)(2,1)S(1)}, f16[96,2560]{1,0:T(8,128)(2,1)S(1)}, u32[]{:S(2)}, u32[]{:S(2)}) %collective-permute-start.19) | collective-permute-done | bytes 491552 | tf_op jit(solution)/shard_map/ppermute | solution.py:24
  89.8 0.7 collective-permute-done.21
  90.5 1.2 %add_bitcast_fusion.1 = f32[1,96,2560]{2,1,0:T(8,128)} fusion(f16[96,2560]{1,0:T(8,128)(2,1)S(1)} %collective-permute-done.19, f32[96,2560]{1,0:T(8,128)S(1)} %get-tuple-element.76, f16[96,2560]{1,0:T(8,128)(2,1)S(1)} %collective-permute-done.18, f32[2560]{0:T(1024)S(1)} %collective-permute-done.15, f32[2560]{0:T(1024)S(1)} %collective-permute-done.14), kind=kLoop, calls=%fused_computation.4 | loop fusion | flops 1474560 | bytes 2969600 | tf_op jit(solution)/shard_map/reshape | solution.py:297
  91.6 1.3 %add_bitcast_fusion = f32[1,96,2560]{2,1,0:T(8,128)} fusion(f16[96,2560]{1,0:T(8,128)(2,1)S(1)} %collective-permute-done.21, f16[96,2560]{1,0:T(8,128)(2,1)S(1)} %collective-permute-done.24, f32[96,2560]{1,0:T(8,128)S(1)} %get-tuple-element.94, f16[96,2560]{1,0:T(8,128)(2,1)S(1)} %collective-permute-done.22, f32[2560]{0:T(1024)S(1)} %collective-permute-done.17, ...), kind=kLoop, calls=%fused_computation | loop fusion | flops 2211840 | bytes 3471360 | tf_op jit(solution)/shard_map/reshape | solution.py:297
  (46 shorter events, 5.6 us)
Async XLA Ops:
  0.6 42.0 %copy-start = (bf16[1,96,2560]{2,1,0:T(8,128)(2,1)S(1)}, bf16[1,96,2560]{2,1,0:T(8,128)(2,1)}, u32[]{:S(2)}) copy-start(bf16[1,96,2560]{2,1,0:T(8,128)(2,1)} %param.6) | copy-start | bytes 1474564
  0.6 42.0 %copy-start.1 = (bf16[1,96,2560]{2,1,0:T(8,128)(2,1)S(1)}, bf16[1,96,2560]{2,1,0:T(8,128)(2,1)}, u32[]{:S(2)}) copy-start(bf16[1,96,2560]{2,1,0:T(8,128)(2,1)} %param.7) | copy-start | bytes 1474564
  0.6 26.2 %collective-permute-start.2 = (bf16[96,2560]{1,0:T(8,128)(2,1)}, bf16[96,2560]{1,0:T(8,128)(2,1)S(1)}, u32[]{:S(2)}, u32[]{:S(2)}) collective-permute-start(bf16[96,2560]{1,0:T(8,128)(2,1)} %bitcast.7), channel_id=1, source_target_pairs={{0,8},{1,9},{2,10},{3,11},{4,12},{5,13},{6,14},{7,15},{8,0},{9,1},... | collective-permute-start | bytes 1474568 | tf_op jit(solution)/shard_map/ppermute | solution.py:24
  4.8 22.1 %collective-permute-start.1 = (bf16[96,2560]{1,0:T(8,128)(2,1)}, bf16[96,2560]{1,0:T(8,128)(2,1)S(1)}, u32[]{:S(2)}, u32[]{:S(2)}) collective-permute-start(bf16[96,2560]{1,0:T(8,128)(2,1)} %bitcast.8), channel_id=1, source_target_pairs={{0,2},{1,3},{2,0},{3,1},{4,6},{5,7},{6,4},{7,5},{8,10},{9,11},{10,... | collective-permute-start | bytes 1474568 | tf_op jit(solution)/shard_map/ppermute | solution.py:24
  6.2 20.6 %collective-permute-start.4 = (bf16[96,2560]{1,0:T(8,128)(2,1)}, bf16[96,2560]{1,0:T(8,128)(2,1)S(1)}, u32[]{:S(2)}, u32[]{:S(2)}) collective-permute-start(bf16[96,2560]{1,0:T(8,128)(2,1)} %bitcast.10), channel_id=1, source_target_pairs={{0,1},{1,0},{2,3},{3,2},{4,5},{5,4},{6,7},{7,6},{8,9},{9,8},{10,11... | collective-permute-start | bytes 1474568 | tf_op jit(solution)/shard_map/ppermute | solution.py:24
  6.2 23.3 %collective-permute-start.3 = (bf16[96,2560]{1,0:T(8,128)(2,1)}, bf16[96,2560]{1,0:T(8,128)(2,1)}, u32[]{:S(2)}, u32[]{:S(2)}) collective-permute-start(bf16[96,2560]{1,0:T(8,128)(2,1)} %bitcast.11), channel_id=1, source_target_pairs={{0,4},{1,5},{2,6},{3,7},{4,0},{5,1},{6,2},{7,3},{8,12},{9,13},{10,... | collective-permute-start | bytes 1474568 | tf_op jit(solution)/shard_map/ppermute | solution.py:24
  7.8 21.7 %collective-permute-start = (bf16[96,2560]{1,0:T(8,128)(2,1)}, bf16[96,2560]{1,0:T(8,128)(2,1)}, u32[]{:S(2)}, u32[]{:S(2)}) collective-permute-start(bf16[96,2560]{1,0:T(8,128)(2,1)} %bitcast.12), channel_id=1, source_target_pairs={{0,16},{1,17},{2,18},{3,19},{4,20},{5,21},{6,22},{7,23},{8,24},{9,... | collective-permute-start | bytes 1474568 | tf_op jit(solution)/shard_map/ppermute | solution.py:24
  11.1 0.7 copy-start.2
  11.7 0.7 copy-start.3
  29.6 13.1 %collective-permute-start.6 = (bf16[96,2560]{1,0:T(8,128)(2,1)}, bf16[96,2560]{1,0:T(8,128)(2,1)S(1)}, u32[]{:S(2)}, u32[]{:S(2)}) collective-permute-start(bf16[96,2560]{1,0:T(8,128)(2,1)} %collective-permute-done.3.refs_6_), channel_id=1, source_target_pairs={{0,16},{1,17},{2,18},{3,19},{4,20},{5,21},{6,22},{7,23},{8,24},{9,... | collective-permute-start | bytes 1474568 | tf_op jit(solution)/shard_map/ppermute | solution.py:24
  31.1 11.5 %collective-permute-start.8 = (bf16[96,2560]{1,0:T(8,128)(2,1)}, bf16[96,2560]{1,0:T(8,128)(2,1)S(1)}, u32[]{:S(2)}, u32[]{:S(2)}) collective-permute-start(bf16[96,2560]{1,0:T(8,128)(2,1)} %collective-permute-done.refs_4_), channel_id=1, source_target_pairs={{0,1},{1,0},{2,3},{3,2},{4,5},{5,4},{6,7},{7,6},{8,9},{9,8},{10,11... | collective-permute-start | bytes 1474568 | tf_op jit(solution)/shard_map/ppermute | solution.py:24
  31.1 11.5 %collective-permute-start.9 = (bf16[96,2560]{1,0:T(8,128)(2,1)}, bf16[96,2560]{1,0:T(8,128)(2,1)S(1)}, u32[]{:S(2)}, u32[]{:S(2)}) collective-permute-start(bf16[96,2560]{1,0:T(8,128)(2,1)} %collective-permute-done.3.refs_6_), channel_id=1, source_target_pairs={{0,1},{1,0},{2,3},{3,2},{4,5},{5,4},{6,7},{7,6},{8,9},{9,8},{10,11... | collective-permute-start | bytes 1474568 | tf_op jit(solution)/shard_map/ppermute | solution.py:24
  31.7 13.6 %collective-permute-start.5 = (bf16[96,2560]{1,0:T(8,128)(2,1)S(1)}, bf16[96,2560]{1,0:T(8,128)(2,1)S(1)}, u32[]{:S(2)}, u32[]{:S(2)}) collective-permute-start(bf16[96,2560]{1,0:T(8,128)(2,1)S(1)} %collective-permute-done.2.refs_1_), channel_id=1, source_target_pairs={{0,2},{1,3},{2,0},{3,1},{4,6},{5,7},{6,4},{7,5},{8,10},{9,11},{10,... | collective-permute-start | bytes 1474568 | tf_op jit(solution)/shard_map/ppermute | solution.py:24
  42.6 2.6 %collective-permute-start.7 = (bf16[96,2560]{1,0:T(8,128)(2,1)S(1)}, bf16[96,2560]{1,0:T(8,128)(2,1)S(1)}, u32[]{:S(2)}, u32[]{:S(2)}) collective-permute-start(bf16[96,2560]{1,0:T(8,128)(2,1)S(1)} %collective-permute-done.6.refs_2_), channel_id=1, source_target_pairs={{0,1},{1,0},{2,3},{3,2},{4,5},{5,4},{6,7},{7,6},{8,9},{9,8},{10,11... | collective-permute-start | bytes 1474568 | tf_op jit(solution)/shard_map/ppermute | solution.py:24
  47.8 1.6 %collective-permute-start.11 = (f32[2560]{0:T(1024)S(1)}, f32[2560]{0:T(1024)S(1)}, u32[]{:S(2)}, u32[]{:S(2)}) collective-permute-start(f32[2560]{0:T(1024)S(1)} %get-tuple-element.70), channel_id=1, source_target_pairs={{0,1},{1,0},{2,3},{3,2},{4,5},{5,4},{6,7},{7,6},{8,9},{9,8},{10,11... | collective-permute-start | bytes 30728 | tf_op jit(solution)/shard_map/ppermute | solution.py:24
  48.5 1.9 %collective-permute-start.10 = (f16[96,2560]{1,0:T(8,128)(2,1)S(1)}, f16[96,2560]{1,0:T(8,128)(2,1)S(1)}, u32[]{:S(2)}, u32[]{:S(2)}) collective-permute-start(f16[96,2560]{1,0:T(8,128)(2,1)S(1)} %multiply_convert_fusion.8), channel_id=1, source_target_pairs={{0,1},{1,0},{2,3},{3,2},{4,5},{5,4},{6,7},{7,6},{8,9},{9,8},{10,11... | collective-permute-start | bytes 1474568 | tf_op jit(solution)/shard_map/ppermute | solution.py:24
  50.6 7.4 %collective-permute-start.14 = (f32[2560]{0:T(1024)S(1)}, f32[2560]{0:T(1024)S(1)}, u32[]{:S(2)}, u32[]{:S(2)}) collective-permute-start(f32[2560]{0:T(1024)S(1)} %get-tuple-element.80), channel_id=1, source_target_pairs={{0,2},{1,3},{2,0},{3,1},{4,6},{5,7},{6,4},{7,5},{8,10},{9,11},{10,... | collective-permute-start | bytes 30728 | tf_op jit(solution)/shard_map/ppermute | solution.py:24
  51.3 7.3 %collective-permute-start.16 = (f32[2560]{0:T(1024)S(1)}, f32[2560]{0:T(1024)S(1)}, u32[]{:S(2)}, u32[]{:S(2)}) collective-permute-start(f32[2560]{0:T(1024)S(1)} %get-tuple-element.81), channel_id=1, source_target_pairs={{0,16},{1,17},{2,18},{3,19},{4,20},{5,21},{6,22},{7,23},{8,24},{9,... | collective-permute-start | bytes 30728 | tf_op jit(solution)/shard_map/ppermute | solution.py:24
  52.8 12.7 %collective-permute-start.12 = (f16[96,2560]{1,0:T(8,128)(2,1)S(1)}, f16[96,2560]{1,0:T(8,128)(2,1)S(1)}, u32[]{:S(2)}, u32[]{:S(2)}) collective-permute-start(f16[96,2560]{1,0:T(8,128)(2,1)S(1)} %multiply_convert_fusion.9), channel_id=1, source_target_pairs={{0,2},{1,3},{2,0},{3,1},{4,6},{5,7},{6,4},{7,5},{8,10},{9,11},{10,... | collective-permute-start | bytes 1474568 | tf_op jit(solution)/shard_map/ppermute | solution.py:24
  54.3 12.4 %collective-permute-start.13 = (f16[96,2560]{1,0:T(8,128)(2,1)S(1)}, f16[96,2560]{1,0:T(8,128)(2,1)S(1)}, u32[]{:S(2)}, u32[]{:S(2)}) collective-permute-start(f16[96,2560]{1,0:T(8,128)(2,1)S(1)} %multiply_convert_fusion.7), channel_id=1, source_target_pairs={{0,16},{1,17},{2,18},{3,19},{4,20},{5,21},{6,22},{7,23},{8,24},{9,... | collective-permute-start | bytes 1474568 | tf_op jit(solution)/shard_map/ppermute | solution.py:24
  58.1 4.7 %collective-permute-start.15 = (f32[2560]{0:T(1024)S(1)}, f32[2560]{0:T(1024)S(1)}, u32[]{:S(2)}, u32[]{:S(2)}) collective-permute-start(f32[2560]{0:T(1024)S(1)} %get-tuple-element.103), channel_id=1, source_target_pairs={{0,8},{1,9},{2,10},{3,11},{4,12},{5,13},{6,14},{7,15},{8,0},{9,1},... | collective-permute-start | bytes 30728 | tf_op jit(solution)/shard_map/ppermute | solution.py:24
  58.6 4.2 %collective-permute-start.17 = (f32[2560]{0:T(1024)S(1)}, f32[2560]{0:T(1024)S(1)}, u32[]{:S(2)}, u32[]{:S(2)}) collective-permute-start(f32[2560]{0:T(1024)S(1)} %get-tuple-element.101), channel_id=1, source_target_pairs={{0,4},{1,5},{2,6},{3,7},{4,0},{5,1},{6,2},{7,3},{8,12},{9,13},{10,... | collective-permute-start | bytes 30728 | tf_op jit(solution)/shard_map/ppermute | solution.py:24
  61.2 6.2 %collective-permute-start.20 = (f16[96,2560]{1,0:T(8,128)(2,1)S(1)}, f16[96,2560]{1,0:T(8,128)(2,1)S(1)}, u32[]{:S(2)}, u32[]{:S(2)}) collective-permute-start(f16[96,2560]{1,0:T(8,128)(2,1)S(1)} %get-tuple-element.107), channel_id=1, source_target_pairs={{0,1},{1,0},{2,3},{3,2},{4,5},{5,4},{6,7},{7,6},{8,9},{9,8},{10,11... | collective-permute-start | bytes 1474568 | tf_op jit(solution)/shard_map/ppermute | solution.py:24
  62.7 4.7 %collective-permute-start.23 = (f16[96,2560]{1,0:T(8,128)(2,1)S(1)}, f16[96,2560]{1,0:T(8,128)(2,1)S(1)}, u32[]{:S(2)}, u32[]{:S(2)}) collective-permute-start(f16[96,2560]{1,0:T(8,128)(2,1)S(1)} %get-tuple-element.108), channel_id=1, source_target_pairs={{0,1},{1,0},{2,3},{3,2},{4,5},{5,4},{6,7},{7,6},{8,9},{9,8},{10,11... | collective-permute-start | bytes 1474568 | tf_op jit(solution)/shard_map/ppermute | solution.py:24
  66.9 22.8 %collective-permute-start.19 = (f16[96,2560]{1,0:T(8,128)(2,1)S(1)}, f16[96,2560]{1,0:T(8,128)(2,1)S(1)}, u32[]{:S(2)}, u32[]{:S(2)}) collective-permute-start(f16[96,2560]{1,0:T(8,128)(2,1)S(1)} %multiply_convert_fusion.5), channel_id=1, source_target_pairs={{0,8},{1,9},{2,10},{3,11},{4,12},{5,13},{6,14},{7,15},{8,0},{9,1},... | collective-permute-start | bytes 1474568 | tf_op jit(solution)/shard_map/ppermute | solution.py:24
  68.0 22.5 %collective-permute-start.21 = (f16[96,2560]{1,0:T(8,128)(2,1)S(1)}, f16[96,2560]{1,0:T(8,128)(2,1)S(1)}, u32[]{:S(2)}, u32[]{:S(2)}) collective-permute-start(f16[96,2560]{1,0:T(8,128)(2,1)S(1)} %get-tuple-element.110), channel_id=1, source_target_pairs={{0,4},{1,5},{2,6},{3,7},{4,0},{5,1},{6,2},{7,3},{8,12},{9,13},{10,... | collective-permute-start | bytes 1474568 | tf_op jit(solution)/shard_map/ppermute | solution.py:24
  70.5 20.0 %collective-permute-start.18 = (f16[96,2560]{1,0:T(8,128)(2,1)S(1)}, f16[96,2560]{1,0:T(8,128)(2,1)S(1)}, u32[]{:S(2)}, u32[]{:S(2)}) collective-permute-start(f16[96,2560]{1,0:T(8,128)(2,1)S(1)} %multiply_convert_fusion.6), channel_id=1, source_target_pairs={{0,2},{1,3},{2,0},{3,1},{4,6},{5,7},{6,4},{7,5},{8,10},{9,11},{10,... | collective-permute-start | bytes 1474568 | tf_op jit(solution)/shard_map/ppermute | solution.py:24
  71.1 20.5 %collective-permute-start.22 = (f16[96,2560]{1,0:T(8,128)(2,1)S(1)}, f16[96,2560]{1,0:T(8,128)(2,1)S(1)}, u32[]{:S(2)}, u32[]{:S(2)}) collective-permute-start(f16[96,2560]{1,0:T(8,128)(2,1)S(1)} %get-tuple-element.106), channel_id=1, source_target_pairs={{0,1},{1,0},{2,3},{3,2},{4,5},{5,4},{6,7},{7,6},{8,9},{9,8},{10,11... | collective-permute-start | bytes 1474568 | tf_op jit(solution)/shard_map/ppermute | solution.py:24
  71.1 20.5 %collective-permute-start.24 = (f16[96,2560]{1,0:T(8,128)(2,1)S(1)}, f16[96,2560]{1,0:T(8,128)(2,1)S(1)}, u32[]{:S(2)}, u32[]{:S(2)}) collective-permute-start(f16[96,2560]{1,0:T(8,128)(2,1)S(1)} %get-tuple-element.109), channel_id=1, source_target_pairs={{0,16},{1,17},{2,18},{3,19},{4,20},{5,21},{6,22},{7,23},{8,24},{9,... | collective-permute-start | bytes 1474568 | tf_op jit(solution)/shard_map/ppermute | solution.py:24

commit v11 on v10

--- a/solution.py
+++ b/solution.py
@@ -156,12 +156,10 @@
         compiler_params=pltpu.CompilerParams(vmem_limit_bytes=6 * MIB),
         name="energies",
     )(me.reshape(1), occ_alpha, occ_beta, virt_alpha[:, None], virt_beta.reshape(slabs, block))
-    beside = exchange(own_b, 0, devices)
-    pieces_b, pieces_a, near_a, near_b, beside, ninv = together((pieces_b, pieces_a, near_a, near_b, beside, ninv))
+    pieces_b, pieces_a, near_a, near_b, ninv = together((pieces_b, pieces_a, near_a, near_b, ninv))
     pieces_a.update(sent_on({1 << first_a: [near_a]}, alpha_bits[1:]))
     pieces_b.update(sent_on({1 << first_b: [near_b]}, beta_bits[1:-1]))
-    pieces_b.update({m | 1: [exchange(v, 0, devices) for v in vs] for m, vs in list(pieces_b.items()) if m})
-    pieces_b[1] = [beside]
+    pieces_b = sent_on(pieces_b, [0])
 
     def blocks(count):
         return [jax.ShapeDtypeStruct((n, aux), jnp.float32) for n in cut * count]

time: 93.2 us -> 91.1 us (0.977)
  waiting for transfers between devices: 51.9 us -> 48.3 us
  starting transfers between devices: 23.6 us -> 25.2 us
    ppermute x25, waiting for transfers between devices: 51.9 us -> 48.3 us  [exchange(): lax.ppermute(value, ('grp', 'slab'), [(d, d ^ 1 << bit) for d in range(de...]
    ppermute x25, starting transfers between devices: 23.6 us -> 25.2 us  [exchange(): lax.ppermute(value, ('grp', 'slab'), [(d, d ^ 1 << bit) for d in range(de...]
  transfers between devices with their start and end apart: 25 -> 25, of which waited for: 10 -> 11; matrix products, arithmetic and copies ran while one was open for 4% -> 5% of each run, Pallas kernels for 8% -> 8%
where the time goes in v11:
time: 91.1 us; the launch traced here: 90.8 us
  waiting for transfers between devices  48.3 us (53%)
  starting transfers between devices  25.2 us (28%)
  Pallas kernels  9.57 us (11%)
  other arithmetic  3.93 us (4%)
  local copies, waits for them, and re-layouts  3.03 us (3%)
    ppermute x25, waiting for transfers between devices, exchange(): lax.ppermute(value, ('grp', 'slab'), [(d, d ^ 1 << bit) for d in range(de...  48.3 us
    ppermute x25, starting transfers between devices, exchange(): lax.ppermute(value, ('grp', 'slab'), [(d, d ^ 1 << bit) for d in range(de...  25.2 us
    pallas_call x3, Pallas kernels, contracted(): pl.pallas_call(functools.partial(rows_out, start * width, cut * len(names...  3.75 us
    pallas_call x1, Pallas kernels, body(): pl.pallas_call(functools.partial(end_amplitudes, [p for _, p in all_a[:la...  2.55 us
    reshape x2, other arithmetic, whole(): return parts[0].reshape(orbital_alpha.shape)  2.46 us
    pallas_call x1, Pallas kernels, body(): pl.pallas_call(functools.partial(begin_amplitudes, [p for _, p in all_a[l...  2.43 us
  transfers between devices with their start and end apart: 25, of which 11 were waited for; matrix products, arithmetic and copies ran while one was open for 5% of the time, Pallas kernels for 8%

profile of v11, /device:TPU:0, one launch (start us, length us, event | category | flops | bytes accessed | tf_op | source)
XLA Modules:
  0.0 90.8 jit_solution(5920454468899319011)
XLA Ops:
  0.6 4.1 %collective-permute-start.2 = (bf16[96,2560]{1,0:T(8,128)(2,1)}, bf16[96,2560]{1,0:T(8,128)(2,1)S(1)}, u32[]{:S(2)}, u32[]{:S(2)}) collective-permute-start(bf16[96,2560]{1,0:T(8,128)(2,1)} %bitcast.7), channel_id=1, source_target_pairs={{0,8},{1,9},{2,10},{3,11},{4,12},{5,13},{6,14},{7,15},{8,0},{9,1},... | collective-permute-start | bytes 1474568 | tf_op jit(solution)/shard_map/ppermute | solution.py:24
  4.8 1.5 %collective-permute-start.1 = (bf16[96,2560]{1,0:T(8,128)(2,1)}, bf16[96,2560]{1,0:T(8,128)(2,1)S(1)}, u32[]{:S(2)}, u32[]{:S(2)}) collective-permute-start(bf16[96,2560]{1,0:T(8,128)(2,1)} %bitcast.8), channel_id=1, source_target_pairs={{0,2},{1,3},{2,0},{3,1},{4,6},{5,7},{6,4},{7,5},{8,10},{9,11},{10,... | collective-permute-start | bytes 1474568 | tf_op jit(solution)/shard_map/ppermute | solution.py:24
  6.2 1.6 %collective-permute-start.3 = (bf16[96,2560]{1,0:T(8,128)(2,1)}, bf16[96,2560]{1,0:T(8,128)(2,1)S(1)}, u32[]{:S(2)}, u32[]{:S(2)}) collective-permute-start(bf16[96,2560]{1,0:T(8,128)(2,1)} %bitcast.10), channel_id=1, source_target_pairs={{0,4},{1,5},{2,6},{3,7},{4,0},{5,1},{6,2},{7,3},{8,12},{9,13},{10,... | collective-permute-start | bytes 1474568 | tf_op jit(solution)/shard_map/ppermute | solution.py:24
  7.8 1.5 %collective-permute-start = (bf16[96,2560]{1,0:T(8,128)(2,1)}, bf16[96,2560]{1,0:T(8,128)(2,1)}, u32[]{:S(2)}, u32[]{:S(2)}) collective-permute-start(bf16[96,2560]{1,0:T(8,128)(2,1)} %bitcast.11), channel_id=1, source_target_pairs={{0,16},{1,17},{2,18},{3,19},{4,20},{5,21},{6,22},{7,23},{8,24},{9,... | collective-permute-start | bytes 1474568 | tf_op jit(solution)/shard_map/ppermute | solution.py:24
  9.3 0.8 reshape.35.vb_ref
  10.1 1.0 %broadcast_in_dim.3.va_ref = f32[1536,1]{1,0:T(8,128)S(1)} reshape(f32[1536]{0:T(1024)} %param.10) | data formatting | bytes 12288 | tf_op jit(solution)/shard_map/broadcast_in_dim | solution.py:158
  11.7 0.7 copy-done.3
  12.4 0.8 energies.1.refs_9_.refs_3_
  13.2 13.6 %collective-permute-done.2.refs_1_ = bf16[96,2560]{1,0:T(8,128)(2,1)S(1)} collective-permute-done((bf16[96,2560]{1,0:T(8,128)(2,1)}, bf16[96,2560]{1,0:T(8,128)(2,1)S(1)}, u32[]{:S(2)}, u32[]{:S(2)}) %collective-permute-start.2) | collective-permute-done | bytes 491552 | tf_op jit(solution)/shard_map/ppermute | solution.py:24
  26.8 1.4 %collective-permute-done.3.refs_6_ = bf16[96,2560]{1,0:T(8,128)(2,1)S(1)} collective-permute-done((bf16[96,2560]{1,0:T(8,128)(2,1)}, bf16[96,2560]{1,0:T(8,128)(2,1)S(1)}, u32[]{:S(2)}, u32[]{:S(2)}) %collective-permute-start.3) | collective-permute-done | bytes 491552 | tf_op jit(solution)/shard_map/ppermute | solution.py:24
  28.2 1.6 %collective-permute-start.5 = (bf16[96,2560]{1,0:T(8,128)(2,1)S(1)}, bf16[96,2560]{1,0:T(8,128)(2,1)S(1)}, u32[]{:S(2)}, u32[]{:S(2)}) collective-permute-start(bf16[96,2560]{1,0:T(8,128)(2,1)S(1)} %collective-permute-done.3.refs_6_), channel_id=1, source_target_pairs={{0,16},{1,17},{2,18},{3,19},{4,20},{5,21},{6,22},{7,23},{8,24},{9,... | collective-permute-start | bytes 1474568 | tf_op jit(solution)/shard_map/ppermute | solution.py:24
  30.9 8.4 %collective-permute-done.5.refs_2_ = bf16[96,2560]{1,0:T(8,128)(2,1)S(1)} collective-permute-done((bf16[96,2560]{1,0:T(8,128)(2,1)S(1)}, bf16[96,2560]{1,0:T(8,128)(2,1)S(1)}, u32[]{:S(2)}, u32[]{:S(2)}) %collective-permute-start.5) | collective-permute-done | bytes 491552 | tf_op jit(solution)/shard_map/ppermute | solution.py:24
  39.3 2.4 %amplitudes_early.1 = (bf16[384,768]{1,0:T(8,128)(2,1)S(1)}, bf16[768,384]{1,0:T(8,128)(2,1)S(1)}, bf16[384,2560]{1,0:T(8,128)(2,1)S(1)}, bf16[768,2560]{1,0:T(8,128)(2,1)S(1)}, f32[8,128]{1,0:T(8,128)S(1)}) custom-call(bf16[96,2560]{1,0:T(8,128)(2,1)S(1)} %collective-permute-done.1.refs_0_, bf16[96,2560]{1,0:T(8,128)(2,1)S(1)} %collective-permute-done.2.refs_1_, ...), custom_call_target="tpu_custom_call" | custom-call | flops 671088640 | bytes 11796480 | tf_op jit(solution)/shard_map/amplitudes_early/pallas_call | solution.py:192
  41.7 2.2 %collective-permute-done.4.refs_0_ = bf16[96,2560]{1,0:T(8,128)(2,1)S(1)} collective-permute-done((bf16[96,2560]{1,0:T(8,128)(2,1)S(1)}, bf16[96,2560]{1,0:T(8,128)(2,1)S(1)}, u32[]{:S(2)}, u32[]{:S(2)}) %collective-permute-start.4) | collective-permute-done | bytes 491552 | tf_op jit(solution)/shard_map/ppermute | solution.py:24
  44.0 2.6 %amplitudes_late.1 = (bf16[384,768]{1,0:T(8,128)(2,1)S(1)}, bf16[768,384]{1,0:T(8,128)(2,1)S(1)}, bf16[384,2560]{1,0:T(8,128)(2,1)S(1)}, bf16[768,2560]{1,0:T(8,...) custom-call(bf16[96,2560]{1,0:T(8,128)(2,1)S(1)} %collective-permute, ...), custom_call_target="tpu_custom_call", output_to_operand_aliasing={{0}: (4, {}), {1}: (5, {}), {2}: (6, {}), {3}: (7, {})} | custom-call | flops 1509949440 | bytes 11796480 | tf_op jit(solution)/shard_map/amplitudes_late/pallas_call | solution.py:200
  47.2 0.8 alpha_first.1
  50.1 1.4 %collective-permute-start.12 = (f16[96,2560]{1,0:T(8,128)(2,1)S(1)}, f16[96,2560]{1,0:T(8,128)(2,1)S(1)}, u32[]{:S(2)}, u32[]{:S(2)}) collective-permute-start(f16[96,2560]{1,0:T(8,128)(2,1)S(1)} %multiply_convert_fusion.9), channel_id=1, source_target_pairs={{0,2},{1,3},{2,0},{3,1},{4,6},{5,7},{6,4},{7,5},{8,10},{9,11},{10,... | collective-permute-start | bytes 1474568 | tf_op jit(solution)/shard_map/ppermute | solution.py:24
  51.5 1.6 %collective-permute-start.13 = (f16[96,2560]{1,0:T(8,128)(2,1)S(1)}, f16[96,2560]{1,0:T(8,128)(2,1)S(1)}, u32[]{:S(2)}, u32[]{:S(2)}) collective-permute-start(f16[96,2560]{1,0:T(8,128)(2,1)S(1)} %multiply_convert_fusion.7), channel_id=1, source_target_pairs={{0,16},{1,17},{2,18},{3,19},{4,20},{5,21},{6,22},{7,23},{8,24},{9,... | collective-permute-start | bytes 1474568 | tf_op jit(solution)/shard_map/ppermute | solution.py:24
  53.1 1.7 %beta.1 = (f32[96,2560]{1,0:T(8,128)S(1)}, f32[96,2560]{1,0:T(8,128)S(1)}, f32[96,2560]{1,0:T(8,128)S(1)}, f32[96,2560]{1,0:T(8,128)S(1)}, f32[96,2560]{1,0:T(8,128)S(1)}, /*index=5*/f32[96,2560]{1,0:T(8,128)S(1)}) custom-call(bf16[768,384]{1,0:T(8,128)(2,1)S(1)} %get-tuple-element.84.left, bf16[384,2560]{1,0:T(8,128)(2,1)S(1)} %get-tuple-element.85.right), custom_call_target="tpu_custom_call" | custom-call | flops 1132462080 | bytes 7864320 | tf_op jit(solution)/shard_map/beta/pallas_call | solution.py:213
  55.0 1.3 %alpha.1 = (f32[96,2560]{1,0:T(8,128)S(1)}, f32[96,2560]{1,0:T(8,128)S(1)}, f32[96,2560]{1,0:T(8,128)S(1)}) custom-call(bf16[384,768]{1,0:T(8,128)(2,1)S(1)} %get-tuple-element.72.left, bf16[768,2560]{1,0:T(8,128)(2,1)S(1)} %get-tuple-element.73.right), custom_call_target="tpu_custom_call" | custom-call | flops 1132462080 | bytes 6881280 | tf_op jit(solution)/shard_map/alpha/pallas_call | solution.py:213
  56.4 0.7 collective-permute-start.15
  57.1 2.4 %collective-permute-start.17 = (f32[2560]{0:T(1024)S(1)}, f32[2560]{0:T(1024)S(1)}, u32[]{:S(2)}, u32[]{:S(2)}) collective-permute-start(f32[2560]{0:T(1024)S(1)} %get-tuple-element.99), channel_id=1, source_target_pairs={{0,4},{1,5},{2,6},{3,7},{4,0},{5,1},{6,2},{7,3},{8,12},{9,13},{10,... | collective-permute-start | bytes 30728 | tf_op jit(solution)/shard_map/ppermute | solution.py:24
  59.7 1.3 %collective-permute-done.15 = f32[2560]{0:T(1024)S(1)} collective-permute-done((f32[2560]{0:T(1024)S(1)}, f32[2560]{0:T(1024)S(1)}, u32[]{:S(2)}, u32[]{:S(2)}) %collective-permute-start.15) | collective-permute-done | bytes 10272 | tf_op jit(solution)/shard_map/ppermute | solution.py:24
  61.2 1.9 %collective-permute-done.12 = f16[96,2560]{1,0:T(8,128)(2,1)S(1)} collective-permute-done((f16[96,2560]{1,0:T(8,128)(2,1)S(1)}, f16[96,2560]{1,0:T(8,128)(2,1)S(1)}, u32[]{:S(2)}, u32[]{:S(2)}) %collective-permute-start.12) | collective-permute-done | bytes 491552 | tf_op jit(solution)/shard_map/ppermute | solution.py:24
  63.1 1.0 %collective-permute-done.13 = f16[96,2560]{1,0:T(8,128)(2,1)S(1)} collective-permute-done((f16[96,2560]{1,0:T(8,128)(2,1)S(1)}, f16[96,2560]{1,0:T(8,128)(2,1)S(1)}, u32[]{:S(2)}, u32[]{:S(2)}) %collective-permute-start.13) | collective-permute-done | bytes 491552 | tf_op jit(solution)/shard_map/ppermute | solution.py:24
  64.4 0.8 collective-permute-start.19
  65.7 3.2 %collective-permute-start.21 = (f16[96,2560]{1,0:T(8,128)(2,1)S(1)}, f16[96,2560]{1,0:T(8,128)(2,1)S(1)}, u32[]{:S(2)}, u32[]{:S(2)}) collective-permute-start(f16[96,2560]{1,0:T(8,128)(2,1)S(1)} %get-tuple-element.108), channel_id=1, source_target_pairs={{0,4},{1,5},{2,6},{3,7},{4,0},{5,1},{6,2},{7,3},{8,12},{9,13},{10,... | collective-permute-start | bytes 1474568 | tf_op jit(solution)/shard_map/ppermute | solution.py:24
  68.8 1.4 %collective-permute-start.18 = (f16[96,2560]{1,0:T(8,128)(2,1)S(1)}, f16[96,2560]{1,0:T(8,128)(2,1)S(1)}, u32[]{:S(2)}, u32[]{:S(2)}) collective-permute-start(f16[96,2560]{1,0:T(8,128)(2,1)S(1)} %multiply_convert_fusion.6), channel_id=1, source_target_pairs={{0,2},{1,3},{2,0},{3,1},{4,6},{5,7},{6,4},{7,5},{8,10},{9,11},{10,... | collective-permute-start | bytes 1474568 | tf_op jit(solution)/shard_map/ppermute | solution.py:24
  70.8 16.9 %collective-permute-done.19 = f16[96,2560]{1,0:T(8,128)(2,1)S(1)} collective-permute-done((f16[96,2560]{1,0:T(8,128)(2,1)S(1)}, f16[96,2560]{1,0:T(8,128)(2,1)S(1)}, u32[]{:S(2)}, u32[]{:S(2)}) %collective-permute-start.19) | collective-permute-done | bytes 491552 | tf_op jit(solution)/shard_map/ppermute | solution.py:24
  87.7 0.7 collective-permute-done.21
  88.4 1.2 %add_bitcast_fusion.1 = f32[1,96,2560]{2,1,0:T(8,128)} fusion(f16[96,2560]{1,0:T(8,128)(2,1)S(1)} %collective-permute-done.19, f32[96,2560]{1,0:T(8,128)S(1)} %get-tuple-element.74, f16[96,2560]{1,0:T(8,128)(2,1)S(1)} %collective-permute-done.18, f32[2560]{0:T(1024)S(1)} %collective-permute-done.15, f32[2560]{0:T(1024)S(1)} %collective-permute-done.14), kind=kLoop, calls=%fused_computation.4 | loop fusion | flops 1474560 | bytes 2969600 | tf_op jit(solution)/shard_map/reshape | solution.py:295
  89.6 1.3 %add_bitcast_fusion = f32[1,96,2560]{2,1,0:T(8,128)} fusion(f16[96,2560]{1,0:T(8,128)(2,1)S(1)} %collective-permute-done.21, f16[96,2560]{1,0:T(8,128)(2,1)S(1)} %collective-permute-done.24, f32[96,2560]{1,0:T(8,128)S(1)} %get-tuple-element.92, f16[96,2560]{1,0:T(8,128)(2,1)S(1)} %collective-permute-done.22, f32[2560]{0:T(1024)S(1)} %collective-permute-done.17, ...), kind=kLoop, calls=%fused_computation | loop fusion | flops 2211840 | bytes 3471360 | tf_op jit(solution)/shard_map/reshape | solution.py:295
  (46 shorter events, 6.3 us)
Async XLA Ops:
  0.6 38.6 %copy-start = (bf16[1,96,2560]{2,1,0:T(8,128)(2,1)S(1)}, bf16[1,96,2560]{2,1,0:T(8,128)(2,1)}, u32[]{:S(2)}) copy-start(bf16[1,96,2560]{2,1,0:T(8,128)(2,1)} %param.6) | copy-start | bytes 1474564
  0.6 29.2 %copy-start.1 = (bf16[1,96,2560]{2,1,0:T(8,128)(2,1)S(1)}, bf16[1,96,2560]{2,1,0:T(8,128)(2,1)}, u32[]{:S(2)}) copy-start(bf16[1,96,2560]{2,1,0:T(8,128)(2,1)} %param.7) | copy-start | bytes 1474564
  0.6 26.2 %collective-permute-start.2 = (bf16[96,2560]{1,0:T(8,128)(2,1)}, bf16[96,2560]{1,0:T(8,128)(2,1)S(1)}, u32[]{:S(2)}, u32[]{:S(2)}) collective-permute-start(bf16[96,2560]{1,0:T(8,128)(2,1)} %bitcast.7), channel_id=1, source_target_pairs={{0,8},{1,9},{2,10},{3,11},{4,12},{5,13},{6,14},{7,15},{8,0},{9,1},... | collective-permute-start | bytes 1474568 | tf_op jit(solution)/shard_map/ppermute | solution.py:24
  4.8 22.1 %collective-permute-start.1 = (bf16[96,2560]{1,0:T(8,128)(2,1)}, bf16[96,2560]{1,0:T(8,128)(2,1)S(1)}, u32[]{:S(2)}, u32[]{:S(2)}) collective-permute-start(bf16[96,2560]{1,0:T(8,128)(2,1)} %bitcast.8), channel_id=1, source_target_pairs={{0,2},{1,3},{2,0},{3,1},{4,6},{5,7},{6,4},{7,5},{8,10},{9,11},{10,... | collective-permute-start | bytes 1474568 | tf_op jit(solution)/shard_map/ppermute | solution.py:24
  6.2 22.0 %collective-permute-start.3 = (bf16[96,2560]{1,0:T(8,128)(2,1)}, bf16[96,2560]{1,0:T(8,128)(2,1)S(1)}, u32[]{:S(2)}, u32[]{:S(2)}) collective-permute-start(bf16[96,2560]{1,0:T(8,128)(2,1)} %bitcast.10), channel_id=1, source_target_pairs={{0,4},{1,5},{2,6},{3,7},{4,0},{5,1},{6,2},{7,3},{8,12},{9,13},{10,... | collective-permute-start | bytes 1474568 | tf_op jit(solution)/shard_map/ppermute | solution.py:24
  7.8 20.4 %collective-permute-start = (bf16[96,2560]{1,0:T(8,128)(2,1)}, bf16[96,2560]{1,0:T(8,128)(2,1)}, u32[]{:S(2)}, u32[]{:S(2)}) collective-permute-start(bf16[96,2560]{1,0:T(8,128)(2,1)} %bitcast.11), channel_id=1, source_target_pairs={{0,16},{1,17},{2,18},{3,19},{4,20},{5,21},{6,22},{7,23},{8,24},{9,... | collective-permute-start | bytes 1474568 | tf_op jit(solution)/shard_map/ppermute | solution.py:24
  11.1 0.7 copy-start.2
  11.7 0.7 copy-start.3
  28.2 11.0 %collective-permute-start.5 = (bf16[96,2560]{1,0:T(8,128)(2,1)S(1)}, bf16[96,2560]{1,0:T(8,128)(2,1)S(1)}, u32[]{:S(2)}, u32[]{:S(2)}) collective-permute-start(bf16[96,2560]{1,0:T(8,128)(2,1)S(1)} %collective-permute-done.3.refs_6_), channel_id=1, source_target_pairs={{0,16},{1,17},{2,18},{3,19},{4,20},{5,21},{6,22},{7,23},{8,24},{9,... | collective-permute-start | bytes 1474568 | tf_op jit(solution)/shard_map/ppermute | solution.py:24
  29.8 9.5 %collective-permute-start.7 = (bf16[96,2560]{1,0:T(8,128)(2,1)}, bf16[96,2560]{1,0:T(8,128)(2,1)S(1)}, u32[]{:S(2)}, u32[]{:S(2)}) collective-permute-start(bf16[96,2560]{1,0:T(8,128)(2,1)} %collective-permute-done.refs_4_), channel_id=1, source_target_pairs={{0,1},{1,0},{2,3},{3,2},{4,5},{5,4},{6,7},{7,6},{8,9},{9,8},{10,11... | collective-permute-start | bytes 1474568 | tf_op jit(solution)/shard_map/ppermute | solution.py:24
  29.8 9.5 %collective-permute-start.9 = (bf16[96,2560]{1,0:T(8,128)(2,1)S(1)}, bf16[96,2560]{1,0:T(8,128)(2,1)S(1)}, u32[]{:S(2)}, u32[]{:S(2)}) collective-permute-start(bf16[96,2560]{1,0:T(8,128)(2,1)S(1)} %bitcast.12), channel_id=1, source_target_pairs={{0,1},{1,0},{2,3},{3,2},{4,5},{5,4},{6,7},{7,6},{8,9},{9,8},{10,11... | collective-permute-start | bytes 1474568 | tf_op jit(solution)/shard_map/ppermute | solution.py:24
  30.3 8.9 %collective-permute-start.8 = (bf16[96,2560]{1,0:T(8,128)(2,1)S(1)}, bf16[96,2560]{1,0:T(8,128)(2,1)S(1)}, u32[]{:S(2)}, u32[]{:S(2)}) collective-permute-start(bf16[96,2560]{1,0:T(8,128)(2,1)S(1)} %collective-permute-done.3.refs_6_), channel_id=1, source_target_pairs={{0,1},{1,0},{2,3},{3,2},{4,5},{5,4},{6,7},{7,6},{8,9},{9,8},{10,11... | collective-permute-start | bytes 1474568 | tf_op jit(solution)/shard_map/ppermute | solution.py:24
  30.3 13.6 %collective-permute-start.4 = (bf16[96,2560]{1,0:T(8,128)(2,1)S(1)}, bf16[96,2560]{1,0:T(8,128)(2,1)S(1)}, u32[]{:S(2)}, u32[]{:S(2)}) collective-permute-start(bf16[96,2560]{1,0:T(8,128)(2,1)S(1)} %collective-permute-done.2.refs_1_), channel_id=1, source_target_pairs={{0,2},{1,3},{2,0},{3,1},{4,6},{5,7},{6,4},{7,5},{8,10},{9,11},{10,... | collective-permute-start | bytes 1474568 | tf_op jit(solution)/shard_map/ppermute | solution.py:24
  39.2 4.7 %collective-permute-start.6 = (bf16[96,2560]{1,0:T(8,128)(2,1)S(1)}, bf16[96,2560]{1,0:T(8,128)(2,1)S(1)}, u32[]{:S(2)}, u32[]{:S(2)}) collective-permute-start(bf16[96,2560]{1,0:T(8,128)(2,1)S(1)} %collective-permute-done.5.refs_2_), channel_id=1, source_target_pairs={{0,1},{1,0},{2,3},{3,2},{4,5},{5,4},{6,7},{7,6},{8,9},{9,8},{10,11... | collective-permute-start | bytes 1474568 | tf_op jit(solution)/shard_map/ppermute | solution.py:24
  46.5 1.6 %collective-permute-start.11 = (f32[2560]{0:T(1024)S(1)}, f32[2560]{0:T(1024)S(1)}, u32[]{:S(2)}, u32[]{:S(2)}) collective-permute-start(f32[2560]{0:T(1024)S(1)} %get-tuple-element.68), channel_id=1, source_target_pairs={{0,1},{1,0},{2,3},{3,2},{4,5},{5,4},{6,7},{7,6},{8,9},{9,8},{10,11... | collective-permute-start | bytes 30728 | tf_op jit(solution)/shard_map/ppermute | solution.py:24
  46.7 2.1 %collective-permute-start.10 = (f16[96,2560]{1,0:T(8,128)(2,1)S(1)}, f16[96,2560]{1,0:T(8,128)(2,1)S(1)}, u32[]{:S(2)}, u32[]{:S(2)}) collective-permute-start(f16[96,2560]{1,0:T(8,128)(2,1)S(1)} %multiply_convert_fusion.8), channel_id=1, source_target_pairs={{0,1},{1,0},{2,3},{3,2},{4,5},{5,4},{6,7},{7,6},{8,9},{9,8},{10,11... | collective-permute-start | bytes 1474568 | tf_op jit(solution)/shard_map/ppermute | solution.py:24
  48.9 7.4 %collective-permute-start.14 = (f32[2560]{0:T(1024)S(1)}, f32[2560]{0:T(1024)S(1)}, u32[]{:S(2)}, u32[]{:S(2)}) collective-permute-start(f32[2560]{0:T(1024)S(1)} %get-tuple-element.78), channel_id=1, source_target_pairs={{0,2},{1,3},{2,0},{3,1},{4,6},{5,7},{6,4},{7,5},{8,10},{9,11},{10,... | collective-permute-start | bytes 30728 | tf_op jit(solution)/shard_map/ppermute | solution.py:24
  49.6 7.5 %collective-permute-start.16 = (f32[2560]{0:T(1024)S(1)}, f32[2560]{0:T(1024)S(1)}, u32[]{:S(2)}, u32[]{:S(2)}) collective-permute-start(f32[2560]{0:T(1024)S(1)} %get-tuple-element.79), channel_id=1, source_target_pairs={{0,16},{1,17},{2,18},{3,19},{4,20},{5,21},{6,22},{7,23},{8,24},{9,... | collective-permute-start | bytes 30728 | tf_op jit(solution)/shard_map/ppermute | solution.py:24
  50.1 13.1 %collective-permute-start.12 = (f16[96,2560]{1,0:T(8,128)(2,1)S(1)}, f16[96,2560]{1,0:T(8,128)(2,1)S(1)}, u32[]{:S(2)}, u32[]{:S(2)}) collective-permute-start(f16[96,2560]{1,0:T(8,128)(2,1)S(1)} %multiply_convert_fusion.9), channel_id=1, source_target_pairs={{0,2},{1,3},{2,0},{3,1},{4,6},{5,7},{6,4},{7,5},{8,10},{9,11},{10,... | collective-permute-start | bytes 1474568 | tf_op jit(solution)/shard_map/ppermute | solution.py:24
  51.5 12.6 %collective-permute-start.13 = (f16[96,2560]{1,0:T(8,128)(2,1)S(1)}, f16[96,2560]{1,0:T(8,128)(2,1)S(1)}, u32[]{:S(2)}, u32[]{:S(2)}) collective-permute-start(f16[96,2560]{1,0:T(8,128)(2,1)S(1)} %multiply_convert_fusion.7), channel_id=1, source_target_pairs={{0,16},{1,17},{2,18},{3,19},{4,20},{5,21},{6,22},{7,23},{8,24},{9,... | collective-permute-start | bytes 1474568 | tf_op jit(solution)/shard_map/ppermute | solution.py:24
  56.4 4.7 %collective-permute-start.15 = (f32[2560]{0:T(1024)S(1)}, f32[2560]{0:T(1024)S(1)}, u32[]{:S(2)}, u32[]{:S(2)}) collective-permute-start(f32[2560]{0:T(1024)S(1)} %get-tuple-element.101), channel_id=1, source_target_pairs={{0,8},{1,9},{2,10},{3,11},{4,12},{5,13},{6,14},{7,15},{8,0},{9,1},... | collective-permute-start | bytes 30728 | tf_op jit(solution)/shard_map/ppermute | solution.py:24
  57.1 4.1 %collective-permute-start.17 = (f32[2560]{0:T(1024)S(1)}, f32[2560]{0:T(1024)S(1)}, u32[]{:S(2)}, u32[]{:S(2)}) collective-permute-start(f32[2560]{0:T(1024)S(1)} %get-tuple-element.99), channel_id=1, source_target_pairs={{0,4},{1,5},{2,6},{3,7},{4,0},{5,1},{6,2},{7,3},{8,12},{9,13},{10,... | collective-permute-start | bytes 30728 | tf_op jit(solution)/shard_map/ppermute | solution.py:24
  59.6 5.5 %collective-permute-start.20 = (f16[96,2560]{1,0:T(8,128)(2,1)S(1)}, f16[96,2560]{1,0:T(8,128)(2,1)S(1)}, u32[]{:S(2)}, u32[]{:S(2)}) collective-permute-start(f16[96,2560]{1,0:T(8,128)(2,1)S(1)} %get-tuple-element.105), channel_id=1, source_target_pairs={{0,1},{1,0},{2,3},{3,2},{4,5},{5,4},{6,7},{7,6},{8,9},{9,8},{10,11... | collective-permute-start | bytes 1474568 | tf_op jit(solution)/shard_map/ppermute | solution.py:24
  61.0 4.1 %collective-permute-start.23 = (f16[96,2560]{1,0:T(8,128)(2,1)S(1)}, f16[96,2560]{1,0:T(8,128)(2,1)S(1)}, u32[]{:S(2)}, u32[]{:S(2)}) collective-permute-start(f16[96,2560]{1,0:T(8,128)(2,1)S(1)} %get-tuple-element.106), channel_id=1, source_target_pairs={{0,1},{1,0},{2,3},{3,2},{4,5},{5,4},{6,7},{7,6},{8,9},{9,8},{10,11... | collective-permute-start | bytes 1474568 | tf_op jit(solution)/shard_map/ppermute | solution.py:24
  64.4 23.3 %collective-permute-start.19 = (f16[96,2560]{1,0:T(8,128)(2,1)S(1)}, f16[96,2560]{1,0:T(8,128)(2,1)S(1)}, u32[]{:S(2)}, u32[]{:S(2)}) collective-permute-start(f16[96,2560]{1,0:T(8,128)(2,1)S(1)} %multiply_convert_fusion.5), channel_id=1, source_target_pairs={{0,8},{1,9},{2,10},{3,11},{4,12},{5,13},{6,14},{7,15},{8,0},{9,1},... | collective-permute-start | bytes 1474568 | tf_op jit(solution)/shard_map/ppermute | solution.py:24
  65.7 22.7 %collective-permute-start.21 = (f16[96,2560]{1,0:T(8,128)(2,1)S(1)}, f16[96,2560]{1,0:T(8,128)(2,1)S(1)}, u32[]{:S(2)}, u32[]{:S(2)}) collective-permute-start(f16[96,2560]{1,0:T(8,128)(2,1)S(1)} %get-tuple-element.108), channel_id=1, source_target_pairs={{0,4},{1,5},{2,6},{3,7},{4,0},{5,1},{6,2},{7,3},{8,12},{9,13},{10,... | collective-permute-start | bytes 1474568 | tf_op jit(solution)/shard_map/ppermute | solution.py:24
  68.8 19.5 %collective-permute-start.18 = (f16[96,2560]{1,0:T(8,128)(2,1)S(1)}, f16[96,2560]{1,0:T(8,128)(2,1)S(1)}, u32[]{:S(2)}, u32[]{:S(2)}) collective-permute-start(f16[96,2560]{1,0:T(8,128)(2,1)S(1)} %multiply_convert_fusion.6), channel_id=1, source_target_pairs={{0,2},{1,3},{2,0},{3,1},{4,6},{5,7},{6,4},{7,5},{8,10},{9,11},{10,... | collective-permute-start | bytes 1474568 | tf_op jit(solution)/shard_map/ppermute | solution.py:24
  70.3 19.3 %collective-permute-start.22 = (f16[96,2560]{1,0:T(8,128)(2,1)S(1)}, f16[96,2560]{1,0:T(8,128)(2,1)S(1)}, u32[]{:S(2)}, u32[]{:S(2)}) collective-permute-start(f16[96,2560]{1,0:T(8,128)(2,1)S(1)} %get-tuple-element.104), channel_id=1, source_target_pairs={{0,1},{1,0},{2,3},{3,2},{4,5},{5,4},{6,7},{7,6},{8,9},{9,8},{10,11... | collective-permute-start | bytes 1474568 | tf_op jit(solution)/shard_map/ppermute | solution.py:24
  70.3 19.3 %collective-permute-start.24 = (f16[96,2560]{1,0:T(8,128)(2,1)S(1)}, f16[96,2560]{1,0:T(8,128)(2,1)S(1)}, u32[]{:S(2)}, u32[]{:S(2)}) collective-permute-start(f16[96,2560]{1,0:T(8,128)(2,1)S(1)} %get-tuple-element.107), channel_id=1, source_target_pairs={{0,16},{1,17},{2,18},{3,19},{4,20},{5,21},{6,22},{7,23},{8,24},{9,... | collective-permute-start | bytes 1474568 | tf_op jit(solution)/shard_map/ppermute | solution.py:24

commit v12 on v11

--- a/solution.py
+++ b/solution.py
@@ -50,7 +50,8 @@
 
 def amplitudes_of(rows, cols, acat, bcat, ninv, t_ref, tt):
     top = jnp.zeros((1, 1), jnp.float32)
-    step = 256 if (cols[1] - cols[0]) % 256 == 0 else cols[1] - cols[0]
+    span = cols[1] - cols[0]
+    step = span if span <= 768 or span % 256 else 256
     for c in range(cols[0], cols[1], step):
         integrals = lax.dot_general(
             acat[rows[0]:rows[1], :], bcat[c:c + step, :], (((1,), (1,)), ((), ())), preferred_element_type=jnp.float32
@@ -106,7 +107,7 @@
 
 def rows_out(start, spans, left, right, *outs):
     aux = right.shape[1]
-    tile = 512 if aux % 512 == 0 else 128
+    tile = 1280 if aux % 1280 == 0 else 128
     rows = left[start:start + sum(spans), :]
 
     for at in range(0, aux, tile):

time: 91.1 us -> 91.1 us (level)
  no operation moved by 1% of the time
where the time goes in v12:
time: 91.1 us; the launch traced here: 90.9 us
  waiting for transfers between devices  48.4 us (53%)
  starting transfers between devices  25.2 us (28%)
  Pallas kernels  9.55 us (10%)
  other arithmetic  3.93 us (4%)
  local copies, waits for them, and re-layouts  3.03 us (3%)
    ppermute x25, waiting for transfers between devices, exchange(): lax.ppermute(value, ('grp', 'slab'), [(d, d ^ 1 << bit) for d in range(de...  48.4 us
    ppermute x25, starting transfers between devices, exchange(): lax.ppermute(value, ('grp', 'slab'), [(d, d ^ 1 << bit) for d in range(de...  25.2 us
    pallas_call x3, Pallas kernels, contracted(): pl.pallas_call(functools.partial(rows_out, start * width, cut * len(names...  3.74 us
    pallas_call x1, Pallas kernels, body(): pl.pallas_call(functools.partial(end_amplitudes, [p for _, p in all_a[:la...  2.57 us
    reshape x2, other arithmetic, whole(): return parts[0].reshape(orbital_alpha.shape)  2.46 us
    pallas_call x1, Pallas kernels, body(): pl.pallas_call(functools.partial(begin_amplitudes, [p for _, p in all_a[l...  2.4 us
  transfers between devices with their start and end apart: 25, of which 11 were waited for; matrix products, arithmetic and copies ran while one was open for 5% of the time, Pallas kernels for 8%

profile of v12, /device:TPU:0, one launch (start us, length us, event | category | flops | bytes accessed | tf_op | source)
XLA Modules:
  0.0 90.9 jit_solution(6690424069991846512)
XLA Ops:
  0.6 4.1 %collective-permute-start.2 = (bf16[96,2560]{1,0:T(8,128)(2,1)}, bf16[96,2560]{1,0:T(8,128)(2,1)S(1)}, u32[]{:S(2)}, u32[]{:S(2)}) collective-permute-start(bf16[96,2560]{1,0:T(8,128)(2,1)} %bitcast.7), channel_id=1, source_target_pairs={{0,8},{1,9},{2,10},{3,11},{4,12},{5,13},{6,14},{7,15},{8,0},{9,1},... | collective-permute-start | bytes 1474568 | tf_op jit(solution)/shard_map/ppermute | solution.py:24
  4.8 1.5 %collective-permute-start.1 = (bf16[96,2560]{1,0:T(8,128)(2,1)}, bf16[96,2560]{1,0:T(8,128)(2,1)S(1)}, u32[]{:S(2)}, u32[]{:S(2)}) collective-permute-start(bf16[96,2560]{1,0:T(8,128)(2,1)} %bitcast.8), channel_id=1, source_target_pairs={{0,2},{1,3},{2,0},{3,1},{4,6},{5,7},{6,4},{7,5},{8,10},{9,11},{10,... | collective-permute-start | bytes 1474568 | tf_op jit(solution)/shard_map/ppermute | solution.py:24
  6.2 1.6 %collective-permute-start.3 = (bf16[96,2560]{1,0:T(8,128)(2,1)}, bf16[96,2560]{1,0:T(8,128)(2,1)S(1)}, u32[]{:S(2)}, u32[]{:S(2)}) collective-permute-start(bf16[96,2560]{1,0:T(8,128)(2,1)} %bitcast.10), channel_id=1, source_target_pairs={{0,4},{1,5},{2,6},{3,7},{4,0},{5,1},{6,2},{7,3},{8,12},{9,13},{10,... | collective-permute-start | bytes 1474568 | tf_op jit(solution)/shard_map/ppermute | solution.py:24
  7.8 1.5 %collective-permute-start = (bf16[96,2560]{1,0:T(8,128)(2,1)}, bf16[96,2560]{1,0:T(8,128)(2,1)}, u32[]{:S(2)}, u32[]{:S(2)}) collective-permute-start(bf16[96,2560]{1,0:T(8,128)(2,1)} %bitcast.11), channel_id=1, source_target_pairs={{0,16},{1,17},{2,18},{3,19},{4,20},{5,21},{6,22},{7,23},{8,24},{9,... | collective-permute-start | bytes 1474568 | tf_op jit(solution)/shard_map/ppermute | solution.py:24
  9.3 0.8 reshape.35.vb_ref
  10.1 1.0 %broadcast_in_dim.3.va_ref = f32[1536,1]{1,0:T(8,128)S(1)} reshape(f32[1536]{0:T(1024)} %param.10) | data formatting | bytes 12288 | tf_op jit(solution)/shard_map/broadcast_in_dim | solution.py:159
  11.7 0.7 copy-done.3
  12.4 0.8 energies.1.refs_9_.refs_3_
  13.2 13.6 %collective-permute-done.2.refs_1_ = bf16[96,2560]{1,0:T(8,128)(2,1)S(1)} collective-permute-done((bf16[96,2560]{1,0:T(8,128)(2,1)}, bf16[96,2560]{1,0:T(8,128)(2,1)S(1)}, u32[]{:S(2)}, u32[]{:S(2)}) %collective-permute-start.2) | collective-permute-done | bytes 491552 | tf_op jit(solution)/shard_map/ppermute | solution.py:24
  26.8 1.4 %collective-permute-done.3.refs_6_ = bf16[96,2560]{1,0:T(8,128)(2,1)S(1)} collective-permute-done((bf16[96,2560]{1,0:T(8,128)(2,1)}, bf16[96,2560]{1,0:T(8,128)(2,1)S(1)}, u32[]{:S(2)}, u32[]{:S(2)}) %collective-permute-start.3) | collective-permute-done | bytes 491552 | tf_op jit(solution)/shard_map/ppermute | solution.py:24
  28.2 1.6 %collective-permute-start.5 = (bf16[96,2560]{1,0:T(8,128)(2,1)S(1)}, bf16[96,2560]{1,0:T(8,128)(2,1)S(1)}, u32[]{:S(2)}, u32[]{:S(2)}) collective-permute-start(bf16[96,2560]{1,0:T(8,128)(2,1)S(1)} %collective-permute-done.3.refs_6_), channel_id=1, source_target_pairs={{0,16},{1,17},{2,18},{3,19},{4,20},{5,21},{6,22},{7,23},{8,24},{9,... | collective-permute-start | bytes 1474568 | tf_op jit(solution)/shard_map/ppermute | solution.py:24
  30.9 8.4 %collective-permute-done.5.refs_2_ = bf16[96,2560]{1,0:T(8,128)(2,1)S(1)} collective-permute-done((bf16[96,2560]{1,0:T(8,128)(2,1)S(1)}, bf16[96,2560]{1,0:T(8,128)(2,1)S(1)}, u32[]{:S(2)}, u32[]{:S(2)}) %collective-permute-start.5) | collective-permute-done | bytes 491552 | tf_op jit(solution)/shard_map/ppermute | solution.py:24
  39.3 2.4 %amplitudes_early.1 = (bf16[384,768]{1,0:T(8,128)(2,1)S(1)}, bf16[768,384]{1,0:T(8,128)(2,1)S(1)}, bf16[384,2560]{1,0:T(8,128)(2,1)S(1)}, bf16[768,2560]{1,0:T(8,128)(2,1)S(1)}, f32[8,128]{1,0:T(8,128)S(1)}) custom-call(bf16[96,2560]{1,0:T(8,128)(2,1)S(1)} %collective-permute-done.1.refs_0_, bf16[96,2560]{1,0:T(8,128)(2,1)S(1)} %collective-permute-done.2.refs_1_, ...), custom_call_target="tpu_custom_call" | custom-call | flops 671088640 | bytes 11796480 | tf_op jit(solution)/shard_map/amplitudes_early/pallas_call | solution.py:193
  41.7 2.3 %collective-permute-done.4.refs_0_ = bf16[96,2560]{1,0:T(8,128)(2,1)S(1)} collective-permute-done((bf16[96,2560]{1,0:T(8,128)(2,1)S(1)}, bf16[96,2560]{1,0:T(8,128)(2,1)S(1)}, u32[]{:S(2)}, u32[]{:S(2)}) %collective-permute-start.4) | collective-permute-done | bytes 491552 | tf_op jit(solution)/shard_map/ppermute | solution.py:24
  44.0 2.6 %amplitudes_late.1 = (bf16[384,768]{1,0:T(8,128)(2,1)S(1)}, bf16[768,384]{1,0:T(8,128)(2,1)S(1)}, bf16[384,2560]{1,0:T(8,128)(2,1)S(1)}, bf16[768,2560]{1,0:T(8,...) custom-call(bf16[96,2560]{1,0:T(8,128)(2,1)S(1)} %collective-permute, ...), custom_call_target="tpu_custom_call", output_to_operand_aliasing={{0}: (4, {}), {1}: (5, {}), {2}: (6, {}), {3}: (7, {})} | custom-call | flops 1509949440 | bytes 11796480 | tf_op jit(solution)/shard_map/amplitudes_late/pallas_call | solution.py:201
  47.3 0.8 alpha_first.1
  50.1 1.4 %collective-permute-start.12 = (f16[96,2560]{1,0:T(8,128)(2,1)S(1)}, f16[96,2560]{1,0:T(8,128)(2,1)S(1)}, u32[]{:S(2)}, u32[]{:S(2)}) collective-permute-start(f16[96,2560]{1,0:T(8,128)(2,1)S(1)} %multiply_convert_fusion.9), channel_id=1, source_target_pairs={{0,2},{1,3},{2,0},{3,1},{4,6},{5,7},{6,4},{7,5},{8,10},{9,11},{10,... | collective-permute-start | bytes 1474568 | tf_op jit(solution)/shard_map/ppermute | solution.py:24
  51.5 1.6 %collective-permute-start.13 = (f16[96,2560]{1,0:T(8,128)(2,1)S(1)}, f16[96,2560]{1,0:T(8,128)(2,1)S(1)}, u32[]{:S(2)}, u32[]{:S(2)}) collective-permute-start(f16[96,2560]{1,0:T(8,128)(2,1)S(1)} %multiply_convert_fusion.7), channel_id=1, source_target_pairs={{0,16},{1,17},{2,18},{3,19},{4,20},{5,21},{6,22},{7,23},{8,24},{9,... | collective-permute-start | bytes 1474568 | tf_op jit(solution)/shard_map/ppermute | solution.py:24
  53.1 1.7 %beta.1 = (f32[96,2560]{1,0:T(8,128)S(1)}, f32[96,2560]{1,0:T(8,128)S(1)}, f32[96,2560]{1,0:T(8,128)S(1)}, f32[96,2560]{1,0:T(8,128)S(1)}, f32[96,2560]{1,0:T(8,128)S(1)}, /*index=5*/f32[96,2560]{1,0:T(8,128)S(1)}) custom-call(bf16[768,384]{1,0:T(8,128)(2,1)S(1)} %get-tuple-element.84.left, bf16[384,2560]{1,0:T(8,128)(2,1)S(1)} %get-tuple-element.85.right), custom_call_target="tpu_custom_call" | custom-call | flops 1132462080 | bytes 7864320 | tf_op jit(solution)/shard_map/beta/pallas_call | solution.py:214
  55.1 1.3 %alpha.1 = (f32[96,2560]{1,0:T(8,128)S(1)}, f32[96,2560]{1,0:T(8,128)S(1)}, f32[96,2560]{1,0:T(8,128)S(1)}) custom-call(bf16[384,768]{1,0:T(8,128)(2,1)S(1)} %get-tuple-element.72.left, bf16[768,2560]{1,0:T(8,128)(2,1)S(1)} %get-tuple-element.73.right), custom_call_target="tpu_custom_call" | custom-call | flops 1132462080 | bytes 6881280 | tf_op jit(solution)/shard_map/alpha/pallas_call | solution.py:214
  56.4 0.7 collective-permute-start.15
  57.1 2.4 %collective-permute-start.17 = (f32[2560]{0:T(1024)S(1)}, f32[2560]{0:T(1024)S(1)}, u32[]{:S(2)}, u32[]{:S(2)}) collective-permute-start(f32[2560]{0:T(1024)S(1)} %get-tuple-element.99), channel_id=1, source_target_pairs={{0,4},{1,5},{2,6},{3,7},{4,0},{5,1},{6,2},{7,3},{8,12},{9,13},{10,... | collective-permute-start | bytes 30728 | tf_op jit(solution)/shard_map/ppermute | solution.py:24
  59.7 1.3 %collective-permute-done.15 = f32[2560]{0:T(1024)S(1)} collective-permute-done((f32[2560]{0:T(1024)S(1)}, f32[2560]{0:T(1024)S(1)}, u32[]{:S(2)}, u32[]{:S(2)}) %collective-permute-start.15) | collective-permute-done | bytes 10272 | tf_op jit(solution)/shard_map/ppermute | solution.py:24
  61.2 1.9 %collective-permute-done.12 = f16[96,2560]{1,0:T(8,128)(2,1)S(1)} collective-permute-done((f16[96,2560]{1,0:T(8,128)(2,1)S(1)}, f16[96,2560]{1,0:T(8,128)(2,1)S(1)}, u32[]{:S(2)}, u32[]{:S(2)}) %collective-permute-start.12) | collective-permute-done | bytes 491552 | tf_op jit(solution)/shard_map/ppermute | solution.py:24
  63.1 1.0 %collective-permute-done.13 = f16[96,2560]{1,0:T(8,128)(2,1)S(1)} collective-permute-done((f16[96,2560]{1,0:T(8,128)(2,1)S(1)}, f16[96,2560]{1,0:T(8,128)(2,1)S(1)}, u32[]{:S(2)}, u32[]{:S(2)}) %collective-permute-start.13) | collective-permute-done | bytes 491552 | tf_op jit(solution)/shard_map/ppermute | solution.py:24
  64.4 0.8 collective-permute-start.19
  65.7 3.1 %collective-permute-start.21 = (f16[96,2560]{1,0:T(8,128)(2,1)S(1)}, f16[96,2560]{1,0:T(8,128)(2,1)S(1)}, u32[]{:S(2)}, u32[]{:S(2)}) collective-permute-start(f16[96,2560]{1,0:T(8,128)(2,1)S(1)} %get-tuple-element.108), channel_id=1, source_target_pairs={{0,4},{1,5},{2,6},{3,7},{4,0},{5,1},{6,2},{7,3},{8,12},{9,13},{10,... | collective-permute-start | bytes 1474568 | tf_op jit(solution)/shard_map/ppermute | solution.py:24
  68.8 1.4 %collective-permute-start.18 = (f16[96,2560]{1,0:T(8,128)(2,1)S(1)}, f16[96,2560]{1,0:T(8,128)(2,1)S(1)}, u32[]{:S(2)}, u32[]{:S(2)}) collective-permute-start(f16[96,2560]{1,0:T(8,128)(2,1)S(1)} %multiply_convert_fusion.6), channel_id=1, source_target_pairs={{0,2},{1,3},{2,0},{3,1},{4,6},{5,7},{6,4},{7,5},{8,10},{9,11},{10,... | collective-permute-start | bytes 1474568 | tf_op jit(solution)/shard_map/ppermute | solution.py:24
  70.8 16.9 %collective-permute-done.19 = f16[96,2560]{1,0:T(8,128)(2,1)S(1)} collective-permute-done((f16[96,2560]{1,0:T(8,128)(2,1)S(1)}, f16[96,2560]{1,0:T(8,128)(2,1)S(1)}, u32[]{:S(2)}, u32[]{:S(2)}) %collective-permute-start.19) | collective-permute-done | bytes 491552 | tf_op jit(solution)/shard_map/ppermute | solution.py:24
  87.7 0.7 collective-permute-done.21
  88.4 1.2 %add_bitcast_fusion.1 = f32[1,96,2560]{2,1,0:T(8,128)} fusion(f16[96,2560]{1,0:T(8,128)(2,1)S(1)} %collective-permute-done.19, f32[96,2560]{1,0:T(8,128)S(1)} %get-tuple-element.74, f16[96,2560]{1,0:T(8,128)(2,1)S(1)} %collective-permute-done.18, f32[2560]{0:T(1024)S(1)} %collective-permute-done.15, f32[2560]{0:T(1024)S(1)} %collective-permute-done.14), kind=kLoop, calls=%fused_computation.4 | loop fusion | flops 1474560 | bytes 2969600 | tf_op jit(solution)/shard_map/reshape | solution.py:296
  89.6 1.3 %add_bitcast_fusion = f32[1,96,2560]{2,1,0:T(8,128)} fusion(f16[96,2560]{1,0:T(8,128)(2,1)S(1)} %collective-permute-done.21, f16[96,2560]{1,0:T(8,128)(2,1)S(1)} %collective-permute-done.24, f32[96,2560]{1,0:T(8,128)S(1)} %get-tuple-element.92, f16[96,2560]{1,0:T(8,128)(2,1)S(1)} %collective-permute-done.22, f32[2560]{0:T(1024)S(1)} %collective-permute-done.17, ...), kind=kLoop, calls=%fused_computation | loop fusion | flops 2211840 | bytes 3471360 | tf_op jit(solution)/shard_map/reshape | solution.py:296
  (46 shorter events, 6.3 us)
Async XLA Ops:
  0.6 38.6 %copy-start = (bf16[1,96,2560]{2,1,0:T(8,128)(2,1)S(1)}, bf16[1,96,2560]{2,1,0:T(8,128)(2,1)}, u32[]{:S(2)}) copy-start(bf16[1,96,2560]{2,1,0:T(8,128)(2,1)} %param.6) | copy-start | bytes 1474564
  0.6 29.2 %copy-start.1 = (bf16[1,96,2560]{2,1,0:T(8,128)(2,1)S(1)}, bf16[1,96,2560]{2,1,0:T(8,128)(2,1)}, u32[]{:S(2)}) copy-start(bf16[1,96,2560]{2,1,0:T(8,128)(2,1)} %param.7) | copy-start | bytes 1474564
  0.6 26.2 %collective-permute-start.2 = (bf16[96,2560]{1,0:T(8,128)(2,1)}, bf16[96,2560]{1,0:T(8,128)(2,1)S(1)}, u32[]{:S(2)}, u32[]{:S(2)}) collective-permute-start(bf16[96,2560]{1,0:T(8,128)(2,1)} %bitcast.7), channel_id=1, source_target_pairs={{0,8},{1,9},{2,10},{3,11},{4,12},{5,13},{6,14},{7,15},{8,0},{9,1},... | collective-permute-start | bytes 1474568 | tf_op jit(solution)/shard_map/ppermute | solution.py:24
  4.8 22.1 %collective-permute-start.1 = (bf16[96,2560]{1,0:T(8,128)(2,1)}, bf16[96,2560]{1,0:T(8,128)(2,1)S(1)}, u32[]{:S(2)}, u32[]{:S(2)}) collective-permute-start(bf16[96,2560]{1,0:T(8,128)(2,1)} %bitcast.8), channel_id=1, source_target_pairs={{0,2},{1,3},{2,0},{3,1},{4,6},{5,7},{6,4},{7,5},{8,10},{9,11},{10,... | collective-permute-start | bytes 1474568 | tf_op jit(solution)/shard_map/ppermute | solution.py:24
  6.2 22.0 %collective-permute-start.3 = (bf16[96,2560]{1,0:T(8,128)(2,1)}, bf16[96,2560]{1,0:T(8,128)(2,1)S(1)}, u32[]{:S(2)}, u32[]{:S(2)}) collective-permute-start(bf16[96,2560]{1,0:T(8,128)(2,1)} %bitcast.10), channel_id=1, source_target_pairs={{0,4},{1,5},{2,6},{3,7},{4,0},{5,1},{6,2},{7,3},{8,12},{9,13},{10,... | collective-permute-start | bytes 1474568 | tf_op jit(solution)/shard_map/ppermute | solution.py:24
  7.8 20.4 %collective-permute-start = (bf16[96,2560]{1,0:T(8,128)(2,1)}, bf16[96,2560]{1,0:T(8,128)(2,1)}, u32[]{:S(2)}, u32[]{:S(2)}) collective-permute-start(bf16[96,2560]{1,0:T(8,128)(2,1)} %bitcast.11), channel_id=1, source_target_pairs={{0,16},{1,17},{2,18},{3,19},{4,20},{5,21},{6,22},{7,23},{8,24},{9,... | collective-permute-start | bytes 1474568 | tf_op jit(solution)/shard_map/ppermute | solution.py:24
  11.1 0.7 copy-start.2
  11.7 0.7 copy-start.3
  28.2 11.0 %collective-permute-start.5 = (bf16[96,2560]{1,0:T(8,128)(2,1)S(1)}, bf16[96,2560]{1,0:T(8,128)(2,1)S(1)}, u32[]{:S(2)}, u32[]{:S(2)}) collective-permute-start(bf16[96,2560]{1,0:T(8,128)(2,1)S(1)} %collective-permute-done.3.refs_6_), channel_id=1, source_target_pairs={{0,16},{1,17},{2,18},{3,19},{4,20},{5,21},{6,22},{7,23},{8,24},{9,... | collective-permute-start | bytes 1474568 | tf_op jit(solution)/shard_map/ppermute | solution.py:24
  29.8 9.5 %collective-permute-start.7 = (bf16[96,2560]{1,0:T(8,128)(2,1)}, bf16[96,2560]{1,0:T(8,128)(2,1)S(1)}, u32[]{:S(2)}, u32[]{:S(2)}) collective-permute-start(bf16[96,2560]{1,0:T(8,128)(2,1)} %collective-permute-done.refs_4_), channel_id=1, source_target_pairs={{0,1},{1,0},{2,3},{3,2},{4,5},{5,4},{6,7},{7,6},{8,9},{9,8},{10,11... | collective-permute-start | bytes 1474568 | tf_op jit(solution)/shard_map/ppermute | solution.py:24
  29.8 9.5 %collective-permute-start.9 = (bf16[96,2560]{1,0:T(8,128)(2,1)S(1)}, bf16[96,2560]{1,0:T(8,128)(2,1)S(1)}, u32[]{:S(2)}, u32[]{:S(2)}) collective-permute-start(bf16[96,2560]{1,0:T(8,128)(2,1)S(1)} %bitcast.12), channel_id=1, source_target_pairs={{0,1},{1,0},{2,3},{3,2},{4,5},{5,4},{6,7},{7,6},{8,9},{9,8},{10,11... | collective-permute-start | bytes 1474568 | tf_op jit(solution)/shard_map/ppermute | solution.py:24
  30.3 8.9 %collective-permute-start.8 = (bf16[96,2560]{1,0:T(8,128)(2,1)S(1)}, bf16[96,2560]{1,0:T(8,128)(2,1)S(1)}, u32[]{:S(2)}, u32[]{:S(2)}) collective-permute-start(bf16[96,2560]{1,0:T(8,128)(2,1)S(1)} %collective-permute-done.3.refs_6_), channel_id=1, source_target_pairs={{0,1},{1,0},{2,3},{3,2},{4,5},{5,4},{6,7},{7,6},{8,9},{9,8},{10,11... | collective-permute-start | bytes 1474568 | tf_op jit(solution)/shard_map/ppermute | solution.py:24
  30.3 13.6 %collective-permute-start.4 = (bf16[96,2560]{1,0:T(8,128)(2,1)S(1)}, bf16[96,2560]{1,0:T(8,128)(2,1)S(1)}, u32[]{:S(2)}, u32[]{:S(2)}) collective-permute-start(bf16[96,2560]{1,0:T(8,128)(2,1)S(1)} %collective-permute-done.2.refs_1_), channel_id=1, source_target_pairs={{0,2},{1,3},{2,0},{3,1},{4,6},{5,7},{6,4},{7,5},{8,10},{9,11},{10,... | collective-permute-start | bytes 1474568 | tf_op jit(solution)/shard_map/ppermute | solution.py:24
  39.2 4.7 %collective-permute-start.6 = (bf16[96,2560]{1,0:T(8,128)(2,1)S(1)}, bf16[96,2560]{1,0:T(8,128)(2,1)S(1)}, u32[]{:S(2)}, u32[]{:S(2)}) collective-permute-start(bf16[96,2560]{1,0:T(8,128)(2,1)S(1)} %collective-permute-done.5.refs_2_), channel_id=1, source_target_pairs={{0,1},{1,0},{2,3},{3,2},{4,5},{5,4},{6,7},{7,6},{8,9},{9,8},{10,11... | collective-permute-start | bytes 1474568 | tf_op jit(solution)/shard_map/ppermute | solution.py:24
  46.5 1.6 %collective-permute-start.11 = (f32[2560]{0:T(1024)S(1)}, f32[2560]{0:T(1024)S(1)}, u32[]{:S(2)}, u32[]{:S(2)}) collective-permute-start(f32[2560]{0:T(1024)S(1)} %get-tuple-element.68), channel_id=1, source_target_pairs={{0,1},{1,0},{2,3},{3,2},{4,5},{5,4},{6,7},{7,6},{8,9},{9,8},{10,11... | collective-permute-start | bytes 30728 | tf_op jit(solution)/shard_map/ppermute | solution.py:24
  46.7 2.1 %collective-permute-start.10 = (f16[96,2560]{1,0:T(8,128)(2,1)S(1)}, f16[96,2560]{1,0:T(8,128)(2,1)S(1)}, u32[]{:S(2)}, u32[]{:S(2)}) collective-permute-start(f16[96,2560]{1,0:T(8,128)(2,1)S(1)} %multiply_convert_fusion.8), channel_id=1, source_target_pairs={{0,1},{1,0},{2,3},{3,2},{4,5},{5,4},{6,7},{7,6},{8,9},{9,8},{10,11... | collective-permute-start | bytes 1474568 | tf_op jit(solution)/shard_map/ppermute | solution.py:24
  49.0 7.4 %collective-permute-start.14 = (f32[2560]{0:T(1024)S(1)}, f32[2560]{0:T(1024)S(1)}, u32[]{:S(2)}, u32[]{:S(2)}) collective-permute-start(f32[2560]{0:T(1024)S(1)} %get-tuple-element.78), channel_id=1, source_target_pairs={{0,2},{1,3},{2,0},{3,1},{4,6},{5,7},{6,4},{7,5},{8,10},{9,11},{10,... | collective-permute-start | bytes 30728 | tf_op jit(solution)/shard_map/ppermute | solution.py:24
  49.6 7.5 %collective-permute-start.16 = (f32[2560]{0:T(1024)S(1)}, f32[2560]{0:T(1024)S(1)}, u32[]{:S(2)}, u32[]{:S(2)}) collective-permute-start(f32[2560]{0:T(1024)S(1)} %get-tuple-element.79), channel_id=1, source_target_pairs={{0,16},{1,17},{2,18},{3,19},{4,20},{5,21},{6,22},{7,23},{8,24},{9,... | collective-permute-start | bytes 30728 | tf_op jit(solution)/shard_map/ppermute | solution.py:24
  50.1 13.1 %collective-permute-start.12 = (f16[96,2560]{1,0:T(8,128)(2,1)S(1)}, f16[96,2560]{1,0:T(8,128)(2,1)S(1)}, u32[]{:S(2)}, u32[]{:S(2)}) collective-permute-start(f16[96,2560]{1,0:T(8,128)(2,1)S(1)} %multiply_convert_fusion.9), channel_id=1, source_target_pairs={{0,2},{1,3},{2,0},{3,1},{4,6},{5,7},{6,4},{7,5},{8,10},{9,11},{10,... | collective-permute-start | bytes 1474568 | tf_op jit(solution)/shard_map/ppermute | solution.py:24
  51.5 12.6 %collective-permute-start.13 = (f16[96,2560]{1,0:T(8,128)(2,1)S(1)}, f16[96,2560]{1,0:T(8,128)(2,1)S(1)}, u32[]{:S(2)}, u32[]{:S(2)}) collective-permute-start(f16[96,2560]{1,0:T(8,128)(2,1)S(1)} %multiply_convert_fusion.7), channel_id=1, source_target_pairs={{0,16},{1,17},{2,18},{3,19},{4,20},{5,21},{6,22},{7,23},{8,24},{9,... | collective-permute-start | bytes 1474568 | tf_op jit(solution)/shard_map/ppermute | solution.py:24
  56.4 4.7 %collective-permute-start.15 = (f32[2560]{0:T(1024)S(1)}, f32[2560]{0:T(1024)S(1)}, u32[]{:S(2)}, u32[]{:S(2)}) collective-permute-start(f32[2560]{0:T(1024)S(1)} %get-tuple-element.101), channel_id=1, source_target_pairs={{0,8},{1,9},{2,10},{3,11},{4,12},{5,13},{6,14},{7,15},{8,0},{9,1},... | collective-permute-start | bytes 30728 | tf_op jit(solution)/shard_map/ppermute | solution.py:24
  57.1 4.1 %collective-permute-start.17 = (f32[2560]{0:T(1024)S(1)}, f32[2560]{0:T(1024)S(1)}, u32[]{:S(2)}, u32[]{:S(2)}) collective-permute-start(f32[2560]{0:T(1024)S(1)} %get-tuple-element.99), channel_id=1, source_target_pairs={{0,4},{1,5},{2,6},{3,7},{4,0},{5,1},{6,2},{7,3},{8,12},{9,13},{10,... | collective-permute-start | bytes 30728 | tf_op jit(solution)/shard_map/ppermute | solution.py:24
  59.6 5.5 %collective-permute-start.20 = (f16[96,2560]{1,0:T(8,128)(2,1)S(1)}, f16[96,2560]{1,0:T(8,128)(2,1)S(1)}, u32[]{:S(2)}, u32[]{:S(2)}) collective-permute-start(f16[96,2560]{1,0:T(8,128)(2,1)S(1)} %get-tuple-element.105), channel_id=1, source_target_pairs={{0,1},{1,0},{2,3},{3,2},{4,5},{5,4},{6,7},{7,6},{8,9},{9,8},{10,11... | collective-permute-start | bytes 1474568 | tf_op jit(solution)/shard_map/ppermute | solution.py:24
  61.1 4.1 %collective-permute-start.23 = (f16[96,2560]{1,0:T(8,128)(2,1)S(1)}, f16[96,2560]{1,0:T(8,128)(2,1)S(1)}, u32[]{:S(2)}, u32[]{:S(2)}) collective-permute-start(f16[96,2560]{1,0:T(8,128)(2,1)S(1)} %get-tuple-element.106), channel_id=1, source_target_pairs={{0,1},{1,0},{2,3},{3,2},{4,5},{5,4},{6,7},{7,6},{8,9},{9,8},{10,11... | collective-permute-start | bytes 1474568 | tf_op jit(solution)/shard_map/ppermute | solution.py:24
  64.4 23.3 %collective-permute-start.19 = (f16[96,2560]{1,0:T(8,128)(2,1)S(1)}, f16[96,2560]{1,0:T(8,128)(2,1)S(1)}, u32[]{:S(2)}, u32[]{:S(2)}) collective-permute-start(f16[96,2560]{1,0:T(8,128)(2,1)S(1)} %multiply_convert_fusion.5), channel_id=1, source_target_pairs={{0,8},{1,9},{2,10},{3,11},{4,12},{5,13},{6,14},{7,15},{8,0},{9,1},... | collective-permute-start | bytes 1474568 | tf_op jit(solution)/shard_map/ppermute | solution.py:24
  65.7 22.7 %collective-permute-start.21 = (f16[96,2560]{1,0:T(8,128)(2,1)S(1)}, f16[96,2560]{1,0:T(8,128)(2,1)S(1)}, u32[]{:S(2)}, u32[]{:S(2)}) collective-permute-start(f16[96,2560]{1,0:T(8,128)(2,1)S(1)} %get-tuple-element.108), channel_id=1, source_target_pairs={{0,4},{1,5},{2,6},{3,7},{4,0},{5,1},{6,2},{7,3},{8,12},{9,13},{10,... | collective-permute-start | bytes 1474568 | tf_op jit(solution)/shard_map/ppermute | solution.py:24
  68.8 19.6 %collective-permute-start.18 = (f16[96,2560]{1,0:T(8,128)(2,1)S(1)}, f16[96,2560]{1,0:T(8,128)(2,1)S(1)}, u32[]{:S(2)}, u32[]{:S(2)}) collective-permute-start(f16[96,2560]{1,0:T(8,128)(2,1)S(1)} %multiply_convert_fusion.6), channel_id=1, source_target_pairs={{0,2},{1,3},{2,0},{3,1},{4,6},{5,7},{6,4},{7,5},{8,10},{9,11},{10,... | collective-permute-start | bytes 1474568 | tf_op jit(solution)/shard_map/ppermute | solution.py:24
  70.3 19.3 %collective-permute-start.22 = (f16[96,2560]{1,0:T(8,128)(2,1)S(1)}, f16[96,2560]{1,0:T(8,128)(2,1)S(1)}, u32[]{:S(2)}, u32[]{:S(2)}) collective-permute-start(f16[96,2560]{1,0:T(8,128)(2,1)S(1)} %get-tuple-element.104), channel_id=1, source_target_pairs={{0,1},{1,0},{2,3},{3,2},{4,5},{5,4},{6,7},{7,6},{8,9},{9,8},{10,11... | collective-permute-start | bytes 1474568 | tf_op jit(solution)/shard_map/ppermute | solution.py:24
  70.3 19.3 %collective-permute-start.24 = (f16[96,2560]{1,0:T(8,128)(2,1)S(1)}, f16[96,2560]{1,0:T(8,128)(2,1)S(1)}, u32[]{:S(2)}, u32[]{:S(2)}) collective-permute-start(f16[96,2560]{1,0:T(8,128)(2,1)S(1)} %get-tuple-element.107), channel_id=1, source_target_pairs={{0,16},{1,17},{2,18},{3,19},{4,20},{5,21},{6,22},{7,23},{8,24},{9,... | collective-permute-start | bytes 1474568 | tf_op jit(solution)/shard_map/ppermute | solution.py:24

commit v13 on v12

--- a/solution.py
+++ b/solution.py
@@ -169,6 +169,7 @@
         return {m: [out] for m, out in zip(names, outs)}
 
     early_a, early_b = max(n_a // 4, 1), max(n_b // 4, 2)
+    ahead_b = 1 if early_b == 2 else early_b
 
     def late_first(names, first):
         late = [m for m in names if m & (1 << first) and m & ~(1 << first) & ~1]
@@ -200,9 +201,9 @@
     count = late_a + late_b + 1
     opening = pl.pallas_call(
         functools.partial(
-            end_amplitudes, [p for _, p in all_a[:late_a]], [p for _, p in all_b[:late_b]], corner, cut * early_b
+            end_amplitudes, [p for _, p in all_a[:late_a]], [p for _, p in all_b[:late_b]], corner, cut * ahead_b
         ),
-        out_shape=shared + [jax.ShapeDtypeStruct((aux,), jnp.float32)] * 4 + blocks(early_b),
+        out_shape=shared + [jax.ShapeDtypeStruct((aux,), jnp.float32)] * 4 + blocks(ahead_b),
         input_output_aliases={count + k: k for k in range(4)},
         compiler_params=pltpu.CompilerParams(vmem_limit_bytes=24 * MIB),
         cost_estimate=estimate(rows * cols),
@@ -249,7 +250,10 @@
 
     unit_b = unit_b + unit_other
     units, scales = [unit_a, unit_b], [scale_a, 1.0 / unit_b]
-    gb = chips_sum(pairs(masks_b, opening[8:]))
+    gb = pairs(masks_b, opening[8:])
+    if ahead_b < early_b:
+        gb.update(contracted(tt, acat, ahead_b, masks_b[ahead_b:early_b], "beta_first"))
+    gb = chips_sum(gb)
     ga = contracted(t, bcat, 0, masks_a[:early_a], "alpha_first")
     for level in range(max(len(bits_a), len(bits_b))):
         jobs = [

time: 91.1 us -> 90.9 us (level)
    pallas_call x3 -> x4, Pallas kernels: 3.74 us -> 4.22 us  [contracted(): pl.pallas_call(functools.partial(rows_out, start * width, cut * len(names...]
where the time goes in v13:
time: 90.9 us; the launch traced here: 90.6 us
  waiting for transfers between devices  47.8 us (53%)
  starting transfers between devices  25.2 us (28%)
  Pallas kernels  9.83 us (11%)
  other arithmetic  3.91 us (4%)
  local copies, waits for them, and re-layouts  3.03 us (3%)
    ppermute x25, waiting for transfers between devices, exchange(): lax.ppermute(value, ('grp', 'slab'), [(d, d ^ 1 << bit) for d in range(de...  47.8 us
    ppermute x25, starting transfers between devices, exchange(): lax.ppermute(value, ('grp', 'slab'), [(d, d ^ 1 << bit) for d in range(de...  25.2 us
    pallas_call x4, Pallas kernels, contracted(): pl.pallas_call(functools.partial(rows_out, start * width, cut * len(names...  4.22 us
    reshape x2, other arithmetic, whole(): return parts[0].reshape(orbital_alpha.shape)  2.51 us
    pallas_call x1, Pallas kernels, body(): pl.pallas_call(functools.partial(begin_amplitudes, [p for _, p in all_a[l...  2.4 us
    pallas_call x1, Pallas kernels, body(): pl.pallas_call(functools.partial(end_amplitudes, [p for _, p in all_a[:la...  2.37 us
  transfers between devices with their start and end apart: 25, of which 11 were waited for; matrix products, arithmetic and copies ran while one was open for 5% of the time, Pallas kernels for 8%

profile of v13, /device:TPU:0, one launch (start us, length us, event | category | flops | bytes accessed | tf_op | source)
XLA Modules:
  0.0 90.6 jit_solution(17154602730702118049)
XLA Ops:
  0.6 4.1 %collective-permute-start.2 = (bf16[96,2560]{1,0:T(8,128)(2,1)}, bf16[96,2560]{1,0:T(8,128)(2,1)S(1)}, u32[]{:S(2)}, u32[]{:S(2)}) collective-permute-start(bf16[96,2560]{1,0:T(8,128)(2,1)} %bitcast.7), channel_id=1, source_target_pairs={{0,8},{1,9},{2,10},{3,11},{4,12},{5,13},{6,14},{7,15},{8,0},{9,1},... | collective-permute-start | bytes 1474568 | tf_op jit(solution)/shard_map/ppermute | solution.py:24
  4.8 1.5 %collective-permute-start.1 = (bf16[96,2560]{1,0:T(8,128)(2,1)}, bf16[96,2560]{1,0:T(8,128)(2,1)S(1)}, u32[]{:S(2)}, u32[]{:S(2)}) collective-permute-start(bf16[96,2560]{1,0:T(8,128)(2,1)} %bitcast.8), channel_id=1, source_target_pairs={{0,2},{1,3},{2,0},{3,1},{4,6},{5,7},{6,4},{7,5},{8,10},{9,11},{10,... | collective-permute-start | bytes 1474568 | tf_op jit(solution)/shard_map/ppermute | solution.py:24
  6.2 1.6 %collective-permute-start.3 = (bf16[96,2560]{1,0:T(8,128)(2,1)}, bf16[96,2560]{1,0:T(8,128)(2,1)S(1)}, u32[]{:S(2)}, u32[]{:S(2)}) collective-permute-start(bf16[96,2560]{1,0:T(8,128)(2,1)} %bitcast.10), channel_id=1, source_target_pairs={{0,4},{1,5},{2,6},{3,7},{4,0},{5,1},{6,2},{7,3},{8,12},{9,13},{10,... | collective-permute-start | bytes 1474568 | tf_op jit(solution)/shard_map/ppermute | solution.py:24
  7.8 1.5 %collective-permute-start = (bf16[96,2560]{1,0:T(8,128)(2,1)}, bf16[96,2560]{1,0:T(8,128)(2,1)}, u32[]{:S(2)}, u32[]{:S(2)}) collective-permute-start(bf16[96,2560]{1,0:T(8,128)(2,1)} %bitcast.11), channel_id=1, source_target_pairs={{0,16},{1,17},{2,18},{3,19},{4,20},{5,21},{6,22},{7,23},{8,24},{9,... | collective-permute-start | bytes 1474568 | tf_op jit(solution)/shard_map/ppermute | solution.py:24
  9.3 0.8 reshape.35.vb_ref
  10.1 1.0 %broadcast_in_dim.3.va_ref = f32[1536,1]{1,0:T(8,128)S(1)} reshape(f32[1536]{0:T(1024)} %param.10) | data formatting | bytes 12288 | tf_op jit(solution)/shard_map/broadcast_in_dim | solution.py:159
  11.1 0.6 copy-done.2
  11.7 0.7 copy-done.3
  12.4 0.8 energies.1.refs_9_.refs_3_
  13.2 13.6 %collective-permute-done.2.refs_1_ = bf16[96,2560]{1,0:T(8,128)(2,1)S(1)} collective-permute-done((bf16[96,2560]{1,0:T(8,128)(2,1)}, bf16[96,2560]{1,0:T(8,128)(2,1)S(1)}, u32[]{:S(2)}, u32[]{:S(2)}) %collective-permute-start.2) | collective-permute-done | bytes 491552 | tf_op jit(solution)/shard_map/ppermute | solution.py:24
  26.8 1.4 %collective-permute-done.3.refs_6_ = bf16[96,2560]{1,0:T(8,128)(2,1)S(1)} collective-permute-done((bf16[96,2560]{1,0:T(8,128)(2,1)}, bf16[96,2560]{1,0:T(8,128)(2,1)S(1)}, u32[]{:S(2)}, u32[]{:S(2)}) %collective-permute-start.3) | collective-permute-done | bytes 491552 | tf_op jit(solution)/shard_map/ppermute | solution.py:24
  28.2 1.6 %collective-permute-start.5 = (bf16[96,2560]{1,0:T(8,128)(2,1)S(1)}, bf16[96,2560]{1,0:T(8,128)(2,1)S(1)}, u32[]{:S(2)}, u32[]{:S(2)}) collective-permute-start(bf16[96,2560]{1,0:T(8,128)(2,1)S(1)} %collective-permute-done.3.refs_6_), channel_id=1, source_target_pairs={{0,16},{1,17},{2,18},{3,19},{4,20},{5,21},{6,22},{7,23},{8,24},{9,... | collective-permute-start | bytes 1474568 | tf_op jit(solution)/shard_map/ppermute | solution.py:24
  30.9 8.4 %collective-permute-done.5.refs_2_ = bf16[96,2560]{1,0:T(8,128)(2,1)S(1)} collective-permute-done((bf16[96,2560]{1,0:T(8,128)(2,1)S(1)}, bf16[96,2560]{1,0:T(8,128)(2,1)S(1)}, u32[]{:S(2)}, u32[]{:S(2)}) %collective-permute-start.5) | collective-permute-done | bytes 491552 | tf_op jit(solution)/shard_map/ppermute | solution.py:24
  39.3 2.4 %amplitudes_early.1 = (bf16[384,768]{1,0:T(8,128)(2,1)S(1)}, bf16[768,384]{1,0:T(8,128)(2,1)S(1)}, bf16[384,2560]{1,0:T(8,128)(2,1)S(1)}, bf16[768,2560]{1,0:T(8,128)(2,1)S(1)}, f32[8,128]{1,0:T(8,128)S(1)}) custom-call(bf16[96,2560]{1,0:T(8,128)(2,1)S(1)} %collective-permute-done.1.refs_0_, bf16[96,2560]{1,0:T(8,128)(2,1)S(1)} %collective-permute-done.2.refs_1_, ...), custom_call_target="tpu_custom_call" | custom-call | flops 671088640 | bytes 11796480 | tf_op jit(solution)/shard_map/amplitudes_early/pallas_call | solution.py:194
  41.7 2.3 %collective-permute-done.4.refs_0_ = bf16[96,2560]{1,0:T(8,128)(2,1)S(1)} collective-permute-done((bf16[96,2560]{1,0:T(8,128)(2,1)S(1)}, bf16[96,2560]{1,0:T(8,128)(2,1)S(1)}, u32[]{:S(2)}, u32[]{:S(2)}) %collective-permute-start.4) | collective-permute-done | bytes 491552 | tf_op jit(solution)/shard_map/ppermute | solution.py:24
  44.0 2.4 %amplitudes_late.1 = (bf16[384,768]{1,0:T(8,128)(2,1)S(1)}, bf16[768,384]{1,0:T(8,128)(2,1)S(1)}, bf16[384,2560]{1,0:T(8,128)(2,1)S(1)}, bf16[768,2560]{1,0:T(8,...) custom-call(bf16[96,2560]{1,0:T(8,128)(2,1)S(1)} %collective-permute, ...), custom_call_target="tpu_custom_call", output_to_operand_aliasing={{0}: (4, {}), {1}: (5, {}), {2}: (6, {}), {3}: (7, {})} | custom-call | flops 1509949440 | bytes 11796480 | tf_op jit(solution)/shard_map/amplitudes_late/pallas_call | solution.py:202
  47.1 0.8 alpha_first.1
  49.9 1.4 %collective-permute-start.12 = (f16[96,2560]{1,0:T(8,128)(2,1)S(1)}, f16[96,2560]{1,0:T(8,128)(2,1)S(1)}, u32[]{:S(2)}, u32[]{:S(2)}) collective-permute-start(f16[96,2560]{1,0:T(8,128)(2,1)S(1)} %multiply_convert_fusion.9), channel_id=1, source_target_pairs={{0,2},{1,3},{2,0},{3,1},{4,6},{5,7},{6,4},{7,5},{8,10},{9,11},{10,... | collective-permute-start | bytes 1474568 | tf_op jit(solution)/shard_map/ppermute | solution.py:24
  51.3 1.6 %collective-permute-start.13 = (f16[96,2560]{1,0:T(8,128)(2,1)S(1)}, f16[96,2560]{1,0:T(8,128)(2,1)S(1)}, u32[]{:S(2)}, u32[]{:S(2)}) collective-permute-start(f16[96,2560]{1,0:T(8,128)(2,1)S(1)} %multiply_convert_fusion.7), channel_id=1, source_target_pairs={{0,16},{1,17},{2,18},{3,19},{4,20},{5,21},{6,22},{7,23},{8,24},{9,... | collective-permute-start | bytes 1474568 | tf_op jit(solution)/shard_map/ppermute | solution.py:24
  52.9 1.7 %beta.1 = (f32[96,2560]{1,0:T(8,128)S(1)}, f32[96,2560]{1,0:T(8,128)S(1)}, f32[96,2560]{1,0:T(8,128)S(1)}, f32[96,2560]{1,0:T(8,128)S(1)}, f32[96,2560]{1,0:T(8,128)S(1)}, /*index=5*/f32[96,2560]{1,0:T(8,128)S(1)}) custom-call(bf16[768,384]{1,0:T(8,128)(2,1)S(1)} %get-tuple-element.82.left, bf16[384,2560]{1,0:T(8,128)(2,1)S(1)} %get-tuple-element.83.right), custom_call_target="tpu_custom_call" | custom-call | flops 1132462080 | bytes 7864320 | tf_op jit(solution)/shard_map/beta/pallas_call | solution.py:215
  54.9 1.3 %alpha.1 = (f32[96,2560]{1,0:T(8,128)S(1)}, f32[96,2560]{1,0:T(8,128)S(1)}, f32[96,2560]{1,0:T(8,128)S(1)}) custom-call(bf16[384,768]{1,0:T(8,128)(2,1)S(1)} %get-tuple-element.70.left, bf16[768,2560]{1,0:T(8,128)(2,1)S(1)} %get-tuple-element.71.right), custom_call_target="tpu_custom_call" | custom-call | flops 1132462080 | bytes 6881280 | tf_op jit(solution)/shard_map/alpha/pallas_call | solution.py:215
  56.2 0.7 collective-permute-start.15
  57.0 2.4 %collective-permute-start.17 = (f32[2560]{0:T(1024)S(1)}, f32[2560]{0:T(1024)S(1)}, u32[]{:S(2)}, u32[]{:S(2)}) collective-permute-start(f32[2560]{0:T(1024)S(1)} %get-tuple-element.97), channel_id=1, source_target_pairs={{0,4},{1,5},{2,6},{3,7},{4,0},{5,1},{6,2},{7,3},{8,12},{9,13},{10,... | collective-permute-start | bytes 30728 | tf_op jit(solution)/shard_map/ppermute | solution.py:24
  59.5 1.3 %collective-permute-done.15 = f32[2560]{0:T(1024)S(1)} collective-permute-done((f32[2560]{0:T(1024)S(1)}, f32[2560]{0:T(1024)S(1)}, u32[]{:S(2)}, u32[]{:S(2)}) %collective-permute-start.15) | collective-permute-done | bytes 10272 | tf_op jit(solution)/shard_map/ppermute | solution.py:24
  61.0 1.9 %collective-permute-done.12 = f16[96,2560]{1,0:T(8,128)(2,1)S(1)} collective-permute-done((f16[96,2560]{1,0:T(8,128)(2,1)S(1)}, f16[96,2560]{1,0:T(8,128)(2,1)S(1)}, u32[]{:S(2)}, u32[]{:S(2)}) %collective-permute-start.12) | collective-permute-done | bytes 491552 | tf_op jit(solution)/shard_map/ppermute | solution.py:24
  62.9 1.0 %collective-permute-done.13 = f16[96,2560]{1,0:T(8,128)(2,1)S(1)} collective-permute-done((f16[96,2560]{1,0:T(8,128)(2,1)S(1)}, f16[96,2560]{1,0:T(8,128)(2,1)S(1)}, u32[]{:S(2)}, u32[]{:S(2)}) %collective-permute-start.13) | collective-permute-done | bytes 491552 | tf_op jit(solution)/shard_map/ppermute | solution.py:24
  64.1 0.8 collective-permute-start.19
  65.4 3.1 %collective-permute-start.21 = (f16[96,2560]{1,0:T(8,128)(2,1)S(1)}, f16[96,2560]{1,0:T(8,128)(2,1)S(1)}, u32[]{:S(2)}, u32[]{:S(2)}) collective-permute-start(f16[96,2560]{1,0:T(8,128)(2,1)S(1)} %get-tuple-element.106), channel_id=1, source_target_pairs={{0,4},{1,5},{2,6},{3,7},{4,0},{5,1},{6,2},{7,3},{8,12},{9,13},{10,... | collective-permute-start | bytes 1474568 | tf_op jit(solution)/shard_map/ppermute | solution.py:24
  68.5 1.4 %collective-permute-start.18 = (f16[96,2560]{1,0:T(8,128)(2,1)S(1)}, f16[96,2560]{1,0:T(8,128)(2,1)S(1)}, u32[]{:S(2)}, u32[]{:S(2)}) collective-permute-start(f16[96,2560]{1,0:T(8,128)(2,1)S(1)} %multiply_convert_fusion.6), channel_id=1, source_target_pairs={{0,2},{1,3},{2,0},{3,1},{4,6},{5,7},{6,4},{7,5},{8,10},{9,11},{10,... | collective-permute-start | bytes 1474568 | tf_op jit(solution)/shard_map/ppermute | solution.py:24
  70.5 17.0 %collective-permute-done.19 = f16[96,2560]{1,0:T(8,128)(2,1)S(1)} collective-permute-done((f16[96,2560]{1,0:T(8,128)(2,1)S(1)}, f16[96,2560]{1,0:T(8,128)(2,1)S(1)}, u32[]{:S(2)}, u32[]{:S(2)}) %collective-permute-start.19) | collective-permute-done | bytes 491552 | tf_op jit(solution)/shard_map/ppermute | solution.py:24
  88.1 1.2 %add_bitcast_fusion.1 = f32[1,96,2560]{2,1,0:T(8,128)} fusion(f16[96,2560]{1,0:T(8,128)(2,1)S(1)} %collective-permute-done.19, f32[96,2560]{1,0:T(8,128)S(1)} %get-tuple-element.72, f16[96,2560]{1,0:T(8,128)(2,1)S(1)} %collective-permute-done.18, f32[2560]{0:T(1024)S(1)} %collective-permute-done.15, f32[2560]{0:T(1024)S(1)} %collective-permute-done.14), kind=kLoop, calls=%fused_computation.4 | loop fusion | flops 1474560 | bytes 2969600 | tf_op jit(solution)/shard_map/reshape | solution.py:300
  89.3 1.3 %add_bitcast_fusion = f32[1,96,2560]{2,1,0:T(8,128)} fusion(f16[96,2560]{1,0:T(8,128)(2,1)S(1)} %collective-permute-done.21, f16[96,2560]{1,0:T(8,128)(2,1)S(1)} %collective-permute-done.24, f32[96,2560]{1,0:T(8,128)S(1)} %get-tuple-element.90, f16[96,2560]{1,0:T(8,128)(2,1)S(1)} %collective-permute-done.22, f32[2560]{0:T(1024)S(1)} %collective-permute-done.17, ...), kind=kLoop, calls=%fused_computation | loop fusion | flops 2211840 | bytes 3471360 | tf_op jit(solution)/shard_map/reshape | solution.py:300
  (47 shorter events, 6.2 us)
Async XLA Ops:
  0.6 38.6 %copy-start = (bf16[1,96,2560]{2,1,0:T(8,128)(2,1)S(1)}, bf16[1,96,2560]{2,1,0:T(8,128)(2,1)}, u32[]{:S(2)}) copy-start(bf16[1,96,2560]{2,1,0:T(8,128)(2,1)} %param.6) | copy-start | bytes 1474564
  0.6 29.2 %copy-start.1 = (bf16[1,96,2560]{2,1,0:T(8,128)(2,1)S(1)}, bf16[1,96,2560]{2,1,0:T(8,128)(2,1)}, u32[]{:S(2)}) copy-start(bf16[1,96,2560]{2,1,0:T(8,128)(2,1)} %param.7) | copy-start | bytes 1474564
  0.6 26.2 %collective-permute-start.2 = (bf16[96,2560]{1,0:T(8,128)(2,1)}, bf16[96,2560]{1,0:T(8,128)(2,1)S(1)}, u32[]{:S(2)}, u32[]{:S(2)}) collective-permute-start(bf16[96,2560]{1,0:T(8,128)(2,1)} %bitcast.7), channel_id=1, source_target_pairs={{0,8},{1,9},{2,10},{3,11},{4,12},{5,13},{6,14},{7,15},{8,0},{9,1},... | collective-permute-start | bytes 1474568 | tf_op jit(solution)/shard_map/ppermute | solution.py:24
  4.8 22.1 %collective-permute-start.1 = (bf16[96,2560]{1,0:T(8,128)(2,1)}, bf16[96,2560]{1,0:T(8,128)(2,1)S(1)}, u32[]{:S(2)}, u32[]{:S(2)}) collective-permute-start(bf16[96,2560]{1,0:T(8,128)(2,1)} %bitcast.8), channel_id=1, source_target_pairs={{0,2},{1,3},{2,0},{3,1},{4,6},{5,7},{6,4},{7,5},{8,10},{9,11},{10,... | collective-permute-start | bytes 1474568 | tf_op jit(solution)/shard_map/ppermute | solution.py:24
  6.2 22.0 %collective-permute-start.3 = (bf16[96,2560]{1,0:T(8,128)(2,1)}, bf16[96,2560]{1,0:T(8,128)(2,1)S(1)}, u32[]{:S(2)}, u32[]{:S(2)}) collective-permute-start(bf16[96,2560]{1,0:T(8,128)(2,1)} %bitcast.10), channel_id=1, source_target_pairs={{0,4},{1,5},{2,6},{3,7},{4,0},{5,1},{6,2},{7,3},{8,12},{9,13},{10,... | collective-permute-start | bytes 1474568 | tf_op jit(solution)/shard_map/ppermute | solution.py:24
  7.8 20.4 %collective-permute-start = (bf16[96,2560]{1,0:T(8,128)(2,1)}, bf16[96,2560]{1,0:T(8,128)(2,1)}, u32[]{:S(2)}, u32[]{:S(2)}) collective-permute-start(bf16[96,2560]{1,0:T(8,128)(2,1)} %bitcast.11), channel_id=1, source_target_pairs={{0,16},{1,17},{2,18},{3,19},{4,20},{5,21},{6,22},{7,23},{8,24},{9,... | collective-permute-start | bytes 1474568 | tf_op jit(solution)/shard_map/ppermute | solution.py:24
  11.1 0.7 copy-start.2
  11.7 0.7 copy-start.3
  28.2 11.0 %collective-permute-start.5 = (bf16[96,2560]{1,0:T(8,128)(2,1)S(1)}, bf16[96,2560]{1,0:T(8,128)(2,1)S(1)}, u32[]{:S(2)}, u32[]{:S(2)}) collective-permute-start(bf16[96,2560]{1,0:T(8,128)(2,1)S(1)} %collective-permute-done.3.refs_6_), channel_id=1, source_target_pairs={{0,16},{1,17},{2,18},{3,19},{4,20},{5,21},{6,22},{7,23},{8,24},{9,... | collective-permute-start | bytes 1474568 | tf_op jit(solution)/shard_map/ppermute | solution.py:24
  29.8 9.5 %collective-permute-start.7 = (bf16[96,2560]{1,0:T(8,128)(2,1)}, bf16[96,2560]{1,0:T(8,128)(2,1)S(1)}, u32[]{:S(2)}, u32[]{:S(2)}) collective-permute-start(bf16[96,2560]{1,0:T(8,128)(2,1)} %collective-permute-done.refs_4_), channel_id=1, source_target_pairs={{0,1},{1,0},{2,3},{3,2},{4,5},{5,4},{6,7},{7,6},{8,9},{9,8},{10,11... | collective-permute-start | bytes 1474568 | tf_op jit(solution)/shard_map/ppermute | solution.py:24
  29.8 9.5 %collective-permute-start.9 = (bf16[96,2560]{1,0:T(8,128)(2,1)S(1)}, bf16[96,2560]{1,0:T(8,128)(2,1)S(1)}, u32[]{:S(2)}, u32[]{:S(2)}) collective-permute-start(bf16[96,2560]{1,0:T(8,128)(2,1)S(1)} %bitcast.12), channel_id=1, source_target_pairs={{0,1},{1,0},{2,3},{3,2},{4,5},{5,4},{6,7},{7,6},{8,9},{9,8},{10,11... | collective-permute-start | bytes 1474568 | tf_op jit(solution)/shard_map/ppermute | solution.py:24
  30.3 8.9 %collective-permute-start.8 = (bf16[96,2560]{1,0:T(8,128)(2,1)S(1)}, bf16[96,2560]{1,0:T(8,128)(2,1)S(1)}, u32[]{:S(2)}, u32[]{:S(2)}) collective-permute-start(bf16[96,2560]{1,0:T(8,128)(2,1)S(1)} %collective-permute-done.3.refs_6_), channel_id=1, source_target_pairs={{0,1},{1,0},{2,3},{3,2},{4,5},{5,4},{6,7},{7,6},{8,9},{9,8},{10,11... | collective-permute-start | bytes 1474568 | tf_op jit(solution)/shard_map/ppermute | solution.py:24
  30.3 13.6 %collective-permute-start.4 = (bf16[96,2560]{1,0:T(8,128)(2,1)S(1)}, bf16[96,2560]{1,0:T(8,128)(2,1)S(1)}, u32[]{:S(2)}, u32[]{:S(2)}) collective-permute-start(bf16[96,2560]{1,0:T(8,128)(2,1)S(1)} %collective-permute-done.2.refs_1_), channel_id=1, source_target_pairs={{0,2},{1,3},{2,0},{3,1},{4,6},{5,7},{6,4},{7,5},{8,10},{9,11},{10,... | collective-permute-start | bytes 1474568 | tf_op jit(solution)/shard_map/ppermute | solution.py:24
  39.2 4.7 %collective-permute-start.6 = (bf16[96,2560]{1,0:T(8,128)(2,1)S(1)}, bf16[96,2560]{1,0:T(8,128)(2,1)S(1)}, u32[]{:S(2)}, u32[]{:S(2)}) collective-permute-start(bf16[96,2560]{1,0:T(8,128)(2,1)S(1)} %collective-permute-done.5.refs_2_), channel_id=1, source_target_pairs={{0,1},{1,0},{2,3},{3,2},{4,5},{5,4},{6,7},{7,6},{8,9},{9,8},{10,11... | collective-permute-start | bytes 1474568 | tf_op jit(solution)/shard_map/ppermute | solution.py:24
  46.3 2.1 %collective-permute-start.11 = (f32[2560]{0:T(1024)S(1)}, f32[2560]{0:T(1024)S(1)}, u32[]{:S(2)}, u32[]{:S(2)}) collective-permute-start(f32[2560]{0:T(1024)S(1)} %get-tuple-element.68), channel_id=1, source_target_pairs={{0,1},{1,0},{2,3},{3,2},{4,5},{5,4},{6,7},{7,6},{8,9},{9,8},{10,11... | collective-permute-start | bytes 30728 | tf_op jit(solution)/shard_map/ppermute | solution.py:24
  46.5 2.1 %collective-permute-start.10 = (f16[96,2560]{1,0:T(8,128)(2,1)S(1)}, f16[96,2560]{1,0:T(8,128)(2,1)S(1)}, u32[]{:S(2)}, u32[]{:S(2)}) collective-permute-start(f16[96,2560]{1,0:T(8,128)(2,1)S(1)} %multiply_convert_fusion.8), channel_id=1, source_target_pairs={{0,1},{1,0},{2,3},{3,2},{4,5},{5,4},{6,7},{7,6},{8,9},{9,8},{10,11... | collective-permute-start | bytes 1474568 | tf_op jit(solution)/shard_map/ppermute | solution.py:24
  48.7 7.4 %collective-permute-start.14 = (f32[2560]{0:T(1024)S(1)}, f32[2560]{0:T(1024)S(1)}, u32[]{:S(2)}, u32[]{:S(2)}) collective-permute-start(f32[2560]{0:T(1024)S(1)} %get-tuple-element.76), channel_id=1, source_target_pairs={{0,2},{1,3},{2,0},{3,1},{4,6},{5,7},{6,4},{7,5},{8,10},{9,11},{10,... | collective-permute-start | bytes 30728 | tf_op jit(solution)/shard_map/ppermute | solution.py:24
  49.4 7.6 %collective-permute-start.16 = (f32[2560]{0:T(1024)S(1)}, f32[2560]{0:T(1024)S(1)}, u32[]{:S(2)}, u32[]{:S(2)}) collective-permute-start(f32[2560]{0:T(1024)S(1)} %get-tuple-element.77), channel_id=1, source_target_pairs={{0,16},{1,17},{2,18},{3,19},{4,20},{5,21},{6,22},{7,23},{8,24},{9,... | collective-permute-start | bytes 30728 | tf_op jit(solution)/shard_map/ppermute | solution.py:24
  49.9 13.1 %collective-permute-start.12 = (f16[96,2560]{1,0:T(8,128)(2,1)S(1)}, f16[96,2560]{1,0:T(8,128)(2,1)S(1)}, u32[]{:S(2)}, u32[]{:S(2)}) collective-permute-start(f16[96,2560]{1,0:T(8,128)(2,1)S(1)} %multiply_convert_fusion.9), channel_id=1, source_target_pairs={{0,2},{1,3},{2,0},{3,1},{4,6},{5,7},{6,4},{7,5},{8,10},{9,11},{10,... | collective-permute-start | bytes 1474568 | tf_op jit(solution)/shard_map/ppermute | solution.py:24
  51.3 12.6 %collective-permute-start.13 = (f16[96,2560]{1,0:T(8,128)(2,1)S(1)}, f16[96,2560]{1,0:T(8,128)(2,1)S(1)}, u32[]{:S(2)}, u32[]{:S(2)}) collective-permute-start(f16[96,2560]{1,0:T(8,128)(2,1)S(1)} %multiply_convert_fusion.7), channel_id=1, source_target_pairs={{0,16},{1,17},{2,18},{3,19},{4,20},{5,21},{6,22},{7,23},{8,24},{9,... | collective-permute-start | bytes 1474568 | tf_op jit(solution)/shard_map/ppermute | solution.py:24
  56.2 4.7 %collective-permute-start.15 = (f32[2560]{0:T(1024)S(1)}, f32[2560]{0:T(1024)S(1)}, u32[]{:S(2)}, u32[]{:S(2)}) collective-permute-start(f32[2560]{0:T(1024)S(1)} %get-tuple-element.99), channel_id=1, source_target_pairs={{0,8},{1,9},{2,10},{3,11},{4,12},{5,13},{6,14},{7,15},{8,0},{9,1},... | collective-permute-start | bytes 30728 | tf_op jit(solution)/shard_map/ppermute | solution.py:24
  57.0 4.1 %collective-permute-start.17 = (f32[2560]{0:T(1024)S(1)}, f32[2560]{0:T(1024)S(1)}, u32[]{:S(2)}, u32[]{:S(2)}) collective-permute-start(f32[2560]{0:T(1024)S(1)} %get-tuple-element.97), channel_id=1, source_target_pairs={{0,4},{1,5},{2,6},{3,7},{4,0},{5,1},{6,2},{7,3},{8,12},{9,13},{10,... | collective-permute-start | bytes 30728 | tf_op jit(solution)/shard_map/ppermute | solution.py:24
  59.4 5.5 %collective-permute-start.20 = (f16[96,2560]{1,0:T(8,128)(2,1)S(1)}, f16[96,2560]{1,0:T(8,128)(2,1)S(1)}, u32[]{:S(2)}, u32[]{:S(2)}) collective-permute-start(f16[96,2560]{1,0:T(8,128)(2,1)S(1)} %get-tuple-element.103), channel_id=1, source_target_pairs={{0,1},{1,0},{2,3},{3,2},{4,5},{5,4},{6,7},{7,6},{8,9},{9,8},{10,11... | collective-permute-start | bytes 1474568 | tf_op jit(solution)/shard_map/ppermute | solution.py:24
  60.9 4.1 %collective-permute-start.23 = (f16[96,2560]{1,0:T(8,128)(2,1)S(1)}, f16[96,2560]{1,0:T(8,128)(2,1)S(1)}, u32[]{:S(2)}, u32[]{:S(2)}) collective-permute-start(f16[96,2560]{1,0:T(8,128)(2,1)S(1)} %get-tuple-element.104), channel_id=1, source_target_pairs={{0,1},{1,0},{2,3},{3,2},{4,5},{5,4},{6,7},{7,6},{8,9},{9,8},{10,11... | collective-permute-start | bytes 1474568 | tf_op jit(solution)/shard_map/ppermute | solution.py:24
  64.1 23.3 %collective-permute-start.19 = (f16[96,2560]{1,0:T(8,128)(2,1)S(1)}, f16[96,2560]{1,0:T(8,128)(2,1)S(1)}, u32[]{:S(2)}, u32[]{:S(2)}) collective-permute-start(f16[96,2560]{1,0:T(8,128)(2,1)S(1)} %multiply_convert_fusion.5), channel_id=1, source_target_pairs={{0,8},{1,9},{2,10},{3,11},{4,12},{5,13},{6,14},{7,15},{8,0},{9,1},... | collective-permute-start | bytes 1474568 | tf_op jit(solution)/shard_map/ppermute | solution.py:24
  65.4 22.7 %collective-permute-start.21 = (f16[96,2560]{1,0:T(8,128)(2,1)S(1)}, f16[96,2560]{1,0:T(8,128)(2,1)S(1)}, u32[]{:S(2)}, u32[]{:S(2)}) collective-permute-start(f16[96,2560]{1,0:T(8,128)(2,1)S(1)} %get-tuple-element.106), channel_id=1, source_target_pairs={{0,4},{1,5},{2,6},{3,7},{4,0},{5,1},{6,2},{7,3},{8,12},{9,13},{10,... | collective-permute-start | bytes 1474568 | tf_op jit(solution)/shard_map/ppermute | solution.py:24
  68.5 19.6 %collective-permute-start.18 = (f16[96,2560]{1,0:T(8,128)(2,1)S(1)}, f16[96,2560]{1,0:T(8,128)(2,1)S(1)}, u32[]{:S(2)}, u32[]{:S(2)}) collective-permute-start(f16[96,2560]{1,0:T(8,128)(2,1)S(1)} %multiply_convert_fusion.6), channel_id=1, source_target_pairs={{0,2},{1,3},{2,0},{3,1},{4,6},{5,7},{6,4},{7,5},{8,10},{9,11},{10,... | collective-permute-start | bytes 1474568 | tf_op jit(solution)/shard_map/ppermute | solution.py:24
  70.0 19.3 %collective-permute-start.22 = (f16[96,2560]{1,0:T(8,128)(2,1)S(1)}, f16[96,2560]{1,0:T(8,128)(2,1)S(1)}, u32[]{:S(2)}, u32[]{:S(2)}) collective-permute-start(f16[96,2560]{1,0:T(8,128)(2,1)S(1)} %get-tuple-element.102), channel_id=1, source_target_pairs={{0,1},{1,0},{2,3},{3,2},{4,5},{5,4},{6,7},{7,6},{8,9},{9,8},{10,11... | collective-permute-start | bytes 1474568 | tf_op jit(solution)/shard_map/ppermute | solution.py:24
  70.0 19.3 %collective-permute-start.24 = (f16[96,2560]{1,0:T(8,128)(2,1)S(1)}, f16[96,2560]{1,0:T(8,128)(2,1)S(1)}, u32[]{:S(2)}, u32[]{:S(2)}) collective-permute-start(f16[96,2560]{1,0:T(8,128)(2,1)S(1)} %get-tuple-element.105), channel_id=1, source_target_pairs={{0,16},{1,17},{2,18},{3,19},{4,20},{5,21},{6,22},{7,23},{8,24},{9,... | collective-permute-start | bytes 1474568 | tf_op jit(solution)/shard_map/ppermute | solution.py:24
